TPU v7x, 32 devices: a whole 2x2x4 slice. The times are simulated.
32 devices in a mesh: group: 4 (over x, core), fsdp: 4 (over z), tp: 2 (over y).
Axes of the slice: x: 2, y: 2, z: 4, core: 2. Of those that a mesh axis runs over, the one named last changes fastest.
Arguments:
- tokens: bfloat16 [128, 4, 5120], P(('group', 'fsdp')), may hold values from -6 to 6
- queries: bfloat16 [128, 4, 5120], P(('group', 'fsdp'), None, 'tp'), may hold values from -6 to 6
- cache_keys: bfloat16 [128, 512, 1024], P(('group', 'fsdp'), None, 'tp'), may hold values from -6 to 6
- cache_values: bfloat16 [128, 512, 1024], P(('group', 'fsdp'), None, 'tp'), may hold values from -6 to 6
- lengths: int32 [128], P(('group', 'fsdp')), may hold values from 16 to 512, as said below
- weights: float32 [5120, 2048], P(('fsdp', 'tp')), may hold values from -0.078125 to 0.078125
- moment1: float32 [5120, 2048], P(('fsdp', 'tp')), may hold values from -3 to 3
- moment2: float32 [5120, 2048], P(('fsdp', 'tp')), may hold values from 0.25 to 4
- grad_parts: float32 [4, 5120, 2048], P('group', ('fsdp', 'tp')), may hold values from -2 to 2
Outputs:
- new_weights: float32 [5120, 2048], P(('fsdp', 'tp'))
- new_moment1: float32 [5120, 2048], P(('fsdp', 'tp'))
- new_moment2: float32 [5120, 2048], P(('fsdp', 'tp'))
- new_kv: bfloat16 [128, 4, 2048], P(('group', 'fsdp'), None, 'tp')
- context: bfloat16 [128, 4, 5120], P(('group', 'fsdp'), None, 'tp')
Inputs may be any that keep to these rules, and one draw needn't show every extreme that they name: Row r's cache holds lengths[r] valid slots; some row holds 512.
All inputs are finite; a program needn't handle non-finite values.
Results may differ from a plain program's by a relative error of at most 0.0065.
Values may be sent and summed in bfloat16 or wider, within the bound.
No kernel may reach another device: no remote copies, remote signals or barrier semaphores. Data moves between devices by JAX's collectives and lax.ppermute only.
A program may use at most 128 MiB of HBM per device.

v0:
```python
import math

import jax
import jax.numpy as jnp
from jax import lax
from jax.sharding import PartitionSpec as P

QH = 40
KVH = 8
HD = 128
STEPS = 4


beta_one = 0.9
beta_two = 0.95
learning_rate = 0.004
decay_rate = 0.1
epsilon = 1e-08
correct_one = 1.0 - 0.9**10
correct_two = 1.0 - 0.95**10
masked_score = -1e30


def adam_update(weights, moment1, moment2, gradient):
    new_moment1 = beta_one * moment1 + (1.0 - beta_one) * gradient
    new_moment2 = beta_two * moment2 + (1.0 - beta_two) * gradient * gradient
    direction = new_moment1 / correct_one / (jnp.sqrt(new_moment2 / correct_two) + epsilon)
    new_weights = weights - learning_rate * (direction + decay_rate * weights)
    return (new_weights, new_moment1, new_moment2)


def rotate_keys(keys, positions):
    half_width = keys.shape[-1] // 2
    frequency = jnp.power(
        jnp.float32(1000000.0), -2.0 * jnp.arange(half_width, dtype=jnp.float32) / keys.shape[-1]
    )
    angles = positions[..., None] * frequency
    leading = keys[..., :half_width]
    trailing = keys[..., half_width:]
    cosine = jnp.cos(angles)
    sine_part = jnp.sin(angles)
    return jnp.concatenate(
        [leading * cosine - trailing * sine_part, trailing * cosine + leading * sine_part], axis=-1
    )


def shards(
    tokens, queries, cache_keys, cache_values, lengths, weights, moment1, moment2, grad_parts
):
    gradient = lax.psum(grad_parts[0], "group")
    new_weights, new_moment1, new_moment2 = adam_update(weights, moment1, moment2, gradient)
    weight_shard = new_weights.astype(jnp.bfloat16)
    tp_count = lax.axis_size("tp")
    fsdp_count = lax.axis_size("fsdp")
    head_cols = weight_shard.shape[1] // tp_count
    row_count = tokens.shape[0]
    block_rows = weight_shard.shape[0]
    split_tokens = tokens.reshape(row_count, STEPS, fsdp_count, tp_count, block_rows)
    own_columns = lax.dynamic_index_in_dim(split_tokens, lax.axis_index("tp"), 3, keepdims=False)
    arrived = lax.all_to_all(own_columns, "fsdp", split_axis=2, concat_axis=0, tiled=True)
    arrived = arrived.reshape(fsdp_count * row_count * STEPS, block_rows)
    partial_terms = jnp.dot(arrived, weight_shard, preferred_element_type=jnp.float32)
    partial_terms = partial_terms.reshape(fsdp_count, row_count * STEPS, tp_count, head_cols)
    partial_terms = partial_terms.transpose(0, 2, 1, 3).reshape(
        fsdp_count * tp_count * row_count * STEPS, head_cols
    )
    projected = lax.psum_scatter(partial_terms, ("fsdp", "tp"), scatter_dimension=0, tiled=True)
    kv_heads = head_cols // (2 * HD)
    projected = projected.reshape(row_count, STEPS, kv_heads, 2, HD)
    positions = (lengths[:, None] + jnp.arange(STEPS, dtype=jnp.int32)[None, :]).astype(jnp.float32)
    new_keys = rotate_keys(projected[:, :, :, 0], positions[:, :, None])
    fresh = jnp.stack([new_keys, projected[:, :, :, 1]], axis=3).astype(jnp.bfloat16)
    new_kv = fresh.reshape(row_count, STEPS, head_cols)
    per_group = QH // KVH
    score_scale = 1.0 / math.sqrt(HD)
    span_length = cache_keys.shape[1]
    grouped = queries.reshape(row_count, STEPS, kv_heads, per_group, HD)
    cached_keys = cache_keys.reshape(row_count, span_length, kv_heads, HD)
    cached_values = cache_values.reshape(row_count, span_length, kv_heads, HD)
    new_scores = (
        jnp.einsum(
            "risgd,rjsd->risgj", grouped, fresh[:, :, :, 0], preferred_element_type=jnp.float32
        )
        * score_scale
    )
    causal = jnp.arange(STEPS)[:, None] >= jnp.arange(STEPS)[None, :]
    new_scores = jnp.where(causal[None, :, None, None, :], new_scores, masked_score)
    scores = (
        jnp.einsum("risgd,rpsd->risgp", grouped, cached_keys, preferred_element_type=jnp.float32)
        * score_scale
    )
    in_range = jnp.arange(span_length, dtype=jnp.int32)[None, :] < lengths[:, None]
    all_scores = jnp.concatenate(
        [jnp.where(in_range[:, None, None, None, :], scores, masked_score), new_scores], axis=-1
    )
    highest = jnp.max(all_scores, axis=-1, keepdims=True)
    exponent = jnp.exp(all_scores - highest)
    probs = (exponent / jnp.sum(exponent, axis=-1, keepdims=True)).astype(jnp.bfloat16)
    context = jnp.einsum(
        "risgp,rpsd->risgd",
        probs[..., :span_length],
        cached_values,
        preferred_element_type=jnp.float32,
    )
    context = context + jnp.einsum(
        "risgj,rjsd->risgd",
        probs[..., span_length:],
        fresh[:, :, :, 1],
        preferred_element_type=jnp.float32,
    )
    context = context.reshape(row_count, STEPS, kv_heads * per_group * HD).astype(jnp.bfloat16)
    return (new_weights, new_moment1, new_moment2, new_kv, context)


def solution(mesh):
    in_specs = (
        P(("group", "fsdp"), None, None),
        P(("group", "fsdp"), None, "tp"),
        P(("group", "fsdp"), None, "tp"),
        P(("group", "fsdp"), None, "tp"),
        P(("group", "fsdp")),
        P(("fsdp", "tp"), None),
        P(("fsdp", "tp"), None),
        P(("fsdp", "tp"), None),
        P("group", ("fsdp", "tp"), None),
    )
    out_specs = (
        P(("fsdp", "tp"), None),
        P(("fsdp", "tp"), None),
        P(("fsdp", "tp"), None),
        P(("group", "fsdp"), None, "tp"),
        P(("group", "fsdp"), None, "tp"),
    )
    return jax.shard_map(shards, mesh=mesh, in_specs=in_specs, out_specs=out_specs, check_vma=False)
```

profile of v0, /device:TPU:0, one launch (start us, length us, event | category | flops | bytes accessed | tf_op | source)
XLA Modules:
  0.0 215.4 jit_solution(5069798997488527414)
XLA Ops:
  7.2 0.7 all-reduce.2.cloned.1.call-update
  8.3 0.3 constant_dynamic-slice_fusion
  8.7 13.1 %all_to_all.15 = bf16[8,4,4,640]{3,1,0,2:T(4,128)(2,1)S(1)} all-to-all(bf16[8,4,4,640]{3,1,0,2:T(4,128)(2,1)S(1)} %bitcast.59), channel_id=1, replica_groups=mesh['group'=4,'fsdp'=4,'tp'=2] {'fsdp'}, dimensions={2} | all-to-all | bytes 327680 | tf_op jit(solution)/shard_map/all_to_all | solution.py:60
  21.8 93.8 %all-reduce.2.cloned.1.call-done = f32[640,2048]{1,0:T(8,128)} async-done(((f32[640,2048]{1,0:T(8,128)}), f32[640,2048]{1,0:T(8,128)}) %all-reduce.2.cloned.1.call-update) | async-done | bytes 5242896 | tf_op jit(solution)/shard_map/psum | solution.py:50
  115.6 13.7 %convert_bitcast_fusion = (bf16[2048,640]{0,1:T(8,128)(2,1)S(1)}, f32[640,2048]{1,0:T(8,128)}, f32[640,2048]{1,0:T(8,128)}, f32[640,2048]{1,0:T(8,128)}) fusion(f32[640,2048]{1,0:T(8,128)} %param.14, f32[640,2048]{1,0:T(8,128)} %all-reduce.2.cloned.1.call-done, f32[640,2048]{1,0:T(8,128)} %param.15, f32[640,2048]{1,0:T(8,128)} %param.16), kind=kLoop, calls=%fused_computation.11 | loop fusion | flops 20971520 | bytes 39321600 | tf_op jit(solution)/shard_map/dot_general | solution.py:62
  129.3 2.6 %copy.93 = bf16[2048,640]{1,0:T(8,128)(2,1)} copy(bf16[2048,640]{0,1:T(8,128)(2,1)S(1)} %get-tuple-element.27) | data formatting | bytes 5242880 | tf_op jit(solution)/shard_map/dot_general | solution.py:62
  131.9 3.8 %fusion.19 = f32[4,32,2,1024]{3,1,2,0:T(8,128)} fusion(bf16[2,1024,640,1]{2,1,0,3:T(8,128)(2,1)} %bitcast.56, bf16[4,32,640,1]{2,1,0,3:T(8,128)(2,1)S(1)} %reshape.115), kind=kOutput, calls=%fused_computation.24 | convolution fusion | flops 335544320 | bytes 3833856 | tf_op jit(solution)/shard_map/dot_general | solution.py:62
  135.7 0.2 reshape.124
  135.9 6.9 %reshape.112 = bf16[8,512,4,128]{3,2,1,0:T(4,128)(2,1)} reshape(bf16[8,512,512]{2,1,0:T(8,128)(2,1)} %param.11) | data formatting | bytes 8388608 | tf_op jit(solution)/shard_map/reshape | solution.py:78
  142.9 7.0 %reshape.114 = bf16[8,512,4,128]{3,2,1,0:T(4,128)(2,1)} reshape(bf16[8,512,512]{2,1,0:T(8,128)(2,1)} %param.12) | data formatting | bytes 8388608 | tf_op jit(solution)/shard_map/reshape | solution.py:79
  150.0 0.2 multiply_cosine_fusion
  150.2 3.8 %fusion.23 = (f32[8,4,4,5]{3,1,2,0:T(4,128)S(1)}, f32[8,4,4,5,512]{4,3,1,2,0:T(8,128)S(1)}) fusion(bf16[8,4,4,5,128]{4,3,2,1,0:T(8,128)(2,1)S(1)} %reshape.124, bf16[8,512,4,128,1]{3,2,1,0,4:T(4,128)(2,1)} %bitcast.55, pred[8,512]{1,0:T(8,128)(4,1)S(1)} %iota_compare_fusion), kind=kOutput, calls=%fused_computation.42 | convolution fusion | flops 84868480 | bytes 5675520 | tf_op jit(solution)/shard_map/risgd,rpsd->risgp/dot_general | solution.py:89
  154.0 45.6 %reduce-scatter.2.cloned.1.call-done = f32[32,1024]{1,0:T(8,128)} async-done(((f32[256,1024]{1,0:T(8,128)}), f32[32,1024]{1,0:T(8,128)}) %reduce-scatter.2.cloned.1.call-update) | async-done | bytes 131088 | tf_op jit(solution)/shard_map/reduce_scatter | solution.py:67
  199.6 1.0 reshape.111
  201.0 1.2 fusion.16
  202.4 0.5 copy.79
  203.2 0.6 copy.80
  203.8 0.8 fusion.6
  204.6 0.6 divide_convert_fusion
  205.2 0.8 copy-done
  206.0 0.9 fusion.10
  206.9 0.2 fusion.13
  207.2 0.8 reshape.123
  208.0 0.6 reshape.122
  (29 shorter events, 1.6 us)
Async XLA Ops:
  7.2 1.0 copy-start.1
  7.2 108.5 %all-reduce.2.cloned.1.call-start = ((), (), s32[]{:S(2)}) async-start(), calls=%async_computation.2 | async-start | bytes 10485760 | tf_op jit(solution)/shard_map/psum | solution.py:50
  7.9 191.7 %reduce-scatter.2.cloned.1.call-start = ((), (), s32[]{:S(2)}) async-start(), calls=%async_computation.3 | async-start | bytes 1179648 | tf_op jit(solution)/shard_map/reduce_scatter | solution.py:67
  131.9 3.8 %copy-start.2 = (bf16[8,4,2560]{2,1,0:T(4,128)(2,1)S(1)}, bf16[8,4,2560]{2,1,0:T(4,128)(2,1)}, u32[]{:S(2)}) copy-start(bf16[8,4,2560]{2,1,0:T(4,128)(2,1)} %param.10) | copy-start | bytes 491524
  142.9 7.0 %copy-start.3 = (s32[8]{0:T(128)S(1)}, s32[8]{0:T(128)}, u32[]{:S(2)}) copy-start(s32[8]{0:T(128)} %param.13) | copy-start | bytes 100
  203.8 2.2 %copy-start = (bf16[8,512,4,128]{3,2,1,0:T(4,128)(2,1)S(1)}, bf16[8,512,4,128]{3,2,1,0:T(4,128)(2,1)}, u32[]{:S(2)}) copy-start(bf16[8,512,4,128]{3,2,1,0:T(4,128)(2,1)} %reshape.114) | copy-start | bytes 12582916
Sparse Core Ops, SparseCore 0:
  10.4 105.2 all-reduce.1
  135.9 63.6 reduce-scatter.1
where the time goes:
time: 216 us; the launch traced here: 215 us
  waiting for transfers between devices  140 us (65%)
  local copies, waits for them, and re-layouts  22.2 us (10%)
  other arithmetic  15.8 us (7%)
  between operations  14.2 us (7%)
  blocking collectives  13.1 us (6%)
  matrix products  10 us (5%)
    psum x1, waiting for transfers between devices, shards(): gradient = lax.psum(grad_parts[0], 'group')  93.8 us
    reduce_scatter x1, waiting for transfers between devices, shards(): lax.psum_scatter(partial_terms, ('fsdp', 'tp'), scatter_dimension=0, tile...  45.6 us
    dot_general x1, other arithmetic, shards(): jnp.dot(arrived, weight_shard, preferred_element_type=jnp.float32)  13.7 us
    all_to_all x1, blocking collectives, shards(): lax.all_to_all(own_columns, 'fsdp', split_axis=2, concat_axis=0, tiled=True)  13.1 us
    reshape x1, local copies, waits for them, and re-layouts, shards(): cached_values = cache_values.reshape(row_count, span_length, kv_heads, HD)  6.95 us
    reshape x1, local copies, waits for them, and re-layouts, shards(): cached_keys = cache_keys.reshape(row_count, span_length, kv_heads, HD)  6.93 us
  transfers between devices with their start and end apart: 2, of which 2 were waited for; matrix products, arithmetic and copies ran while one was open for 9% of the time, Pallas kernels for 0%

commit v1 on v0

--- a/solution.py
+++ b/solution.py
@@ -1,14 +1,19 @@
+import functools
 import math
 
 import jax
 import jax.numpy as jnp
 from jax import lax
+from jax.experimental import pallas as pl
+from jax.experimental.pallas import tpu as pltpu
 from jax.sharding import PartitionSpec as P
 
 QH = 40
 KVH = 8
 HD = 128
 STEPS = 4
+PER_GROUP = QH // KVH
+HEAD_COLS = 2 * HD
 
 
 beta_one = 0.9
@@ -19,6 +24,8 @@
 correct_one = 1.0 - 0.9**10
 correct_two = 1.0 - 0.95**10
 masked_score = -1e30
+score_scale = 1.0 / math.sqrt(HD)
+VMEM_LIMIT = 40 * 1024 * 1024
 
 
 def adam_update(weights, moment1, moment2, gradient):
@@ -27,6 +34,314 @@
     direction = new_moment1 / correct_one / (jnp.sqrt(new_moment2 / correct_two) + epsilon)
     new_weights = weights - learning_rate * (direction + decay_rate * weights)
     return (new_weights, new_moment1, new_moment2)
+
+
+def rotation_tables(lengths):
+    half_width = HD // 2
+    frequency = jnp.power(
+        jnp.float32(1000000.0), -2.0 * jnp.arange(half_width, dtype=jnp.float32) / HD
+    )
+    positions = (lengths[:, None] + jnp.arange(STEPS, dtype=jnp.int32)[None, :]).astype(jnp.float32)
+    angles = positions.reshape(-1)[:, None] * frequency
+    cosine = jnp.cos(angles)
+    sine = jnp.sin(angles)
+    return (
+        jnp.concatenate([cosine, cosine], axis=-1),
+        jnp.concatenate([-sine, sine], axis=-1),
+    )
+
+
+def adam_kernel(n_parts, n_tok, place, *refs):
+    totals = refs[:n_parts]
+    w, m1, m2 = refs[n_parts : n_parts + 3]
+    toks = refs[n_parts + 3 : n_parts + 3 + n_tok]
+    new_w, new_m1, new_m2 = refs[-3 - n_parts : -n_parts]
+    sums = refs[-n_parts:]
+    part = pl.program_id(0)
+    cols = pl.program_id(1)
+    for j in range(n_parts):
+
+        @pl.when(part == j)
+        def _():
+            gradient = totals[j][...].astype(jnp.float32)
+            weights, moment1, moment2 = adam_update(w[...], m1[...], m2[...], gradient)
+            new_w[...] = weights
+            new_m1[...] = moment1
+            new_m2[...] = moment2
+            rollout = weights.astype(jnp.bfloat16)
+            tok = jnp.concatenate([t[...] for t in toks], axis=0)
+            terms = jnp.dot(tok, rollout, preferred_element_type=jnp.float32)
+            sums[j][:, pl.ds(pl.multiple_of(cols * HD, HD), HD)] = terms.astype(jnp.bfloat16)
+
+
+def adam_and_project(place, parts, totals, weights, moment1, moment2, toks, previous, chunk, n_chunks):
+    rows, width = weights.shape
+    per_head = HEAD_COLS // HD
+    n = len(parts)
+
+    def column(j, b, place):
+        half = jnp.int32(0)
+        for i, p in enumerate(parts):
+            half = jnp.where(j == i, place[0] if p == 0 else 1 - place[0], half)
+        return (0, (half * n_chunks + chunk) * per_head + b)
+
+    def total_map(i):
+        return lambda j, b, place: (0, jnp.where(j == i, b, jnp.where(j < i, 0, per_head - 1)))
+
+    block = pl.BlockSpec((rows, HD), column)
+    n_tokens = sum(t.shape[0] for t in toks)
+    whole = lambda shape: pl.BlockSpec(shape, lambda j, b, place: (0,) * len(shape))
+    in_specs = (
+        [pl.BlockSpec((rows, HD), total_map(i)) for i in range(n)]
+        + [block] * 3
+        + [whole(t.shape) for t in toks]
+    )
+    operands = [*totals, weights, moment1, moment2, *toks]
+    aliases = {}
+    if previous is not None:
+        for i, p in enumerate(previous):
+            aliases[1 + len(operands)] = i
+            operands.append(p)
+            in_specs.append(pl.BlockSpec(memory_space=pl.ANY))
+    full = jax.ShapeDtypeStruct((rows, width), jnp.float32)
+    out = pl.pallas_call(
+        functools.partial(adam_kernel, n, len(toks)),
+        grid_spec=pltpu.PrefetchScalarGridSpec(
+            num_scalar_prefetch=1,
+            grid=(n, per_head),
+            in_specs=in_specs,
+            out_specs=[block] * 3 + [whole((n_tokens, HEAD_COLS))] * n,
+        ),
+        out_shape=[full] * 3 + [jax.ShapeDtypeStruct((n_tokens, HEAD_COLS), jnp.bfloat16)] * n,
+        input_output_aliases=aliases,
+        compiler_params=pltpu.CompilerParams(vmem_limit_bytes=VMEM_LIMIT),
+        cost_estimate=pl.CostEstimate(
+            flops=2 * n_tokens * rows * HEAD_COLS * n,
+            bytes_accessed=26 * rows * HEAD_COLS * n,
+            transcendentals=0,
+        ),
+        name="adam_project",
+    )(place, *operands)
+    return tuple(out[:3]), tuple(out[3:])
+
+
+SLOT = 32
+
+
+def cache_kernel(heads, lens, q, k, v, stacked, acc, stats):
+    row = pl.program_id(0)
+    length = lens[row]
+    query = q[0].astype(jnp.float32)
+    used = PER_GROUP * STEPS
+    blocks = []
+    for h in range(heads):
+        pieces = [
+            query[:, (h * PER_GROUP + g) * HD : (h * PER_GROUP + g + 1) * HD] for g in range(PER_GROUP)
+        ]
+        pieces.append(jnp.zeros((SLOT - used, HD), jnp.float32))
+        one = jnp.concatenate(pieces, axis=0).astype(jnp.bfloat16)
+        stacked[h, 0] = one
+        blocks.append(one)
+    keys = k[0]
+    values = v[0]
+    span = keys.shape[0]
+    in_range = lax.broadcasted_iota(jnp.int32, (1, span), 1) < length
+    for h in range(heads):
+        cols = slice(h * HD, (h + 1) * HD)
+        scores = (
+            lax.dot_general(
+                blocks[h], keys[:, cols], (((1,), (1,)), ((), ())), preferred_element_type=jnp.float32
+            )
+            * score_scale
+        )
+        scores = jnp.where(in_range, scores, masked_score)
+        highest = jnp.max(scores, axis=-1, keepdims=True)
+        weight = jnp.exp(scores - highest)
+        total = jnp.sum(weight, axis=-1, keepdims=True)
+        acc[h, 0] = jnp.dot(
+            weight.astype(jnp.bfloat16), values[:, cols], preferred_element_type=jnp.float32
+        )
+        lane = lax.broadcasted_iota(jnp.int32, (SLOT, HD), 1)
+        stats[h, 0] = jnp.where(lane < HD // 2, highest, total)
+
+
+def cache_attention(queries, cache_keys, cache_values, lengths):
+    row_count, span, kv_cols = cache_keys.shape
+    heads = kv_cols // HD
+    shape = (heads, row_count, SLOT, HD)
+    out_block = pl.BlockSpec((heads, 1, SLOT, HD), lambda r, lens: (0, r, 0, 0))
+    return pl.pallas_call(
+        functools.partial(cache_kernel, heads),
+        grid_spec=pltpu.PrefetchScalarGridSpec(
+            num_scalar_prefetch=1,
+            grid=(row_count,),
+            in_specs=[
+                pl.BlockSpec((1, STEPS, queries.shape[2]), lambda r, lens: (r, 0, 0)),
+                pl.BlockSpec((1, span, kv_cols), lambda r, lens: (r, 0, 0)),
+                pl.BlockSpec((1, span, kv_cols), lambda r, lens: (r, 0, 0)),
+            ],
+            out_specs=[out_block] * 3,
+        ),
+        out_shape=[
+            jax.ShapeDtypeStruct(shape, jnp.bfloat16),
+            jax.ShapeDtypeStruct(shape, jnp.float32),
+            jax.ShapeDtypeStruct(shape, jnp.float32),
+        ],
+        compiler_params=pltpu.CompilerParams(vmem_limit_bytes=VMEM_LIMIT),
+        cost_estimate=pl.CostEstimate(
+            flops=8 * row_count * SLOT * span * kv_cols,
+            bytes_accessed=4 * row_count * span * kv_cols,
+            transcendentals=row_count * heads * SLOT * span,
+        ),
+        name="cache_attention",
+    )(lengths, queries, cache_keys, cache_values)
+
+
+def fold_kernel(n, arrived, kept, *outs):
+    total = arrived[...].astype(jnp.float32) + kept[...].astype(jnp.float32)
+    step = total.shape[0] // n
+    for d in range(n):
+        outs[d][...] = total[d * step : (d + 1) * step].astype(outs[d].dtype)
+
+
+def fold(arrived, kept, n):
+    rows, width = kept.shape
+    step = rows // n
+    return pl.pallas_call(
+        functools.partial(fold_kernel, n),
+        out_shape=[
+            jax.ShapeDtypeStruct((step, width), jnp.float32 if d == 0 else jnp.bfloat16) for d in range(n)
+        ],
+        name="fold_halves",
+    )(arrived, kept)
+
+
+def merge_kernel(n, row_count, *refs):
+    pieces = refs[:n]
+    cosine, sine, stacked, acc, stats = refs[n : n + 5]
+    new_kv, context = refs[-2:]
+    total = pieces[0][...].astype(jnp.float32)
+    for piece in pieces[1:]:
+        total = total + piece[...].astype(jnp.float32)
+    keys = total[:, :HD]
+    keys = keys * cosine[...] + pltpu.roll(keys, HD // 2, 1) * sine[...]
+    keys = keys.astype(jnp.bfloat16)
+    values = total[:, HD:].astype(jnp.bfloat16)
+    both = jnp.concatenate([keys, values], axis=1).astype(jnp.float32)
+    for r in range(row_count):
+        new_kv[r] = both[r * STEPS : (r + 1) * STEPS].astype(jnp.bfloat16)
+    query = stacked[0].reshape(row_count * SLOT, HD)
+    scores = (
+        lax.dot_general(query, keys, (((1,), (1,)), ((), ())), preferred_element_type=jnp.float32)
+        * score_scale
+    )
+    at = lax.broadcasted_iota(jnp.int32, scores.shape, 0)
+    to = lax.broadcasted_iota(jnp.int32, scores.shape, 1)
+    seen = (at // SLOT == to // STEPS) & (at % STEPS >= to % STEPS)
+    scores = jnp.where(seen, scores, masked_score)
+    stat = stats[0].reshape(row_count * SLOT, HD)
+    old_highest = stat[:, :1]
+    old_total = stat[:, HD // 2 : HD // 2 + 1]
+    highest = jnp.maximum(jnp.max(scores, axis=-1, keepdims=True), old_highest)
+    weight = jnp.exp(scores - highest)
+    scale = jnp.exp(old_highest - highest)
+    denominator = jnp.sum(weight, axis=-1, keepdims=True) + scale * old_total
+    out = jnp.dot(weight.astype(jnp.bfloat16), values, preferred_element_type=jnp.float32)
+    out = (out + scale * acc[0].reshape(row_count * SLOT, HD)) / denominator
+    for r in range(row_count):
+        for g in range(PER_GROUP):
+            first = r * SLOT + g * STEPS
+            context[r, :, g * HD : (g + 1) * HD] = out[first : first + STEPS].astype(jnp.bfloat16)
+
+
+def merge(pieces, cosine, sine, stacked, acc, stats, previous, head):
+    heads, row_count = stacked.shape[:2]
+    whole = lambda a: pl.BlockSpec(a.shape, lambda i: (0,) * a.ndim)
+    one_head = pl.BlockSpec((1, row_count, SLOT, HD), lambda i: (head, 0, 0, 0))
+    operands = [*pieces, cosine, sine, stacked, acc, stats]
+    in_specs = [whole(p) for p in pieces] + [whole(cosine), whole(sine)] + [one_head] * 3
+    aliases = {}
+    if previous is not None:
+        for i, p in enumerate(previous):
+            aliases[len(operands)] = i
+            operands.append(p)
+            in_specs.append(pl.BlockSpec(memory_space=pl.ANY))
+    return pl.pallas_call(
+        functools.partial(merge_kernel, len(pieces), row_count),
+        grid=(1,),
+        in_specs=in_specs,
+        out_specs=[
+            pl.BlockSpec((row_count, STEPS, HEAD_COLS), lambda i: (0, 0, head)),
+            pl.BlockSpec((row_count, STEPS, PER_GROUP * HD), lambda i: (0, 0, head)),
+        ],
+        out_shape=[
+            jax.ShapeDtypeStruct((row_count, STEPS, heads * HEAD_COLS), jnp.bfloat16),
+            jax.ShapeDtypeStruct((row_count, STEPS, heads * PER_GROUP * HD), jnp.bfloat16),
+        ],
+        input_output_aliases=aliases,
+        compiler_params=pltpu.CompilerParams(vmem_limit_bytes=VMEM_LIMIT),
+        name="merge_new",
+    )(*operands)
+
+
+def swap(array, axis, bit):
+    size = lax.axis_size(axis)
+    return lax.ppermute(array, axis, [(i, i ^ bit) for i in range(size)])
+
+
+def add_rounded(a, b):
+    return (a.astype(jnp.float32) + b.astype(jnp.float32)).astype(jnp.bfloat16)
+
+
+def butterfly_shards(
+    tokens, queries, cache_keys, cache_values, lengths, weights, moment1, moment2, grad_parts
+):
+    group_count = lax.axis_size("group")
+    fsdp_count = lax.axis_size("fsdp")
+    tp_count = lax.axis_size("tp")
+    core = lax.axis_index("group") % 2
+    fsdp = lax.axis_index("fsdp")
+    tp = lax.axis_index("tp")
+    place = jnp.stack([core, tp]).astype(jnp.int32)
+    rows, width = weights.shape
+    row_count = tokens.shape[0]
+    n_chunks = width // (tp_count * HEAD_COLS)
+    local = grad_parts[0]
+
+    def columns(half, chunk):
+        return lax.dynamic_slice(local, (0, (half * n_chunks + chunk) * HEAD_COLS), (rows, HEAD_COLS))
+
+    arrived = [swap(columns(1 - core, k).astype(jnp.bfloat16), "group", 1) for k in range(n_chunks)]
+    own = [add_rounded(columns(core, k), arrived[k]) for k in range(n_chunks)]
+    bit = 2
+    while bit < group_count:
+        own = [add_rounded(o, swap(o, "group", bit)) for o in own]
+        bit *= 2
+    partner = [swap(o, "group", 1) for o in own]
+
+    toks = []
+    for d in range(fsdp_count):
+        first = ((fsdp ^ d) * tp_count + tp) * rows
+        piece = lax.dynamic_slice(tokens, (0, 0, first), (row_count, STEPS, rows))
+        piece = piece.reshape(row_count * STEPS, rows)
+        toks.append(piece if d == 0 else swap(piece, "fsdp", d))
+
+    cosine, sine = rotation_tables(lengths)
+    stacked, acc, stats = cache_attention(queries, cache_keys, cache_values, lengths)
+
+    updated = None
+    outs = None
+    same = core == tp
+    for k in range(n_chunks):
+        updated, (own_sums, partner_sums) = adam_and_project(
+            place, (0, 1), (own[k], partner[k]), weights, moment1, moment2, toks, updated, k, n_chunks
+        )
+        kept = jnp.where(same, own_sums, partner_sums)
+        sent = jnp.where(same, partner_sums, own_sums)
+        pieces = fold(swap(sent, "tp", 1), kept, fsdp_count)
+        pieces = [pieces[0]] + [swap(pieces[d], "fsdp", d) for d in range(1, fsdp_count)]
+        outs = merge(pieces, cosine, sine, stacked, acc, stats, outs, k)
+    return (*updated, *outs)
 
 
 def rotate_keys(keys, positions):
@@ -44,7 +359,7 @@
     )
 
 
-def shards(
+def plain_shards(
     tokens, queries, cache_keys, cache_values, lengths, weights, moment1, moment2, grad_parts
 ):
     gradient = lax.psum(grad_parts[0], "group")
@@ -71,10 +386,8 @@
     new_keys = rotate_keys(projected[:, :, :, 0], positions[:, :, None])
     fresh = jnp.stack([new_keys, projected[:, :, :, 1]], axis=3).astype(jnp.bfloat16)
     new_kv = fresh.reshape(row_count, STEPS, head_cols)
-    per_group = QH // KVH
-    score_scale = 1.0 / math.sqrt(HD)
     span_length = cache_keys.shape[1]
-    grouped = queries.reshape(row_count, STEPS, kv_heads, per_group, HD)
+    grouped = queries.reshape(row_count, STEPS, kv_heads, PER_GROUP, HD)
     cached_keys = cache_keys.reshape(row_count, span_length, kv_heads, HD)
     cached_values = cache_values.reshape(row_count, span_length, kv_heads, HD)
     new_scores = (
@@ -108,8 +421,12 @@
         fresh[:, :, :, 1],
         preferred_element_type=jnp.float32,
     )
-    context = context.reshape(row_count, STEPS, kv_heads * per_group * HD).astype(jnp.bfloat16)
+    context = context.reshape(row_count, STEPS, kv_heads * PER_GROUP * HD).astype(jnp.bfloat16)
     return (new_weights, new_moment1, new_moment2, new_kv, context)
+
+
+def power_of_two(n):
+    return n > 1 and n & (n - 1) == 0
 
 
 def solution(mesh):
@@ -131,4 +448,7 @@
         P(("group", "fsdp"), None, "tp"),
         P(("group", "fsdp"), None, "tp"),
     )
+    sizes = mesh.shape
+    pairwise = power_of_two(sizes["group"]) and power_of_two(sizes["fsdp"]) and sizes["tp"] == 2
+    shards = butterfly_shards if pairwise else plain_shards
     return jax.shard_map(shards, mesh=mesh, in_specs=in_specs, out_specs=out_specs, check_vma=False)

time: 216 us -> 132 us (0.61)
  waiting for transfers between devices: 140 us -> 30.9 us
  Pallas kernels: 0 us -> 44.2 us
  starting transfers between devices: 0.08 us -> 37.4 us
  between operations: 14.2 us -> 0.88 us
  blocking collectives: 13.1 us -> 0 us
  other arithmetic: 15.8 us -> 5.4 us
  matrix products: 10 us -> 0 us
  local copies, waits for them, and re-layouts: 22.2 us -> 12.7 us
    psum x1 -> x0, waiting for transfers between devices: 93.8 us -> none  [shards(): gradient = lax.psum(grad_parts[0], 'group')]
    reduce_scatter x1 -> x0, waiting for transfers between devices: 45.6 us -> none  [shards(): lax.psum_scatter(partial_terms, ('fsdp', 'tp'), scatter_dimension=0, tile...]
    pallas_call x0 -> x13, Pallas kernels: none -> 44.2 us  [the longest x4 23.6 us: adam_and_project(): pl.pallas_call(functools.partial(adam_kernel, n, len(toks)), grid_spec=pl...]
    ppermute x0 -> x31, starting transfers between devices: none -> 37.4 us  [swap(): return lax.ppermute(array, axis, [(i, i ^ bit) for i in range(size)])]
    ppermute x0 -> x31, waiting for transfers between devices: none -> 30.9 us  [swap(): return lax.ppermute(array, axis, [(i, i ^ bit) for i in range(size)])]
    reshape x5 -> x4, local copies, waits for them, and re-layouts: 15.2 us -> 0.07 us  [butterfly_shards(): piece = piece.reshape(row_count * STEPS, rows)]
    dot_general x1 -> x0, other arithmetic: 13.7 us -> none  [shards(): jnp.dot(arrived, weight_shard, preferred_element_type=jnp.float32)]
    all_to_all x1 -> x0, blocking collectives: 13.1 us -> none  [shards(): lax.all_to_all(own_columns, 'fsdp', split_axis=2, concat_axis=0, tiled=True)]
  transfers between devices with their start and end apart: 2 -> 31, of which waited for: 2 -> 11; matrix products, arithmetic and copies ran while one was open for 9% -> 2% of each run, Pallas kernels for 0% -> 28%
where the time goes in v1:
time: 132 us
  Pallas kernels  44.2 us (33%)
  starting transfers between devices  37.4 us (28%)
  waiting for transfers between devices  30.9 us (23%)
  local copies, waits for them, and re-layouts  12.7 us (10%)
  other arithmetic  5.4 us (4%)
    ppermute x31, starting transfers between devices, swap(): return lax.ppermute(array, axis, [(i, i ^ bit) for i in range(size)])  37.4 us
    ppermute x31, waiting for transfers between devices, swap(): return lax.ppermute(array, axis, [(i, i ^ bit) for i in range(size)])  30.9 us
    pallas_call x4, Pallas kernels, adam_and_project(): pl.pallas_call(functools.partial(adam_kernel, n, len(toks)), grid_spec=pl...  23.6 us
    unnamed x34, local copies, waits for them, and re-layouts  10.6 us
    pallas_call x1, Pallas kernels, cache_attention(): pl.pallas_call(functools.partial(cache_kernel, heads), grid_spec=pltpu.Pr...  9.63 us
    pallas_call x4, Pallas kernels, fold(): pl.pallas_call(functools.partial(fold_kernel, n), out_shape=[jax.ShapeDty...  6.06 us
    pallas_call x4, Pallas kernels, merge(): pl.pallas_call(functools.partial(merge_kernel, len(pieces), row_count), g...  4.97 us
  transfers between devices with their start and end apart: 31, of which 11 were waited for; matrix products, arithmetic and copies ran while one was open for 2% of the time, Pallas kernels for 28%

profile of v1, /device:TPU:0, one launch (start us, length us, event | category | flops | bytes accessed | tf_op | source)
XLA Modules:
  0.0 131.5 jit_solution(6894362699382739275)
XLA Ops:
  0.7 1.9 %fusion.7 = (bf16[640,256]{1,0:T(8,128)(2,1)S(1)}, bf16[640,256]{1,0:T(8,128)(2,1)S(1)}, bf16[640,256]{1,0:T(8,128)(2,1)S(1)}, bf16[640,256]{1,0:T(8,128)(2,1)S(1)}) fusion(f32[1,640,2048]{2,1,0:T(8,128)} %param.17, s32[]{:T(128)S(6)} %select_n.91, s32[]{:T(128)S(6)} %select_n.89, s32[]{:T(128)S(6)} %select_n.87, s32[]{:T(128)S(6)} %select_n.81), kind=kLoop, calls=%fused_computation.19 | loop fusion | bytes 2621456 | tf_op jit(solution)/shard_map/convert_element_type | solution.py:314
  5.7 2.1 %fusion = (bf16[640,256]{1,0:T(8,128)(2,1)S(1)}, bf16[640,256]{1,0:T(8,128)(2,1)S(1)}, bf16[640,256]{1,0:T(8,128)(2,1)S(1)}, bf16[640,256]{1,0:T(8,128)(2,1)S(1)}) fusion(bf16[640,256]{1,0:T(8,128)(2,1)S(1)} %collective-permute-done.12, f32[1,640,2048]{2,1,0:T(8,128)} %param.17, s32[]{:T(128)S(6)} %select_n.90, ...), kind=kLoop, calls=%fused_computation.1 | loop fusion | flops 1966080 | bytes 5242896 | tf_op jit(solution)/shard_map/convert_element_type | solution.py:293
  7.8 2.9 %collective-permute-start.1 = (bf16[640,256]{1,0:T(8,128)(2,1)S(1)}, bf16[640,256]{1,0:T(8,128)(2,1)S(1)}, u32[]{:S(2)}, u32[]{:S(2)}) collective-permute-start(bf16[640,256]{1,0:T(8,128)(2,1)S(1)} %get-tuple-element.102), channel_id=1, source_target_pairs={{0,16},{8,24},{16,0},{24,8},{1,17},{9,25},{17,1},{25,9},{2,18},{10... | collective-permute-start | bytes 983048 | tf_op jit(solution)/shard_map/ppermute | solution.py:289
  11.0 2.1 %collective-permute-start.3 = (bf16[32,640]{1,0:T(8,128)(2,1)S(1)}, bf16[32,640]{1,0:T(8,128)(2,1)S(1)}, u32[]{:S(2)}, u32[]{:S(2)}) collective-permute-start(bf16[32,640]{1,0:T(8,128)(2,1)S(1)} %reshape.57), channel_id=1, source_target_pairs={{0,2},{2,0},{4,6},{6,4},{1,3},{3,1},{5,7},{7,5},{8,10},{10,8},{12,... | collective-permute-start | bytes 122888 | tf_op jit(solution)/shard_map/ppermute | solution.py:289
  15.1 4.2 %collective-permute-done.1 = bf16[640,256]{1,0:T(8,128)(2,1)S(1)} collective-permute-done((bf16[640,256]{1,0:T(8,128)(2,1)S(1)}, bf16[640,256]{1,0:T(8,128)(2,1)S(1)}, u32[]{:S(2)}, u32[]{:S(2)}) %collective-permute-start.1) | collective-permute-done | bytes 327712 | tf_op jit(solution)/shard_map/ppermute | solution.py:289
  19.4 6.9 %collective-permute-done.7 = bf16[640,256]{1,0:T(8,128)(2,1)S(1)} collective-permute-done((bf16[640,256]{1,0:T(8,128)(2,1)S(1)}, bf16[640,256]{1,0:T(8,128)(2,1)S(1)}, u32[]{:S(2)}, u32[]{:S(2)}) %collective-permute-start.7) | collective-permute-done | bytes 327712 | tf_op jit(solution)/shard_map/ppermute | solution.py:289
  26.5 6.8 %collective-permute-done.10 = bf16[640,256]{1,0:T(8,128)(2,1)S(1)} collective-permute-done((bf16[640,256]{1,0:T(8,128)(2,1)S(1)}, bf16[640,256]{1,0:T(8,128)(2,1)S(1)}, u32[]{:S(2)}, u32[]{:S(2)}) %collective-permute-start.10) | collective-permute-done | bytes 327712 | tf_op jit(solution)/shard_map/ppermute | solution.py:289
  33.5 6.4 %collective-permute-done.13 = bf16[640,256]{1,0:T(8,128)(2,1)S(1)} collective-permute-done((bf16[640,256]{1,0:T(8,128)(2,1)S(1)}, bf16[640,256]{1,0:T(8,128)(2,1)S(1)}, u32[]{:S(2)}, u32[]{:S(2)}) %collective-permute-start.13) | collective-permute-done | bytes 327712 | tf_op jit(solution)/shard_map/ppermute | solution.py:289
  40.1 2.9 %collective-permute-start.4 = (bf16[32,640]{1,0:T(8,128)(2,1)S(1)}, bf16[32,640]{1,0:T(8,128)(2,1)S(1)}, u32[]{:S(2)}, u32[]{:S(2)}) collective-permute-start(bf16[32,640]{1,0:T(8,128)(2,1)S(1)} %reshape.58), channel_id=1, source_target_pairs={{0,4},{2,6},{4,0},{6,2},{1,5},{3,7},{5,1},{7,3},{8,12},{10,14},{12... | collective-permute-start | bytes 122888 | tf_op jit(solution)/shard_map/ppermute | solution.py:289
  43.1 2.2 %collective-permute-done.4.refs_7_ = bf16[32,640]{1,0:T(8,128)(2,1)S(1)} collective-permute-done((bf16[32,640]{1,0:T(8,128)(2,1)S(1)}, bf16[32,640]{1,0:T(8,128)(2,1)S(1)}, u32[]{:S(2)}, u32[]{:S(2)}) %collective-permute-start.4) | collective-permute-done | bytes 40992 | tf_op jit(solution)/shard_map/ppermute | solution.py:289
  45.3 4.4 %collective-permute-start.5 = (bf16[32,640]{1,0:T(8,128)(2,1)S(1)}, bf16[32,640]{1,0:T(8,128)(2,1)S(1)}, u32[]{:S(2)}, u32[]{:S(2)}) collective-permute-start(bf16[32,640]{1,0:T(8,128)(2,1)S(1)} %reshape.59), channel_id=1, source_target_pairs={{0,6},{2,4},{4,2},{6,0},{1,7},{3,5},{5,3},{7,1},{8,14},{10,12},{12... | collective-permute-start | bytes 122888 | tf_op jit(solution)/shard_map/ppermute | solution.py:289
  51.7 2.5 %copy-done = f32[640,2048]{1,0:T(8,128)S(1)} copy-done((f32[640,2048]{1,0:T(8,128)S(1)}, f32[640,2048]{1,0:T(8,128)}, u32[]{:S(2)}) %copy-start) | copy-done | bytes 5242904
  54.1 2.5 %copy-done.2 = f32[640,2048]{1,0:T(8,128)S(1)} copy-done((f32[640,2048]{1,0:T(8,128)S(1)}, f32[640,2048]{1,0:T(8,128)}, u32[]{:S(2)}) %copy-start.2) | copy-done | bytes 5242904
  56.6 6.8 %adam_project.4 = (f32[640,2048]{1,0:T(8,128)}, f32[640,2048]{1,0:T(8,128)}, f32[640,2048]{1,0:T(8,128)}, bf16[128,256]{1,0:T(8,128)(2,1)S(1)}, bf16[128,256]{1,0:T(8,128)(2,1)S(1)}) custom-call(s32[2]{0:T(128)S(1)} %pad_add_fusion.place, bf16[640,256]{1,0:T(8,128)(2,1)S(1)} %add_convert_fusion.refs_0_, ...), custom_call_target="tpu_custom_call" | custom-call | flops 83886080 | bytes 8519680 | tf_op jit(solution)/shard_map/adam_project/pallas_call | solution.py:107
  63.4 5.6 %adam_project.5 = (f32[640,2048]{1,0:T(8,128)}, f32[640,2048]{1,0:T(8,128)}, f32[640,2048]{1,0:T(8,128)}, bf16[128,256]{1,0:T(8,128)(2,1)S(1)}, bf16[128,256]{1,0:T(8,128)(2,1)S(1)}) custom-call(s32[2]{0:T(128)S(1)} %pad_add_fusion.place, ...), custom_call_target="tpu_custom_call", output_to_operand_aliasing={{0}: (10, {}), {1}: (11, {}), {2}: (12, {})} | custom-call | flops 83886080 | bytes 8519680 | tf_op jit(solution)/shard_map/adam_project/pallas_call | solution.py:107
  69.0 5.6 %adam_project.6 = (f32[640,2048]{1,0:T(8,128)}, f32[640,2048]{1,0:T(8,128)}, f32[640,2048]{1,0:T(8,128)}, bf16[128,256]{1,0:T(8,128)(2,1)S(1)}, bf16[128,256]{1,0:T(8,128)(2,1)S(1)}) custom-call(s32[2]{0:T(128)S(1)} %pad_add_fusion.place, ...), custom_call_target="tpu_custom_call", output_to_operand_aliasing={{0}: (10, {}), {1}: (11, {}), {2}: (12, {})} | custom-call | flops 83886080 | bytes 8519680 | tf_op jit(solution)/shard_map/adam_project/pallas_call | solution.py:107
  74.6 5.6 %adam_project.7 = (f32[640,2048]{1,0:T(8,128)}, f32[640,2048]{1,0:T(8,128)}, f32[640,2048]{1,0:T(8,128)}, bf16[128,256]{1,0:T(8,128)(2,1)S(1)}, bf16[128,256]{1,0:T(8,128)(2,1)S(1)}) custom-call(s32[2]{0:T(128)S(1)} %pad_add_fusion.place, ...), custom_call_target="tpu_custom_call", output_to_operand_aliasing={{0}: (10, {}), {1}: (11, {}), {2}: (12, {})} | custom-call | flops 83886080 | bytes 8519680 | tf_op jit(solution)/shard_map/adam_project/pallas_call | solution.py:107
  91.6 2.0 %collective-permute-start.24 = (bf16[32,256]{1,0:T(8,128)(2,1)}, bf16[32,256]{1,0:T(8,128)(2,1)S(1)}, u32[]{:S(2)}, u32[]{:S(2)}) collective-permute-start(bf16[32,256]{1,0:T(8,128)(2,1)} %get-tuple-element.82), channel_id=1, source_target_pairs={{0,2},{2,0},{4,6},{6,4},{1,3},{3,1},{5,7},{7,5},{8,10},{10,8},{12,... | collective-permute-start | bytes 49160 | tf_op jit(solution)/shard_map/ppermute | solution.py:289
  93.8 2.8 %collective-permute-start.25 = (bf16[32,256]{1,0:T(8,128)(2,1)}, bf16[32,256]{1,0:T(8,128)(2,1)S(1)}, u32[]{:S(2)}, u32[]{:S(2)}) collective-permute-start(bf16[32,256]{1,0:T(8,128)(2,1)} %get-tuple-element.83), channel_id=1, source_target_pairs={{0,4},{2,6},{4,0},{6,2},{1,5},{3,7},{5,1},{7,3},{8,12},{10,14},{12... | collective-permute-start | bytes 49160 | tf_op jit(solution)/shard_map/ppermute | solution.py:289
  105.9 2.6 %collective-permute-start.17 = (bf16[32,256]{1,0:T(8,128)(2,1)}, bf16[32,256]{1,0:T(8,128)(2,1)S(1)}, u32[]{:S(2)}, u32[]{:S(2)}) collective-permute-start(bf16[32,256]{1,0:T(8,128)(2,1)} %get-tuple-element.68), channel_id=1, source_target_pairs={{0,4},{2,6},{4,0},{6,2},{1,5},{3,7},{5,1},{7,3},{8,12},{10,14},{12... | collective-permute-start | bytes 49160 | tf_op jit(solution)/shard_map/ppermute | solution.py:289
  110.3 2.2 %collective-permute-start.22 = (bf16[32,256]{1,0:T(8,128)(2,1)}, bf16[32,256]{1,0:T(8,128)(2,1)S(1)}, u32[]{:S(2)}, u32[]{:S(2)}) collective-permute-start(bf16[32,256]{1,0:T(8,128)(2,1)} %get-tuple-element.78), channel_id=1, source_target_pairs={{0,6},{2,4},{4,2},{6,0},{1,7},{3,5},{5,3},{7,1},{8,14},{10,12},{12... | collective-permute-start | bytes 49160 | tf_op jit(solution)/shard_map/ppermute | solution.py:289
  112.5 2.2 %copy-done.4 = bf16[8,512,512]{2,1,0:T(8,128)(2,1)S(1)} copy-done((bf16[8,512,512]{2,1,0:T(8,128)(2,1)S(1)}, bf16[8,512,512]{2,1,0:T(8,128)(2,1)}, u32[]{:S(2)}) %copy-start.4) | copy-done | bytes 4194328
  114.7 2.2 %copy-done.5 = bf16[8,512,512]{2,1,0:T(8,128)(2,1)S(1)} copy-done((bf16[8,512,512]{2,1,0:T(8,128)(2,1)S(1)}, bf16[8,512,512]{2,1,0:T(8,128)(2,1)}, u32[]{:S(2)}) %copy-start.5) | copy-done | bytes 4194328
  116.9 9.6 %cache_attention.1 = (bf16[4,8,32,128]{3,2,1,0:T(8,128)(2,1)S(1)}, f32[4,8,32,128]{3,2,1,0:T(8,128)S(1)}, f32[4,8,32,128]{3,2,1,0:T(8,128)S(1)}) custom-call(s32[8]{0:T(128)S(1)} %copy-done.11, bf16[8,4,2560]{2,1,0:T(4,128)(2,1)S(1)} %copy-done.6, bf16[8,512,512]{2,1,0:T(8,128)(2,1)S(1)} %copy-done.4, bf16[8,512,512]{2,1,0:T(8,128)(2,1)S(1)} %copy-done.5), custom_call_target="tpu_custom_call" | custom-call | flops 536870912 | bytes 8388608 | tf_op jit(solution)/shard_map/cache_attention/pallas_call | solution.py:173
  (106 shorter events, 35.7 us)
Async XLA Ops:
  7.8 11.4 %collective-permute-start.1 = (bf16[640,256]{1,0:T(8,128)(2,1)S(1)}, bf16[640,256]{1,0:T(8,128)(2,1)S(1)}, u32[]{:S(2)}, u32[]{:S(2)}) collective-permute-start(bf16[640,256]{1,0:T(8,128)(2,1)S(1)} %get-tuple-element.102), channel_id=1, source_target_pairs={{0,16},{8,24},{16,0},{24,8},{1,17},{9,25},{17,1},{25,9},{2,18},{10... | collective-permute-start | bytes 983048 | tf_op jit(solution)/shard_map/ppermute | solution.py:289
  10.8 15.5 %collective-permute-start.7 = (bf16[640,256]{1,0:T(8,128)(2,1)S(1)}, bf16[640,256]{1,0:T(8,128)(2,1)S(1)}, u32[]{:S(2)}, u32[]{:S(2)}) collective-permute-start(bf16[640,256]{1,0:T(8,128)(2,1)S(1)} %get-tuple-element.101), channel_id=1, source_target_pairs={{0,16},{8,24},{16,0},{24,8},{1,17},{9,25},{17,1},{25,9},{2,18},{10... | collective-permute-start | bytes 983048 | tf_op jit(solution)/shard_map/ppermute | solution.py:289
  11.0 29.2 %collective-permute-start.3 = (bf16[32,640]{1,0:T(8,128)(2,1)S(1)}, bf16[32,640]{1,0:T(8,128)(2,1)S(1)}, u32[]{:S(2)}, u32[]{:S(2)}) collective-permute-start(bf16[32,640]{1,0:T(8,128)(2,1)S(1)} %reshape.57), channel_id=1, source_target_pairs={{0,2},{2,0},{4,6},{6,4},{1,3},{3,1},{5,7},{7,5},{8,10},{10,8},{12,... | collective-permute-start | bytes 122888 | tf_op jit(solution)/shard_map/ppermute | solution.py:289
  13.0 20.3 %collective-permute-start.10 = (bf16[640,256]{1,0:T(8,128)(2,1)S(1)}, bf16[640,256]{1,0:T(8,128)(2,1)S(1)}, u32[]{:S(2)}, u32[]{:S(2)}) collective-permute-start(bf16[640,256]{1,0:T(8,128)(2,1)S(1)} %get-tuple-element.100), channel_id=1, source_target_pairs={{0,16},{8,24},{16,0},{24,8},{1,17},{9,25},{17,1},{25,9},{2,18},{10... | collective-permute-start | bytes 983048 | tf_op jit(solution)/shard_map/ppermute | solution.py:289
  14.6 25.3 %collective-permute-start.13 = (bf16[640,256]{1,0:T(8,128)(2,1)S(1)}, bf16[640,256]{1,0:T(8,128)(2,1)S(1)}, u32[]{:S(2)}, u32[]{:S(2)}) collective-permute-start(bf16[640,256]{1,0:T(8,128)(2,1)S(1)} %get-tuple-element.99), channel_id=1, source_target_pairs={{0,16},{8,24},{16,0},{24,8},{1,17},{9,25},{17,1},{25,9},{2,18},{10... | collective-permute-start | bytes 983048 | tf_op jit(solution)/shard_map/ppermute | solution.py:289
  19.4 55.3 %collective-permute-start.2 = (bf16[640,256]{1,0:T(8,128)(2,1)S(1)}, bf16[640,256]{1,0:T(8,128)(2,1)S(1)}, u32[]{:S(2)}, u32[]{:S(2)}) collective-permute-start(bf16[640,256]{1,0:T(8,128)(2,1)S(1)} %add_convert_fusion.3.refs_0_), channel_id=1, source_target_pairs={{0,8},{8,0},{16,24},{24,16},{1,9},{9,1},{17,25},{25,17},{2,10},{10... | collective-permute-start | bytes 983048 | tf_op jit(solution)/shard_map/ppermute | solution.py:289
  26.4 42.7 %collective-permute-start.8 = (bf16[640,256]{1,0:T(8,128)(2,1)S(1)}, bf16[640,256]{1,0:T(8,128)(2,1)S(1)}, u32[]{:S(2)}, u32[]{:S(2)}) collective-permute-start(bf16[640,256]{1,0:T(8,128)(2,1)S(1)} %add_convert_fusion.2.refs_0_), channel_id=1, source_target_pairs={{0,8},{8,0},{16,24},{24,16},{1,9},{9,1},{17,25},{25,17},{2,10},{10... | collective-permute-start | bytes 983048 | tf_op jit(solution)/shard_map/ppermute | solution.py:289
  33.4 30.0 %collective-permute-start.11 = (bf16[640,256]{1,0:T(8,128)(2,1)S(1)}, bf16[640,256]{1,0:T(8,128)(2,1)S(1)}, u32[]{:S(2)}, u32[]{:S(2)}) collective-permute-start(bf16[640,256]{1,0:T(8,128)(2,1)S(1)} %add_convert_fusion.1.refs_0_), channel_id=1, source_target_pairs={{0,8},{8,0},{16,24},{24,16},{1,9},{9,1},{17,25},{25,17},{2,10},{10... | collective-permute-start | bytes 983048 | tf_op jit(solution)/shard_map/ppermute | solution.py:289
  39.9 11.7 %collective-permute-start.14 = (bf16[640,256]{1,0:T(8,128)(2,1)S(1)}, bf16[640,256]{1,0:T(8,128)(2,1)S(1)}, u32[]{:S(2)}, u32[]{:S(2)}) collective-permute-start(bf16[640,256]{1,0:T(8,128)(2,1)S(1)} %add_convert_fusion.refs_0_), channel_id=1, source_target_pairs={{0,8},{8,0},{16,24},{24,16},{1,9},{9,1},{17,25},{25,17},{2,10},{10... | collective-permute-start | bytes 983048 | tf_op jit(solution)/shard_map/ppermute | solution.py:289
  45.3 6.4 %collective-permute-start.5 = (bf16[32,640]{1,0:T(8,128)(2,1)S(1)}, bf16[32,640]{1,0:T(8,128)(2,1)S(1)}, u32[]{:S(2)}, u32[]{:S(2)}) collective-permute-start(bf16[32,640]{1,0:T(8,128)(2,1)S(1)} %reshape.59), channel_id=1, source_target_pairs={{0,6},{2,4},{4,2},{6,0},{1,7},{3,5},{5,3},{7,1},{8,14},{10,12},{12... | collective-permute-start | bytes 122888 | tf_op jit(solution)/shard_map/ppermute | solution.py:289
  80.9 18.8 %collective-permute-start.15 = (bf16[128,256]{1,0:T(8,128)(2,1)S(1)}, bf16[128,256]{1,0:T(8,128)(2,1)S(1)}, u32[]{:S(2)}, u32[]{:S(2)}) collective-permute-start(bf16[128,256]{1,0:T(8,128)(2,1)S(1)} %get-tuple-element.118), channel_id=1, source_target_pairs={{0,1},{1,0},{2,3},{3,2},{4,5},{5,4},{6,7},{7,6},{8,9},{9,8},{10,11... | collective-permute-start | bytes 196616 | tf_op jit(solution)/shard_map/ppermute | solution.py:289
  86.3 10.2 %collective-permute-start.27 = (bf16[128,256]{1,0:T(8,128)(2,1)S(1)}, bf16[128,256]{1,0:T(8,128)(2,1)S(1)}, u32[]{:S(2)}, u32[]{:S(2)}) collective-permute-start(bf16[128,256]{1,0:T(8,128)(2,1)S(1)} %get-tuple-element.112), channel_id=1, source_target_pairs={{0,1},{1,0},{2,3},{3,2},{4,5},{5,4},{6,7},{7,6},{8,9},{9,8},{10,11... | collective-permute-start | bytes 196616 | tf_op jit(solution)/shard_map/ppermute | solution.py:289
  89.5 11.3 %collective-permute-start.20 = (bf16[32,256]{1,0:T(8,128)(2,1)}, bf16[32,256]{1,0:T(8,128)(2,1)S(1)}, u32[]{:S(2)}, u32[]{:S(2)}) collective-permute-start(bf16[32,256]{1,0:T(8,128)(2,1)} %get-tuple-element.76), channel_id=1, source_target_pairs={{0,2},{2,0},{4,6},{6,4},{1,3},{3,1},{5,7},{7,5},{8,10},{10,8},{12,... | collective-permute-start | bytes 49160 | tf_op jit(solution)/shard_map/ppermute | solution.py:289
  91.6 10.9 %collective-permute-start.24 = (bf16[32,256]{1,0:T(8,128)(2,1)}, bf16[32,256]{1,0:T(8,128)(2,1)S(1)}, u32[]{:S(2)}, u32[]{:S(2)}) collective-permute-start(bf16[32,256]{1,0:T(8,128)(2,1)} %get-tuple-element.82), channel_id=1, source_target_pairs={{0,2},{2,0},{4,6},{6,4},{1,3},{3,1},{5,7},{7,5},{8,10},{10,8},{12,... | collective-permute-start | bytes 49160 | tf_op jit(solution)/shard_map/ppermute | solution.py:289
  93.8 11.9 %collective-permute-start.25 = (bf16[32,256]{1,0:T(8,128)(2,1)}, bf16[32,256]{1,0:T(8,128)(2,1)S(1)}, u32[]{:S(2)}, u32[]{:S(2)}) collective-permute-start(bf16[32,256]{1,0:T(8,128)(2,1)} %get-tuple-element.83), channel_id=1, source_target_pairs={{0,4},{2,6},{4,0},{6,2},{1,5},{3,7},{5,1},{7,3},{8,12},{10,14},{12... | collective-permute-start | bytes 49160 | tf_op jit(solution)/shard_map/ppermute | solution.py:289
  96.6 9.4 %collective-permute-start.26 = (bf16[32,256]{1,0:T(8,128)(2,1)}, bf16[32,256]{1,0:T(8,128)(2,1)S(1)}, u32[]{:S(2)}, u32[]{:S(2)}) collective-permute-start(bf16[32,256]{1,0:T(8,128)(2,1)} %get-tuple-element.84), channel_id=1, source_target_pairs={{0,6},{2,4},{4,2},{6,0},{1,7},{3,5},{5,3},{7,1},{8,14},{10,12},{12... | collective-permute-start | bytes 49160 | tf_op jit(solution)/shard_map/ppermute | solution.py:289
  99.7 8.9 %collective-permute-start.28 = (bf16[32,256]{1,0:T(8,128)(2,1)}, bf16[32,256]{1,0:T(8,128)(2,1)S(1)}, u32[]{:S(2)}, u32[]{:S(2)}) collective-permute-start(bf16[32,256]{1,0:T(8,128)(2,1)} %get-tuple-element.88), channel_id=1, source_target_pairs={{0,2},{2,0},{4,6},{6,4},{1,3},{3,1},{5,7},{7,5},{8,10},{10,8},{12,... | collective-permute-start | bytes 49160 | tf_op jit(solution)/shard_map/ppermute | solution.py:289
  100.8 9.3 %collective-permute-start.29 = (bf16[32,256]{1,0:T(8,128)(2,1)}, bf16[32,256]{1,0:T(8,128)(2,1)S(1)}, u32[]{:S(2)}, u32[]{:S(2)}) collective-permute-start(bf16[32,256]{1,0:T(8,128)(2,1)} %get-tuple-element.89), channel_id=1, source_target_pairs={{0,4},{2,6},{4,0},{6,2},{1,5},{3,7},{5,1},{7,3},{8,12},{10,14},{12... | collective-permute-start | bytes 49160 | tf_op jit(solution)/shard_map/ppermute | solution.py:289
  102.6 7.7 %collective-permute-start.30 = (bf16[32,256]{1,0:T(8,128)(2,1)}, bf16[32,256]{1,0:T(8,128)(2,1)S(1)}, u32[]{:S(2)}, u32[]{:S(2)}) collective-permute-start(bf16[32,256]{1,0:T(8,128)(2,1)} %get-tuple-element.90), channel_id=1, source_target_pairs={{0,6},{2,4},{4,2},{6,0},{1,7},{3,5},{5,3},{7,1},{8,14},{10,12},{12... | collective-permute-start | bytes 49160 | tf_op jit(solution)/shard_map/ppermute | solution.py:289
  105.7 24.5 %collective-permute-start.16 = (bf16[32,256]{1,0:T(8,128)(2,1)}, bf16[32,256]{1,0:T(8,128)(2,1)S(1)}, u32[]{:S(2)}, u32[]{:S(2)}) collective-permute-start(bf16[32,256]{1,0:T(8,128)(2,1)} %get-tuple-element.67), channel_id=1, source_target_pairs={{0,2},{2,0},{4,6},{6,4},{1,3},{3,1},{5,7},{7,5},{8,10},{10,8},{12,... | collective-permute-start | bytes 49160 | tf_op jit(solution)/shard_map/ppermute | solution.py:289
  105.9 24.3 %collective-permute-start.17 = (bf16[32,256]{1,0:T(8,128)(2,1)}, bf16[32,256]{1,0:T(8,128)(2,1)S(1)}, u32[]{:S(2)}, u32[]{:S(2)}) collective-permute-start(bf16[32,256]{1,0:T(8,128)(2,1)} %get-tuple-element.68), channel_id=1, source_target_pairs={{0,4},{2,6},{4,0},{6,2},{1,5},{3,7},{5,1},{7,3},{8,12},{10,14},{12... | collective-permute-start | bytes 49160 | tf_op jit(solution)/shard_map/ppermute | solution.py:289
  108.6 21.7 %collective-permute-start.18 = (bf16[32,256]{1,0:T(8,128)(2,1)}, bf16[32,256]{1,0:T(8,128)(2,1)S(1)}, u32[]{:S(2)}, u32[]{:S(2)}) collective-permute-start(bf16[32,256]{1,0:T(8,128)(2,1)} %get-tuple-element.69), channel_id=1, source_target_pairs={{0,6},{2,4},{4,2},{6,0},{1,7},{3,5},{5,3},{7,1},{8,14},{10,12},{12... | collective-permute-start | bytes 49160 | tf_op jit(solution)/shard_map/ppermute | solution.py:289
  110.1 18.9 %collective-permute-start.21 = (bf16[32,256]{1,0:T(8,128)(2,1)}, bf16[32,256]{1,0:T(8,128)(2,1)S(1)}, u32[]{:S(2)}, u32[]{:S(2)}) collective-permute-start(bf16[32,256]{1,0:T(8,128)(2,1)} %get-tuple-element.77), channel_id=1, source_target_pairs={{0,4},{2,6},{4,0},{6,2},{1,5},{3,7},{5,1},{7,3},{8,12},{10,14},{12... | collective-permute-start | bytes 49160 | tf_op jit(solution)/shard_map/ppermute | solution.py:289
  110.3 18.7 %collective-permute-start.22 = (bf16[32,256]{1,0:T(8,128)(2,1)}, bf16[32,256]{1,0:T(8,128)(2,1)S(1)}, u32[]{:S(2)}, u32[]{:S(2)}) collective-permute-start(bf16[32,256]{1,0:T(8,128)(2,1)} %get-tuple-element.78), channel_id=1, source_target_pairs={{0,6},{2,4},{4,2},{6,0},{1,7},{3,5},{5,3},{7,1},{8,14},{10,12},{12... | collective-permute-start | bytes 49160 | tf_op jit(solution)/shard_map/ppermute | solution.py:289
  (24 other events, 226.9 us)

commit v2 on v0

--- a/solution.py
+++ b/solution.py
@@ -1,14 +1,19 @@
+import functools
 import math
 
 import jax
 import jax.numpy as jnp
 from jax import lax
+from jax.experimental import pallas as pl
+from jax.experimental.pallas import tpu as pltpu
 from jax.sharding import PartitionSpec as P
 
 QH = 40
 KVH = 8
 HD = 128
 STEPS = 4
+PER_GROUP = QH // KVH
+HEAD_COLS = 2 * HD
 
 
 beta_one = 0.9
@@ -19,6 +24,8 @@
 correct_one = 1.0 - 0.9**10
 correct_two = 1.0 - 0.95**10
 masked_score = -1e30
+score_scale = 1.0 / math.sqrt(HD)
+VMEM_LIMIT = 60 * 1024 * 1024
 
 
 def adam_update(weights, moment1, moment2, gradient):
@@ -27,6 +34,345 @@
     direction = new_moment1 / correct_one / (jnp.sqrt(new_moment2 / correct_two) + epsilon)
     new_weights = weights - learning_rate * (direction + decay_rate * weights)
     return (new_weights, new_moment1, new_moment2)
+
+
+def rotation_tables(lengths):
+    half_width = HD // 2
+    frequency = jnp.power(
+        jnp.float32(1000000.0), -2.0 * jnp.arange(half_width, dtype=jnp.float32) / HD
+    )
+    positions = (lengths[:, None] + jnp.arange(STEPS, dtype=jnp.int32)[None, :]).astype(jnp.float32)
+    angles = positions.reshape(-1)[:, None] * frequency
+    cosine = jnp.cos(angles)
+    sine = jnp.sin(angles)
+    return (
+        jnp.concatenate([cosine, cosine], axis=-1),
+        jnp.concatenate([-sine, sine], axis=-1),
+    )
+
+
+def whole(a):
+    return pl.BlockSpec(a.shape, lambda *_: (0,) * len(a.shape))
+
+
+def adam_kernel(n_parts, n_tok, update, project, place, *refs):
+    totals = refs[:n_parts]
+    w, m1, m2 = refs[n_parts : n_parts + 3]
+    toks = refs[n_parts + 3 : n_parts + 3 + n_tok]
+    outs = refs[len(refs) - 3 * update - 2 * project :]
+    part = pl.program_id(0)
+    cols = pl.program_id(1)
+    gradient = totals[0][...]
+    for j in range(1, n_parts):
+        gradient = jnp.where(part == j, totals[j][...], gradient)
+    results = adam_update(w[...], m1[...], m2[...], gradient.astype(jnp.float32))
+    if update:
+        for ref, value in zip(outs, results):
+            ref[...] = value
+    if project:
+        sent, kept = outs[-2:]
+        tok = jnp.concatenate([t[...] for t in toks], axis=0)
+        terms = jnp.dot(tok, results[0].astype(jnp.bfloat16), preferred_element_type=jnp.float32)
+        width = terms.shape[1]
+        at = pl.ds(pl.multiple_of(cols * width, width), width)
+        half = half_of(place, part)
+        stays = half == place[1]
+
+        @pl.when(stays)
+        def _():
+            kept[:, at] = terms
+
+        @pl.when(jnp.logical_not(stays))
+        def _():
+            sent[:, at] = terms.astype(jnp.bfloat16)
+
+
+def half_of(place, part):
+    return jnp.where(part + place[2] == 1, 1 - place[0], place[0])
+
+
+def adam_call(place, totals, state, toks, first, n_units, n_chunks, update, project, previous=None, sums=None):
+    weights = state[0]
+    rows, width = weights.shape
+    n = len(totals)
+
+    def column(j, b, place):
+        return (0, half_of(place, j) * n_chunks + first + b)
+
+    def total_map(i):
+        return lambda j, b, place: (0, jnp.where(j == i, b, jnp.where(j < i, 0, n_units - 1)))
+
+    block = pl.BlockSpec((rows, HEAD_COLS), column)
+    in_specs = [pl.BlockSpec((rows, HEAD_COLS), total_map(i)) for i in range(n)] + [block] * 3
+    operands = [*totals, *state]
+    if project:
+        operands += toks
+        in_specs += [whole(t) for t in toks]
+    out_specs, out_shape, aliases = [], [], {}
+    if update:
+        out_specs += [block] * 3
+        out_shape += [jax.ShapeDtypeStruct((rows, width), jnp.float32)] * 3
+        if previous is not None:
+            for i, p in enumerate(previous):
+                aliases[1 + len(operands)] = i
+                operands.append(p)
+                in_specs.append(pl.BlockSpec(memory_space=pl.ANY))
+    n_tokens = sum(t.shape[0] for t in toks)
+    if project:
+        for dtype in (jnp.bfloat16, jnp.float32):
+            out_shape.append(jax.ShapeDtypeStruct((n_tokens, n_units * HEAD_COLS), dtype))
+            out_specs.append(whole(out_shape[-1]))
+    out = pl.pallas_call(
+        functools.partial(adam_kernel, n, len(toks) if project else 0, update, project),
+        grid_spec=pltpu.PrefetchScalarGridSpec(
+            num_scalar_prefetch=1,
+            grid=(n, n_units),
+            in_specs=in_specs,
+            out_specs=out_specs,
+        ),
+        out_shape=out_shape,
+        input_output_aliases=aliases,
+        compiler_params=pltpu.CompilerParams(vmem_limit_bytes=VMEM_LIMIT),
+        cost_estimate=pl.CostEstimate(
+            flops=2 * n_tokens * rows * HEAD_COLS * n * n_units,
+            bytes_accessed=(14 + 12 * update) * rows * HEAD_COLS * n * n_units,
+            transcendentals=0,
+        ),
+        name="adam_project" if project else "adam_update",
+    )(place, *operands)
+    return (tuple(out[:3]) if update else None), (tuple(out[-2:]) if project else None)
+
+
+SLOT = 32
+
+
+def cache_kernel(heads, lens, q, k, v, stacked, acc, stats):
+    rows = q.shape[0]
+    span = k.shape[1]
+    used = PER_GROUP * STEPS
+    for i in range(rows):
+        length = lens[pl.program_id(0) * rows + i]
+        query = q[i].astype(jnp.float32)
+        scores = []
+        for h in range(heads):
+            pieces = [
+                query[:, (h * PER_GROUP + g) * HD : (h * PER_GROUP + g + 1) * HD] for g in range(PER_GROUP)
+            ]
+            pieces.append(jnp.zeros((SLOT - used, HD), jnp.float32))
+            one = jnp.concatenate(pieces, axis=0).astype(jnp.bfloat16)
+            stacked[h, i] = one
+            scores.append(
+                lax.dot_general(
+                    one,
+                    k[i, :, h * HD : (h + 1) * HD],
+                    (((1,), (1,)), ((), ())),
+                    preferred_element_type=jnp.float32,
+                )
+            )
+        scores = jnp.concatenate(scores, axis=0) * score_scale
+        in_range = lax.broadcasted_iota(jnp.int32, (1, span), 1) < length
+        scores = jnp.where(in_range, scores, masked_score)
+        highest = jnp.max(scores, axis=-1, keepdims=True)
+        weight = jnp.exp(scores - highest)
+        total = jnp.sum(weight, axis=-1, keepdims=True)
+        weight = weight.astype(jnp.bfloat16)
+        lane = lax.broadcasted_iota(jnp.int32, (heads * SLOT, HD), 1)
+        stat = jnp.where(lane < HD // 2, highest, total)
+        for h in range(heads):
+            at = slice(h * SLOT, (h + 1) * SLOT)
+            acc[h, i] = jnp.dot(
+                weight[at], v[i, :, h * HD : (h + 1) * HD], preferred_element_type=jnp.float32
+            )
+            stats[h, i] = stat[at]
+
+
+def cache_attention(queries, cache_keys, cache_values, lengths):
+    row_count, span, kv_cols = cache_keys.shape
+    heads = kv_cols // HD
+    rows = 2 if row_count % 2 == 0 else 1
+    shape = (heads, row_count, SLOT, HD)
+    out_block = pl.BlockSpec((heads, rows, SLOT, HD), lambda r, lens: (0, r, 0, 0))
+    in_block = lambda a: pl.BlockSpec((rows, *a.shape[1:]), lambda r, lens: (r, 0, 0))
+    return pl.pallas_call(
+        functools.partial(cache_kernel, heads),
+        grid_spec=pltpu.PrefetchScalarGridSpec(
+            num_scalar_prefetch=1,
+            grid=(row_count // rows,),
+            in_specs=[in_block(queries), in_block(cache_keys), in_block(cache_values)],
+            out_specs=[out_block] * 3,
+        ),
+        out_shape=[
+            jax.ShapeDtypeStruct(shape, jnp.bfloat16),
+            jax.ShapeDtypeStruct(shape, jnp.float32),
+            jax.ShapeDtypeStruct(shape, jnp.float32),
+        ],
+        compiler_params=pltpu.CompilerParams(vmem_limit_bytes=VMEM_LIMIT),
+        cost_estimate=pl.CostEstimate(
+            flops=8 * row_count * SLOT * span * kv_cols,
+            bytes_accessed=4 * row_count * span * kv_cols,
+            transcendentals=row_count * heads * SLOT * span,
+        ),
+        name="cache_attention",
+    )(lengths, queries, cache_keys, cache_values)
+
+
+def merge_kernel(n_units, row_count, *refs):
+    arrived, kept, cosine, sine, stacked, acc, stats = refs[:7]
+    new_kv, context = refs[-2:]
+    every = arrived[...].astype(jnp.float32) + kept[...]
+    for u in range(n_units):
+        total = every[:, u * HEAD_COLS : (u + 1) * HEAD_COLS]
+        keys = total[:, :HD]
+        keys = keys * cosine[...] + pltpu.roll(keys, HD // 2, 1) * sine[...]
+        keys = keys.astype(jnp.bfloat16)
+        values = total[:, HD:].astype(jnp.bfloat16)
+        both = jnp.concatenate([keys, values], axis=1).astype(jnp.float32)
+        for r in range(row_count):
+            new_kv[r, :, u * HEAD_COLS : (u + 1) * HEAD_COLS] = both[
+                r * STEPS : (r + 1) * STEPS
+            ].astype(jnp.bfloat16)
+        query = stacked[u].reshape(row_count * SLOT, HD)
+        scores = (
+            lax.dot_general(query, keys, (((1,), (1,)), ((), ())), preferred_element_type=jnp.float32)
+            * score_scale
+        )
+        at = lax.broadcasted_iota(jnp.int32, scores.shape, 0)
+        to = lax.broadcasted_iota(jnp.int32, scores.shape, 1)
+        seen = (at // SLOT == to // STEPS) & (at % STEPS >= to % STEPS)
+        scores = jnp.where(seen, scores, masked_score)
+        stat = stats[u].reshape(row_count * SLOT, HD)
+        old_highest = stat[:, :1]
+        old_total = stat[:, HD // 2 : HD // 2 + 1]
+        highest = jnp.maximum(jnp.max(scores, axis=-1, keepdims=True), old_highest)
+        weight = jnp.exp(scores - highest)
+        scale = jnp.exp(old_highest - highest)
+        denominator = jnp.sum(weight, axis=-1, keepdims=True) + scale * old_total
+        out = jnp.dot(weight.astype(jnp.bfloat16), values, preferred_element_type=jnp.float32)
+        out = (out + scale * acc[u].reshape(row_count * SLOT, HD)) / denominator
+        for r in range(row_count):
+            for g in range(PER_GROUP):
+                at_row = r * SLOT + g * STEPS
+                at_col = (u * PER_GROUP + g) * HD
+                context[r, :, at_col : at_col + HD] = out[at_row : at_row + STEPS].astype(jnp.bfloat16)
+
+
+def merge(arrived, kept, cosine, sine, attended, previous, first, n_units):
+    heads, row_count = attended[0].shape[:2]
+    at = first // n_units
+    some = pl.BlockSpec((n_units, row_count, SLOT, HD), lambda i: (at, 0, 0, 0))
+    operands = [arrived, kept, cosine, sine]
+    in_specs = [whole(a) for a in operands] + [some] * 3
+    operands += attended
+    aliases = {}
+    if previous is not None:
+        for i, p in enumerate(previous):
+            aliases[len(operands)] = i
+            operands.append(p)
+            in_specs.append(pl.BlockSpec(memory_space=pl.ANY))
+    widths = (HEAD_COLS, PER_GROUP * HD)
+    return pl.pallas_call(
+        functools.partial(merge_kernel, n_units, row_count),
+        grid=(1,),
+        in_specs=in_specs,
+        out_specs=[pl.BlockSpec((row_count, STEPS, n_units * w), lambda i: (0, 0, at)) for w in widths],
+        out_shape=[jax.ShapeDtypeStruct((row_count, STEPS, heads * w), jnp.bfloat16) for w in widths],
+        input_output_aliases=aliases,
+        compiler_params=pltpu.CompilerParams(vmem_limit_bytes=VMEM_LIMIT),
+        name="merge_new",
+    )(*operands)
+
+
+def swap(array, axis, bit):
+    size = lax.axis_size(axis)
+    return lax.ppermute(array, axis, [(i, i ^ bit) for i in range(size)])
+
+
+def add_rounded(a, b):
+    return (a.astype(jnp.float32) + b.astype(jnp.float32)).astype(jnp.bfloat16)
+
+
+def after(value, *earlier):
+    return lax.optimization_barrier((value, *earlier))[0]
+
+
+def fold_rows(arrived, kept, n):
+    total = arrived.astype(jnp.float32) + kept
+    half = total.shape[0] // 2
+    return total[half:].astype(jnp.bfloat16), total[:half]
+
+
+def butterfly_shards(
+    tokens, queries, cache_keys, cache_values, lengths, weights, moment1, moment2, grad_parts
+):
+    group_count = lax.axis_size("group")
+    fsdp_count = lax.axis_size("fsdp")
+    tp_count = lax.axis_size("tp")
+    core = lax.axis_index("group") % 2
+    fsdp = lax.axis_index("fsdp")
+    tp = lax.axis_index("tp")
+    rows, width = weights.shape
+    row_count = tokens.shape[0]
+    n_chunks = width // (tp_count * HEAD_COLS)
+    local = grad_parts[0]
+    state = (weights, moment1, moment2)
+    zero = jnp.zeros_like(core)
+    both_parts = jnp.stack([core, tp, zero]).astype(jnp.int32)
+
+    cut = n_chunks // 2
+    chunks = [(0, cut), (cut, n_chunks - cut)]
+
+    def columns(source, half, first, n):
+        return lax.dynamic_slice(
+            source, (0, (half * n_chunks + first) * HEAD_COLS), (rows, n * HEAD_COLS)
+        )
+
+    cast, arrived, own, crossed = [], [], [], []
+    source = local
+    for first, n in chunks:
+        cast.append(columns(source, 1 - core, first, n).astype(jnp.bfloat16))
+        arrived.append(swap(cast[-1], "group", 1))
+        source = after(local, cast[-1])
+    source = local
+    for (first, n), got in zip(chunks, arrived):
+        own.append(add_rounded(columns(source, core, first, n), got))
+        crossed.append(swap(own[-1], "group", 2))
+        source = after(local, own[-1])
+
+    toks = []
+    early = after(tokens, own[-1])
+    for d in range(fsdp_count):
+        at = ((fsdp ^ d) * tp_count + tp) * rows
+        piece = lax.dynamic_slice(early, (0, 0, at), (row_count, STEPS, rows))
+        piece = piece.reshape(row_count * STEPS, rows)
+        toks.append(piece if d == 0 else swap(piece, "fsdp", d))
+
+    cosine, sine = rotation_tables(lengths)
+    attended = cache_attention(after(queries, own[-1]), cache_keys, cache_values, lengths)
+
+    updated = None
+    outs = None
+    done = (attended[1],)
+    for (first, n), mine, other in zip(chunks, own, crossed):
+        bit = 2
+        while True:
+            mine = add_rounded(mine, after(other, *done))
+            bit *= 2
+            if bit >= group_count:
+                break
+            other = swap(mine, "group", bit)
+        totals = (mine, swap(mine, "group", 1))
+        updated, (sent, kept) = adam_call(
+            both_parts, totals, state, toks, first, n, n_chunks, True, True, updated
+        )
+        done = (kept,)
+        got = swap(sent, "tp", 1)
+        distance = fsdp_count // 2
+        while distance:
+            sent, kept = fold_rows(got, kept, fsdp_count)
+            got = swap(sent, "fsdp", distance)
+            distance //= 2
+        outs = merge(got, kept, cosine, sine, attended, outs, first, n)
+    return (*updated, *outs)
 
 
 def rotate_keys(keys, positions):
@@ -44,7 +390,7 @@
     )
 
 
-def shards(
+def plain_shards(
     tokens, queries, cache_keys, cache_values, lengths, weights, moment1, moment2, grad_parts
 ):
     gradient = lax.psum(grad_parts[0], "group")
@@ -71,10 +417,8 @@
     new_keys = rotate_keys(projected[:, :, :, 0], positions[:, :, None])
     fresh = jnp.stack([new_keys, projected[:, :, :, 1]], axis=3).astype(jnp.bfloat16)
     new_kv = fresh.reshape(row_count, STEPS, head_cols)
-    per_group = QH // KVH
-    score_scale = 1.0 / math.sqrt(HD)
     span_length = cache_keys.shape[1]
-    grouped = queries.reshape(row_count, STEPS, kv_heads, per_group, HD)
+    grouped = queries.reshape(row_count, STEPS, kv_heads, PER_GROUP, HD)
     cached_keys = cache_keys.reshape(row_count, span_length, kv_heads, HD)
     cached_values = cache_values.reshape(row_count, span_length, kv_heads, HD)
     new_scores = (
@@ -108,8 +452,12 @@
         fresh[:, :, :, 1],
         preferred_element_type=jnp.float32,
     )
-    context = context.reshape(row_count, STEPS, kv_heads * per_group * HD).astype(jnp.bfloat16)
+    context = context.reshape(row_count, STEPS, kv_heads * PER_GROUP * HD).astype(jnp.bfloat16)
     return (new_weights, new_moment1, new_moment2, new_kv, context)
+
+
+def power_of_two(n):
+    return n > 1 and n & (n - 1) == 0
 
 
 def solution(mesh):
@@ -131,4 +479,7 @@
         P(("group", "fsdp"), None, "tp"),
         P(("group", "fsdp"), None, "tp"),
     )
+    sizes = mesh.shape
+    pairwise = power_of_two(sizes["group"]) and power_of_two(sizes["fsdp"]) and sizes["tp"] == 2
+    shards = butterfly_shards if pairwise else plain_shards
     return jax.shard_map(shards, mesh=mesh, in_specs=in_specs, out_specs=out_specs, check_vma=False)

time: 216 us -> 80.7 us (0.37)
  waiting for transfers between devices: 140 us -> 18.1 us
  Pallas kernels: 0 us -> 32 us
  starting transfers between devices: 0.08 us -> 14.9 us
  local copies, waits for them, and re-layouts: 22.2 us -> 8.5 us
  between operations: 14.2 us -> 0.87 us
  blocking collectives: 13.1 us -> 0 us
  matrix products: 10 us -> 0 us
  other arithmetic: 15.8 us -> 5.92 us
    psum x1 -> x0, waiting for transfers between devices: 93.8 us -> none  [shards(): gradient = lax.psum(grad_parts[0], 'group')]
    reduce_scatter x1 -> x0, waiting for transfers between devices: 45.6 us -> none  [shards(): lax.psum_scatter(partial_terms, ('fsdp', 'tp'), scatter_dimension=0, tile...]
    pallas_call x0 -> x5, Pallas kernels: none -> 32 us  [the longest x2 18.7 us: adam_call(): pl.pallas_call(functools.partial(adam_kernel, n, len(toks) if project els...]
    ppermute x0 -> x15, waiting for transfers between devices: none -> 18.1 us  [swap(): return lax.ppermute(array, axis, [(i, i ^ bit) for i in range(size)])]
    ppermute x0 -> x15, starting transfers between devices: none -> 14.9 us  [swap(): return lax.ppermute(array, axis, [(i, i ^ bit) for i in range(size)])]
    reshape x5 -> x4, local copies, waits for them, and re-layouts: 15.2 us -> 0.68 us  [butterfly_shards(): piece = piece.reshape(row_count * STEPS, rows)]
    dot_general x1 -> x0, other arithmetic: 13.7 us -> none  [shards(): jnp.dot(arrived, weight_shard, preferred_element_type=jnp.float32)]
    all_to_all x1 -> x0, blocking collectives: 13.1 us -> none  [shards(): lax.all_to_all(own_columns, 'fsdp', split_axis=2, concat_axis=0, tiled=True)]
  transfers between devices with their start and end apart: 2 -> 15, of which waited for: 2 -> 7; matrix products, arithmetic and copies ran while one was open for 9% -> 11% of each run, Pallas kernels for 0% -> 36%
where the time goes in v2:
time: 80.7 us; the launch traced here: 80.2 us
  Pallas kernels  32 us (40%)
  waiting for transfers between devices  18.1 us (22%)
  starting transfers between devices  14.9 us (18%)
  local copies, waits for them, and re-layouts  8.5 us (11%)
  other arithmetic  5.92 us (7%)
  between operations  0.87 us (1%)
    pallas_call x2, Pallas kernels, adam_call(): pl.pallas_call(functools.partial(adam_kernel, n, len(toks) if project els...  18.7 us
    ppermute x15, waiting for transfers between devices, swap(): return lax.ppermute(array, axis, [(i, i ^ bit) for i in range(size)])  18.1 us
    ppermute x15, starting transfers between devices, swap(): return lax.ppermute(array, axis, [(i, i ^ bit) for i in range(size)])  14.9 us
    pallas_call x1, Pallas kernels, cache_attention(): pl.pallas_call(functools.partial(cache_kernel, heads), grid_spec=pltpu.Pr...  7.8 us
    pallas_call x2, Pallas kernels, merge(): pl.pallas_call(functools.partial(merge_kernel, n_units, row_count), grid=...  5.48 us
    unnamed x24, local copies, waits for them, and re-layouts  3.58 us
    convert_element_type x4, other arithmetic, add_rounded(): return (a.astype(jnp.float32) + b.astype(jnp.float32)).astype(jnp.bfloat16)  3.39 us
    convert_element_type x2, local copies, waits for them, and re-layouts, butterfly_shards(): cast.append(columns(source, 1 - core, first, n).astype(jnp.bfloat16))  2.8 us
  transfers between devices with their start and end apart: 15, of which 7 were waited for; matrix products, arithmetic and copies ran while one was open for 11% of the time, Pallas kernels for 36%

profile of v2, /device:TPU:0, one launch (start us, length us, event | category | flops | bytes accessed | tf_op | source)
XLA Modules:
  0.0 80.2 jit_solution(13040855355909872403)
XLA Ops:
  0.6 1.4 %fusion.1 = bf16[640,512]{1,0:T(8,128)(2,1)S(1)} fusion(f32[1,640,2048]{2,1,0:T(8,128)} %param.17, s32[]{:T(128)S(6)} %select_n.33), kind=kLoop, calls=%fused_computation.7 | loop fusion | bytes 1310724 | tf_op jit(solution)/shard_map/convert_element_type | solution.py:332
  2.6 1.4 %dynamic-slice_convert_fusion = bf16[640,512]{1,0:T(8,128)(2,1)S(1)} fusion(f32[640,2048]{1,0:T(8,128)} %bitcast.9, s32[]{:T(128)S(6)} %select_n.35), kind=kLoop, calls=%fused_computation.5 | loop fusion | bytes 1310724 | tf_op jit(solution)/shard_map/convert_element_type | solution.py:332
  4.3 1.5 %fusion = bf16[640,512]{1,0:T(8,128)(2,1)S(1)} fusion(bf16[640,512]{1,0:T(8,128)(2,1)S(1)} %collective-permute-done, f32[1,640,2048]{2,1,0:T(8,128)} %param.17, s32[]{:T(128)S(6)} %select_n.32), kind=kLoop, calls=%fused_computation.1 | loop fusion | flops 983040 | bytes 2621444 | tf_op jit(solution)/shard_map/convert_element_type | solution.py:291
  5.8 2.9 %collective-permute-start.3 = (bf16[640,512]{1,0:T(8,128)(2,1)S(1)}, bf16[640,512]{1,0:T(8,128)(2,1)S(1)}, u32[]{:S(2)}, u32[]{:S(2)}) collective-permute-start(bf16[640,512]{1,0:T(8,128)(2,1)S(1)} %fusion), channel_id=1, source_target_pairs={{0,16},{8,24},{16,0},{24,8},{1,17},{9,25},{17,1},{25,9},{2,18},{10... | collective-permute-start | bytes 1966088 | tf_op jit(solution)/shard_map/ppermute | solution.py:287
  8.8 1.5 %add_convert_fusion.2 = bf16[640,512]{1,0:T(8,128)(2,1)S(1)} fusion(bf16[640,512]{1,0:T(8,128)(2,1)S(1)} %collective-permute-done.1, f32[640,2048]{1,0:T(8,128)} %bitcast.10, s32[]{:T(128)S(6)} %select_n.34), kind=kLoop, calls=%fused_computation.4 | loop fusion | flops 983040 | bytes 2621444 | tf_op jit(solution)/shard_map/convert_element_type | solution.py:291
  10.3 7.8 %cache_attention.1 = (bf16[4,8,32,128]{3,2,1,0:T(8,128)(2,1)}, f32[4,8,32,128]{3,2,1,0:T(8,128)}, f32[4,8,32,128]{3,2,1,0:T(8,128)}) custom-call(s32[8]{0:T(128)} %lens.1, bf16[8,4,2560]{2,1,0:T(4,128)(2,1)} %q, bf16[8,512,512]{2,1,0:T(8,128)(2,1)} %k.1, bf16[8,512,512]{2,1,0:T(8,128)(2,1)} %v.1), custom_call_target="tpu_custom_call" | custom-call | flops 536870912 | bytes 8388608 | tf_op jit(solution)/shard_map/cache_attention/pallas_call | solution.py:196
  18.1 5.7 %collective-permute-done.3 = bf16[640,512]{1,0:T(8,128)(2,1)S(1)} collective-permute-done((bf16[640,512]{1,0:T(8,128)(2,1)S(1)}, bf16[640,512]{1,0:T(8,128)(2,1)S(1)}, u32[]{:S(2)}, u32[]{:S(2)}) %collective-permute-start.3) | collective-permute-done | bytes 655392 | tf_op jit(solution)/shard_map/ppermute | solution.py:287
  24.0 1.8 %collective-permute-start.2 = (bf16[640,512]{1,0:T(8,128)(2,1)S(1)}, bf16[640,512]{1,0:T(8,128)(2,1)S(1)}, u32[]{:S(2)}, u32[]{:S(2)}) collective-permute-start(bf16[640,512]{1,0:T(8,128)(2,1)S(1)} %add_convert_fusion.2), channel_id=1, source_target_pairs={{0,16},{8,24},{16,0},{24,8},{1,17},{9,25},{17,1},{25,9},{2,18},{10... | collective-permute-start | bytes 1966088 | tf_op jit(solution)/shard_map/ppermute | solution.py:287
  26.0 1.6 %collective-permute-start.5 = (bf16[32,640]{1,0:T(8,128)(2,1)S(1)}, bf16[32,640]{1,0:T(8,128)(2,1)S(1)}, u32[]{:S(2)}, u32[]{:S(2)}) collective-permute-start(bf16[32,640]{1,0:T(8,128)(2,1)S(1)} %reshape.48), channel_id=1, source_target_pairs={{0,2},{2,0},{4,6},{6,4},{1,3},{3,1},{5,7},{7,5},{8,10},{10,8},{12,... | collective-permute-start | bytes 122888 | tf_op jit(solution)/shard_map/ppermute | solution.py:287
  27.6 2.6 %collective-permute-start.6 = (bf16[32,640]{1,0:T(8,128)(2,1)S(1)}, bf16[32,640]{1,0:T(8,128)(2,1)S(1)}, u32[]{:S(2)}, u32[]{:S(2)}) collective-permute-start(bf16[32,640]{1,0:T(8,128)(2,1)S(1)} %reshape.49), channel_id=1, source_target_pairs={{0,4},{2,6},{4,0},{6,2},{1,5},{3,7},{5,1},{7,3},{8,12},{10,14},{12... | collective-permute-start | bytes 122888 | tf_op jit(solution)/shard_map/ppermute | solution.py:287
  31.7 1.7 %collective-permute-done.6.refs_7_ = bf16[32,640]{1,0:T(8,128)(2,1)S(1)} collective-permute-done((bf16[32,640]{1,0:T(8,128)(2,1)S(1)}, bf16[32,640]{1,0:T(8,128)(2,1)S(1)}, u32[]{:S(2)}, u32[]{:S(2)}) %collective-permute-start.6) | collective-permute-done | bytes 40992 | tf_op jit(solution)/shard_map/ppermute | solution.py:287
  33.3 2.7 %collective-permute-done.7.refs_8_ = bf16[32,640]{1,0:T(8,128)(2,1)S(1)} collective-permute-done((bf16[32,640]{1,0:T(8,128)(2,1)S(1)}, bf16[32,640]{1,0:T(8,128)(2,1)S(1)}, u32[]{:S(2)}, u32[]{:S(2)}) %collective-permute-start.7) | collective-permute-done | bytes 40992 | tf_op jit(solution)/shard_map/ppermute | solution.py:287
  36.6 0.9 %copy-done.2 = bf16[640,512]{1,0:T(8,128)(2,1)} copy-done((bf16[640,512]{1,0:T(8,128)(2,1)}, bf16[640,512]{1,0:T(8,128)(2,1)S(1)}, u32[]{:S(2)}) %copy-start.2) | copy-done | bytes 655384
  37.5 9.3 %adam_project.2 = (f32[640,2048]{1,0:T(8,128)}, f32[640,2048]{1,0:T(8,128)}, f32[640,2048]{1,0:T(8,128)}, bf16[128,512]{1,0:T(8,128)(2,1)}, f32[128,512]{1,0:T(8,128)}) custom-call(s32[3]{0:T(128)} %pad_add_fusion.place, bf16[640,512]{1,0:T(8,128)(2,1)} %copy-done, bf16[640,512]{1,0:T(8,128)(2,1)} %copy-done.2, f32[640,2048]{1,0:T(8,128)} %refs_2_.3, ...), custom_call_target="tpu_custom_call" | custom-call | flops 167772160 | bytes 17039360 | tf_op jit(solution)/shard_map/adam_project/pallas_call | solution.py:125
  47.2 1.6 %collective-permute-start.12 = (bf16[128,512]{1,0:T(8,128)(2,1)}, bf16[128,512]{1,0:T(8,128)(2,1)S(1)}, u32[]{:S(2)}, u32[]{:S(2)}) collective-permute-start(bf16[128,512]{1,0:T(8,128)(2,1)} %get-tuple-element.46), channel_id=1, source_target_pairs={{0,1},{1,0},{2,3},{3,2},{4,5},{5,4},{6,7},{7,6},{8,9},{9,8},{10,11... | collective-permute-start | bytes 393224 | tf_op jit(solution)/shard_map/ppermute | solution.py:287
  49.2 0.9 %copy-done.3 = bf16[640,512]{1,0:T(8,128)(2,1)} copy-done((bf16[640,512]{1,0:T(8,128)(2,1)}, bf16[640,512]{1,0:T(8,128)(2,1)S(1)}, u32[]{:S(2)}) %copy-start.3) | copy-done | bytes 655384
  50.0 9.4 %adam_project.3 = (f32[640,2048]{1,0:T(8,128)}, f32[640,2048]{1,0:T(8,128)}, f32[640,2048]{1,0:T(8,128)}, bf16[128,512]{1,0:T(8,128)(2,1)}, f32[128,512]{1,0:T(8,128)}) custom-call(s32[3]{0:T(128)} %pad_add_fusion.place, bf16[640,512]{1,0:T(8,128)(2,1)} %copy-done.1, ...), custom_call_target="tpu_custom_call", output_to_operand_aliasing={{0}: (10, {}), {1}: (11, {}), {2}: (12, {})} | custom-call | flops 167772160 | bytes 17039360 | tf_op jit(solution)/shard_map/adam_project/pallas_call | solution.py:125
  59.5 1.6 %collective-permute-start.9 = (bf16[128,512]{1,0:T(8,128)(2,1)}, bf16[128,512]{1,0:T(8,128)(2,1)S(1)}, u32[]{:S(2)}, u32[]{:S(2)}) collective-permute-start(bf16[128,512]{1,0:T(8,128)(2,1)} %get-tuple-element.42), channel_id=1, source_target_pairs={{0,1},{1,0},{2,3},{3,2},{4,5},{5,4},{6,7},{7,6},{8,9},{9,8},{10,11... | collective-permute-start | bytes 393224 | tf_op jit(solution)/shard_map/ppermute | solution.py:287
  61.4 3.8 %collective-permute-done.9 = bf16[128,512]{1,0:T(8,128)(2,1)S(1)} collective-permute-done((bf16[128,512]{1,0:T(8,128)(2,1)}, bf16[128,512]{1,0:T(8,128)(2,1)S(1)}, u32[]{:S(2)}, u32[]{:S(2)}) %collective-permute-start.9) | collective-permute-done | bytes 131104 | tf_op jit(solution)/shard_map/ppermute | solution.py:287
  65.2 1.0 %convert_add_fusion.1 = f32[128,512]{1,0:T(8,128)S(1)} fusion(f32[128,512]{1,0:T(8,128)} %get-tuple-element.43, bf16[128,512]{1,0:T(8,128)(2,1)S(1)} %collective-permute-done.9), kind=kLoop, calls=%fused_computation.9 | loop fusion | flops 131072 | bytes 655360 | tf_op jit(solution)/shard_map/add | solution.py:299
  66.6 1.1 %collective-permute-start.14 = (bf16[32,512]{1,0:T(8,128)(2,1)S(1)}, bf16[32,512]{1,0:T(8,128)(2,1)S(1)}, u32[]{:S(2)}, u32[]{:S(2)}) collective-permute-start(bf16[32,512]{1,0:T(8,128)(2,1)S(1)} %slice.52), channel_id=1, source_target_pairs={{0,2},{2,0},{4,6},{6,4},{1,3},{3,1},{5,7},{7,5},{8,10},{10,8},{12,... | collective-permute-start | bytes 98312 | tf_op jit(solution)/shard_map/ppermute | solution.py:287
  67.7 3.8 %collective-permute-done.10 = bf16[64,512]{1,0:T(8,128)(2,1)S(1)} collective-permute-done((bf16[64,512]{1,0:T(8,128)(2,1)S(1)}, bf16[64,512]{1,0:T(8,128)(2,1)S(1)}, u32[]{:S(2)}, u32[]{:S(2)}) %collective-permute-start.10) | collective-permute-done | bytes 65568 | tf_op jit(solution)/shard_map/ppermute | solution.py:287
  73.5 2.7 %merge_new.2 = (bf16[8,4,1024]{2,1,0:T(4,128)(2,1)}, bf16[8,4,2560]{2,1,0:T(4,128)(2,1)}) custom-call(bf16[32,512]{1,0:T(8,128)(2,1)} %copy-done.10, f32[32,512]{1,0:T(8,128)} %slice.43.refs_1_, f32[32,128]{1,0:T(8,128)} %get-tuple-element.58.refs_2_, f32[32,128]{1,0:T(8,128)} %get-tuple-element.59.refs_3_, ...), custom_call_target="tpu_custom_call" | custom-call | tf_op jit(solution)/shard_map/merge_new/pallas_call | solution.py:273
  77.5 2.7 %merge_new.3 = (bf16[8,4,1024]{2,1,0:T(4,128)(2,1)}, bf16[8,4,2560]{2,1,0:T(4,128)(2,1)}) custom-call(bf16[32,512]{1,0:T(8,128)(2,1)} %copy-done.9, f32[32,512]{1,0:T(8,128)} %slice.39.refs_1_, f32[32,128]{1,0:T(8,128)} %get-tuple-element.58.refs_2_, f32[32,128]{1,0:T(8,128)} %get-tuple-element.59.refs_3_, ...), custom_call_target="tpu_custom_call", output_to_operand_aliasing={{0}: (7, {}), {1}: (8, {})} | custom-call | tf_op jit(solution)/shard_map/merge_new/pallas_call | solution.py:273
  (62 shorter events, 7.9 us)
Async XLA Ops:
  2.1 2.2 %collective-permute-start = (bf16[640,512]{1,0:T(8,128)(2,1)S(1)}, bf16[640,512]{1,0:T(8,128)(2,1)S(1)}, u32[]{:S(2)}, u32[]{:S(2)}) collective-permute-start(bf16[640,512]{1,0:T(8,128)(2,1)S(1)} %fusion.1), channel_id=1, source_target_pairs={{0,8},{8,0},{16,24},{24,16},{1,9},{9,1},{17,25},{25,17},{2,10},{10... | collective-permute-start | bytes 1966088 | tf_op jit(solution)/shard_map/ppermute | solution.py:287
  4.0 4.8 %collective-permute-start.1 = (bf16[640,512]{1,0:T(8,128)(2,1)S(1)}, bf16[640,512]{1,0:T(8,128)(2,1)S(1)}, u32[]{:S(2)}, u32[]{:S(2)}) collective-permute-start(bf16[640,512]{1,0:T(8,128)(2,1)S(1)} %dynamic-slice_convert_fusion), channel_id=1, source_target_pairs={{0,8},{8,0},{16,24},{24,16},{1,9},{9,1},{17,25},{25,17},{2,10},{10... | collective-permute-start | bytes 1966088 | tf_op jit(solution)/shard_map/ppermute | solution.py:287
  5.8 18.0 %collective-permute-start.3 = (bf16[640,512]{1,0:T(8,128)(2,1)S(1)}, bf16[640,512]{1,0:T(8,128)(2,1)S(1)}, u32[]{:S(2)}, u32[]{:S(2)}) collective-permute-start(bf16[640,512]{1,0:T(8,128)(2,1)S(1)} %fusion), channel_id=1, source_target_pairs={{0,16},{8,24},{16,0},{24,8},{1,17},{9,25},{17,1},{25,9},{2,18},{10... | collective-permute-start | bytes 1966088 | tf_op jit(solution)/shard_map/ppermute | solution.py:287
  10.3 15.6 %copy-start.8 = (bf16[8,4,5120]{2,1,0:T(4,128)(2,1)S(1)}, bf16[8,4,5120]{2,1,0:T(4,128)(2,1)}, u32[]{:S(2)}) copy-start(bf16[8,4,5120]{2,1,0:T(4,128)(2,1)} %param.9) | copy-start | bytes 983044
  24.0 12.1 %copy-start = (bf16[640,512]{1,0:T(8,128)(2,1)}, bf16[640,512]{1,0:T(8,128)(2,1)S(1)}, u32[]{:S(2)}) copy-start(bf16[640,512]{1,0:T(8,128)(2,1)S(1)} %add_convert_fusion.1.refs_0_) | copy-start | bytes 1966084
  24.0 12.1 %collective-permute-start.4 = (bf16[640,512]{1,0:T(8,128)(2,1)S(1)}, bf16[640,512]{1,0:T(8,128)(2,1)S(1)}, u32[]{:S(2)}, u32[]{:S(2)}) collective-permute-start(bf16[640,512]{1,0:T(8,128)(2,1)S(1)} %add_convert_fusion.1.refs_0_), channel_id=1, source_target_pairs={{0,8},{8,0},{16,24},{24,16},{1,9},{9,1},{17,25},{25,17},{2,10},{10... | collective-permute-start | bytes 1966088 | tf_op jit(solution)/shard_map/ppermute | solution.py:287
  24.0 22.8 %collective-permute-start.2 = (bf16[640,512]{1,0:T(8,128)(2,1)S(1)}, bf16[640,512]{1,0:T(8,128)(2,1)S(1)}, u32[]{:S(2)}, u32[]{:S(2)}) collective-permute-start(bf16[640,512]{1,0:T(8,128)(2,1)S(1)} %add_convert_fusion.2), channel_id=1, source_target_pairs={{0,16},{8,24},{16,0},{24,8},{1,17},{9,25},{17,1},{25,9},{2,18},{10... | collective-permute-start | bytes 1966088 | tf_op jit(solution)/shard_map/ppermute | solution.py:287
  26.0 5.7 %collective-permute-start.5 = (bf16[32,640]{1,0:T(8,128)(2,1)S(1)}, bf16[32,640]{1,0:T(8,128)(2,1)S(1)}, u32[]{:S(2)}, u32[]{:S(2)}) collective-permute-start(bf16[32,640]{1,0:T(8,128)(2,1)S(1)} %reshape.48), channel_id=1, source_target_pairs={{0,2},{2,0},{4,6},{6,4},{1,3},{3,1},{5,7},{7,5},{8,10},{10,8},{12,... | collective-permute-start | bytes 122888 | tf_op jit(solution)/shard_map/ppermute | solution.py:287
  27.6 5.7 %collective-permute-start.6 = (bf16[32,640]{1,0:T(8,128)(2,1)S(1)}, bf16[32,640]{1,0:T(8,128)(2,1)S(1)}, u32[]{:S(2)}, u32[]{:S(2)}) collective-permute-start(bf16[32,640]{1,0:T(8,128)(2,1)S(1)} %reshape.49), channel_id=1, source_target_pairs={{0,4},{2,6},{4,0},{6,2},{1,5},{3,7},{5,1},{7,3},{8,12},{10,14},{12... | collective-permute-start | bytes 122888 | tf_op jit(solution)/shard_map/ppermute | solution.py:287
  30.2 5.8 %collective-permute-start.7 = (bf16[32,640]{1,0:T(8,128)(2,1)S(1)}, bf16[32,640]{1,0:T(8,128)(2,1)S(1)}, u32[]{:S(2)}, u32[]{:S(2)}) collective-permute-start(bf16[32,640]{1,0:T(8,128)(2,1)S(1)} %reshape.50), channel_id=1, source_target_pairs={{0,6},{2,4},{4,2},{6,0},{1,7},{3,5},{5,3},{7,1},{8,14},{10,12},{12... | collective-permute-start | bytes 122888 | tf_op jit(solution)/shard_map/ppermute | solution.py:287
  31.7 15.4 %copy-start.11 = (s32[8]{0:T(128)S(1)}, s32[8]{0:T(128)}, u32[]{:S(2)}) copy-start(s32[8]{0:T(128)} %lens.1) | copy-start | bytes 100
  31.7 4.4 %copy-start.5 = (bf16[32,640]{1,0:T(8,128)(2,1)}, bf16[32,640]{1,0:T(8,128)(2,1)S(1)}, u32[]{:S(2)}) copy-start(bf16[32,640]{1,0:T(8,128)(2,1)S(1)} %collective-permute-done.5.refs_6_) | copy-start | bytes 122884
  33.3 2.7 %copy-start.6 = (bf16[32,640]{1,0:T(8,128)(2,1)}, bf16[32,640]{1,0:T(8,128)(2,1)S(1)}, u32[]{:S(2)}) copy-start(bf16[32,640]{1,0:T(8,128)(2,1)S(1)} %collective-permute-done.6.refs_7_) | copy-start | bytes 122884
  36.6 0.9 %copy-start.2 = (bf16[640,512]{1,0:T(8,128)(2,1)}, bf16[640,512]{1,0:T(8,128)(2,1)S(1)}, u32[]{:S(2)}) copy-start(bf16[640,512]{1,0:T(8,128)(2,1)S(1)} %collective-permute-done.4.refs_1_) | copy-start | bytes 1966084
  47.0 2.2 %copy-start.1 = (bf16[640,512]{1,0:T(8,128)(2,1)}, bf16[640,512]{1,0:T(8,128)(2,1)S(1)}, u32[]{:S(2)}) copy-start(bf16[640,512]{1,0:T(8,128)(2,1)S(1)} %add_convert_fusion.refs_0_) | copy-start | bytes 1966084
  47.0 2.2 %collective-permute-start.8 = (bf16[640,512]{1,0:T(8,128)(2,1)S(1)}, bf16[640,512]{1,0:T(8,128)(2,1)S(1)}, u32[]{:S(2)}, u32[]{:S(2)}) collective-permute-start(bf16[640,512]{1,0:T(8,128)(2,1)S(1)} %add_convert_fusion.refs_0_), channel_id=1, source_target_pairs={{0,8},{8,0},{16,24},{24,16},{1,9},{9,1},{17,25},{25,17},{2,10},{10... | collective-permute-start | bytes 1966088 | tf_op jit(solution)/shard_map/ppermute | solution.py:287
  47.2 13.8 %collective-permute-start.12 = (bf16[128,512]{1,0:T(8,128)(2,1)}, bf16[128,512]{1,0:T(8,128)(2,1)S(1)}, u32[]{:S(2)}, u32[]{:S(2)}) collective-permute-start(bf16[128,512]{1,0:T(8,128)(2,1)} %get-tuple-element.46), channel_id=1, source_target_pairs={{0,1},{1,0},{2,3},{3,2},{4,5},{5,4},{6,7},{7,6},{8,9},{9,8},{10,11... | collective-permute-start | bytes 393224 | tf_op jit(solution)/shard_map/ppermute | solution.py:287
  49.2 0.9 %copy-start.3 = (bf16[640,512]{1,0:T(8,128)(2,1)}, bf16[640,512]{1,0:T(8,128)(2,1)S(1)}, u32[]{:S(2)}) copy-start(bf16[640,512]{1,0:T(8,128)(2,1)S(1)} %collective-permute-done.8.refs_1_) | copy-start | bytes 1966084
  50.0 11.0 %copy-start.4 = (f32[128,512]{1,0:T(8,128)S(1)}, f32[128,512]{1,0:T(8,128)}, u32[]{:S(2)}) copy-start(f32[128,512]{1,0:T(8,128)} %get-tuple-element.34) | copy-start | bytes 786436
  59.5 5.8 %collective-permute-start.9 = (bf16[128,512]{1,0:T(8,128)(2,1)}, bf16[128,512]{1,0:T(8,128)(2,1)S(1)}, u32[]{:S(2)}, u32[]{:S(2)}) collective-permute-start(bf16[128,512]{1,0:T(8,128)(2,1)} %get-tuple-element.42), channel_id=1, source_target_pairs={{0,1},{1,0},{2,3},{3,2},{4,5},{5,4},{6,7},{7,6},{8,9},{9,8},{10,11... | collective-permute-start | bytes 393224 | tf_op jit(solution)/shard_map/ppermute | solution.py:287
  61.1 5.4 %collective-permute-start.13 = (bf16[64,512]{1,0:T(8,128)(2,1)S(1)}, bf16[64,512]{1,0:T(8,128)(2,1)S(1)}, u32[]{:S(2)}, u32[]{:S(2)}) collective-permute-start(bf16[64,512]{1,0:T(8,128)(2,1)S(1)} %slice.50), channel_id=1, source_target_pairs={{0,4},{2,6},{4,0},{6,2},{1,5},{3,7},{5,1},{7,3},{8,12},{10,14},{12... | collective-permute-start | bytes 196616 | tf_op jit(solution)/shard_map/ppermute | solution.py:287
  66.2 5.2 %collective-permute-start.10 = (bf16[64,512]{1,0:T(8,128)(2,1)S(1)}, bf16[64,512]{1,0:T(8,128)(2,1)S(1)}, u32[]{:S(2)}, u32[]{:S(2)}) collective-permute-start(bf16[64,512]{1,0:T(8,128)(2,1)S(1)} %slice.51), channel_id=1, source_target_pairs={{0,4},{2,6},{4,0},{6,2},{1,5},{3,7},{5,1},{7,3},{8,12},{10,14},{12... | collective-permute-start | bytes 196616 | tf_op jit(solution)/shard_map/ppermute | solution.py:287
  66.6 6.3 %collective-permute-start.14 = (bf16[32,512]{1,0:T(8,128)(2,1)S(1)}, bf16[32,512]{1,0:T(8,128)(2,1)S(1)}, u32[]{:S(2)}, u32[]{:S(2)}) collective-permute-start(bf16[32,512]{1,0:T(8,128)(2,1)S(1)} %slice.52), channel_id=1, source_target_pairs={{0,2},{2,0},{4,6},{6,4},{1,3},{3,1},{5,7},{7,5},{8,10},{10,8},{12,... | collective-permute-start | bytes 98312 | tf_op jit(solution)/shard_map/ppermute | solution.py:287
  71.5 5.4 %collective-permute-start.11 = (bf16[32,512]{1,0:T(8,128)(2,1)S(1)}, bf16[32,512]{1,0:T(8,128)(2,1)S(1)}, u32[]{:S(2)}, u32[]{:S(2)}) collective-permute-start(bf16[32,512]{1,0:T(8,128)(2,1)S(1)} %slice.53), channel_id=1, source_target_pairs={{0,2},{2,0},{4,6},{6,4},{1,3},{3,1},{5,7},{7,5},{8,10},{10,8},{12,... | collective-permute-start | bytes 98312 | tf_op jit(solution)/shard_map/ppermute | solution.py:287
  (3 other events, 1.8 us)

commit v3 on v2

--- a/solution.py
+++ b/solution.py
@@ -25,7 +25,7 @@
 correct_two = 1.0 - 0.95**10
 masked_score = -1e30
 score_scale = 1.0 / math.sqrt(HD)
-VMEM_LIMIT = 60 * 1024 * 1024
+VMEM_LIMIT = 12 * 1024 * 1024
 
 
 def adam_update(weights, moment1, moment2, gradient):
@@ -55,103 +55,195 @@
     return pl.BlockSpec(a.shape, lambda *_: (0,) * len(a.shape))
 
 
-def adam_kernel(n_parts, n_tok, update, project, place, *refs):
-    totals = refs[:n_parts]
-    w, m1, m2 = refs[n_parts : n_parts + 3]
-    toks = refs[n_parts + 3 : n_parts + 3 + n_tok]
-    outs = refs[len(refs) - 3 * update - 2 * project :]
-    part = pl.program_id(0)
-    cols = pl.program_id(1)
-    gradient = totals[0][...]
-    for j in range(1, n_parts):
-        gradient = jnp.where(part == j, totals[j][...], gradient)
-    results = adam_update(w[...], m1[...], m2[...], gradient.astype(jnp.float32))
-    if update:
-        for ref, value in zip(outs, results):
-            ref[...] = value
-    if project:
-        sent, kept = outs[-2:]
-        tok = jnp.concatenate([t[...] for t in toks], axis=0)
-        terms = jnp.dot(tok, results[0].astype(jnp.bfloat16), preferred_element_type=jnp.float32)
-        width = terms.shape[1]
-        at = pl.ds(pl.multiple_of(cols * width, width), width)
-        half = half_of(place, part)
-        stays = half == place[1]
-
-        @pl.when(stays)
-        def _():
-            kept[:, at] = terms
-
-        @pl.when(jnp.logical_not(stays))
-        def _():
-            sent[:, at] = terms.astype(jnp.bfloat16)
-
-
-def half_of(place, part):
-    return jnp.where(part + place[2] == 1, 1 - place[0], place[0])
-
-
-def adam_call(place, totals, state, toks, first, n_units, n_chunks, update, project, previous=None, sums=None):
-    weights = state[0]
-    rows, width = weights.shape
-    n = len(totals)
-
-    def column(j, b, place):
-        return (0, half_of(place, j) * n_chunks + first + b)
-
-    def total_map(i):
-        return lambda j, b, place: (0, jnp.where(j == i, b, jnp.where(j < i, 0, n_units - 1)))
-
-    block = pl.BlockSpec((rows, HEAD_COLS), column)
-    in_specs = [pl.BlockSpec((rows, HEAD_COLS), total_map(i)) for i in range(n)] + [block] * 3
-    operands = [*totals, *state]
-    if project:
-        operands += toks
-        in_specs += [whole(t) for t in toks]
-    out_specs, out_shape, aliases = [], [], {}
-    if update:
-        out_specs += [block] * 3
-        out_shape += [jax.ShapeDtypeStruct((rows, width), jnp.float32)] * 3
-        if previous is not None:
-            for i, p in enumerate(previous):
-                aliases[1 + len(operands)] = i
-                operands.append(p)
-                in_specs.append(pl.BlockSpec(memory_space=pl.ANY))
-    n_tokens = sum(t.shape[0] for t in toks)
-    if project:
-        for dtype in (jnp.bfloat16, jnp.float32):
-            out_shape.append(jax.ShapeDtypeStruct((n_tokens, n_units * HEAD_COLS), dtype))
-            out_specs.append(whole(out_shape[-1]))
+def after(value, *earlier):
+    return lax.optimization_barrier((value, *earlier))[0] if earlier else value
+
+
+def cost(busy_us):
+    return pl.CostEstimate(flops=1, bytes_accessed=max(1, int(busy_us * 2.5e6)), transcendentals=0)
+
+
+def in_hbm(a):
+    return pltpu.with_memory_space_constraint(a, pltpu.HBM)
+
+
+VMEM = pl.BlockSpec(memory_space=pltpu.VMEM)
+ANYWHERE = pl.BlockSpec(memory_space=pl.ANY)
+
+
+def block_columns(place, part, unit):
+    half = place[0] if part == 0 else 1 - place[0]
+    return pl.ds(pl.multiple_of((half * place[2] + unit) * HEAD_COLS, HEAD_COLS), HEAD_COLS)
+
+
+def cast_kernel(wanted, place, source, *refs):
+    outs, (buffer, sems) = refs[:-2], refs[-2:]
+    blocks = [(o, k, part, unit) for o, (part, units, _) in enumerate(wanted) for k, unit in enumerate(units)]
+    copies = [
+        pltpu.make_async_copy(source.at[:, block_columns(place, part, unit)], buffer.at[i], sems.at[i])
+        for i, (_, _, part, unit) in enumerate(blocks)
+    ]
+    for copy in copies:
+        copy.start()
+    first = [sum(w[2] for w in wanted[:o]) for o in range(len(wanted))]
+    for i, (o, k, _, _) in enumerate(blocks):
+        copies[i].wait()
+        n_pieces = wanted[o][2]
+        rows = buffer.shape[1] // n_pieces
+        for p in range(n_pieces):
+            piece = buffer[i, p * rows : (p + 1) * rows].astype(jnp.bfloat16)
+            outs[first[o] + p][:, k * HEAD_COLS : (k + 1) * HEAD_COLS] = piece
+
+
+def cast_units(place, local, wanted):
+    rows = local.shape[0]
+    n = sum(len(units) for _, units, _ in wanted)
+    shapes = [(rows // p, len(units) * HEAD_COLS) for _, units, p in wanted for _ in range(p)]
     out = pl.pallas_call(
-        functools.partial(adam_kernel, n, len(toks) if project else 0, update, project),
+        functools.partial(cast_kernel, wanted),
         grid_spec=pltpu.PrefetchScalarGridSpec(
             num_scalar_prefetch=1,
-            grid=(n, n_units),
-            in_specs=in_specs,
-            out_specs=out_specs,
+            grid=(),
+            in_specs=[ANYWHERE],
+            out_specs=[VMEM] * len(shapes),
+            scratch_shapes=[pltpu.VMEM((n, rows, HEAD_COLS), jnp.float32), pltpu.SemaphoreType.DMA((n,))],
+        ),
+        out_shape=[jax.ShapeDtypeStruct(shape, jnp.bfloat16) for shape in shapes],
+        compiler_params=pltpu.CompilerParams(vmem_limit_bytes=VMEM_LIMIT),
+        cost_estimate=cost(0),
+        name="cast_units",
+    )(place, in_hbm(local))
+    results = []
+    for _, _, p in wanted:
+        results.append(out[:p])
+        out = out[p:]
+    return results
+
+
+def join(halves):
+    return jnp.concatenate([h[...] for h in halves], axis=0)
+
+
+def adam_kernel(units, n_pieces, n_tok, held, projects, updates, place, *refs):
+    refs = list(refs)
+    take = lambda n: [refs.pop(0) for _ in range(n)]
+    mine = take(1)[0]
+    partner = take(n_pieces)
+    state = take(1 if held else 3)
+    toks = take(n_tok)
+    if updates:
+        take(0 if updates == 1 else 3)
+        updated = take(3)
+    sums = take(2) if projects else None
+    in_sems = None if held else take(1)[0]
+    out_sems = take(1)[0] if updates else None
+    buffer = refs.pop(0) if refs else None
+
+    n = len(units)
+    columns = [block_columns(place, i // n, units[i % n]) for i in range(2 * n)]
+    incoming = []
+    if not held:
+        for i in range(2 * n):
+            incoming.append(
+                [
+                    pltpu.make_async_copy(state[q].at[:, columns[i]], buffer.at[q, i], in_sems.at[q, i])
+                    for q in range(3)
+                ]
+            )
+            for copy in incoming[i]:
+                copy.start()
+    if projects:
+        tok = join(toks)
+    source = state[0] if held else buffer
+    totals = [mine[...], join(partner)]
+    outgoing, products = [], []
+    for i in range(2 * n):
+        for copy in incoming[i] if incoming else ():
+            copy.wait()
+        at = slice((i % n) * HEAD_COLS, (i % n + 1) * HEAD_COLS)
+        gradient = totals[i // n][:, at].astype(jnp.float32)
+        results = adam_update(source[0, i], source[1, i], source[2, i], gradient)
+        if updates:
+            for q in range(3):
+                buffer[q, i] = results[q]
+                outgoing.append(
+                    pltpu.make_async_copy(buffer.at[q, i], updated[q].at[:, columns[i]], out_sems.at[q, i])
+                )
+                outgoing[-1].start()
+        if projects:
+            products.append(
+                jnp.dot(tok, results[0].astype(jnp.bfloat16), preferred_element_type=jnp.float32)
+            )
+    if projects:
+        sent, kept = sums
+        stays = place[0] == place[1]
+        for k in range(n):
+            at = slice(k * HEAD_COLS, (k + 1) * HEAD_COLS)
+            kept[:, at] = jnp.where(stays, products[k], products[n + k])
+            sent[:, at] = jnp.where(stays, products[n + k], products[k]).astype(jnp.bfloat16)
+    for copy in outgoing:
+        copy.wait()
+
+
+def adam_units(place, total, state, toks, units, width, projects=True, updates=True, previous=None):
+    mine, partner = total
+    held = not isinstance(state, tuple)
+    n = 2 * len(units)
+    rows = mine.shape[0]
+    toks = toks if projects else []
+    operands = [mine, *partner]
+    in_specs = [VMEM] * len(operands)
+    operands += [state] if held else [in_hbm(a) for a in state]
+    in_specs += [VMEM] if held else [ANYWHERE] * 3
+    operands += toks
+    in_specs += [VMEM] * len(toks)
+    out_specs, out_shape, scratch, aliases = [], [], [], {}
+    if updates:
+        if previous is not None:
+            aliases = {1 + len(operands) + i: i for i in range(3)}
+            operands += previous
+            in_specs += [ANYWHERE] * 3
+        out_specs += [ANYWHERE] * 3
+        out_shape += [jax.ShapeDtypeStruct((rows, width), jnp.float32)] * 3
+    if projects:
+        shape = (sum(t.shape[0] for t in toks), len(units) * HEAD_COLS)
+        out_specs += [VMEM] * 2
+        out_shape += [jax.ShapeDtypeStruct(shape, jnp.bfloat16), jax.ShapeDtypeStruct(shape, jnp.float32)]
+    scratch += [pltpu.SemaphoreType.DMA((3, n))] * (int(not held) + int(updates))
+    if updates or not held:
+        scratch.append(pltpu.VMEM((3, n, rows, HEAD_COLS), jnp.float32))
+    out = pl.pallas_call(
+        functools.partial(
+            adam_kernel,
+            units,
+            len(partner),
+            len(toks),
+            held,
+            projects,
+            0 if not updates else 1 if previous is None else 2,
+        ),
+        grid_spec=pltpu.PrefetchScalarGridSpec(
+            num_scalar_prefetch=1, grid=(), in_specs=in_specs, out_specs=out_specs, scratch_shapes=scratch
         ),
         out_shape=out_shape,
         input_output_aliases=aliases,
         compiler_params=pltpu.CompilerParams(vmem_limit_bytes=VMEM_LIMIT),
-        cost_estimate=pl.CostEstimate(
-            flops=2 * n_tokens * rows * HEAD_COLS * n * n_units,
-            bytes_accessed=(14 + 12 * update) * rows * HEAD_COLS * n * n_units,
-            transcendentals=0,
-        ),
-        name="adam_project" if project else "adam_update",
+        cost_estimate=cost(0),
+        name="adam_project" if projects else "adam_update",
     )(place, *operands)
-    return (tuple(out[:3]) if update else None), (tuple(out[-2:]) if project else None)
+    return (out[:3] if updates else None), (out[-2:] if projects else None)
 
 
 SLOT = 32
 
 
 def cache_kernel(heads, lens, q, k, v, stacked, acc, stats):
+    step = pl.program_id(0)
     rows = q.shape[0]
     span = k.shape[1]
     used = PER_GROUP * STEPS
     for i in range(rows):
-        length = lens[pl.program_id(0) * rows + i]
+        length = lens[step * rows + i]
         query = q[i].astype(jnp.float32)
         scores = []
         for h in range(heads):
@@ -207,20 +299,22 @@
             jax.ShapeDtypeStruct(shape, jnp.float32),
         ],
         compiler_params=pltpu.CompilerParams(vmem_limit_bytes=VMEM_LIMIT),
-        cost_estimate=pl.CostEstimate(
-            flops=8 * row_count * SLOT * span * kv_cols,
-            bytes_accessed=4 * row_count * span * kv_cols,
-            transcendentals=row_count * heads * SLOT * span,
-        ),
+        cost_estimate=cost(0),
         name="cache_attention",
-    )(lengths, queries, cache_keys, cache_values)
-
-
-def merge_kernel(n_units, row_count, *refs):
-    arrived, kept, cosine, sine, stacked, acc, stats = refs[:7]
-    new_kv, context = refs[-2:]
-    every = arrived[...].astype(jnp.float32) + kept[...]
-    for u in range(n_units):
+    )(lengths, in_hbm(queries), in_hbm(cache_keys), in_hbm(cache_values))
+
+
+def merge_kernel(n_folds, row_count, *refs):
+    folds, refs = refs[: 2 * n_folds], refs[2 * n_folds :]
+    cosine, sine, stacked, acc, stats, new_kv, context = refs
+    every = jnp.concatenate(
+        [folds[2 * f][...].astype(jnp.float32) + folds[2 * f + 1][...] for f in range(n_folds)], axis=1
+    )
+    heads = stacked.shape[0]
+    at = lax.broadcasted_iota(jnp.int32, (row_count * SLOT, row_count * STEPS), 0)
+    to = lax.broadcasted_iota(jnp.int32, (row_count * SLOT, row_count * STEPS), 1)
+    seen = (at // SLOT == to // STEPS) & (at % STEPS >= to % STEPS)
+    for u in range(heads):
         total = every[:, u * HEAD_COLS : (u + 1) * HEAD_COLS]
         keys = total[:, :HD]
         keys = keys * cosine[...] + pltpu.roll(keys, HD // 2, 1) * sine[...]
@@ -236,9 +330,6 @@
             lax.dot_general(query, keys, (((1,), (1,)), ((), ())), preferred_element_type=jnp.float32)
             * score_scale
         )
-        at = lax.broadcasted_iota(jnp.int32, scores.shape, 0)
-        to = lax.broadcasted_iota(jnp.int32, scores.shape, 1)
-        seen = (at // SLOT == to // STEPS) & (at % STEPS >= to % STEPS)
         scores = jnp.where(seen, scores, masked_score)
         stat = stats[u].reshape(row_count * SLOT, HD)
         old_highest = stat[:, :1]
@@ -256,28 +347,17 @@
                 context[r, :, at_col : at_col + HD] = out[at_row : at_row + STEPS].astype(jnp.bfloat16)
 
 
-def merge(arrived, kept, cosine, sine, attended, previous, first, n_units):
+def merge(folds, cosine, sine, attended):
     heads, row_count = attended[0].shape[:2]
-    at = first // n_units
-    some = pl.BlockSpec((n_units, row_count, SLOT, HD), lambda i: (at, 0, 0, 0))
-    operands = [arrived, kept, cosine, sine]
-    in_specs = [whole(a) for a in operands] + [some] * 3
-    operands += attended
-    aliases = {}
-    if previous is not None:
-        for i, p in enumerate(previous):
-            aliases[len(operands)] = i
-            operands.append(p)
-            in_specs.append(pl.BlockSpec(memory_space=pl.ANY))
+    operands = [a for fold in folds for a in fold] + [cosine, sine, *attended]
     widths = (HEAD_COLS, PER_GROUP * HD)
     return pl.pallas_call(
-        functools.partial(merge_kernel, n_units, row_count),
-        grid=(1,),
-        in_specs=in_specs,
-        out_specs=[pl.BlockSpec((row_count, STEPS, n_units * w), lambda i: (0, 0, at)) for w in widths],
+        functools.partial(merge_kernel, len(folds), row_count),
+        in_specs=[VMEM] * len(operands),
+        out_specs=[VMEM] * 2,
         out_shape=[jax.ShapeDtypeStruct((row_count, STEPS, heads * w), jnp.bfloat16) for w in widths],
-        input_output_aliases=aliases,
         compiler_params=pltpu.CompilerParams(vmem_limit_bytes=VMEM_LIMIT),
+        cost_estimate=cost(0),
         name="merge_new",
     )(*operands)
 
@@ -289,10 +369,6 @@
 
 def add_rounded(a, b):
     return (a.astype(jnp.float32) + b.astype(jnp.float32)).astype(jnp.bfloat16)
-
-
-def after(value, *earlier):
-    return lax.optimization_barrier((value, *earlier))[0]
 
 
 def fold_rows(arrived, kept, n):
@@ -312,66 +388,89 @@
     tp = lax.axis_index("tp")
     rows, width = weights.shape
     row_count = tokens.shape[0]
-    n_chunks = width // (tp_count * HEAD_COLS)
+    n_units = width // (tp_count * HEAD_COLS)
     local = grad_parts[0]
-    state = (weights, moment1, moment2)
-    zero = jnp.zeros_like(core)
-    both_parts = jnp.stack([core, tp, zero]).astype(jnp.int32)
-
-    cut = n_chunks // 2
-    chunks = [(0, cut), (cut, n_chunks - cut)]
-
-    def columns(source, half, first, n):
-        return lax.dynamic_slice(
-            source, (0, (half * n_chunks + first) * HEAD_COLS), (rows, n * HEAD_COLS)
-        )
-
-    cast, arrived, own, crossed = [], [], [], []
-    source = local
-    for first, n in chunks:
-        cast.append(columns(source, 1 - core, first, n).astype(jnp.bfloat16))
-        arrived.append(swap(cast[-1], "group", 1))
-        source = after(local, cast[-1])
-    source = local
-    for (first, n), got in zip(chunks, arrived):
-        own.append(add_rounded(columns(source, core, first, n), got))
-        crossed.append(swap(own[-1], "group", 2))
-        source = after(local, own[-1])
-
+    place = jnp.stack([core, tp, jnp.full_like(core, n_units)]).astype(jnp.int32)
+
+    crossings = [[*range(n_units // 2)], [*range(n_units // 2, n_units)]]
+    crossings = [c for c in crossings if c]
+    cut = 1
+    folds = [range(cut), range(cut, len(crossings))]
+    folds = [f for f in folds if len(f)]
+
+    def chip_sum(away, home):
+        return add_rounded(home, jnp.concatenate([swap(a, "group", 1) for a in away], axis=0))
+
+    (away,) = cast_units(place, local, [(1, crossings[0], 1)])
+    later = [u for units in crossings[1:] for u in units]
+    (home,), away_later, (home_later,) = cast_units(
+        place, after(local, *away), [(0, crossings[0], 1), (1, later, 4), (0, later, 1)]
+    )
+    first = chip_sum(away, home)
+    mine, crossed = [first], [swap(first, "group", 2)]
+    rest = chip_sum(away_later, home_later)
+    at = 0
+    for units in crossings[1:]:
+        mine.append(rest[:, at * HEAD_COLS : (at + len(units)) * HEAD_COLS])
+        at += len(units)
+        crossed.append(swap(mine[-1], "group", 2))
+    started = mine[-1]
+
+    cosine, sine = rotation_tables(lengths)
+    attended = cache_attention(after(queries, *mine), cache_keys, cache_values, lengths)
+
+    source = after(tokens, started)
     toks = []
-    early = after(tokens, own[-1])
     for d in range(fsdp_count):
         at = ((fsdp ^ d) * tp_count + tp) * rows
-        piece = lax.dynamic_slice(early, (0, 0, at), (row_count, STEPS, rows))
-        piece = piece.reshape(row_count * STEPS, rows)
-        toks.append(piece if d == 0 else swap(piece, "fsdp", d))
-
-    cosine, sine = rotation_tables(lengths)
-    attended = cache_attention(after(queries, own[-1]), cache_keys, cache_values, lengths)
-
+        piece = lax.dynamic_slice(source, (0, 0, at), (row_count, STEPS, rows))
+        toks.append(piece.reshape(1, row_count * STEPS, rows))
+    distance = 1
+    while distance < fsdp_count:
+        stay = toks[::2]
+        away = toks[1::2]
+        away_all = jnp.concatenate(away, axis=0) if len(away) > 1 else away[0]
+        if distance > 1:
+            away_all = after(away_all, attended[1])
+        got = swap(away_all, "fsdp", distance)
+        got = jnp.split(got, len(away), axis=0) if len(away) > 1 else [got]
+        toks = [jnp.concatenate([s, g], axis=0) for s, g in zip(stay, got)]
+        distance *= 2
+    toks = [toks[0].reshape(fsdp_count * row_count * STEPS, rows)]
+
+    state = (weights, moment1, moment2)
+    last = crossings[-1]
+
+    totals, sums = [], []
     updated = None
-    outs = None
-    done = (attended[1],)
-    for (first, n), mine, other in zip(chunks, own, crossed):
+    step = (attended[1],)
+    for c, units in enumerate(crossings):
+        one, other = mine[c], after(crossed[c], *step)
         bit = 2
         while True:
-            mine = add_rounded(mine, after(other, *done))
+            one = add_rounded(one, other)
             bit *= 2
             if bit >= group_count:
                 break
-            other = swap(mine, "group", bit)
-        totals = (mine, swap(mine, "group", 1))
-        updated, (sent, kept) = adam_call(
-            both_parts, totals, state, toks, first, n, n_chunks, True, True, updated
-        )
-        done = (kept,)
-        got = swap(sent, "tp", 1)
-        distance = fsdp_count // 2
-        while distance:
+            other = swap(one, "group", bit)
+        totals.append((one, [swap(p, "group", 1) for p in jnp.split(one, 4, axis=0)]))
+        updated, both = adam_units(place, totals[c], state, toks, units, width, previous=updated)
+        sums.append(both)
+        step = (sums[c][0],)
+
+    moving = []
+    for members in folds:
+        sent = jnp.concatenate([sums[c][0] for c in members], axis=1)
+        kept = jnp.concatenate([sums[c][1] for c in members], axis=1)
+        moving.append((swap(sent, "tp", 1), kept))
+    distance = fsdp_count // 2
+    while distance:
+        for f, (got, kept) in enumerate(moving):
             sent, kept = fold_rows(got, kept, fsdp_count)
-            got = swap(sent, "fsdp", distance)
-            distance //= 2
-        outs = merge(got, kept, cosine, sine, attended, outs, first, n)
+            moving[f] = (swap(sent, "fsdp", distance), kept)
+        distance //= 2
+
+    outs = merge(moving, cosine, sine, attended)
     return (*updated, *outs)
 
 

time: 80.7 us -> 72.2 us (0.89)
  starting transfers between devices: 14.9 us -> 23.8 us
  waiting for transfers between devices: 18.1 us -> 11.3 us
  local copies, waits for them, and re-layouts: 8.5 us -> 2.57 us
  Pallas kernels: 32 us -> 26.6 us
    ppermute x15 -> x23, starting transfers between devices: 14.9 us -> 23.8 us  [swap(): return lax.ppermute(array, axis, [(i, i ^ bit) for i in range(size)])]
    ppermute x15 -> x23, waiting for transfers between devices: 18.1 us -> 11.3 us  [swap(): return lax.ppermute(array, axis, [(i, i ^ bit) for i in range(size)])]
    pallas_call x4 -> x5, Pallas kernels: 24.2 us -> 19.8 us  [the longest x2 13.1 us: adam_units(): pl.pallas_call(functools.partial(adam_kernel, units, len(partner), len(to...]
    convert_element_type x2 -> x0, local copies, waits for them, and re-layouts: 2.8 us -> none  [butterfly_shards(): cast.append(columns(source, 1 - core, first, n).astype(jnp.bfloat16))]
    unnamed x24 -> x6, local copies, waits for them, and re-layouts: 3.58 us -> 0.84 us
    convert_element_type x4, other arithmetic: 3.39 us -> 5.19 us  [add_rounded(): return (a.astype(jnp.float32) + b.astype(jnp.float32)).astype(jnp.bfloat16)]
    slice x6, local copies, waits for them, and re-layouts: 1.29 us -> 0.05 us  [fold_rows(): return (total[half:].astype(jnp.bfloat16), total[:half])]
    pallas_call x1, Pallas kernels: 7.8 us -> 6.72 us  [cache_attention(): pl.pallas_call(functools.partial(cache_kernel, heads), grid_spec=pltpu.Pr...]
  transfers between devices with their start and end apart: 15 -> 23, of which waited for: 7 -> 14; matrix products, arithmetic and copies ran while one was open for 11% -> 10% of each run, Pallas kernels for 36% -> 31%
where the time goes in v3:
time: 72.2 us; the launch traced here: 71.8 us
  Pallas kernels  26.6 us (37%)
  starting transfers between devices  23.8 us (33%)
  waiting for transfers between devices  11.3 us (16%)
  other arithmetic  6.59 us (9%)
  local copies, waits for them, and re-layouts  2.57 us (4%)
  between operations  0.9 us (1%)
    ppermute x23, starting transfers between devices, swap(): return lax.ppermute(array, axis, [(i, i ^ bit) for i in range(size)])  23.8 us
    pallas_call x2, Pallas kernels, adam_units(): pl.pallas_call(functools.partial(adam_kernel, units, len(partner), len(to...  13.1 us
    ppermute x23, waiting for transfers between devices, swap(): return lax.ppermute(array, axis, [(i, i ^ bit) for i in range(size)])  11.3 us
    pallas_call x1, Pallas kernels, cache_attention(): pl.pallas_call(functools.partial(cache_kernel, heads), grid_spec=pltpu.Pr...  6.72 us
    convert_element_type x4, other arithmetic, add_rounded(): return (a.astype(jnp.float32) + b.astype(jnp.float32)).astype(jnp.bfloat16)  5.19 us
    pallas_call x2, Pallas kernels, cast_units(): pl.pallas_call(functools.partial(cast_kernel, wanted), grid_spec=pltpu.Pr...  4.61 us
    pallas_call x1, Pallas kernels, merge(): pl.pallas_call(functools.partial(merge_kernel, len(folds), row_count), in...  2.16 us
  transfers between devices with their start and end apart: 23, of which 14 were waited for; matrix products, arithmetic and copies ran while one was open for 10% of the time, Pallas kernels for 31%

profile of v3, /device:TPU:0, one launch (start us, length us, event | category | flops | bytes accessed | tf_op | source)
XLA Modules:
  0.0 71.8 jit_solution(5349664580470947095)
XLA Ops:
  0.7 1.9 %cast_units.2 = bf16[640,512]{1,0:T(8,128)(2,1)S(1)} custom-call(s32[3]{0:T(128)S(1)} %pad_add_fusion.place, f32[640,2048]{1,0:T(8,128)} %bitcast.6), custom_call_target="tpu_custom_call" | custom-call | flops 1 | bytes 1 | tf_op jit(solution)/shard_map/cast_units/pallas_call | solution.py:102
  3.1 2.7 %cast_units.3 = (bf16[640,512]{1,0:T(8,128)(2,1)S(1)}, bf16[160,512]{1,0:T(8,128)(2,1)S(1)}, bf16[160,512]{1,0:T(8,128)(2,1)S(1)}, bf16[160,512]{1,0:T(8,128)(2,...) custom-call(s32[3]{0:T(128)S(1)} %pad_add_fusion.place, f32[640,2048]{1,0:T(8,128)} %bitcast.7), custom_call_target="tpu_custom_call" | custom-call | flops 1 | bytes 1 | tf_op jit(solution)/shard_map/cast_units/pallas_call | solution.py:102
  8.2 1.3 %add_convert_fusion.3 = bf16[640,512]{1,0:T(8,128)(2,1)S(1)} fusion(bf16[640,512]{1,0:T(8,128)(2,1)S(1)} %get-tuple-element.33, bf16[160,512]{1,0:T(8,128)(2,1)} %collective-permute-done.3, bf16[160,512]{1,0:T(8,128)(2,1)} %collective-permute-done.2, bf16[160,512]{1,0:T(8,128)(2,1)} %collective-permute-done.1, bf16[160,512]{1,0:T(8,128)(2,1)S(1)} %collective-permute-done), kind=kLoop, calls=%fused_computation.3 | loop fusion | flops 3604480 | bytes 1966080 | tf_op jit(solution)/shard_map/convert_element_type | solution.py:371
  10.5 1.3 %add_convert_fusion.2 = bf16[640,512]{1,0:T(8,128)(2,1)S(1)} fusion(bf16[640,512]{1,0:T(8,128)(2,1)} %copy-done.1, bf16[640,512]{1,0:T(8,128)(2,1)S(1)} %get-tuple-element.38), kind=kLoop, calls=%fused_computation.2 | loop fusion | flops 1310720 | bytes 1966080 | tf_op jit(solution)/shard_map/convert_element_type | solution.py:371
  11.8 2.8 %collective-permute-start.6 = (bf16[640,512]{1,0:T(8,128)(2,1)S(1)}, bf16[640,512]{1,0:T(8,128)(2,1)}, u32[]{:S(2)}, u32[]{:S(2)}) collective-permute-start(bf16[640,512]{1,0:T(8,128)(2,1)S(1)} %add_convert_fusion.2), channel_id=1, source_target_pairs={{0,16},{8,24},{16,0},{24,8},{1,17},{9,25},{17,1},{25,9},{2,18},{10... | collective-permute-start | bytes 1966088 | tf_op jit(solution)/shard_map/ppermute | solution.py:367
  14.6 1.6 %collective-permute-start.11 = (bf16[2,32,640]{2,1,0:T(8,128)(2,1)S(1)}, bf16[2,32,640]{2,1,0:T(8,128)(2,1)S(1)}, u32[]{:S(2)}, u32[]{:S(2)}) collective-permute-start(bf16[2,32,640]{2,1,0:T(8,128)(2,1)S(1)} %pad_maximum_fusion.1), channel_id=1, source_target_pairs={{0,2},{2,0},{4,6},{6,4},{1,3},{3,1},{5,7},{7,5},{8,10},{10,8},{12,... | collective-permute-start | bytes 245768 | tf_op jit(solution)/shard_map/ppermute | solution.py:367
  16.9 2.2 %collective-permute-done.11 = bf16[2,32,640]{2,1,0:T(8,128)(2,1)S(1)} collective-permute-done((bf16[2,32,640]{2,1,0:T(8,128)(2,1)S(1)}, bf16[2,32,640]{2,1,0:T(8,128)(2,1)S(1)}, u32[]{:S(2)}, u32[]{:S(2)}) %collective-permute-start.11) | collective-permute-done | bytes 81952 | tf_op jit(solution)/shard_map/ppermute | solution.py:367
  19.2 6.7 %cache_attention.1 = (bf16[4,8,32,128]{3,2,1,0:T(8,128)(2,1)S(1)}, f32[4,8,32,128]{3,2,1,0:T(8,128)S(1)}, f32[4,8,32,128]{3,2,1,0:T(8,128)S(1)}) custom-call(s32[8]{0:T(128)S(1)} %copy-done, bf16[8,4,2560]{2,1,0:T(4,128)(2,1)} %q, bf16[8,512,512]{2,1,0:T(8,128)(2,1)} %k.1, bf16[8,512,512]{2,1,0:T(8,128)(2,1)} %v.1), custom_call_target="tpu_custom_call" | custom-call | flops 1 | bytes 1 | tf_op jit(solution)/shard_map/cache_attention/pallas_call | solution.py:288
  25.9 2.7 %collective-permute-start.12 = (bf16[2,32,640]{2,1,0:T(8,128)(2,1)S(1)}, bf16[2,32,640]{2,1,0:T(8,128)(2,1)}, u32[]{:S(2)}, u32[]{:S(2)}) collective-permute-start(bf16[2,32,640]{2,1,0:T(8,128)(2,1)S(1)} %pad_maximum_fusion.2), channel_id=1, source_target_pairs={{0,4},{2,6},{4,0},{6,2},{1,5},{3,7},{5,1},{7,3},{8,12},{10,14},{12... | collective-permute-start | bytes 245768 | tf_op jit(solution)/shard_map/ppermute | solution.py:367
  28.5 1.7 %collective-permute-done.6 = bf16[640,512]{1,0:T(8,128)(2,1)} collective-permute-done((bf16[640,512]{1,0:T(8,128)(2,1)S(1)}, bf16[640,512]{1,0:T(8,128)(2,1)}, u32[]{:S(2)}, u32[]{:S(2)}) %collective-permute-start.6) | collective-permute-done | bytes 655392 | tf_op jit(solution)/shard_map/ppermute | solution.py:367
  30.2 1.3 %add_convert_fusion.1.refs_0_ = bf16[640,512]{1,0:T(8,128)(2,1)S(1)} fusion(bf16[640,512]{1,0:T(8,128)(2,1)} %collective-permute-done.6, bf16[640,512]{1,0:T(8,128)(2,1)S(1)} %add_convert_fusion.2), kind=kLoop, calls=%fused_computation.1 | loop fusion | flops 1310720 | bytes 1966080 | tf_op jit(solution)/shard_map/convert_element_type | solution.py:371
  35.0 6.5 %adam_project.2 = (f32[640,2048]{1,0:T(8,128)}, f32[640,2048]{1,0:T(8,128)}, f32[640,2048]{1,0:T(8,128)}, bf16[128,512]{1,0:T(8,128)(2,1)S(1)}, f32[128,512]{1,0:T(8,128)S(1)}) custom-call(s32[3]{0:T(128)S(1)} %pad_add_fusion.place, bf16[640,512]{1,0:T(8,128)(2,1)S(1)} %add_convert_fusion.1.refs_0_, bf16[160,512]{1,0:T(8,128)(2,1)S(1)} %collective-permute-done.7.refs_1_, ...), custom_call_target="tpu_custom_call" | custom-call | flops 1 | bytes 1 | tf_op jit(solution)/shard_map/adam_project/pallas_call | solution.py:215
  41.6 2.2 %collective-permute-start.17 = (bf16[128,512]{1,0:T(8,128)(2,1)S(1)}, bf16[128,512]{1,0:T(8,128)(2,1)S(1)}, u32[]{:S(2)}, u32[]{:S(2)}) collective-permute-start(bf16[128,512]{1,0:T(8,128)(2,1)S(1)} %get-tuple-element.44), channel_id=1, source_target_pairs={{0,1},{1,0},{2,3},{3,2},{4,5},{5,4},{6,7},{7,6},{8,9},{9,8},{10,11... | collective-permute-start | bytes 393224 | tf_op jit(solution)/shard_map/ppermute | solution.py:367
  43.9 1.3 %add_convert_fusion.refs_0_ = bf16[640,512]{1,0:T(8,128)(2,1)S(1)} fusion(bf16[640,512]{1,0:T(8,128)(2,1)} %collective-permute-done.4, bf16[640,512]{1,0:T(8,128)(2,1)S(1)} %add_convert_fusion.3), kind=kLoop, calls=%fused_computation | loop fusion | flops 1310720 | bytes 1966080 | tf_op jit(solution)/shard_map/convert_element_type | solution.py:371
  47.5 6.5 %adam_project.3 = (f32[640,2048]{1,0:T(8,128)}, f32[640,2048]{1,0:T(8,128)}, f32[640,2048]{1,0:T(8,128)}, bf16[128,512]{1,0:T(8,128)(2,1)S(1)}, f32[128,512]{1,0:T(8,128)S(1)}) custom-call(s32[3]{0:T(128)S(1)} %pad_add_fusion.place, bf16[640,512]{1,0:T(8,128)(2,1)S(1)} %add_convert_fusion.refs_0_, ...), custom_call_target="tpu_custom_call", output_to_operand_aliasing={{0}: (10, {}), {1}: (11, {}), {2}: (12, {})} | custom-call | flops 1 | bytes 1 | tf_op jit(solution)/shard_map/adam_project/pallas_call | solution.py:215
  54.0 1.8 %collective-permute-start.20 = (bf16[128,512]{1,0:T(8,128)(2,1)S(1)}, bf16[128,512]{1,0:T(8,128)(2,1)S(1)}, u32[]{:S(2)}, u32[]{:S(2)}) collective-permute-start(bf16[128,512]{1,0:T(8,128)(2,1)S(1)} %get-tuple-element.53), channel_id=1, source_target_pairs={{0,1},{1,0},{2,3},{3,2},{4,5},{5,4},{6,7},{7,6},{8,9},{9,8},{10,11... | collective-permute-start | bytes 393224 | tf_op jit(solution)/shard_map/ppermute | solution.py:367
  55.9 2.7 %collective-permute-start.18 = (bf16[64,512]{1,0:T(8,128)(2,1)S(1)}, bf16[64,512]{1,0:T(8,128)(2,1)S(1)}, u32[]{:S(2)}, u32[]{:S(2)}) collective-permute-start(bf16[64,512]{1,0:T(8,128)(2,1)S(1)} %slice.51), channel_id=1, source_target_pairs={{0,4},{2,6},{4,0},{6,2},{1,5},{3,7},{5,1},{7,3},{8,12},{10,14},{12... | collective-permute-start | bytes 196616 | tf_op jit(solution)/shard_map/ppermute | solution.py:367
  58.5 1.2 %collective-permute-done.20 = bf16[128,512]{1,0:T(8,128)(2,1)S(1)} collective-permute-done((bf16[128,512]{1,0:T(8,128)(2,1)S(1)}, bf16[128,512]{1,0:T(8,128)(2,1)S(1)}, u32[]{:S(2)}, u32[]{:S(2)}) %collective-permute-start.20) | collective-permute-done | bytes 131104 | tf_op jit(solution)/shard_map/ppermute | solution.py:367
  59.8 2.9 %collective-permute-start.21 = (bf16[64,512]{1,0:T(8,128)(2,1)S(1)}, bf16[64,512]{1,0:T(8,128)(2,1)S(1)}, u32[]{:S(2)}, u32[]{:S(2)}) collective-permute-start(bf16[64,512]{1,0:T(8,128)(2,1)S(1)} %slice.50), channel_id=1, source_target_pairs={{0,4},{2,6},{4,0},{6,2},{1,5},{3,7},{5,1},{7,3},{8,12},{10,14},{12... | collective-permute-start | bytes 196616 | tf_op jit(solution)/shard_map/ppermute | solution.py:367
  62.7 1.6 %collective-permute-start.19 = (bf16[32,512]{1,0:T(8,128)(2,1)S(1)}, bf16[32,512]{1,0:T(8,128)(2,1)S(1)}, u32[]{:S(2)}, u32[]{:S(2)}) collective-permute-start(bf16[32,512]{1,0:T(8,128)(2,1)S(1)} %slice.53), channel_id=1, source_target_pairs={{0,2},{2,0},{4,6},{6,4},{1,3},{3,1},{5,7},{7,5},{8,10},{10,8},{12,... | collective-permute-start | bytes 98312 | tf_op jit(solution)/shard_map/ppermute | solution.py:367
  64.4 1.2 %collective-permute-done.21 = bf16[64,512]{1,0:T(8,128)(2,1)S(1)} collective-permute-done((bf16[64,512]{1,0:T(8,128)(2,1)S(1)}, bf16[64,512]{1,0:T(8,128)(2,1)S(1)}, u32[]{:S(2)}, u32[]{:S(2)}) %collective-permute-start.21) | collective-permute-done | bytes 65568 | tf_op jit(solution)/shard_map/ppermute | solution.py:367
  65.6 1.3 %collective-permute-start.22 = (bf16[32,512]{1,0:T(8,128)(2,1)S(1)}, bf16[32,512]{1,0:T(8,128)(2,1)S(1)}, u32[]{:S(2)}, u32[]{:S(2)}) collective-permute-start(bf16[32,512]{1,0:T(8,128)(2,1)S(1)} %slice.52), channel_id=1, source_target_pairs={{0,2},{2,0},{4,6},{6,4},{1,3},{3,1},{5,7},{7,5},{8,10},{10,8},{12,... | collective-permute-start | bytes 98312 | tf_op jit(solution)/shard_map/ppermute | solution.py:367
  67.1 2.5 %collective-permute-done.22.refs_2_ = bf16[32,512]{1,0:T(8,128)(2,1)S(1)} collective-permute-done((bf16[32,512]{1,0:T(8,128)(2,1)S(1)}, bf16[32,512]{1,0:T(8,128)(2,1)S(1)}, u32[]{:S(2)}, u32[]{:S(2)}) %collective-permute-start.22) | collective-permute-done | bytes 32800 | tf_op jit(solution)/shard_map/ppermute | solution.py:367
  69.6 2.2 %merge_new.1 = (bf16[8,4,1024]{2,1,0:T(4,128)(2,1)}, bf16[8,4,2560]{2,1,0:T(4,128)(2,1)}) custom-call(bf16[32,512]{1,0:T(8,128)(2,1)S(1)} %collective-permute-done.19.refs_0_, f32[32,512]{1,0:T(8,128)S(1)} %slice.39.refs_1_, bf16[32,512]{1,0:T(8,128)(2,1)S(1)} %collective-permute-done.22.refs_2_, f32[32,512]{1,0:T(8,128)S(1)} %slice.43.refs_3_, ...), custom_call_target="tpu_custom_call" | custom-call | flops 1 | bytes 1 | tf_op jit(solution)/shard_map/merge_new/pallas_call | solution.py:354
  (65 shorter events, 10.6 us)
Async XLA Ops:
  2.6 7.0 %collective-permute-start.5 = (bf16[640,512]{1,0:T(8,128)(2,1)S(1)}, bf16[640,512]{1,0:T(8,128)(2,1)S(1)}, u32[]{:S(2)}, u32[]{:S(2)}) collective-permute-start(bf16[640,512]{1,0:T(8,128)(2,1)S(1)} %cast_units.2), channel_id=1, source_target_pairs={{0,8},{8,0},{16,24},{24,16},{1,9},{9,1},{17,25},{25,17},{2,10},{10... | collective-permute-start | bytes 1966088 | tf_op jit(solution)/shard_map/ppermute | solution.py:367
  5.9 1.5 %collective-permute-start = (bf16[160,512]{1,0:T(8,128)(2,1)S(1)}, bf16[160,512]{1,0:T(8,128)(2,1)S(1)}, u32[]{:S(2)}, u32[]{:S(2)}) collective-permute-start(bf16[160,512]{1,0:T(8,128)(2,1)S(1)} %get-tuple-element.34), channel_id=1, source_target_pairs={{0,8},{8,0},{16,24},{24,16},{1,9},{9,1},{17,25},{25,17},{2,10},{10... | collective-permute-start | bytes 491528 | tf_op jit(solution)/shard_map/ppermute | solution.py:367
  6.0 1.7 %collective-permute-start.1 = (bf16[160,512]{1,0:T(8,128)(2,1)S(1)}, bf16[160,512]{1,0:T(8,128)(2,1)}, u32[]{:S(2)}, u32[]{:S(2)}) collective-permute-start(bf16[160,512]{1,0:T(8,128)(2,1)S(1)} %get-tuple-element.35), channel_id=1, source_target_pairs={{0,8},{8,0},{16,24},{24,16},{1,9},{9,1},{17,25},{25,17},{2,10},{10... | collective-permute-start | bytes 491528 | tf_op jit(solution)/shard_map/ppermute | solution.py:367
  6.4 1.5 %collective-permute-start.2 = (bf16[160,512]{1,0:T(8,128)(2,1)S(1)}, bf16[160,512]{1,0:T(8,128)(2,1)}, u32[]{:S(2)}, u32[]{:S(2)}) collective-permute-start(bf16[160,512]{1,0:T(8,128)(2,1)S(1)} %get-tuple-element.36), channel_id=1, source_target_pairs={{0,8},{8,0},{16,24},{24,16},{1,9},{9,1},{17,25},{25,17},{2,10},{10... | collective-permute-start | bytes 491528 | tf_op jit(solution)/shard_map/ppermute | solution.py:367
  6.5 1.7 %collective-permute-start.3 = (bf16[160,512]{1,0:T(8,128)(2,1)S(1)}, bf16[160,512]{1,0:T(8,128)(2,1)}, u32[]{:S(2)}, u32[]{:S(2)}) collective-permute-start(bf16[160,512]{1,0:T(8,128)(2,1)S(1)} %get-tuple-element.37), channel_id=1, source_target_pairs={{0,8},{8,0},{16,24},{24,16},{1,9},{9,1},{17,25},{25,17},{2,10},{10... | collective-permute-start | bytes 491528 | tf_op jit(solution)/shard_map/ppermute | solution.py:367
  9.5 6.8 %copy-start = (s32[8]{0:T(128)S(1)}, s32[8]{0:T(128)}, u32[]{:S(2)}) copy-start(s32[8]{0:T(128)} %lens.1) | copy-start | bytes 100
  11.8 18.4 %collective-permute-start.6 = (bf16[640,512]{1,0:T(8,128)(2,1)S(1)}, bf16[640,512]{1,0:T(8,128)(2,1)}, u32[]{:S(2)}, u32[]{:S(2)}) collective-permute-start(bf16[640,512]{1,0:T(8,128)(2,1)S(1)} %add_convert_fusion.2), channel_id=1, source_target_pairs={{0,16},{8,24},{16,0},{24,8},{1,17},{9,25},{17,1},{25,9},{2,18},{10... | collective-permute-start | bytes 1966088 | tf_op jit(solution)/shard_map/ppermute | solution.py:367
  14.6 4.5 %collective-permute-start.11 = (bf16[2,32,640]{2,1,0:T(8,128)(2,1)S(1)}, bf16[2,32,640]{2,1,0:T(8,128)(2,1)S(1)}, u32[]{:S(2)}, u32[]{:S(2)}) collective-permute-start(bf16[2,32,640]{2,1,0:T(8,128)(2,1)S(1)} %pad_maximum_fusion.1), channel_id=1, source_target_pairs={{0,2},{2,0},{4,6},{6,4},{1,3},{3,1},{5,7},{7,5},{8,10},{10,8},{12,... | collective-permute-start | bytes 245768 | tf_op jit(solution)/shard_map/ppermute | solution.py:367
  16.3 27.5 %collective-permute-start.4 = (bf16[640,512]{1,0:T(8,128)(2,1)S(1)}, bf16[640,512]{1,0:T(8,128)(2,1)}, u32[]{:S(2)}, u32[]{:S(2)}) collective-permute-start(bf16[640,512]{1,0:T(8,128)(2,1)S(1)} %add_convert_fusion.3), channel_id=1, source_target_pairs={{0,16},{8,24},{16,0},{24,8},{1,17},{9,25},{17,1},{25,9},{2,18},{10... | collective-permute-start | bytes 1966088 | tf_op jit(solution)/shard_map/ppermute | solution.py:367
  25.9 6.9 %collective-permute-start.12 = (bf16[2,32,640]{2,1,0:T(8,128)(2,1)S(1)}, bf16[2,32,640]{2,1,0:T(8,128)(2,1)}, u32[]{:S(2)}, u32[]{:S(2)}) collective-permute-start(bf16[2,32,640]{2,1,0:T(8,128)(2,1)S(1)} %pad_maximum_fusion.2), channel_id=1, source_target_pairs={{0,4},{2,6},{4,0},{6,2},{1,5},{3,7},{5,1},{7,3},{8,12},{10,14},{12... | collective-permute-start | bytes 245768 | tf_op jit(solution)/shard_map/ppermute | solution.py:367
  32.3 2.7 %collective-permute-start.10 = (bf16[160,512]{1,0:T(8,128)(2,1)}, bf16[160,512]{1,0:T(8,128)(2,1)S(1)}, u32[]{:S(2)}, u32[]{:S(2)}) collective-permute-start(bf16[160,512]{1,0:T(8,128)(2,1)} %get-tuple-element.63), channel_id=1, source_target_pairs={{0,8},{8,0},{16,24},{24,16},{1,9},{9,1},{17,25},{25,17},{2,10},{10... | collective-permute-start | bytes 491528 | tf_op jit(solution)/shard_map/ppermute | solution.py:367
  32.3 2.7 %collective-permute-start.9 = (bf16[160,512]{1,0:T(8,128)(2,1)}, bf16[160,512]{1,0:T(8,128)(2,1)S(1)}, u32[]{:S(2)}, u32[]{:S(2)}) collective-permute-start(bf16[160,512]{1,0:T(8,128)(2,1)} %get-tuple-element.64), channel_id=1, source_target_pairs={{0,8},{8,0},{16,24},{24,16},{1,9},{9,1},{17,25},{25,17},{2,10},{10... | collective-permute-start | bytes 491528 | tf_op jit(solution)/shard_map/ppermute | solution.py:367
  32.8 2.2 %collective-permute-start.8 = (bf16[160,512]{1,0:T(8,128)(2,1)}, bf16[160,512]{1,0:T(8,128)(2,1)S(1)}, u32[]{:S(2)}, u32[]{:S(2)}) collective-permute-start(bf16[160,512]{1,0:T(8,128)(2,1)} %get-tuple-element.65), channel_id=1, source_target_pairs={{0,8},{8,0},{16,24},{24,16},{1,9},{9,1},{17,25},{25,17},{2,10},{10... | collective-permute-start | bytes 491528 | tf_op jit(solution)/shard_map/ppermute | solution.py:367
  32.8 2.2 %collective-permute-start.7 = (bf16[160,512]{1,0:T(8,128)(2,1)S(1)}, bf16[160,512]{1,0:T(8,128)(2,1)S(1)}, u32[]{:S(2)}, u32[]{:S(2)}) collective-permute-start(bf16[160,512]{1,0:T(8,128)(2,1)S(1)} %get-tuple-element.66), channel_id=1, source_target_pairs={{0,8},{8,0},{16,24},{24,16},{1,9},{9,1},{17,25},{25,17},{2,10},{10... | collective-permute-start | bytes 491528 | tf_op jit(solution)/shard_map/ppermute | solution.py:367
  41.6 14.3 %collective-permute-start.17 = (bf16[128,512]{1,0:T(8,128)(2,1)S(1)}, bf16[128,512]{1,0:T(8,128)(2,1)S(1)}, u32[]{:S(2)}, u32[]{:S(2)}) collective-permute-start(bf16[128,512]{1,0:T(8,128)(2,1)S(1)} %get-tuple-element.44), channel_id=1, source_target_pairs={{0,1},{1,0},{2,3},{3,2},{4,5},{5,4},{6,7},{7,6},{8,9},{9,8},{10,11... | collective-permute-start | bytes 393224 | tf_op jit(solution)/shard_map/ppermute | solution.py:367
  45.3 1.5 %collective-permute-start.16 = (bf16[160,512]{1,0:T(8,128)(2,1)S(1)}, bf16[160,512]{1,0:T(8,128)(2,1)S(1)}, u32[]{:S(2)}, u32[]{:S(2)}) collective-permute-start(bf16[160,512]{1,0:T(8,128)(2,1)S(1)} %get-tuple-element.59), channel_id=1, source_target_pairs={{0,8},{8,0},{16,24},{24,16},{1,9},{9,1},{17,25},{25,17},{2,10},{10... | collective-permute-start | bytes 491528 | tf_op jit(solution)/shard_map/ppermute | solution.py:367
  45.3 1.6 %collective-permute-start.15 = (bf16[160,512]{1,0:T(8,128)(2,1)S(1)}, bf16[160,512]{1,0:T(8,128)(2,1)S(1)}, u32[]{:S(2)}, u32[]{:S(2)}) collective-permute-start(bf16[160,512]{1,0:T(8,128)(2,1)S(1)} %get-tuple-element.60), channel_id=1, source_target_pairs={{0,8},{8,0},{16,24},{24,16},{1,9},{9,1},{17,25},{25,17},{2,10},{10... | collective-permute-start | bytes 491528 | tf_op jit(solution)/shard_map/ppermute | solution.py:367
  45.8 1.4 %collective-permute-start.14 = (bf16[160,512]{1,0:T(8,128)(2,1)S(1)}, bf16[160,512]{1,0:T(8,128)(2,1)S(1)}, u32[]{:S(2)}, u32[]{:S(2)}) collective-permute-start(bf16[160,512]{1,0:T(8,128)(2,1)S(1)} %get-tuple-element.61), channel_id=1, source_target_pairs={{0,8},{8,0},{16,24},{24,16},{1,9},{9,1},{17,25},{25,17},{2,10},{10... | collective-permute-start | bytes 491528 | tf_op jit(solution)/shard_map/ppermute | solution.py:367
  45.9 1.6 %collective-permute-start.13 = (bf16[160,512]{1,0:T(8,128)(2,1)S(1)}, bf16[160,512]{1,0:T(8,128)(2,1)S(1)}, u32[]{:S(2)}, u32[]{:S(2)}) collective-permute-start(bf16[160,512]{1,0:T(8,128)(2,1)S(1)} %get-tuple-element.62), channel_id=1, source_target_pairs={{0,8},{8,0},{16,24},{24,16},{1,9},{9,1},{17,25},{25,17},{2,10},{10... | collective-permute-start | bytes 491528 | tf_op jit(solution)/shard_map/ppermute | solution.py:367
  54.0 5.8 %collective-permute-start.20 = (bf16[128,512]{1,0:T(8,128)(2,1)S(1)}, bf16[128,512]{1,0:T(8,128)(2,1)S(1)}, u32[]{:S(2)}, u32[]{:S(2)}) collective-permute-start(bf16[128,512]{1,0:T(8,128)(2,1)S(1)} %get-tuple-element.53), channel_id=1, source_target_pairs={{0,1},{1,0},{2,3},{3,2},{4,5},{5,4},{6,7},{7,6},{8,9},{9,8},{10,11... | collective-permute-start | bytes 393224 | tf_op jit(solution)/shard_map/ppermute | solution.py:367
  55.9 6.8 %collective-permute-start.18 = (bf16[64,512]{1,0:T(8,128)(2,1)S(1)}, bf16[64,512]{1,0:T(8,128)(2,1)S(1)}, u32[]{:S(2)}, u32[]{:S(2)}) collective-permute-start(bf16[64,512]{1,0:T(8,128)(2,1)S(1)} %slice.51), channel_id=1, source_target_pairs={{0,4},{2,6},{4,0},{6,2},{1,5},{3,7},{5,1},{7,3},{8,12},{10,14},{12... | collective-permute-start | bytes 196616 | tf_op jit(solution)/shard_map/ppermute | solution.py:367
  59.8 5.8 %collective-permute-start.21 = (bf16[64,512]{1,0:T(8,128)(2,1)S(1)}, bf16[64,512]{1,0:T(8,128)(2,1)S(1)}, u32[]{:S(2)}, u32[]{:S(2)}) collective-permute-start(bf16[64,512]{1,0:T(8,128)(2,1)S(1)} %slice.50), channel_id=1, source_target_pairs={{0,4},{2,6},{4,0},{6,2},{1,5},{3,7},{5,1},{7,3},{8,12},{10,14},{12... | collective-permute-start | bytes 196616 | tf_op jit(solution)/shard_map/ppermute | solution.py:367
  62.7 4.3 %collective-permute-start.19 = (bf16[32,512]{1,0:T(8,128)(2,1)S(1)}, bf16[32,512]{1,0:T(8,128)(2,1)S(1)}, u32[]{:S(2)}, u32[]{:S(2)}) collective-permute-start(bf16[32,512]{1,0:T(8,128)(2,1)S(1)} %slice.53), channel_id=1, source_target_pairs={{0,2},{2,0},{4,6},{6,4},{1,3},{3,1},{5,7},{7,5},{8,10},{10,8},{12,... | collective-permute-start | bytes 98312 | tf_op jit(solution)/shard_map/ppermute | solution.py:367
  65.6 4.0 %collective-permute-start.22 = (bf16[32,512]{1,0:T(8,128)(2,1)S(1)}, bf16[32,512]{1,0:T(8,128)(2,1)S(1)}, u32[]{:S(2)}, u32[]{:S(2)}) collective-permute-start(bf16[32,512]{1,0:T(8,128)(2,1)S(1)} %slice.52), channel_id=1, source_target_pairs={{0,2},{2,0},{4,6},{6,4},{1,3},{3,1},{5,7},{7,5},{8,10},{10,8},{12,... | collective-permute-start | bytes 98312 | tf_op jit(solution)/shard_map/ppermute | solution.py:367
  (2 other events, 3.4 us)

commit v4 on v3

--- a/solution.py
+++ b/solution.py
@@ -120,15 +120,59 @@
     return results
 
 
+def sum_kernel(n_a, n_b, *refs):
+    a, b, outs = refs[:n_a], refs[n_a : n_a + n_b], refs[n_a + n_b :]
+    total = join(a).astype(jnp.float32) + join(b).astype(jnp.float32)
+    step = total.shape[0] // len(outs)
+    for p, out in enumerate(outs):
+        out[...] = total[p * step : (p + 1) * step].astype(out.dtype)
+
+
+def sum_pieces(a, b, n_pieces):
+    rows = sum(x.shape[0] for x in a)
+    return pl.pallas_call(
+        functools.partial(sum_kernel, len(a), len(b)),
+        in_specs=[VMEM] * (len(a) + len(b)),
+        out_specs=[VMEM] * n_pieces,
+        out_shape=[jax.ShapeDtypeStruct((rows // n_pieces, a[0].shape[1]), jnp.bfloat16)] * n_pieces,
+        compiler_params=pltpu.CompilerParams(vmem_limit_bytes=VMEM_LIMIT),
+        cost_estimate=cost(0),
+        name="sum_pieces",
+    )(*a, *b)
+
+
+def token_kernel(n, place, source, *outs):
+    rows, steps, _ = source.shape
+    width = outs[0].shape[1]
+    for d in range(n):
+        at = pl.ds(pl.multiple_of((place[3] ^ d) * place[4] + place[5], HD), width)
+        pieces = [source[r, :, at].astype(jnp.float32) for r in range(rows)]
+        outs[d][...] = jnp.concatenate(pieces, axis=0).astype(jnp.bfloat16)
+
+
+def token_pieces(place, tokens, n, width):
+    row_count, steps, _ = tokens.shape
+    return pl.pallas_call(
+        functools.partial(token_kernel, n),
+        grid_spec=pltpu.PrefetchScalarGridSpec(
+            num_scalar_prefetch=1, grid=(), in_specs=[VMEM], out_specs=[VMEM] * n
+        ),
+        out_shape=[jax.ShapeDtypeStruct((row_count * steps, width), jnp.bfloat16)] * n,
+        compiler_params=pltpu.CompilerParams(vmem_limit_bytes=VMEM_LIMIT),
+        cost_estimate=cost(0),
+        name="token_pieces",
+    )(place, tokens)
+
+
 def join(halves):
     return jnp.concatenate([h[...] for h in halves], axis=0)
 
 
-def adam_kernel(units, n_pieces, n_tok, held, projects, updates, place, *refs):
+def adam_kernel(units, n_mine, n_partner, n_tok, held, projects, updates, place, *refs):
     refs = list(refs)
     take = lambda n: [refs.pop(0) for _ in range(n)]
-    mine = take(1)[0]
-    partner = take(n_pieces)
+    mine = take(n_mine)
+    partner = take(n_partner)
     state = take(1 if held else 3)
     toks = take(n_tok)
     if updates:
@@ -155,7 +199,7 @@
     if projects:
         tok = join(toks)
     source = state[0] if held else buffer
-    totals = [mine[...], join(partner)]
+    totals = [join(mine), join(partner)]
     outgoing, products = [], []
     for i in range(2 * n):
         for copy in incoming[i] if incoming else ():
@@ -189,9 +233,9 @@
     mine, partner = total
     held = not isinstance(state, tuple)
     n = 2 * len(units)
-    rows = mine.shape[0]
+    rows = sum(m.shape[0] for m in mine)
     toks = toks if projects else []
-    operands = [mine, *partner]
+    operands = [*mine, *partner]
     in_specs = [VMEM] * len(operands)
     operands += [state] if held else [in_hbm(a) for a in state]
     in_specs += [VMEM] if held else [ANYWHERE] * 3
@@ -216,6 +260,7 @@
         functools.partial(
             adam_kernel,
             units,
+            len(mine),
             len(partner),
             len(toks),
             held,
@@ -367,10 +412,6 @@
     return lax.ppermute(array, axis, [(i, i ^ bit) for i in range(size)])
 
 
-def add_rounded(a, b):
-    return (a.astype(jnp.float32) + b.astype(jnp.float32)).astype(jnp.bfloat16)
-
-
 def fold_rows(arrived, kept, n):
     total = arrived.astype(jnp.float32) + kept
     half = total.shape[0] // 2
@@ -390,7 +431,9 @@
     row_count = tokens.shape[0]
     n_units = width // (tp_count * HEAD_COLS)
     local = grad_parts[0]
-    place = jnp.stack([core, tp, jnp.full_like(core, n_units)]).astype(jnp.int32)
+    place = jnp.stack(
+        [core, tp, jnp.full_like(core, n_units), fsdp, jnp.full_like(core, tp_count * rows), tp * rows]
+    ).astype(jnp.int32)
 
     crossings = [[*range(n_units // 2)], [*range(n_units // 2, n_units)]]
     crossings = [c for c in crossings if c]
@@ -398,45 +441,25 @@
     folds = [range(cut), range(cut, len(crossings))]
     folds = [f for f in folds if len(f)]
 
-    def chip_sum(away, home):
-        return add_rounded(home, jnp.concatenate([swap(a, "group", 1) for a in away], axis=0))
-
-    (away,) = cast_units(place, local, [(1, crossings[0], 1)])
-    later = [u for units in crossings[1:] for u in units]
-    (home,), away_later, (home_later,) = cast_units(
-        place, after(local, *away), [(0, crossings[0], 1), (1, later, 4), (0, later, 1)]
-    )
-    first = chip_sum(away, home)
-    mine, crossed = [first], [swap(first, "group", 2)]
-    rest = chip_sum(away_later, home_later)
-    at = 0
-    for units in crossings[1:]:
-        mine.append(rest[:, at * HEAD_COLS : (at + len(units)) * HEAD_COLS])
-        at += len(units)
-        crossed.append(swap(mine[-1], "group", 2))
-    started = mine[-1]
-
+    pieces = [1] + [4] * (len(crossings) - 1)
+    cast = cast_units(
+        place, local, [(part, units, p if part else 1) for units, p in zip(crossings, pieces) for part in (1, 0)]
+    )
+    mine, crossed = [], []
+    for away, home in zip(cast[::2], cast[1::2]):
+        (one,) = sum_pieces(home, [swap(a, "group", 1) for a in away], 1)
+        mine.append(one)
+        crossed.append(swap(one, "group", 2))
+
+    toks = token_pieces(place, after(tokens, *mine), fsdp_count, rows)
     cosine, sine = rotation_tables(lengths)
     attended = cache_attention(after(queries, *mine), cache_keys, cache_values, lengths)
-
-    source = after(tokens, started)
-    toks = []
-    for d in range(fsdp_count):
-        at = ((fsdp ^ d) * tp_count + tp) * rows
-        piece = lax.dynamic_slice(source, (0, 0, at), (row_count, STEPS, rows))
-        toks.append(piece.reshape(1, row_count * STEPS, rows))
     distance = 1
     while distance < fsdp_count:
-        stay = toks[::2]
-        away = toks[1::2]
-        away_all = jnp.concatenate(away, axis=0) if len(away) > 1 else away[0]
-        if distance > 1:
-            away_all = after(away_all, attended[1])
-        got = swap(away_all, "fsdp", distance)
-        got = jnp.split(got, len(away), axis=0) if len(away) > 1 else [got]
-        toks = [jnp.concatenate([s, g], axis=0) for s, g in zip(stay, got)]
+        toks = [swap(t, "fsdp", distance) if d & distance else t for d, t in enumerate(toks)]
+        if distance == 1:
+            toks = list(lax.optimization_barrier((*toks, attended[1])))[:-1]
         distance *= 2
-    toks = [toks[0].reshape(fsdp_count * row_count * STEPS, rows)]
 
     state = (weights, moment1, moment2)
     last = crossings[-1]
@@ -445,15 +468,15 @@
     updated = None
     step = (attended[1],)
     for c, units in enumerate(crossings):
-        one, other = mine[c], after(crossed[c], *step)
+        one, other = [mine[c]], after(crossed[c], *step)
         bit = 2
         while True:
-            one = add_rounded(one, other)
             bit *= 2
+            one = sum_pieces(one, [other], 4 if bit >= group_count else 1)
             if bit >= group_count:
                 break
-            other = swap(one, "group", bit)
-        totals.append((one, [swap(p, "group", 1) for p in jnp.split(one, 4, axis=0)]))
+            other = swap(one[0], "group", bit)
+        totals.append((one, [swap(p, "group", 1) for p in one]))
         updated, both = adam_units(place, totals[c], state, toks, units, width, previous=updated)
         sums.append(both)
         step = (sums[c][0],)

time: 72.2 us -> 66.5 us (0.921)
  other arithmetic: 6.59 us -> 0.39 us
  waiting for transfers between devices: 11.3 us -> 17.1 us
  starting transfers between devices: 23.8 us -> 20.3 us
  local copies, waits for them, and re-layouts: 2.57 us -> 0.22 us
  Pallas kernels: 26.6 us -> 27.5 us
    ppermute x23 -> x25, waiting for transfers between devices: 11.3 us -> 17.1 us  [swap(): return lax.ppermute(array, axis, [(i, i ^ bit) for i in range(size)])]
    convert_element_type x4 -> x0, other arithmetic: 5.19 us -> none  [add_rounded(): return (a.astype(jnp.float32) + b.astype(jnp.float32)).astype(jnp.bfloat16)]
    ppermute x23 -> x25, starting transfers between devices: 23.8 us -> 20.3 us  [swap(): return lax.ppermute(array, axis, [(i, i ^ bit) for i in range(size)])]
    pallas_call x2 -> x7, Pallas kernels: 13.1 us -> 15.5 us  [the longest x2 14.3 us: adam_units(): pl.pallas_call(functools.partial(adam_kernel, units, len(mine), len(partn...]
    pallas_call x2 -> x1, Pallas kernels: 4.61 us -> 3.15 us  [cast_units(): pl.pallas_call(functools.partial(cast_kernel, wanted), grid_spec=pltpu.Pr...]
    concatenate x3 -> x0, other arithmetic: 0.94 us -> none  [the longest x2 0.92 us: butterfly_shards(): toks = [jnp.concatenate([s, g], axis=0) for s, g in zip(stay, got)]]
    split x3 -> x0, local copies, waits for them, and re-layouts: 0.84 us -> none  [the longest x2 0.83 us: butterfly_shards(): jnp.split(one, 4, axis=0)]
    unnamed x6 -> x4, local copies, waits for them, and re-layouts: 0.84 us -> 0.01 us
  transfers between devices with their start and end apart: 23 -> 25, of which waited for: 14 -> 17; matrix products, arithmetic and copies ran while one was open for 10% -> 1% of each run, Pallas kernels for 31% -> 33%
where the time goes in v4:
time: 66.5 us; the launch traced here: 66.3 us
  Pallas kernels  27.5 us (41%)
  starting transfers between devices  20.3 us (31%)
  waiting for transfers between devices  17.1 us (26%)
  between operations  0.86 us (1%)
    ppermute x25, starting transfers between devices, swap(): return lax.ppermute(array, axis, [(i, i ^ bit) for i in range(size)])  20.3 us
    ppermute x25, waiting for transfers between devices, swap(): return lax.ppermute(array, axis, [(i, i ^ bit) for i in range(size)])  17.1 us
    pallas_call x2, Pallas kernels, adam_units(): pl.pallas_call(functools.partial(adam_kernel, units, len(mine), len(partn...  14.3 us
    pallas_call x1, Pallas kernels, cache_attention(): pl.pallas_call(functools.partial(cache_kernel, heads), grid_spec=pltpu.Pr...  6.71 us
    pallas_call x1, Pallas kernels, cast_units(): pl.pallas_call(functools.partial(cast_kernel, wanted), grid_spec=pltpu.Pr...  3.15 us
    pallas_call x1, Pallas kernels, merge(): pl.pallas_call(functools.partial(merge_kernel, len(folds), row_count), in...  2.16 us
  transfers between devices with their start and end apart: 25, of which 17 were waited for; matrix products, arithmetic and copies ran while one was open for 1% of the time, Pallas kernels for 33%

profile of v4, /device:TPU:0, one launch (start us, length us, event | category | flops | bytes accessed | tf_op | source)
XLA Modules:
  0.0 66.3 jit_solution(6902858854299143872)
XLA Ops:
  0.7 3.2 %cast_units.1 = (bf16[640,512]{1,0:T(8,128)(2,1)S(1)}, bf16[640,512]{1,0:T(8,128)(2,1)S(1)}, bf16[160,512]{1,0:T(8,128)(2,1)S(1)}, bf16[160,512]{1,0:T(8,128)(2,...) custom-call(s32[6]{0:T(128)S(1)} %stack.19.place, ...), custom_call_target="tpu_custom_call" | custom-call | flops 1 | bytes 1 | tf_op jit(solution)/shard_map/cast_units/pallas_call | solution.py:102
  3.9 0.5 collective-permute-start.5
  4.4 1.7 %collective-permute-done.5.refs_1_ = bf16[640,512]{1,0:T(8,128)(2,1)S(1)} collective-permute-done((bf16[640,512]{1,0:T(8,128)(2,1)S(1)}, bf16[640,512]{1,0:T(8,128)(2,1)S(1)}, u32[]{:S(2)}, u32[]{:S(2)}) %collective-permute-start.5) | collective-permute-done | bytes 655392 | tf_op jit(solution)/shard_map/ppermute | solution.py:412
  6.3 2.9 %collective-permute-start.6 = (bf16[640,512]{1,0:T(8,128)(2,1)S(1)}, bf16[640,512]{1,0:T(8,128)(2,1)S(1)}, u32[]{:S(2)}, u32[]{:S(2)}) collective-permute-start(bf16[640,512]{1,0:T(8,128)(2,1)S(1)} %sum_pieces.5.refs_0_), channel_id=1, source_target_pairs={{0,16},{8,24},{16,0},{24,8},{1,17},{9,25},{17,1},{25,9},{2,18},{10... | collective-permute-start | bytes 1966088 | tf_op jit(solution)/shard_map/ppermute | solution.py:412
  9.2 0.5 collective-permute-start.1
  11.7 0.6 token_pieces.1
  12.3 2.1 %collective-permute-start.11 = (bf16[32,640]{1,0:T(8,128)(2,1)S(1)}, bf16[32,640]{1,0:T(8,128)(2,1)S(1)}, u32[]{:S(2)}, u32[]{:S(2)}) collective-permute-start(bf16[32,640]{1,0:T(8,128)(2,1)S(1)} %get-tuple-element.63), channel_id=1, source_target_pairs={{0,2},{2,0},{4,6},{6,4},{1,3},{3,1},{5,7},{7,5},{8,10},{10,8},{12,... | collective-permute-start | bytes 122888 | tf_op jit(solution)/shard_map/ppermute | solution.py:412
  14.4 6.7 %cache_attention.1 = (bf16[4,8,32,128]{3,2,1,0:T(8,128)(2,1)S(1)}, f32[4,8,32,128]{3,2,1,0:T(8,128)S(1)}, f32[4,8,32,128]{3,2,1,0:T(8,128)S(1)}) custom-call(s32[8]{0:T(128)S(1)} %copy-done.1, bf16[8,4,2560]{2,1,0:T(4,128)(2,1)} %q, bf16[8,512,512]{2,1,0:T(8,128)(2,1)} %k.1, bf16[8,512,512]{2,1,0:T(8,128)(2,1)} %v.1), custom_call_target="tpu_custom_call" | custom-call | flops 1 | bytes 1 | tf_op jit(solution)/shard_map/cache_attention/pallas_call | solution.py:333
  21.2 3.0 %collective-permute-start.13 = (bf16[32,640]{1,0:T(8,128)(2,1)S(1)}, bf16[32,640]{1,0:T(8,128)(2,1)S(1)}, u32[]{:S(2)}, u32[]{:S(2)}) collective-permute-start(bf16[32,640]{1,0:T(8,128)(2,1)S(1)} %get-tuple-element.68), channel_id=1, source_target_pairs={{0,4},{2,6},{4,0},{6,2},{1,5},{3,7},{5,1},{7,3},{8,12},{10,14},{12... | collective-permute-start | bytes 122888 | tf_op jit(solution)/shard_map/ppermute | solution.py:412
  25.5 1.0 %collective-permute-done.13.refs_13_ = bf16[32,640]{1,0:T(8,128)(2,1)S(1)} collective-permute-done((bf16[32,640]{1,0:T(8,128)(2,1)S(1)}, bf16[32,640]{1,0:T(8,128)(2,1)S(1)}, u32[]{:S(2)}, u32[]{:S(2)}) %collective-permute-start.13) | collective-permute-done | bytes 40992 | tf_op jit(solution)/shard_map/ppermute | solution.py:412
  26.4 2.7 %collective-permute-done.14.refs_14_ = bf16[32,640]{1,0:T(8,128)(2,1)S(1)} collective-permute-done((bf16[32,640]{1,0:T(8,128)(2,1)S(1)}, bf16[32,640]{1,0:T(8,128)(2,1)S(1)}, u32[]{:S(2)}, u32[]{:S(2)}) %collective-permute-start.14) | collective-permute-done | bytes 40992 | tf_op jit(solution)/shard_map/ppermute | solution.py:412
  29.3 1.3 %collective-permute-done.10.refs_7_ = bf16[160,512]{1,0:T(8,128)(2,1)} collective-permute-done((bf16[160,512]{1,0:T(8,128)(2,1)S(1)}, bf16[160,512]{1,0:T(8,128)(2,1)}, u32[]{:S(2)}, u32[]{:S(2)}) %collective-permute-start.10) | collective-permute-done | bytes 163872 | tf_op jit(solution)/shard_map/ppermute | solution.py:412
  30.6 7.7 %adam_project.2 = (f32[640,2048]{1,0:T(8,128)}, f32[640,2048]{1,0:T(8,128)}, f32[640,2048]{1,0:T(8,128)}, bf16[128,512]{1,0:T(8,128)(2,1)S(1)}, f32[128,512]{1,0:T(8,128)S(1)}) custom-call(s32[6]{0:T(128)S(1)} %stack.19.place, bf16[160,512]{1,0:T(8,128)(2,1)S(1)} %get-tuple-element.57.refs_0_, bf16[160,512]{1,0:T(8,128)(2,1)S(1)} %get-tuple-element.58.refs_1_, ...), custom_call_target="tpu_custom_call" | custom-call | flops 1 | bytes 1 | tf_op jit(solution)/shard_map/adam_project/pallas_call | solution.py:259
  38.4 1.6 %collective-permute-start.19 = (bf16[128,512]{1,0:T(8,128)(2,1)S(1)}, bf16[128,512]{1,0:T(8,128)(2,1)S(1)}, u32[]{:S(2)}, u32[]{:S(2)}) collective-permute-start(bf16[128,512]{1,0:T(8,128)(2,1)S(1)} %get-tuple-element.70), channel_id=1, source_target_pairs={{0,1},{1,0},{2,3},{3,2},{4,5},{5,4},{6,7},{7,6},{8,9},{9,8},{10,11... | collective-permute-start | bytes 393224 | tf_op jit(solution)/shard_map/ppermute | solution.py:412
  42.4 6.5 %adam_project.3 = (f32[640,2048]{1,0:T(8,128)}, f32[640,2048]{1,0:T(8,128)}, f32[640,2048]{1,0:T(8,128)}, bf16[128,512]{1,0:T(8,128)(2,1)S(1)}, f32[128,512]{1,0:T(8,128)S(1)}) custom-call(s32[6]{0:T(128)S(1)} %stack.19.place, bf16[160,512]{1,0:T(8,128)(2,1)S(1)} %get-tuple-element.72.refs_0_, ...), custom_call_target="tpu_custom_call", output_to_operand_aliasing={{0}: (16, {}), {1}: (17, {}), {2}: (18, {})} | custom-call | flops 1 | bytes 1 | tf_op jit(solution)/shard_map/adam_project/pallas_call | solution.py:259
  48.9 0.5 collective-permute-start.22
  49.5 2.3 %collective-permute-start.20 = (bf16[64,512]{1,0:T(8,128)(2,1)S(1)}, bf16[64,512]{1,0:T(8,128)(2,1)S(1)}, u32[]{:S(2)}, u32[]{:S(2)}) collective-permute-start(bf16[64,512]{1,0:T(8,128)(2,1)S(1)} %slice.51), channel_id=1, source_target_pairs={{0,4},{2,6},{4,0},{6,2},{1,5},{3,7},{5,1},{7,3},{8,12},{10,14},{12... | collective-permute-start | bytes 196616 | tf_op jit(solution)/shard_map/ppermute | solution.py:412
  51.8 2.9 %collective-permute-done.22 = bf16[128,512]{1,0:T(8,128)(2,1)S(1)} collective-permute-done((bf16[128,512]{1,0:T(8,128)(2,1)S(1)}, bf16[128,512]{1,0:T(8,128)(2,1)S(1)}, u32[]{:S(2)}, u32[]{:S(2)}) %collective-permute-start.22) | collective-permute-done | bytes 131104 | tf_op jit(solution)/shard_map/ppermute | solution.py:412
  54.7 1.2 %collective-permute-start.23 = (bf16[64,512]{1,0:T(8,128)(2,1)S(1)}, bf16[64,512]{1,0:T(8,128)(2,1)S(1)}, u32[]{:S(2)}, u32[]{:S(2)}) collective-permute-start(bf16[64,512]{1,0:T(8,128)(2,1)S(1)} %slice.50), channel_id=1, source_target_pairs={{0,4},{2,6},{4,0},{6,2},{1,5},{3,7},{5,1},{7,3},{8,12},{10,14},{12... | collective-permute-start | bytes 196616 | tf_op jit(solution)/shard_map/ppermute | solution.py:412
  56.2 1.7 %collective-permute-start.21 = (bf16[32,512]{1,0:T(8,128)(2,1)S(1)}, bf16[32,512]{1,0:T(8,128)(2,1)S(1)}, u32[]{:S(2)}, u32[]{:S(2)}) collective-permute-start(bf16[32,512]{1,0:T(8,128)(2,1)S(1)} %slice.53), channel_id=1, source_target_pairs={{0,2},{2,0},{4,6},{6,4},{1,3},{3,1},{5,7},{7,5},{8,10},{10,8},{12,... | collective-permute-start | bytes 98312 | tf_op jit(solution)/shard_map/ppermute | solution.py:412
  57.9 2.3 %collective-permute-done.23 = bf16[64,512]{1,0:T(8,128)(2,1)S(1)} collective-permute-done((bf16[64,512]{1,0:T(8,128)(2,1)S(1)}, bf16[64,512]{1,0:T(8,128)(2,1)S(1)}, u32[]{:S(2)}, u32[]{:S(2)}) %collective-permute-start.23) | collective-permute-done | bytes 65568 | tf_op jit(solution)/shard_map/ppermute | solution.py:412
  60.2 1.4 %collective-permute-start.24 = (bf16[32,512]{1,0:T(8,128)(2,1)S(1)}, bf16[32,512]{1,0:T(8,128)(2,1)S(1)}, u32[]{:S(2)}, u32[]{:S(2)}) collective-permute-start(bf16[32,512]{1,0:T(8,128)(2,1)S(1)} %slice.52), channel_id=1, source_target_pairs={{0,2},{2,0},{4,6},{6,4},{1,3},{3,1},{5,7},{7,5},{8,10},{10,8},{12,... | collective-permute-start | bytes 98312 | tf_op jit(solution)/shard_map/ppermute | solution.py:412
  61.7 2.5 %collective-permute-done.24.refs_2_ = bf16[32,512]{1,0:T(8,128)(2,1)S(1)} collective-permute-done((bf16[32,512]{1,0:T(8,128)(2,1)S(1)}, bf16[32,512]{1,0:T(8,128)(2,1)S(1)}, u32[]{:S(2)}, u32[]{:S(2)}) %collective-permute-start.24) | collective-permute-done | bytes 32800 | tf_op jit(solution)/shard_map/ppermute | solution.py:412
  64.1 2.2 %merge_new.1 = (bf16[8,4,1024]{2,1,0:T(4,128)(2,1)}, bf16[8,4,2560]{2,1,0:T(4,128)(2,1)}) custom-call(bf16[32,512]{1,0:T(8,128)(2,1)S(1)} %collective-permute-done.21.refs_0_, f32[32,512]{1,0:T(8,128)S(1)} %slice.39.refs_1_, bf16[32,512]{1,0:T(8,128)(2,1)S(1)} %collective-permute-done.24.refs_2_, f32[32,512]{1,0:T(8,128)S(1)} %slice.43.refs_3_, ...), custom_call_target="tpu_custom_call" | custom-call | flops 1 | bytes 1 | tf_op jit(solution)/shard_map/merge_new/pallas_call | solution.py:399
  (56 shorter events, 6.5 us)
Async XLA Ops:
  3.9 2.2 %collective-permute-start.5 = (bf16[640,512]{1,0:T(8,128)(2,1)S(1)}, bf16[640,512]{1,0:T(8,128)(2,1)S(1)}, u32[]{:S(2)}, u32[]{:S(2)}) collective-permute-start(bf16[640,512]{1,0:T(8,128)(2,1)S(1)} %get-tuple-element.53), channel_id=1, source_target_pairs={{0,8},{8,0},{16,24},{24,16},{1,9},{9,1},{17,25},{25,17},{2,10},{10... | collective-permute-start | bytes 1966088 | tf_op jit(solution)/shard_map/ppermute | solution.py:412
  6.3 18.4 %collective-permute-start.6 = (bf16[640,512]{1,0:T(8,128)(2,1)S(1)}, bf16[640,512]{1,0:T(8,128)(2,1)S(1)}, u32[]{:S(2)}, u32[]{:S(2)}) collective-permute-start(bf16[640,512]{1,0:T(8,128)(2,1)S(1)} %sum_pieces.5.refs_0_), channel_id=1, source_target_pairs={{0,16},{8,24},{16,0},{24,8},{1,17},{9,25},{17,1},{25,9},{2,18},{10... | collective-permute-start | bytes 1966088 | tf_op jit(solution)/shard_map/ppermute | solution.py:412
  9.2 1.4 %collective-permute-start = (bf16[160,512]{1,0:T(8,128)(2,1)S(1)}, bf16[160,512]{1,0:T(8,128)(2,1)S(1)}, u32[]{:S(2)}, u32[]{:S(2)}) collective-permute-start(bf16[160,512]{1,0:T(8,128)(2,1)S(1)} %get-tuple-element.48), channel_id=1, source_target_pairs={{0,8},{8,0},{16,24},{24,16},{1,9},{9,1},{17,25},{25,17},{2,10},{10... | collective-permute-start | bytes 491528 | tf_op jit(solution)/shard_map/ppermute | solution.py:412
  9.2 1.6 %collective-permute-start.1 = (bf16[160,512]{1,0:T(8,128)(2,1)S(1)}, bf16[160,512]{1,0:T(8,128)(2,1)S(1)}, u32[]{:S(2)}, u32[]{:S(2)}) collective-permute-start(bf16[160,512]{1,0:T(8,128)(2,1)S(1)} %get-tuple-element.49), channel_id=1, source_target_pairs={{0,8},{8,0},{16,24},{24,16},{1,9},{9,1},{17,25},{25,17},{2,10},{10... | collective-permute-start | bytes 491528 | tf_op jit(solution)/shard_map/ppermute | solution.py:412
  9.7 1.4 %collective-permute-start.2 = (bf16[160,512]{1,0:T(8,128)(2,1)S(1)}, bf16[160,512]{1,0:T(8,128)(2,1)S(1)}, u32[]{:S(2)}, u32[]{:S(2)}) collective-permute-start(bf16[160,512]{1,0:T(8,128)(2,1)S(1)} %get-tuple-element.50), channel_id=1, source_target_pairs={{0,8},{8,0},{16,24},{24,16},{1,9},{9,1},{17,25},{25,17},{2,10},{10... | collective-permute-start | bytes 491528 | tf_op jit(solution)/shard_map/ppermute | solution.py:412
  9.7 1.6 %collective-permute-start.3 = (bf16[160,512]{1,0:T(8,128)(2,1)S(1)}, bf16[160,512]{1,0:T(8,128)(2,1)S(1)}, u32[]{:S(2)}, u32[]{:S(2)}) collective-permute-start(bf16[160,512]{1,0:T(8,128)(2,1)S(1)} %get-tuple-element.51), channel_id=1, source_target_pairs={{0,8},{8,0},{16,24},{24,16},{1,9},{9,1},{17,25},{25,17},{2,10},{10... | collective-permute-start | bytes 491528 | tf_op jit(solution)/shard_map/ppermute | solution.py:412
  11.5 28.5 %collective-permute-start.4 = (bf16[640,512]{1,0:T(8,128)(2,1)S(1)}, bf16[640,512]{1,0:T(8,128)(2,1)S(1)}, u32[]{:S(2)}, u32[]{:S(2)}) collective-permute-start(bf16[640,512]{1,0:T(8,128)(2,1)S(1)} %sum_pieces.4.refs_0_), channel_id=1, source_target_pairs={{0,16},{8,24},{16,0},{24,8},{1,17},{9,25},{17,1},{25,9},{2,18},{10... | collective-permute-start | bytes 1966088 | tf_op jit(solution)/shard_map/ppermute | solution.py:412
  12.3 8.9 %collective-permute-start.11 = (bf16[32,640]{1,0:T(8,128)(2,1)S(1)}, bf16[32,640]{1,0:T(8,128)(2,1)S(1)}, u32[]{:S(2)}, u32[]{:S(2)}) collective-permute-start(bf16[32,640]{1,0:T(8,128)(2,1)S(1)} %get-tuple-element.63), channel_id=1, source_target_pairs={{0,2},{2,0},{4,6},{6,4},{1,3},{3,1},{5,7},{7,5},{8,10},{10,8},{12,... | collective-permute-start | bytes 122888 | tf_op jit(solution)/shard_map/ppermute | solution.py:412
  14.4 6.8 %collective-permute-start.12 = (bf16[32,640]{1,0:T(8,128)(2,1)S(1)}, bf16[32,640]{1,0:T(8,128)(2,1)S(1)}, u32[]{:S(2)}, u32[]{:S(2)}) collective-permute-start(bf16[32,640]{1,0:T(8,128)(2,1)S(1)} %get-tuple-element.65), channel_id=1, source_target_pairs={{0,2},{2,0},{4,6},{6,4},{1,3},{3,1},{5,7},{7,5},{8,10},{10,8},{12,... | collective-permute-start | bytes 122888 | tf_op jit(solution)/shard_map/ppermute | solution.py:412
  21.2 5.3 %collective-permute-start.13 = (bf16[32,640]{1,0:T(8,128)(2,1)S(1)}, bf16[32,640]{1,0:T(8,128)(2,1)S(1)}, u32[]{:S(2)}, u32[]{:S(2)}) collective-permute-start(bf16[32,640]{1,0:T(8,128)(2,1)S(1)} %get-tuple-element.68), channel_id=1, source_target_pairs={{0,4},{2,6},{4,0},{6,2},{1,5},{3,7},{5,1},{7,3},{8,12},{10,14},{12... | collective-permute-start | bytes 122888 | tf_op jit(solution)/shard_map/ppermute | solution.py:412
  24.2 4.9 %collective-permute-start.14 = (bf16[32,640]{1,0:T(8,128)(2,1)S(1)}, bf16[32,640]{1,0:T(8,128)(2,1)S(1)}, u32[]{:S(2)}, u32[]{:S(2)}) collective-permute-start(bf16[32,640]{1,0:T(8,128)(2,1)S(1)} %collective-permute-done.12), channel_id=1, source_target_pairs={{0,4},{2,6},{4,0},{6,2},{1,5},{3,7},{5,1},{7,3},{8,12},{10,14},{12... | collective-permute-start | bytes 122888 | tf_op jit(solution)/shard_map/ppermute | solution.py:412
  24.9 4.4 %collective-permute-start.7 = (bf16[160,512]{1,0:T(8,128)(2,1)S(1)}, bf16[160,512]{1,0:T(8,128)(2,1)}, u32[]{:S(2)}, u32[]{:S(2)}) collective-permute-start(bf16[160,512]{1,0:T(8,128)(2,1)S(1)} %get-tuple-element.57.refs_0_), channel_id=1, source_target_pairs={{0,8},{8,0},{16,24},{24,16},{1,9},{9,1},{17,25},{25,17},{2,10},{10... | collective-permute-start | bytes 491528 | tf_op jit(solution)/shard_map/ppermute | solution.py:412
  25.0 4.3 %collective-permute-start.8 = (bf16[160,512]{1,0:T(8,128)(2,1)S(1)}, bf16[160,512]{1,0:T(8,128)(2,1)}, u32[]{:S(2)}, u32[]{:S(2)}) collective-permute-start(bf16[160,512]{1,0:T(8,128)(2,1)S(1)} %get-tuple-element.58.refs_1_), channel_id=1, source_target_pairs={{0,8},{8,0},{16,24},{24,16},{1,9},{9,1},{17,25},{25,17},{2,10},{10... | collective-permute-start | bytes 491528 | tf_op jit(solution)/shard_map/ppermute | solution.py:412
  26.4 2.9 %collective-permute-start.9 = (bf16[160,512]{1,0:T(8,128)(2,1)S(1)}, bf16[160,512]{1,0:T(8,128)(2,1)}, u32[]{:S(2)}, u32[]{:S(2)}) collective-permute-start(bf16[160,512]{1,0:T(8,128)(2,1)S(1)} %get-tuple-element.59.refs_2_), channel_id=1, source_target_pairs={{0,8},{8,0},{16,24},{24,16},{1,9},{9,1},{17,25},{25,17},{2,10},{10... | collective-permute-start | bytes 491528 | tf_op jit(solution)/shard_map/ppermute | solution.py:412
  29.1 1.5 %collective-permute-start.10 = (bf16[160,512]{1,0:T(8,128)(2,1)S(1)}, bf16[160,512]{1,0:T(8,128)(2,1)}, u32[]{:S(2)}, u32[]{:S(2)}) collective-permute-start(bf16[160,512]{1,0:T(8,128)(2,1)S(1)} %get-tuple-element.60.refs_3_), channel_id=1, source_target_pairs={{0,8},{8,0},{16,24},{24,16},{1,9},{9,1},{17,25},{25,17},{2,10},{10... | collective-permute-start | bytes 491528 | tf_op jit(solution)/shard_map/ppermute | solution.py:412
  38.4 11.1 %collective-permute-start.19 = (bf16[128,512]{1,0:T(8,128)(2,1)S(1)}, bf16[128,512]{1,0:T(8,128)(2,1)S(1)}, u32[]{:S(2)}, u32[]{:S(2)}) collective-permute-start(bf16[128,512]{1,0:T(8,128)(2,1)S(1)} %get-tuple-element.70), channel_id=1, source_target_pairs={{0,1},{1,0},{2,3},{3,2},{4,5},{5,4},{6,7},{7,6},{8,9},{9,8},{10,11... | collective-permute-start | bytes 393224 | tf_op jit(solution)/shard_map/ppermute | solution.py:412
  40.2 1.5 %collective-permute-start.15 = (bf16[160,512]{1,0:T(8,128)(2,1)S(1)}, bf16[160,512]{1,0:T(8,128)(2,1)S(1)}, u32[]{:S(2)}, u32[]{:S(2)}) collective-permute-start(bf16[160,512]{1,0:T(8,128)(2,1)S(1)} %get-tuple-element.72.refs_0_), channel_id=1, source_target_pairs={{0,8},{8,0},{16,24},{24,16},{1,9},{9,1},{17,25},{25,17},{2,10},{10... | collective-permute-start | bytes 491528 | tf_op jit(solution)/shard_map/ppermute | solution.py:412
  40.2 1.6 %collective-permute-start.16 = (bf16[160,512]{1,0:T(8,128)(2,1)S(1)}, bf16[160,512]{1,0:T(8,128)(2,1)S(1)}, u32[]{:S(2)}, u32[]{:S(2)}) collective-permute-start(bf16[160,512]{1,0:T(8,128)(2,1)S(1)} %get-tuple-element.73.refs_1_), channel_id=1, source_target_pairs={{0,8},{8,0},{16,24},{24,16},{1,9},{9,1},{17,25},{25,17},{2,10},{10... | collective-permute-start | bytes 491528 | tf_op jit(solution)/shard_map/ppermute | solution.py:412
  40.8 1.6 %collective-permute-start.18 = (bf16[160,512]{1,0:T(8,128)(2,1)S(1)}, bf16[160,512]{1,0:T(8,128)(2,1)S(1)}, u32[]{:S(2)}, u32[]{:S(2)}) collective-permute-start(bf16[160,512]{1,0:T(8,128)(2,1)S(1)} %get-tuple-element.75.refs_3_), channel_id=1, source_target_pairs={{0,8},{8,0},{16,24},{24,16},{1,9},{9,1},{17,25},{25,17},{2,10},{10... | collective-permute-start | bytes 491528 | tf_op jit(solution)/shard_map/ppermute | solution.py:412
  48.9 5.7 %collective-permute-start.22 = (bf16[128,512]{1,0:T(8,128)(2,1)S(1)}, bf16[128,512]{1,0:T(8,128)(2,1)S(1)}, u32[]{:S(2)}, u32[]{:S(2)}) collective-permute-start(bf16[128,512]{1,0:T(8,128)(2,1)S(1)} %get-tuple-element.83), channel_id=1, source_target_pairs={{0,1},{1,0},{2,3},{3,2},{4,5},{5,4},{6,7},{7,6},{8,9},{9,8},{10,11... | collective-permute-start | bytes 393224 | tf_op jit(solution)/shard_map/ppermute | solution.py:412
  49.5 6.6 %collective-permute-start.20 = (bf16[64,512]{1,0:T(8,128)(2,1)S(1)}, bf16[64,512]{1,0:T(8,128)(2,1)S(1)}, u32[]{:S(2)}, u32[]{:S(2)}) collective-permute-start(bf16[64,512]{1,0:T(8,128)(2,1)S(1)} %slice.51), channel_id=1, source_target_pairs={{0,4},{2,6},{4,0},{6,2},{1,5},{3,7},{5,1},{7,3},{8,12},{10,14},{12... | collective-permute-start | bytes 196616 | tf_op jit(solution)/shard_map/ppermute | solution.py:412
  54.7 5.4 %collective-permute-start.23 = (bf16[64,512]{1,0:T(8,128)(2,1)S(1)}, bf16[64,512]{1,0:T(8,128)(2,1)S(1)}, u32[]{:S(2)}, u32[]{:S(2)}) collective-permute-start(bf16[64,512]{1,0:T(8,128)(2,1)S(1)} %slice.50), channel_id=1, source_target_pairs={{0,4},{2,6},{4,0},{6,2},{1,5},{3,7},{5,1},{7,3},{8,12},{10,14},{12... | collective-permute-start | bytes 196616 | tf_op jit(solution)/shard_map/ppermute | solution.py:412
  56.2 5.5 %collective-permute-start.21 = (bf16[32,512]{1,0:T(8,128)(2,1)S(1)}, bf16[32,512]{1,0:T(8,128)(2,1)S(1)}, u32[]{:S(2)}, u32[]{:S(2)}) collective-permute-start(bf16[32,512]{1,0:T(8,128)(2,1)S(1)} %slice.53), channel_id=1, source_target_pairs={{0,2},{2,0},{4,6},{6,4},{1,3},{3,1},{5,7},{7,5},{8,10},{10,8},{12,... | collective-permute-start | bytes 98312 | tf_op jit(solution)/shard_map/ppermute | solution.py:412
  60.2 4.0 %collective-permute-start.24 = (bf16[32,512]{1,0:T(8,128)(2,1)S(1)}, bf16[32,512]{1,0:T(8,128)(2,1)S(1)}, u32[]{:S(2)}, u32[]{:S(2)}) collective-permute-start(bf16[32,512]{1,0:T(8,128)(2,1)S(1)} %slice.52), channel_id=1, source_target_pairs={{0,2},{2,0},{4,6},{6,4},{1,3},{3,1},{5,7},{7,5},{8,10},{10,8},{12,... | collective-permute-start | bytes 98312 | tf_op jit(solution)/shard_map/ppermute | solution.py:412
  (3 other events, 26.2 us)

commit v5 on v4

--- a/solution.py
+++ b/solution.py
@@ -25,7 +25,8 @@
 correct_two = 1.0 - 0.95**10
 masked_score = -1e30
 score_scale = 1.0 / math.sqrt(HD)
-VMEM_LIMIT = 12 * 1024 * 1024
+N_PIECES = 2
+MIB = 1024 * 1024
 
 
 def adam_update(weights, moment1, moment2, gradient):
@@ -76,7 +77,8 @@
     return pl.ds(pl.multiple_of((half * place[2] + unit) * HEAD_COLS, HEAD_COLS), HEAD_COLS)
 
 
-def cast_kernel(wanted, place, source, *refs):
+def cast_kernel(wanted, n_units, source, *refs):
+    place = (lax.axis_index("group") % 2, None, n_units)
     outs, (buffer, sems) = refs[:-2], refs[-2:]
     blocks = [(o, k, part, unit) for o, (part, units, _) in enumerate(wanted) for k, unit in enumerate(units)]
     copies = [
@@ -95,24 +97,20 @@
             outs[first[o] + p][:, k * HEAD_COLS : (k + 1) * HEAD_COLS] = piece
 
 
-def cast_units(place, local, wanted):
+def cast_units(local, n_units, wanted):
     rows = local.shape[0]
     n = sum(len(units) for _, units, _ in wanted)
     shapes = [(rows // p, len(units) * HEAD_COLS) for _, units, p in wanted for _ in range(p)]
     out = pl.pallas_call(
-        functools.partial(cast_kernel, wanted),
-        grid_spec=pltpu.PrefetchScalarGridSpec(
-            num_scalar_prefetch=1,
-            grid=(),
-            in_specs=[ANYWHERE],
-            out_specs=[VMEM] * len(shapes),
-            scratch_shapes=[pltpu.VMEM((n, rows, HEAD_COLS), jnp.float32), pltpu.SemaphoreType.DMA((n,))],
-        ),
+        functools.partial(cast_kernel, wanted, n_units),
+        in_specs=[ANYWHERE],
+        out_specs=[VMEM] * len(shapes),
+        scratch_shapes=[pltpu.VMEM((n, rows, HEAD_COLS), jnp.float32), pltpu.SemaphoreType.DMA((n,))],
         out_shape=[jax.ShapeDtypeStruct(shape, jnp.bfloat16) for shape in shapes],
-        compiler_params=pltpu.CompilerParams(vmem_limit_bytes=VMEM_LIMIT),
+        compiler_params=pltpu.CompilerParams(vmem_limit_bytes=6 * MIB),
         cost_estimate=cost(0),
         name="cast_units",
-    )(place, in_hbm(local))
+    )(in_hbm(local))
     results = []
     for _, _, p in wanted:
         results.append(out[:p])
@@ -135,7 +133,7 @@
         in_specs=[VMEM] * (len(a) + len(b)),
         out_specs=[VMEM] * n_pieces,
         out_shape=[jax.ShapeDtypeStruct((rows // n_pieces, a[0].shape[1]), jnp.bfloat16)] * n_pieces,
-        compiler_params=pltpu.CompilerParams(vmem_limit_bytes=VMEM_LIMIT),
+        compiler_params=pltpu.CompilerParams(vmem_limit_bytes=6 * MIB),
         cost_estimate=cost(0),
         name="sum_pieces",
     )(*a, *b)
@@ -158,7 +156,7 @@
             num_scalar_prefetch=1, grid=(), in_specs=[VMEM], out_specs=[VMEM] * n
         ),
         out_shape=[jax.ShapeDtypeStruct((row_count * steps, width), jnp.bfloat16)] * n,
-        compiler_params=pltpu.CompilerParams(vmem_limit_bytes=VMEM_LIMIT),
+        compiler_params=pltpu.CompilerParams(vmem_limit_bytes=4 * MIB),
         cost_estimate=cost(0),
         name="token_pieces",
     )(place, tokens)
@@ -272,7 +270,7 @@
         ),
         out_shape=out_shape,
         input_output_aliases=aliases,
-        compiler_params=pltpu.CompilerParams(vmem_limit_bytes=VMEM_LIMIT),
+        compiler_params=pltpu.CompilerParams(vmem_limit_bytes=12 * MIB),
         cost_estimate=cost(0),
         name="adam_project" if projects else "adam_update",
     )(place, *operands)
@@ -282,13 +280,13 @@
 SLOT = 32
 
 
-def cache_kernel(heads, lens, q, k, v, stacked, acc, stats):
+def cache_kernel(heads, first, lens, q, k, v, stacked, acc, stats):
     step = pl.program_id(0)
     rows = q.shape[0]
     span = k.shape[1]
     used = PER_GROUP * STEPS
     for i in range(rows):
-        length = lens[step * rows + i]
+        length = lens[first + step * rows + i]
         query = q[i].astype(jnp.float32)
         scores = []
         for h in range(heads):
@@ -323,15 +321,15 @@
             stats[h, i] = stat[at]
 
 
-def cache_attention(queries, cache_keys, cache_values, lengths):
-    row_count, span, kv_cols = cache_keys.shape
+def cache_attention(queries, cache_keys, cache_values, lengths, first, row_count):
+    _, span, kv_cols = cache_keys.shape
     heads = kv_cols // HD
-    rows = 2 if row_count % 2 == 0 else 1
+    rows = 2 if row_count % 2 == 0 and first % 2 == 0 else 1
     shape = (heads, row_count, SLOT, HD)
     out_block = pl.BlockSpec((heads, rows, SLOT, HD), lambda r, lens: (0, r, 0, 0))
-    in_block = lambda a: pl.BlockSpec((rows, *a.shape[1:]), lambda r, lens: (r, 0, 0))
+    in_block = lambda a: pl.BlockSpec((rows, *a.shape[1:]), lambda r, lens: (first // rows + r, 0, 0))
     return pl.pallas_call(
-        functools.partial(cache_kernel, heads),
+        functools.partial(cache_kernel, heads, first),
         grid_spec=pltpu.PrefetchScalarGridSpec(
             num_scalar_prefetch=1,
             grid=(row_count // rows,),
@@ -343,23 +341,23 @@
             jax.ShapeDtypeStruct(shape, jnp.float32),
             jax.ShapeDtypeStruct(shape, jnp.float32),
         ],
-        compiler_params=pltpu.CompilerParams(vmem_limit_bytes=VMEM_LIMIT),
-        cost_estimate=cost(0),
+        compiler_params=pltpu.CompilerParams(vmem_limit_bytes=10 * MIB),
+        cost_estimate=cost(7),
         name="cache_attention",
     )(lengths, in_hbm(queries), in_hbm(cache_keys), in_hbm(cache_values))
 
 
-def merge_kernel(n_folds, row_count, *refs):
-    folds, refs = refs[: 2 * n_folds], refs[2 * n_folds :]
-    cosine, sine, stacked, acc, stats, new_kv, context = refs
-    every = jnp.concatenate(
-        [folds[2 * f][...].astype(jnp.float32) + folds[2 * f + 1][...] for f in range(n_folds)], axis=1
-    )
-    heads = stacked.shape[0]
+def merge_kernel(n_parts, *refs):
+    arrived, kept, cosine, sine = refs[:4]
+    stacked, acc, stats = (refs[4 + i : 4 + 3 * n_parts : 3] for i in range(3))
+    new_kv, context = refs[-2:]
+    row_count = new_kv.shape[0]
+    every = arrived[...].astype(jnp.float32) + kept[...]
     at = lax.broadcasted_iota(jnp.int32, (row_count * SLOT, row_count * STEPS), 0)
     to = lax.broadcasted_iota(jnp.int32, (row_count * SLOT, row_count * STEPS), 1)
     seen = (at // SLOT == to // STEPS) & (at % STEPS >= to % STEPS)
-    for u in range(heads):
+    rows_of = lambda parts, u: jnp.concatenate([p[u].reshape(-1, HD) for p in parts], axis=0)
+    for u in range(stacked[0].shape[0]):
         total = every[:, u * HEAD_COLS : (u + 1) * HEAD_COLS]
         keys = total[:, :HD]
         keys = keys * cosine[...] + pltpu.roll(keys, HD // 2, 1) * sine[...]
@@ -370,13 +368,14 @@
             new_kv[r, :, u * HEAD_COLS : (u + 1) * HEAD_COLS] = both[
                 r * STEPS : (r + 1) * STEPS
             ].astype(jnp.bfloat16)
-        query = stacked[u].reshape(row_count * SLOT, HD)
         scores = (
-            lax.dot_general(query, keys, (((1,), (1,)), ((), ())), preferred_element_type=jnp.float32)
+            lax.dot_general(
+                rows_of(stacked, u), keys, (((1,), (1,)), ((), ())), preferred_element_type=jnp.float32
+            )
             * score_scale
         )
         scores = jnp.where(seen, scores, masked_score)
-        stat = stats[u].reshape(row_count * SLOT, HD)
+        stat = rows_of(stats, u)
         old_highest = stat[:, :1]
         old_total = stat[:, HD // 2 : HD // 2 + 1]
         highest = jnp.maximum(jnp.max(scores, axis=-1, keepdims=True), old_highest)
@@ -384,7 +383,7 @@
         scale = jnp.exp(old_highest - highest)
         denominator = jnp.sum(weight, axis=-1, keepdims=True) + scale * old_total
         out = jnp.dot(weight.astype(jnp.bfloat16), values, preferred_element_type=jnp.float32)
-        out = (out + scale * acc[u].reshape(row_count * SLOT, HD)) / denominator
+        out = (out + scale * rows_of(acc, u)) / denominator
         for r in range(row_count):
             for g in range(PER_GROUP):
                 at_row = r * SLOT + g * STEPS
@@ -392,16 +391,28 @@
                 context[r, :, at_col : at_col + HD] = out[at_row : at_row + STEPS].astype(jnp.bfloat16)
 
 
-def merge(folds, cosine, sine, attended):
-    heads, row_count = attended[0].shape[:2]
-    operands = [a for fold in folds for a in fold] + [cosine, sine, *attended]
+def merge(arrived, kept, cosine, sine, attended, row_count, first, n_units, previous):
+    heads = attended[0][0].shape[0]
+    block = first // n_units
+    operands = [arrived, kept, cosine, sine]
+    in_specs = [whole(a) for a in operands]
+    for part in attended:
+        operands += part
+        in_specs += [pl.BlockSpec((n_units, *p.shape[1:]), lambda i: (block, 0, 0, 0)) for p in part]
+    aliases = {}
+    if previous is not None:
+        aliases = {len(operands) + i: i for i in range(2)}
+        operands += previous
+        in_specs += [ANYWHERE] * 2
     widths = (HEAD_COLS, PER_GROUP * HD)
     return pl.pallas_call(
-        functools.partial(merge_kernel, len(folds), row_count),
-        in_specs=[VMEM] * len(operands),
-        out_specs=[VMEM] * 2,
+        functools.partial(merge_kernel, len(attended)),
+        grid=(1,),
+        in_specs=in_specs,
+        out_specs=[pl.BlockSpec((row_count, STEPS, n_units * w), lambda i: (0, 0, block)) for w in widths],
         out_shape=[jax.ShapeDtypeStruct((row_count, STEPS, heads * w), jnp.bfloat16) for w in widths],
-        compiler_params=pltpu.CompilerParams(vmem_limit_bytes=VMEM_LIMIT),
+        input_output_aliases=aliases,
+        compiler_params=pltpu.CompilerParams(vmem_limit_bytes=8 * MIB),
         cost_estimate=cost(0),
         name="merge_new",
     )(*operands)
@@ -410,6 +421,13 @@
 def swap(array, axis, bit):
     size = lax.axis_size(axis)
     return lax.ppermute(array, axis, [(i, i ^ bit) for i in range(size)])
+
+
+def reversed_bits(n):
+    order = [0]
+    while len(order) < n:
+        order = [2 * i for i in order] + [2 * i + 1 for i in order]
+    return order
 
 
 def fold_rows(arrived, kept, n):
@@ -441,38 +459,42 @@
     folds = [range(cut), range(cut, len(crossings))]
     folds = [f for f in folds if len(f)]
 
-    pieces = [1] + [4] * (len(crossings) - 1)
-    cast = cast_units(
-        place, local, [(part, units, p if part else 1) for units, p in zip(crossings, pieces) for part in (1, 0)]
-    )
-    mine, crossed = [], []
-    for away, home in zip(cast[::2], cast[1::2]):
-        (one,) = sum_pieces(home, [swap(a, "group", 1) for a in away], 1)
+    pieces = [1] + [N_PIECES] * (len(crossings) - 1)
+    mine, crossed, toks = [], [], None
+    distance = 1
+    for units, p in zip(crossings, pieces):
+        away, home = cast_units(after(local, *mine), n_units, [(1, units, p), (0, units, 1)])
+        got = [swap(a, "group", 1) for a in away]
+        if toks is None:
+            toks = token_pieces(place, after(tokens, *away), fsdp_count, rows)
+            home = [after(home[0], *toks)]
+        (one,) = sum_pieces(home, got, 1)
         mine.append(one)
         crossed.append(swap(one, "group", 2))
-
-    toks = token_pieces(place, after(tokens, *mine), fsdp_count, rows)
+        if distance == 1:
+            toks = [swap(t, "fsdp", distance) if d & distance else t for d, t in enumerate(toks)]
+            distance *= 2
     cosine, sine = rotation_tables(lengths)
-    attended = cache_attention(after(queries, *mine), cache_keys, cache_values, lengths)
-    distance = 1
+    attended = [
+        cache_attention(after(queries, *mine, *toks), cache_keys, cache_values, lengths, 0, row_count)
+    ]
     while distance < fsdp_count:
         toks = [swap(t, "fsdp", distance) if d & distance else t for d, t in enumerate(toks)]
-        if distance == 1:
-            toks = list(lax.optimization_barrier((*toks, attended[1])))[:-1]
         distance *= 2
+    toks = [toks[d] for d in reversed_bits(fsdp_count)]
 
     state = (weights, moment1, moment2)
     last = crossings[-1]
 
     totals, sums = [], []
     updated = None
-    step = (attended[1],)
+    step = (attended[0][1], *toks)
     for c, units in enumerate(crossings):
         one, other = [mine[c]], after(crossed[c], *step)
         bit = 2
         while True:
             bit *= 2
-            one = sum_pieces(one, [other], 4 if bit >= group_count else 1)
+            one = sum_pieces(one, [other], N_PIECES if bit >= group_count else 1)
             if bit >= group_count:
                 break
             other = swap(one[0], "group", bit)
@@ -486,14 +508,17 @@
         sent = jnp.concatenate([sums[c][0] for c in members], axis=1)
         kept = jnp.concatenate([sums[c][1] for c in members], axis=1)
         moving.append((swap(sent, "tp", 1), kept))
-    distance = fsdp_count // 2
-    while distance:
+    distance = 1
+    while distance < fsdp_count:
         for f, (got, kept) in enumerate(moving):
             sent, kept = fold_rows(got, kept, fsdp_count)
             moving[f] = (swap(sent, "fsdp", distance), kept)
-        distance //= 2
-
-    outs = merge(moving, cosine, sine, attended)
+        distance *= 2
+
+    outs = None
+    for members, (got, kept) in zip(folds, moving):
+        units = [u for c in members for u in crossings[c]]
+        outs = merge(got, kept, cosine, sine, attended, row_count, units[0], len(units), outs)
     return (*updated, *outs)
 
 

time: 66.5 us -> 62.7 us (0.943)
  waiting for transfers between devices: 17.1 us -> 7.56 us
  starting transfers between devices: 20.3 us -> 24.6 us
  Pallas kernels: 27.5 us -> 28.8 us
    ppermute x25 -> x19, waiting for transfers between devices: 17.1 us -> 7.56 us  [swap(): return lax.ppermute(array, axis, [(i, i ^ bit) for i in range(size)])]
    ppermute x25 -> x19, starting transfers between devices: 20.3 us -> 24.6 us  [swap(): return lax.ppermute(array, axis, [(i, i ^ bit) for i in range(size)])]
    pallas_call x3 -> x5, Pallas kernels: 12 us -> 13.4 us  [the longest x1 6.71 us: cache_attention(): pl.pallas_call(functools.partial(cache_kernel, heads, first), grid_spec=p...]
  transfers between devices with their start and end apart: 25 -> 19, of which waited for: 17 -> 9; matrix products, arithmetic and copies ran while one was open for 1% -> 1% of each run, Pallas kernels for 33% -> 40%
where the time goes in v5:
time: 62.7 us; the launch traced here: 62.5 us
  Pallas kernels  28.8 us (46%)
  starting transfers between devices  24.6 us (39%)
  waiting for transfers between devices  7.56 us (12%)
  between operations  0.85 us (1%)
    ppermute x19, starting transfers between devices, swap(): return lax.ppermute(array, axis, [(i, i ^ bit) for i in range(size)])  24.6 us
    pallas_call x2, Pallas kernels, adam_units(): pl.pallas_call(functools.partial(adam_kernel, units, len(mine), len(partn...  14.2 us
    ppermute x19, waiting for transfers between devices, swap(): return lax.ppermute(array, axis, [(i, i ^ bit) for i in range(size)])  7.56 us
    pallas_call x1, Pallas kernels, cache_attention(): pl.pallas_call(functools.partial(cache_kernel, heads, first), grid_spec=p...  6.71 us
    pallas_call x2, Pallas kernels, cast_units(): pl.pallas_call(functools.partial(cast_kernel, wanted, n_units), in_specs=...  3.58 us
    pallas_call x2, Pallas kernels, merge(): pl.pallas_call(functools.partial(merge_kernel, len(attended)), grid=(1,),...  3.12 us
  transfers between devices with their start and end apart: 19, of which 9 were waited for; matrix products, arithmetic and copies ran while one was open for 1% of the time, Pallas kernels for 40%

profile of v5, /device:TPU:0, one launch (start us, length us, event | category | flops | bytes accessed | tf_op | source)
XLA Modules:
  0.0 62.5 jit_solution(6540371318665736406)
XLA Ops:
  0.6 1.8 %cast_units.2 = (bf16[640,512]{1,0:T(8,128)(2,1)S(1)}, bf16[640,512]{1,0:T(8,128)(2,1)S(1)}) custom-call(f32[640,2048]{1,0:T(8,128)} %bitcast.5), custom_call_target="tpu_custom_call" | custom-call | flops 1 | bytes 1 | tf_op jit(solution)/shard_map/cast_units/pallas_call | solution.py:104
  2.5 0.5 collective-permute-start
  3.1 0.6 token_pieces.1
  3.7 1.0 %collective-permute-done.refs_1_ = bf16[640,512]{1,0:T(8,128)(2,1)S(1)} collective-permute-done((bf16[640,512]{1,0:T(8,128)(2,1)S(1)}, bf16[640,512]{1,0:T(8,128)(2,1)S(1)}, u32[]{:S(2)}, u32[]{:S(2)}) %collective-permute-start) | collective-permute-done | bytes 655392 | tf_op jit(solution)/shard_map/ppermute | solution.py:423
  4.9 2.9 %collective-permute-start.4 = (bf16[640,512]{1,0:T(8,128)(2,1)S(1)}, bf16[640,512]{1,0:T(8,128)(2,1)S(1)}, u32[]{:S(2)}, u32[]{:S(2)}) collective-permute-start(bf16[640,512]{1,0:T(8,128)(2,1)S(1)} %sum_pieces.4.refs_0_), channel_id=1, source_target_pairs={{0,16},{8,24},{16,0},{24,8},{1,17},{9,25},{17,1},{25,9},{2,18},{10... | collective-permute-start | bytes 1966088 | tf_op jit(solution)/shard_map/ppermute | solution.py:423
  7.8 1.8 %cast_units.3 = (bf16[320,512]{1,0:T(8,128)(2,1)S(1)}, bf16[320,512]{1,0:T(8,128)(2,1)S(1)}, bf16[640,512]{1,0:T(8,128)(2,1)S(1)}) custom-call(f32[640,2048]{1,0:T(8,128)} %bitcast.6), custom_call_target="tpu_custom_call" | custom-call | flops 1 | bytes 1 | tf_op jit(solution)/shard_map/cast_units/pallas_call | solution.py:104
  10.1 1.1 %collective-permute-done.1.refs_1_ = bf16[320,512]{1,0:T(8,128)(2,1)S(1)} collective-permute-done((bf16[320,512]{1,0:T(8,128)(2,1)S(1)}, bf16[320,512]{1,0:T(8,128)(2,1)S(1)}, u32[]{:S(2)}, u32[]{:S(2)}) %collective-permute-start.1) | collective-permute-done | bytes 327712 | tf_op jit(solution)/shard_map/ppermute | solution.py:423
  12.0 2.1 %collective-permute-start.6 = (bf16[32,640]{1,0:T(8,128)(2,1)S(1)}, bf16[32,640]{1,0:T(8,128)(2,1)S(1)}, u32[]{:S(2)}, u32[]{:S(2)}) collective-permute-start(bf16[32,640]{1,0:T(8,128)(2,1)S(1)} %get-tuple-element.47), channel_id=1, source_target_pairs={{0,2},{2,0},{4,6},{6,4},{1,3},{3,1},{5,7},{7,5},{8,10},{10,8},{12,... | collective-permute-start | bytes 122888 | tf_op jit(solution)/shard_map/ppermute | solution.py:423
  14.1 3.0 %collective-permute-start.7 = (bf16[32,640]{1,0:T(8,128)(2,1)S(1)}, bf16[32,640]{1,0:T(8,128)(2,1)S(1)}, u32[]{:S(2)}, u32[]{:S(2)}) collective-permute-start(bf16[32,640]{1,0:T(8,128)(2,1)S(1)} %get-tuple-element.46), channel_id=1, source_target_pairs={{0,4},{2,6},{4,0},{6,2},{1,5},{3,7},{5,1},{7,3},{8,12},{10,14},{12... | collective-permute-start | bytes 122888 | tf_op jit(solution)/shard_map/ppermute | solution.py:423
  17.1 2.2 %collective-permute-start.8 = (bf16[32,640]{1,0:T(8,128)(2,1)S(1)}, bf16[32,640]{1,0:T(8,128)(2,1)S(1)}, u32[]{:S(2)}, u32[]{:S(2)}) collective-permute-start(bf16[32,640]{1,0:T(8,128)(2,1)S(1)} %collective-permute-done.6), channel_id=1, source_target_pairs={{0,4},{2,6},{4,0},{6,2},{1,5},{3,7},{5,1},{7,3},{8,12},{10,14},{12... | collective-permute-start | bytes 122888 | tf_op jit(solution)/shard_map/ppermute | solution.py:423
  19.3 6.7 %cache_attention.1 = (bf16[4,8,32,128]{3,2,1,0:T(8,128)(2,1)S(1)}, f32[4,8,32,128]{3,2,1,0:T(8,128)S(1)}, f32[4,8,32,128]{3,2,1,0:T(8,128)S(1)}) custom-call(s32[8]{0:T(128)S(1)} %copy-done.1, bf16[8,4,2560]{2,1,0:T(4,128)(2,1)} %q, bf16[8,512,512]{2,1,0:T(8,128)(2,1)} %k.1, bf16[8,512,512]{2,1,0:T(8,128)(2,1)} %v.1), custom_call_target="tpu_custom_call" | custom-call | flops 1 | bytes 17500000 | tf_op jit(solution)/shard_map/cache_attention/pallas_call | solution.py:331
  27.0 1.1 %collective-permute-done.9.refs_2_ = bf16[320,512]{1,0:T(8,128)(2,1)} collective-permute-done((bf16[320,512]{1,0:T(8,128)(2,1)S(1)}, bf16[320,512]{1,0:T(8,128)(2,1)}, u32[]{:S(2)}, u32[]{:S(2)}) %collective-permute-start.9) | collective-permute-done | bytes 327712 | tf_op jit(solution)/shard_map/ppermute | solution.py:423
  28.6 7.7 %adam_project.2 = (f32[640,2048]{1,0:T(8,128)}, f32[640,2048]{1,0:T(8,128)}, f32[640,2048]{1,0:T(8,128)}, bf16[128,512]{1,0:T(8,128)(2,1)S(1)}, f32[128,512]{1,0:T(8,128)S(1)}) custom-call(s32[6]{0:T(128)S(1)} %stack.19.place, bf16[320,512]{1,0:T(8,128)(2,1)S(1)} %get-tuple-element.56.refs_0_, bf16[320,512]{1,0:T(8,128)(2,1)S(1)} %get-tuple-element.57.refs_1_, ...), custom_call_target="tpu_custom_call" | custom-call | flops 1 | bytes 1 | tf_op jit(solution)/shard_map/adam_project/pallas_call | solution.py:257
  36.2 0.7 %collective-permute-done.3.refs_1_ = bf16[640,512]{1,0:T(8,128)(2,1)S(1)} collective-permute-done((bf16[640,512]{1,0:T(8,128)(2,1)S(1)}, bf16[640,512]{1,0:T(8,128)(2,1)S(1)}, u32[]{:S(2)}, u32[]{:S(2)}) %collective-permute-start.3) | collective-permute-done | bytes 655392 | tf_op jit(solution)/shard_map/ppermute | solution.py:423
  37.6 1.8 %collective-permute-start.16 = (bf16[128,512]{1,0:T(8,128)(2,1)S(1)}, bf16[128,512]{1,0:T(8,128)(2,1)S(1)}, u32[]{:S(2)}, u32[]{:S(2)}) collective-permute-start(bf16[128,512]{1,0:T(8,128)(2,1)S(1)} %get-tuple-element.58), channel_id=1, source_target_pairs={{0,1},{1,0},{2,3},{3,2},{4,5},{5,4},{6,7},{7,6},{8,9},{9,8},{10,11... | collective-permute-start | bytes 393224 | tf_op jit(solution)/shard_map/ppermute | solution.py:423
  39.6 6.5 %adam_project.3 = (f32[640,2048]{1,0:T(8,128)}, f32[640,2048]{1,0:T(8,128)}, f32[640,2048]{1,0:T(8,128)}, bf16[128,512]{1,0:T(8,128)(2,1)S(1)}, f32[128,512]{1,0:T(8,128)S(1)}) custom-call(s32[6]{0:T(128)S(1)} %stack.19.place, bf16[320,512]{1,0:T(8,128)(2,1)S(1)} %get-tuple-element.60.refs_0_, ...), custom_call_target="tpu_custom_call", output_to_operand_aliasing={{0}: (12, {}), {1}: (13, {}), {2}: (14, {})} | custom-call | flops 1 | bytes 1 | tf_op jit(solution)/shard_map/adam_project/pallas_call | solution.py:257
  46.1 1.5 %collective-permute-start.13 = (bf16[128,512]{1,0:T(8,128)(2,1)S(1)}, bf16[128,512]{1,0:T(8,128)(2,1)S(1)}, u32[]{:S(2)}, u32[]{:S(2)}) collective-permute-start(bf16[128,512]{1,0:T(8,128)(2,1)S(1)} %get-tuple-element.68), channel_id=1, source_target_pairs={{0,1},{1,0},{2,3},{3,2},{4,5},{5,4},{6,7},{7,6},{8,9},{9,8},{10,11... | collective-permute-start | bytes 393224 | tf_op jit(solution)/shard_map/ppermute | solution.py:423
  47.6 1.6 %collective-permute-start.17 = (bf16[64,512]{1,0:T(8,128)(2,1)S(1)}, bf16[64,512]{1,0:T(8,128)(2,1)S(1)}, u32[]{:S(2)}, u32[]{:S(2)}) collective-permute-start(bf16[64,512]{1,0:T(8,128)(2,1)S(1)} %slice.50), channel_id=1, source_target_pairs={{0,2},{2,0},{4,6},{6,4},{1,3},{3,1},{5,7},{7,5},{8,10},{10,8},{12,... | collective-permute-start | bytes 196616 | tf_op jit(solution)/shard_map/ppermute | solution.py:423
  49.3 2.1 %collective-permute-done.13 = bf16[128,512]{1,0:T(8,128)(2,1)S(1)} collective-permute-done((bf16[128,512]{1,0:T(8,128)(2,1)S(1)}, bf16[128,512]{1,0:T(8,128)(2,1)S(1)}, u32[]{:S(2)}, u32[]{:S(2)}) %collective-permute-start.13) | collective-permute-done | bytes 131104 | tf_op jit(solution)/shard_map/ppermute | solution.py:423
  51.4 1.8 %collective-permute-start.14 = (bf16[64,512]{1,0:T(8,128)(2,1)S(1)}, bf16[64,512]{1,0:T(8,128)(2,1)S(1)}, u32[]{:S(2)}, u32[]{:S(2)}) collective-permute-start(bf16[64,512]{1,0:T(8,128)(2,1)S(1)} %slice.51), channel_id=1, source_target_pairs={{0,2},{2,0},{4,6},{6,4},{1,3},{3,1},{5,7},{7,5},{8,10},{10,8},{12,... | collective-permute-start | bytes 196616 | tf_op jit(solution)/shard_map/ppermute | solution.py:423
  53.3 2.7 %collective-permute-start.18 = (bf16[32,512]{1,0:T(8,128)(2,1)S(1)}, bf16[32,512]{1,0:T(8,128)(2,1)S(1)}, u32[]{:S(2)}, u32[]{:S(2)}) collective-permute-start(bf16[32,512]{1,0:T(8,128)(2,1)S(1)} %slice.52), channel_id=1, source_target_pairs={{0,4},{2,6},{4,0},{6,2},{1,5},{3,7},{5,1},{7,3},{8,12},{10,14},{12... | collective-permute-start | bytes 98312 | tf_op jit(solution)/shard_map/ppermute | solution.py:423
  56.0 2.6 %collective-permute-start.15 = (bf16[32,512]{1,0:T(8,128)(2,1)S(1)}, bf16[32,512]{1,0:T(8,128)(2,1)S(1)}, u32[]{:S(2)}, u32[]{:S(2)}) collective-permute-start(bf16[32,512]{1,0:T(8,128)(2,1)S(1)} %slice.53), channel_id=1, source_target_pairs={{0,4},{2,6},{4,0},{6,2},{1,5},{3,7},{5,1},{7,3},{8,12},{10,14},{12... | collective-permute-start | bytes 98312 | tf_op jit(solution)/shard_map/ppermute | solution.py:423
  59.0 1.6 %merge_new.2 = (bf16[8,4,1024]{2,1,0:T(4,128)(2,1)}, bf16[8,4,2560]{2,1,0:T(4,128)(2,1)}) custom-call(bf16[32,512]{1,0:T(8,128)(2,1)S(1)} %collective-permute-done.18.refs_0_, f32[32,512]{1,0:T(8,128)S(1)} %slice.43.refs_1_, f32[32,128]{1,0:T(8,128)S(1)} %get-tuple-element.80.refs_2_, f32[32,128]{1,0:T(8,128)S(1)} %get-tuple-element.81.refs_3_, ...), custom_call_target="tpu_custom_call" | custom-call | flops 1 | bytes 1 | tf_op jit(solution)/shard_map/merge_new/pallas_call | solution.py:408
  60.9 1.6 %merge_new.3 = (bf16[8,4,1024]{2,1,0:T(4,128)(2,1)}, bf16[8,4,2560]{2,1,0:T(4,128)(2,1)}) custom-call(bf16[32,512]{1,0:T(8,128)(2,1)S(1)} %collective-permute-done.15.refs_0_, f32[32,512]{1,0:T(8,128)S(1)} %slice.39.refs_1_, f32[32,128]{1,0:T(8,128)S(1)} %get-tuple-element.80.refs_2_, ...), custom_call_target="tpu_custom_call", output_to_operand_aliasing={{0}: (7, {}), {1}: (8, {})} | custom-call | flops 1 | bytes 1 | tf_op jit(solution)/shard_map/merge_new/pallas_call | solution.py:408
  (46 shorter events, 4.6 us)
Async XLA Ops:
  0.6 2.5 %copy-start = (bf16[8,4,5120]{2,1,0:T(4,128)(2,1)S(1)}, bf16[8,4,5120]{2,1,0:T(4,128)(2,1)}, u32[]{:S(2)}) copy-start(bf16[8,4,5120]{2,1,0:T(4,128)(2,1)} %source) | copy-start | bytes 983044
  2.5 16.9 %copy-start.1 = (s32[8]{0:T(128)S(1)}, s32[8]{0:T(128)}, u32[]{:S(2)}) copy-start(s32[8]{0:T(128)} %lens.1) | copy-start | bytes 100
  2.5 2.2 %collective-permute-start = (bf16[640,512]{1,0:T(8,128)(2,1)S(1)}, bf16[640,512]{1,0:T(8,128)(2,1)S(1)}, u32[]{:S(2)}, u32[]{:S(2)}) collective-permute-start(bf16[640,512]{1,0:T(8,128)(2,1)S(1)} %get-tuple-element.42), channel_id=1, source_target_pairs={{0,8},{8,0},{16,24},{24,16},{1,9},{9,1},{17,25},{25,17},{2,10},{10... | collective-permute-start | bytes 1966088 | tf_op jit(solution)/shard_map/ppermute | solution.py:423
  4.9 21.2 %collective-permute-start.4 = (bf16[640,512]{1,0:T(8,128)(2,1)S(1)}, bf16[640,512]{1,0:T(8,128)(2,1)S(1)}, u32[]{:S(2)}, u32[]{:S(2)}) collective-permute-start(bf16[640,512]{1,0:T(8,128)(2,1)S(1)} %sum_pieces.4.refs_0_), channel_id=1, source_target_pairs={{0,16},{8,24},{16,0},{24,8},{1,17},{9,25},{17,1},{25,9},{2,18},{10... | collective-permute-start | bytes 1966088 | tf_op jit(solution)/shard_map/ppermute | solution.py:423
  9.6 1.7 %collective-permute-start.1 = (bf16[320,512]{1,0:T(8,128)(2,1)S(1)}, bf16[320,512]{1,0:T(8,128)(2,1)S(1)}, u32[]{:S(2)}, u32[]{:S(2)}) collective-permute-start(bf16[320,512]{1,0:T(8,128)(2,1)S(1)} %get-tuple-element.51), channel_id=1, source_target_pairs={{0,8},{8,0},{16,24},{24,16},{1,9},{9,1},{17,25},{25,17},{2,10},{10... | collective-permute-start | bytes 983048 | tf_op jit(solution)/shard_map/ppermute | solution.py:423
  9.6 2.1 %collective-permute-start.2 = (bf16[320,512]{1,0:T(8,128)(2,1)S(1)}, bf16[320,512]{1,0:T(8,128)(2,1)S(1)}, u32[]{:S(2)}, u32[]{:S(2)}) collective-permute-start(bf16[320,512]{1,0:T(8,128)(2,1)S(1)} %get-tuple-element.52), channel_id=1, source_target_pairs={{0,8},{8,0},{16,24},{24,16},{1,9},{9,1},{17,25},{25,17},{2,10},{10... | collective-permute-start | bytes 983048 | tf_op jit(solution)/shard_map/ppermute | solution.py:423
  11.9 25.0 %collective-permute-start.3 = (bf16[640,512]{1,0:T(8,128)(2,1)S(1)}, bf16[640,512]{1,0:T(8,128)(2,1)S(1)}, u32[]{:S(2)}, u32[]{:S(2)}) collective-permute-start(bf16[640,512]{1,0:T(8,128)(2,1)S(1)} %sum_pieces.5.refs_0_), channel_id=1, source_target_pairs={{0,16},{8,24},{16,0},{24,8},{1,17},{9,25},{17,1},{25,9},{2,18},{10... | collective-permute-start | bytes 1966088 | tf_op jit(solution)/shard_map/ppermute | solution.py:423
  12.0 5.1 %collective-permute-start.6 = (bf16[32,640]{1,0:T(8,128)(2,1)S(1)}, bf16[32,640]{1,0:T(8,128)(2,1)S(1)}, u32[]{:S(2)}, u32[]{:S(2)}) collective-permute-start(bf16[32,640]{1,0:T(8,128)(2,1)S(1)} %get-tuple-element.47), channel_id=1, source_target_pairs={{0,2},{2,0},{4,6},{6,4},{1,3},{3,1},{5,7},{7,5},{8,10},{10,8},{12,... | collective-permute-start | bytes 122888 | tf_op jit(solution)/shard_map/ppermute | solution.py:423
  14.1 5.3 %collective-permute-start.5 = (bf16[32,640]{1,0:T(8,128)(2,1)S(1)}, bf16[32,640]{1,0:T(8,128)(2,1)S(1)}, u32[]{:S(2)}, u32[]{:S(2)}) collective-permute-start(bf16[32,640]{1,0:T(8,128)(2,1)S(1)} %get-tuple-element.45), channel_id=1, source_target_pairs={{0,2},{2,0},{4,6},{6,4},{1,3},{3,1},{5,7},{7,5},{8,10},{10,8},{12,... | collective-permute-start | bytes 122888 | tf_op jit(solution)/shard_map/ppermute | solution.py:423
  14.1 12.0 %collective-permute-start.7 = (bf16[32,640]{1,0:T(8,128)(2,1)S(1)}, bf16[32,640]{1,0:T(8,128)(2,1)S(1)}, u32[]{:S(2)}, u32[]{:S(2)}) collective-permute-start(bf16[32,640]{1,0:T(8,128)(2,1)S(1)} %get-tuple-element.46), channel_id=1, source_target_pairs={{0,4},{2,6},{4,0},{6,2},{1,5},{3,7},{5,1},{7,3},{8,12},{10,14},{12... | collective-permute-start | bytes 122888 | tf_op jit(solution)/shard_map/ppermute | solution.py:423
  17.1 9.0 %collective-permute-start.8 = (bf16[32,640]{1,0:T(8,128)(2,1)S(1)}, bf16[32,640]{1,0:T(8,128)(2,1)S(1)}, u32[]{:S(2)}, u32[]{:S(2)}) collective-permute-start(bf16[32,640]{1,0:T(8,128)(2,1)S(1)} %collective-permute-done.6), channel_id=1, source_target_pairs={{0,4},{2,6},{4,0},{6,2},{1,5},{3,7},{5,1},{7,3},{8,12},{10,14},{12... | collective-permute-start | bytes 122888 | tf_op jit(solution)/shard_map/ppermute | solution.py:423
  26.3 1.8 %collective-permute-start.9 = (bf16[320,512]{1,0:T(8,128)(2,1)S(1)}, bf16[320,512]{1,0:T(8,128)(2,1)}, u32[]{:S(2)}, u32[]{:S(2)}) collective-permute-start(bf16[320,512]{1,0:T(8,128)(2,1)S(1)} %get-tuple-element.56.refs_0_), channel_id=1, source_target_pairs={{0,8},{8,0},{16,24},{24,16},{1,9},{9,1},{17,25},{25,17},{2,10},{10... | collective-permute-start | bytes 983048 | tf_op jit(solution)/shard_map/ppermute | solution.py:423
  26.3 2.2 %collective-permute-start.10 = (bf16[320,512]{1,0:T(8,128)(2,1)S(1)}, bf16[320,512]{1,0:T(8,128)(2,1)}, u32[]{:S(2)}, u32[]{:S(2)}) collective-permute-start(bf16[320,512]{1,0:T(8,128)(2,1)S(1)} %get-tuple-element.57.refs_1_), channel_id=1, source_target_pairs={{0,8},{8,0},{16,24},{24,16},{1,9},{9,1},{17,25},{25,17},{2,10},{10... | collective-permute-start | bytes 983048 | tf_op jit(solution)/shard_map/ppermute | solution.py:423
  37.0 2.5 %collective-permute-start.11 = (bf16[320,512]{1,0:T(8,128)(2,1)S(1)}, bf16[320,512]{1,0:T(8,128)(2,1)S(1)}, u32[]{:S(2)}, u32[]{:S(2)}) collective-permute-start(bf16[320,512]{1,0:T(8,128)(2,1)S(1)} %get-tuple-element.60.refs_0_), channel_id=1, source_target_pairs={{0,8},{8,0},{16,24},{24,16},{1,9},{9,1},{17,25},{25,17},{2,10},{10... | collective-permute-start | bytes 983048 | tf_op jit(solution)/shard_map/ppermute | solution.py:423
  37.1 2.4 %collective-permute-start.12 = (bf16[320,512]{1,0:T(8,128)(2,1)S(1)}, bf16[320,512]{1,0:T(8,128)(2,1)S(1)}, u32[]{:S(2)}, u32[]{:S(2)}) collective-permute-start(bf16[320,512]{1,0:T(8,128)(2,1)S(1)} %get-tuple-element.61.refs_1_), channel_id=1, source_target_pairs={{0,8},{8,0},{16,24},{24,16},{1,9},{9,1},{17,25},{25,17},{2,10},{10... | collective-permute-start | bytes 983048 | tf_op jit(solution)/shard_map/ppermute | solution.py:423
  37.6 10.0 %collective-permute-start.16 = (bf16[128,512]{1,0:T(8,128)(2,1)S(1)}, bf16[128,512]{1,0:T(8,128)(2,1)S(1)}, u32[]{:S(2)}, u32[]{:S(2)}) collective-permute-start(bf16[128,512]{1,0:T(8,128)(2,1)S(1)} %get-tuple-element.58), channel_id=1, source_target_pairs={{0,1},{1,0},{2,3},{3,2},{4,5},{5,4},{6,7},{7,6},{8,9},{9,8},{10,11... | collective-permute-start | bytes 393224 | tf_op jit(solution)/shard_map/ppermute | solution.py:423
  46.1 5.3 %collective-permute-start.13 = (bf16[128,512]{1,0:T(8,128)(2,1)S(1)}, bf16[128,512]{1,0:T(8,128)(2,1)S(1)}, u32[]{:S(2)}, u32[]{:S(2)}) collective-permute-start(bf16[128,512]{1,0:T(8,128)(2,1)S(1)} %get-tuple-element.68), channel_id=1, source_target_pairs={{0,1},{1,0},{2,3},{3,2},{4,5},{5,4},{6,7},{7,6},{8,9},{9,8},{10,11... | collective-permute-start | bytes 393224 | tf_op jit(solution)/shard_map/ppermute | solution.py:423
  47.6 5.7 %collective-permute-start.17 = (bf16[64,512]{1,0:T(8,128)(2,1)S(1)}, bf16[64,512]{1,0:T(8,128)(2,1)S(1)}, u32[]{:S(2)}, u32[]{:S(2)}) collective-permute-start(bf16[64,512]{1,0:T(8,128)(2,1)S(1)} %slice.50), channel_id=1, source_target_pairs={{0,2},{2,0},{4,6},{6,4},{1,3},{3,1},{5,7},{7,5},{8,10},{10,8},{12,... | collective-permute-start | bytes 196616 | tf_op jit(solution)/shard_map/ppermute | solution.py:423
  51.4 4.5 %collective-permute-start.14 = (bf16[64,512]{1,0:T(8,128)(2,1)S(1)}, bf16[64,512]{1,0:T(8,128)(2,1)S(1)}, u32[]{:S(2)}, u32[]{:S(2)}) collective-permute-start(bf16[64,512]{1,0:T(8,128)(2,1)S(1)} %slice.51), channel_id=1, source_target_pairs={{0,2},{2,0},{4,6},{6,4},{1,3},{3,1},{5,7},{7,5},{8,10},{10,8},{12,... | collective-permute-start | bytes 196616 | tf_op jit(solution)/shard_map/ppermute | solution.py:423
  53.3 5.7 %collective-permute-start.18 = (bf16[32,512]{1,0:T(8,128)(2,1)S(1)}, bf16[32,512]{1,0:T(8,128)(2,1)S(1)}, u32[]{:S(2)}, u32[]{:S(2)}) collective-permute-start(bf16[32,512]{1,0:T(8,128)(2,1)S(1)} %slice.52), channel_id=1, source_target_pairs={{0,4},{2,6},{4,0},{6,2},{1,5},{3,7},{5,1},{7,3},{8,12},{10,14},{12... | collective-permute-start | bytes 98312 | tf_op jit(solution)/shard_map/ppermute | solution.py:423
  56.0 4.9 %collective-permute-start.15 = (bf16[32,512]{1,0:T(8,128)(2,1)S(1)}, bf16[32,512]{1,0:T(8,128)(2,1)S(1)}, u32[]{:S(2)}, u32[]{:S(2)}) collective-permute-start(bf16[32,512]{1,0:T(8,128)(2,1)S(1)} %slice.53), channel_id=1, source_target_pairs={{0,4},{2,6},{4,0},{6,2},{1,5},{3,7},{5,1},{7,3},{8,12},{10,14},{12... | collective-permute-start | bytes 98312 | tf_op jit(solution)/shard_map/ppermute | solution.py:423

commit v6 on v5

--- a/solution.py
+++ b/solution.py
@@ -25,6 +25,7 @@
 correct_two = 1.0 - 0.95**10
 masked_score = -1e30
 score_scale = 1.0 / math.sqrt(HD)
+
 N_PIECES = 2
 MIB = 1024 * 1024
 
@@ -72,67 +73,85 @@
 ANYWHERE = pl.BlockSpec(memory_space=pl.ANY)
 
 
-def block_columns(place, part, unit):
+def columns_at(place, part, first, n):
     half = place[0] if part == 0 else 1 - place[0]
-    return pl.ds(pl.multiple_of((half * place[2] + unit) * HEAD_COLS, HEAD_COLS), HEAD_COLS)
+    return pl.ds(pl.multiple_of((half * place[2] + first) * HD, HD), n * HD)
+
+
+def slab_ends(rows):
+    if rows % HD:
+        return [(0, rows)]
+    return [(r, min(r + 2 * HD, rows)) for r in range(0, rows, 2 * HD)]
 
 
 def cast_kernel(wanted, n_units, source, *refs):
+    outs, buffers, sems = refs[: -len(wanted) - 1], refs[-len(wanted) - 1 : -1], refs[-1]
     place = (lax.axis_index("group") % 2, None, n_units)
-    outs, (buffer, sems) = refs[:-2], refs[-2:]
-    blocks = [(o, k, part, unit) for o, (part, units, _) in enumerate(wanted) for k, unit in enumerate(units)]
+    ends = slab_ends(source.shape[0])
     copies = [
-        pltpu.make_async_copy(source.at[:, block_columns(place, part, unit)], buffer.at[i], sems.at[i])
-        for i, (_, _, part, unit) in enumerate(blocks)
+        [
+            pltpu.make_async_copy(
+                source.at[r:e, columns_at(place, part, first, n)], buffers[w].at[r:e], sems.at[w, i]
+            )
+            for i, (r, e) in enumerate(ends)
+        ]
+        for w, (part, first, n, _) in enumerate(wanted)
     ]
-    for copy in copies:
+    for copy in sum(copies, []):
         copy.start()
-    first = [sum(w[2] for w in wanted[:o]) for o in range(len(wanted))]
-    for i, (o, k, _, _) in enumerate(blocks):
-        copies[i].wait()
-        n_pieces = wanted[o][2]
-        rows = buffer.shape[1] // n_pieces
-        for p in range(n_pieces):
-            piece = buffer[i, p * rows : (p + 1) * rows].astype(jnp.bfloat16)
-            outs[first[o] + p][:, k * HEAD_COLS : (k + 1) * HEAD_COLS] = piece
+    at = 0
+    for w, (_, _, _, n_pieces) in enumerate(wanted):
+        if n_pieces == 1:
+            for copy, (r, e) in zip(copies[w], ends):
+                copy.wait()
+                outs[at][r:e] = buffers[w][r:e].astype(jnp.bfloat16)
+        else:
+            for copy in copies[w]:
+                copy.wait()
+            step = buffers[w].shape[0] // n_pieces
+            for p in range(n_pieces):
+                outs[at + p][...] = buffers[w][p * step : (p + 1) * step].astype(jnp.bfloat16)
+        at += n_pieces
 
 
 def cast_units(local, n_units, wanted):
     rows = local.shape[0]
-    n = sum(len(units) for _, units, _ in wanted)
-    shapes = [(rows // p, len(units) * HEAD_COLS) for _, units, p in wanted for _ in range(p)]
+    shapes = [(rows // p, n * HD) for _, _, n, p in wanted for _ in range(p)]
     out = pl.pallas_call(
         functools.partial(cast_kernel, wanted, n_units),
         in_specs=[ANYWHERE],
         out_specs=[VMEM] * len(shapes),
-        scratch_shapes=[pltpu.VMEM((n, rows, HEAD_COLS), jnp.float32), pltpu.SemaphoreType.DMA((n,))],
+        scratch_shapes=[pltpu.VMEM((rows, n * HD), jnp.float32) for _, _, n, _ in wanted]
+        + [pltpu.SemaphoreType.DMA((len(wanted), len(slab_ends(rows))))],
         out_shape=[jax.ShapeDtypeStruct(shape, jnp.bfloat16) for shape in shapes],
         compiler_params=pltpu.CompilerParams(vmem_limit_bytes=6 * MIB),
         cost_estimate=cost(0),
         name="cast_units",
     )(in_hbm(local))
     results = []
-    for _, _, p in wanted:
+    for _, _, _, p in wanted:
         results.append(out[:p])
         out = out[p:]
     return results
 
 
-def sum_kernel(n_a, n_b, *refs):
+def sum_kernel(axis, cuts, n_a, n_b, *refs):
     a, b, outs = refs[:n_a], refs[n_a : n_a + n_b], refs[n_a + n_b :]
-    total = join(a).astype(jnp.float32) + join(b).astype(jnp.float32)
-    step = total.shape[0] // len(outs)
-    for p, out in enumerate(outs):
-        out[...] = total[p * step : (p + 1) * step].astype(out.dtype)
-
-
-def sum_pieces(a, b, n_pieces):
-    rows = sum(x.shape[0] for x in a)
+    total = join(a, axis).astype(jnp.float32) + join(b, axis).astype(jnp.float32)
+    at = 0
+    for out, n in zip(outs, cuts):
+        piece = total[at : at + n] if axis else total[:, at : at + n]
+        out[...] = piece.astype(out.dtype)
+        at += n
+
+
+def sum_pieces(a, b, axis, cuts):
+    joined = sum(x.shape[axis] for x in a)
     return pl.pallas_call(
-        functools.partial(sum_kernel, len(a), len(b)),
+        functools.partial(sum_kernel, axis, cuts, len(a), len(b)),
         in_specs=[VMEM] * (len(a) + len(b)),
-        out_specs=[VMEM] * n_pieces,
-        out_shape=[jax.ShapeDtypeStruct((rows // n_pieces, a[0].shape[1]), jnp.bfloat16)] * n_pieces,
+        out_specs=[VMEM] * len(cuts),
+        out_shape=[jax.ShapeDtypeStruct((n, joined) if axis else (joined, n), jnp.bfloat16) for n in cuts],
         compiler_params=pltpu.CompilerParams(vmem_limit_bytes=6 * MIB),
         cost_estimate=cost(0),
         name="sum_pieces",
@@ -162,119 +181,113 @@
     )(place, tokens)
 
 
-def join(halves):
-    return jnp.concatenate([h[...] for h in halves], axis=0)
-
-
-def adam_kernel(units, n_mine, n_partner, n_tok, held, projects, updates, place, *refs):
+def stack_kernel(takes, *refs):
+    refs[-1][...] = jnp.concatenate([r[at * n : (at + 1) * n] for r, (at, n) in zip(refs[:-1], takes)], axis=0)
+
+
+def stack_blocks(blocks, rows):
+    arrays = [a for a, _ in blocks]
+    return pl.pallas_call(
+        functools.partial(stack_kernel, [(at, rows) for _, at in blocks]),
+        in_specs=[VMEM] * len(arrays),
+        out_specs=VMEM,
+        out_shape=jax.ShapeDtypeStruct((rows * len(arrays), arrays[0].shape[1]), arrays[0].dtype),
+        compiler_params=pltpu.CompilerParams(vmem_limit_bytes=4 * MIB),
+        cost_estimate=cost(0),
+        name="stack_blocks",
+    )(*arrays)
+
+
+def join(pieces, axis=0):
+    return jnp.concatenate([p[...] for p in pieces], axis=axis)
+
+
+def adam_kernel(first, n, n_mine, n_partner, tok_places, previous, place, *refs):
     refs = list(refs)
     take = lambda n: [refs.pop(0) for _ in range(n)]
-    mine = take(n_mine)
-    partner = take(n_partner)
-    state = take(1 if held else 3)
-    toks = take(n_tok)
-    if updates:
-        take(0 if updates == 1 else 3)
-        updated = take(3)
-    sums = take(2) if projects else None
-    in_sems = None if held else take(1)[0]
-    out_sems = take(1)[0] if updates else None
-    buffer = refs.pop(0) if refs else None
-
-    n = len(units)
-    columns = [block_columns(place, i // n, units[i % n]) for i in range(2 * n)]
+    pieces = take(n_mine + n_partner)
+    state = take(3)
+    toks = take(len(tok_places))
+    take(3 * previous)
+    updated = take(3)
+    sent, kept, in_sems, out_sems, buffer = refs
+
+    slabs = [(part, slice(*ends)) for part in range(2) for ends in slab_ends(buffer.shape[2])]
+    columns = [columns_at(place, part, first, n) for part in range(2)]
     incoming = []
-    if not held:
-        for i in range(2 * n):
-            incoming.append(
-                [
-                    pltpu.make_async_copy(state[q].at[:, columns[i]], buffer.at[q, i], in_sems.at[q, i])
-                    for q in range(3)
-                ]
+    for i, (part, at) in enumerate(slabs):
+        incoming.append(
+            [
+                pltpu.make_async_copy(
+                    state[q].at[at, columns[part]], buffer.at[q, part, at], in_sems.at[q, i]
+                )
+                for q in range(3)
+            ]
+        )
+        for copy in incoming[i]:
+            copy.start()
+    block = sent.shape[0] // len(toks)
+    tok = jnp.concatenate([t[k * block : (k + 1) * block] for t, k in zip(toks, tok_places)], axis=0)
+    totals = [join(pieces[:n_mine]), join(pieces[n_mine:])]
+    outgoing, products = [], [None, None]
+    for i, (part, at) in enumerate(slabs):
+        for copy in incoming[i]:
+            copy.wait()
+        gradient = totals[part][at].astype(jnp.float32)
+        results = adam_update(buffer[0, part, at], buffer[1, part, at], buffer[2, part, at], gradient)
+        for q in range(3):
+            buffer[q, part, at] = results[q]
+            outgoing.append(
+                pltpu.make_async_copy(
+                    buffer.at[q, part, at], updated[q].at[at, columns[part]], out_sems.at[q, i]
+                )
             )
-            for copy in incoming[i]:
-                copy.start()
-    if projects:
-        tok = join(toks)
-    source = state[0] if held else buffer
-    totals = [join(mine), join(partner)]
-    outgoing, products = [], []
-    for i in range(2 * n):
-        for copy in incoming[i] if incoming else ():
-            copy.wait()
-        at = slice((i % n) * HEAD_COLS, (i % n + 1) * HEAD_COLS)
-        gradient = totals[i // n][:, at].astype(jnp.float32)
-        results = adam_update(source[0, i], source[1, i], source[2, i], gradient)
-        if updates:
-            for q in range(3):
-                buffer[q, i] = results[q]
-                outgoing.append(
-                    pltpu.make_async_copy(buffer.at[q, i], updated[q].at[:, columns[i]], out_sems.at[q, i])
-                )
-                outgoing[-1].start()
-        if projects:
-            products.append(
-                jnp.dot(tok, results[0].astype(jnp.bfloat16), preferred_element_type=jnp.float32)
-            )
-    if projects:
-        sent, kept = sums
-        stays = place[0] == place[1]
-        for k in range(n):
-            at = slice(k * HEAD_COLS, (k + 1) * HEAD_COLS)
-            kept[:, at] = jnp.where(stays, products[k], products[n + k])
-            sent[:, at] = jnp.where(stays, products[n + k], products[k]).astype(jnp.bfloat16)
+            outgoing[-1].start()
+        terms = jnp.dot(tok[:, at], results[0].astype(jnp.bfloat16), preferred_element_type=jnp.float32)
+        products[part] = terms if products[part] is None else products[part] + terms
+    stays = place[0] == place[1]
+    kept[...] = jnp.where(stays, products[0], products[1])
+    sent[...] = jnp.where(stays, products[1], products[0]).astype(jnp.bfloat16)
     for copy in outgoing:
         copy.wait()
 
 
-def adam_units(place, total, state, toks, units, width, projects=True, updates=True, previous=None):
+def adam_units(place, total, state, toks, first, n, previous):
     mine, partner = total
-    held = not isinstance(state, tuple)
-    n = 2 * len(units)
-    rows = sum(m.shape[0] for m in mine)
-    toks = toks if projects else []
-    operands = [*mine, *partner]
-    in_specs = [VMEM] * len(operands)
-    operands += [state] if held else [in_hbm(a) for a in state]
-    in_specs += [VMEM] if held else [ANYWHERE] * 3
-    operands += toks
-    in_specs += [VMEM] * len(toks)
-    out_specs, out_shape, scratch, aliases = [], [], [], {}
-    if updates:
-        if previous is not None:
-            aliases = {1 + len(operands) + i: i for i in range(3)}
-            operands += previous
-            in_specs += [ANYWHERE] * 3
-        out_specs += [ANYWHERE] * 3
-        out_shape += [jax.ShapeDtypeStruct((rows, width), jnp.float32)] * 3
-    if projects:
-        shape = (sum(t.shape[0] for t in toks), len(units) * HEAD_COLS)
-        out_specs += [VMEM] * 2
-        out_shape += [jax.ShapeDtypeStruct(shape, jnp.bfloat16), jax.ShapeDtypeStruct(shape, jnp.float32)]
-    scratch += [pltpu.SemaphoreType.DMA((3, n))] * (int(not held) + int(updates))
-    if updates or not held:
-        scratch.append(pltpu.VMEM((3, n, rows, HEAD_COLS), jnp.float32))
+    rows, width = state[0].shape
+    n_slabs = 2 * len(slab_ends(rows))
+    n_tokens = min(t.shape[0] for t, _ in toks) * len(toks)
+    operands = [*mine, *partner, *[in_hbm(a) for a in state], *[t for t, _ in toks]]
+    in_specs = [VMEM] * (len(mine) + len(partner)) + [ANYWHERE] * 3 + [VMEM] * len(toks)
+    aliases = {}
+    if previous is not None:
+        aliases = {1 + len(operands) + i: i for i in range(3)}
+        operands += previous
+        in_specs += [ANYWHERE] * 3
+    shape = (n_tokens, n * HD)
     out = pl.pallas_call(
         functools.partial(
-            adam_kernel,
-            units,
-            len(mine),
-            len(partner),
-            len(toks),
-            held,
-            projects,
-            0 if not updates else 1 if previous is None else 2,
+            adam_kernel, first, n, len(mine), len(partner), [at for _, at in toks], previous is not None
         ),
         grid_spec=pltpu.PrefetchScalarGridSpec(
-            num_scalar_prefetch=1, grid=(), in_specs=in_specs, out_specs=out_specs, scratch_shapes=scratch
+            num_scalar_prefetch=1,
+            grid=(),
+            in_specs=in_specs,
+            out_specs=[ANYWHERE] * 3 + [VMEM] * 2,
+            scratch_shapes=[
+                pltpu.SemaphoreType.DMA((3, n_slabs)),
+                pltpu.SemaphoreType.DMA((3, n_slabs)),
+                pltpu.VMEM((3, 2, rows, n * HD), jnp.float32),
+            ],
         ),
-        out_shape=out_shape,
+        out_shape=[jax.ShapeDtypeStruct((rows, width), jnp.float32)] * 3
+        + [jax.ShapeDtypeStruct(shape, jnp.bfloat16), jax.ShapeDtypeStruct(shape, jnp.float32)],
         input_output_aliases=aliases,
-        compiler_params=pltpu.CompilerParams(vmem_limit_bytes=12 * MIB),
+        compiler_params=pltpu.CompilerParams(vmem_limit_bytes=15 * MIB),
         cost_estimate=cost(0),
-        name="adam_project" if projects else "adam_update",
+        name="adam_project",
     )(place, *operands)
-    return (out[:3] if updates else None), (out[-2:] if projects else None)
+    return out[:3], out[3:]
 
 
 SLOT = 32
@@ -347,17 +360,23 @@
     )(lengths, in_hbm(queries), in_hbm(cache_keys), in_hbm(cache_values))
 
 
-def merge_kernel(n_parts, *refs):
-    arrived, kept, cosine, sine = refs[:4]
-    stacked, acc, stats = (refs[4 + i : 4 + 3 * n_parts : 3] for i in range(3))
+def merge_kernel(spans, first, n_heads, *refs):
+    folds, refs = refs[: 2 * len(spans)], refs[2 * len(spans) :]
+    cosine, sine, stacked, acc, stats = refs[:5]
     new_kv, context = refs[-2:]
     row_count = new_kv.shape[0]
-    every = arrived[...].astype(jnp.float32) + kept[...]
+    every = jnp.concatenate(
+        [
+            folds[2 * f][:, span].astype(jnp.float32) + folds[2 * f + 1][:, span]
+            for f, span in enumerate(spans)
+        ],
+        axis=1,
+    )
     at = lax.broadcasted_iota(jnp.int32, (row_count * SLOT, row_count * STEPS), 0)
     to = lax.broadcasted_iota(jnp.int32, (row_count * SLOT, row_count * STEPS), 1)
     seen = (at // SLOT == to // STEPS) & (at % STEPS >= to % STEPS)
-    rows_of = lambda parts, u: jnp.concatenate([p[u].reshape(-1, HD) for p in parts], axis=0)
-    for u in range(stacked[0].shape[0]):
+    rows_of = lambda a, u: a[first + u].reshape(-1, HD)
+    for u in range(n_heads):
         total = every[:, u * HEAD_COLS : (u + 1) * HEAD_COLS]
         keys = total[:, :HD]
         keys = keys * cosine[...] + pltpu.roll(keys, HD // 2, 1) * sine[...]
@@ -391,14 +410,11 @@
                 context[r, :, at_col : at_col + HD] = out[at_row : at_row + STEPS].astype(jnp.bfloat16)
 
 
-def merge(arrived, kept, cosine, sine, attended, row_count, first, n_units, previous):
-    heads = attended[0][0].shape[0]
-    block = first // n_units
-    operands = [arrived, kept, cosine, sine]
-    in_specs = [whole(a) for a in operands]
-    for part in attended:
-        operands += part
-        in_specs += [pl.BlockSpec((n_units, *p.shape[1:]), lambda i: (block, 0, 0, 0)) for p in part]
+def merge(folds, cosine, sine, attended, row_count, first, n_heads, previous):
+    heads = attended[0].shape[0]
+    block = first // n_heads
+    operands = [a for fold in folds for a in fold[:2]] + [cosine, sine, *attended]
+    in_specs = [VMEM] * len(operands)
     aliases = {}
     if previous is not None:
         aliases = {len(operands) + i: i for i in range(2)}
@@ -406,10 +422,10 @@
         in_specs += [ANYWHERE] * 2
     widths = (HEAD_COLS, PER_GROUP * HD)
     return pl.pallas_call(
-        functools.partial(merge_kernel, len(attended)),
+        functools.partial(merge_kernel, [fold[2] for fold in folds], first, n_heads),
         grid=(1,),
         in_specs=in_specs,
-        out_specs=[pl.BlockSpec((row_count, STEPS, n_units * w), lambda i: (0, 0, block)) for w in widths],
+        out_specs=[pl.BlockSpec((row_count, STEPS, n_heads * w), lambda i: (0, 0, block)) for w in widths],
         out_shape=[jax.ShapeDtypeStruct((row_count, STEPS, heads * w), jnp.bfloat16) for w in widths],
         input_output_aliases=aliases,
         compiler_params=pltpu.CompilerParams(vmem_limit_bytes=8 * MIB),
@@ -439,7 +455,6 @@
 def butterfly_shards(
     tokens, queries, cache_keys, cache_values, lengths, weights, moment1, moment2, grad_parts
 ):
-    group_count = lax.axis_size("group")
     fsdp_count = lax.axis_size("fsdp")
     tp_count = lax.axis_size("tp")
     core = lax.axis_index("group") % 2
@@ -447,67 +462,65 @@
     tp = lax.axis_index("tp")
     rows, width = weights.shape
     row_count = tokens.shape[0]
-    n_units = width // (tp_count * HEAD_COLS)
+    n_units = width // (tp_count * HD)
     local = grad_parts[0]
     place = jnp.stack(
         [core, tp, jnp.full_like(core, n_units), fsdp, jnp.full_like(core, tp_count * rows), tp * rows]
     ).astype(jnp.int32)
 
-    crossings = [[*range(n_units // 2)], [*range(n_units // 2, n_units)]]
-    crossings = [c for c in crossings if c]
-    cut = 1
-    folds = [range(cut), range(cut, len(crossings))]
-    folds = [f for f in folds if len(f)]
-
-    pieces = [1] + [N_PIECES] * (len(crossings) - 1)
-    mine, crossed, toks = [], [], None
-    distance = 1
-    for units, p in zip(crossings, pieces):
-        away, home = cast_units(after(local, *mine), n_units, [(1, units, p), (0, units, 1)])
-        got = [swap(a, "group", 1) for a in away]
-        if toks is None:
-            toks = token_pieces(place, after(tokens, *away), fsdp_count, rows)
-            home = [after(home[0], *toks)]
-        (one,) = sum_pieces(home, got, 1)
-        mine.append(one)
-        crossed.append(swap(one, "group", 2))
-        if distance == 1:
-            toks = [swap(t, "fsdp", distance) if d & distance else t for d, t in enumerate(toks)]
-            distance *= 2
+    n_first = n_units // 2 + n_units // 8
+    n_early = n_first
+    n_late = n_units - n_early
+
+    def chip_sum(away, home, cuts):
+        return sum_pieces([home], [swap(a, "group", 1) for a in away], 0, cuts)
+
+    (away,) = cast_units(local, n_units, [(1, 0, n_first, 1)])
+    ((home,),) = cast_units(after(local, *away), n_units, [(0, 0, n_first, 1)])
+    (begun,) = chip_sum(away, home, [n_first * HD])
+    early, crossed = [begun], [swap(begun, "group", 2)]
+
+    n_tokens = row_count * STEPS
+    blocks = [(t, 0) for t in token_pieces(place, after(tokens, begun), fsdp_count, rows)]
+    source = after(local, begun, *[t for t, _ in blocks])
+    n_rest = n_units - n_first
+    away, (home,) = cast_units(source, n_units, [(1, n_first, n_rest, N_PIECES), (0, n_first, n_rest, 1)])
+    *more, last = chip_sum(away, home, [n_late * HD])
+    early += more
+    crossed += [swap(m, "group", 2) for m in more]
+    crossed_last = swap(last, "group", 2)
+
     cosine, sine = rotation_tables(lengths)
-    attended = [
-        cache_attention(after(queries, *mine, *toks), cache_keys, cache_values, lengths, 0, row_count)
-    ]
-    while distance < fsdp_count:
-        toks = [swap(t, "fsdp", distance) if d & distance else t for d, t in enumerate(toks)]
-        distance *= 2
-    toks = [toks[d] for d in reversed_bits(fsdp_count)]
+    ready = [*early, last]
+    attended = cache_attention(after(queries, *ready), cache_keys, cache_values, lengths, 0, row_count)
+    distance = fsdp_count // 2
+    step = (attended[1],)
+    while distance:
+        going = [d for d in range(fsdp_count) if d & distance]
+        leaving = [blocks[d] for d in going]
+        if distance < fsdp_count // 2:
+            leaving = [(after(t, attended[1]), at) for t, at in leaving]
+        stacked = stack_blocks(leaving, n_tokens)
+        got = swap(stacked, "fsdp", distance)
+        for i, d in enumerate(going):
+            blocks[d] = (got, i)
+        distance //= 2
+        step = (attended[1], got)
+    toks = [blocks[d] for d in reversed_bits(fsdp_count)]
 
     state = (weights, moment1, moment2)
-    last = crossings[-1]
-
-    totals, sums = [], []
-    updated = None
-    step = (attended[0][1], *toks)
-    for c, units in enumerate(crossings):
-        one, other = [mine[c]], after(crossed[c], *step)
-        bit = 2
-        while True:
-            bit *= 2
-            one = sum_pieces(one, [other], N_PIECES if bit >= group_count else 1)
-            if bit >= group_count:
-                break
-            other = swap(one[0], "group", bit)
-        totals.append((one, [swap(p, "group", 1) for p in one]))
-        updated, both = adam_units(place, totals[c], state, toks, units, width, previous=updated)
-        sums.append(both)
-        step = (sums[c][0],)
-
-    moving = []
-    for members in folds:
-        sent = jnp.concatenate([sums[c][0] for c in members], axis=1)
-        kept = jnp.concatenate([sums[c][1] for c in members], axis=1)
-        moving.append((swap(sent, "tp", 1), kept))
+
+    def total(parts, arrived, n_pieces, *earlier):
+        arrived = list(lax.optimization_barrier((*arrived, *earlier)))[: len(arrived)]
+        one = sum_pieces(parts, arrived, 1, [rows // n_pieces] * n_pieces)
+        return one, [swap(p, "group", 1) for p in one]
+
+    both = total(early, crossed, N_PIECES, *step)
+    updated, (sent, kept) = adam_units(place, both, state, toks, 0, n_early, None)
+    moving = [(swap(sent, "tp", 1), kept)]
+    both = total([last], [crossed_last], N_PIECES, sent)
+    updated, (sent, kept) = adam_units(place, both, state, toks, n_early, n_late, updated)
+    moving.append((swap(sent, "tp", 1), kept))
     distance = 1
     while distance < fsdp_count:
         for f, (got, kept) in enumerate(moving):
@@ -515,10 +528,23 @@
             moving[f] = (swap(sent, "fsdp", distance), kept)
         distance *= 2
 
-    outs = None
-    for members, (got, kept) in zip(folds, moving):
-        units = [u for c in members for u in crossings[c]]
-        outs = merge(got, kept, cosine, sine, attended, row_count, units[0], len(units), outs)
+    n_heads = n_units * HD // HEAD_COLS
+    whole_heads = n_heads // 2
+    split = whole_heads * HEAD_COLS
+    outs = merge(
+        [(*moving[0], slice(0, split))], cosine, sine, attended, row_count, 0, whole_heads, None
+    )
+    parts = [(*moving[0], slice(split, n_early * HD)), (*moving[1], slice(0, n_late * HD))]
+    outs = merge(
+        parts[0 if split < n_early * HD else 1 :],
+        cosine,
+        sine,
+        attended,
+        row_count,
+        whole_heads,
+        n_heads - whole_heads,
+        outs,
+    )
     return (*updated, *outs)
 
 
@@ -627,6 +653,6 @@
         P(("group", "fsdp"), None, "tp"),
     )
     sizes = mesh.shape
-    pairwise = power_of_two(sizes["group"]) and power_of_two(sizes["fsdp"]) and sizes["tp"] == 2
+    pairwise = sizes["group"] == 4 and power_of_two(sizes["fsdp"]) and sizes["tp"] == 2
     shards = butterfly_shards if pairwise else plain_shards
     return jax.shard_map(shards, mesh=mesh, in_specs=in_specs, out_specs=out_specs, check_vma=False)

time: 62.7 us -> 61.6 us (0.982)
  starting transfers between devices: 24.6 us -> 21.4 us
  waiting for transfers between devices: 7.56 us -> 9.8 us
    ppermute x19 -> x17, starting transfers between devices: 24.6 us -> 21.4 us  [swap(): return lax.ppermute(array, axis, [(i, i ^ bit) for i in range(size)])]
    ppermute x19 -> x17, waiting for transfers between devices: 7.56 us -> 9.8 us  [swap(): return lax.ppermute(array, axis, [(i, i ^ bit) for i in range(size)])]
    pallas_call x8 -> x10, Pallas kernels: 17.9 us -> 17 us  [the longest x2 13.3 us: adam_units(): pl.pallas_call(functools.partial(adam_kernel, first, n, len(mine), len(pa...]
    pallas_call x2 -> x3, Pallas kernels: 3.58 us -> 4.39 us  [cast_units(): pl.pallas_call(functools.partial(cast_kernel, wanted, n_units), in_specs=...]
  transfers between devices with their start and end apart: 19 -> 17, of which waited for: 9 -> 9; matrix products, arithmetic and copies ran while one was open for 1% -> 1% of each run, Pallas kernels for 40% -> 41%
where the time goes in v6:
time: 61.6 us; the launch traced here: 61.3 us
  Pallas kernels  28.7 us (47%)
  starting transfers between devices  21.4 us (35%)
  waiting for transfers between devices  9.8 us (16%)
  between operations  0.86 us (1%)
    ppermute x17, starting transfers between devices, swap(): return lax.ppermute(array, axis, [(i, i ^ bit) for i in range(size)])  21.4 us
    pallas_call x2, Pallas kernels, adam_units(): pl.pallas_call(functools.partial(adam_kernel, first, n, len(mine), len(pa...  13.3 us
    ppermute x17, waiting for transfers between devices, swap(): return lax.ppermute(array, axis, [(i, i ^ bit) for i in range(size)])  9.8 us
    pallas_call x1, Pallas kernels, cache_attention(): pl.pallas_call(functools.partial(cache_kernel, heads, first), grid_spec=p...  6.71 us
    pallas_call x3, Pallas kernels, cast_units(): pl.pallas_call(functools.partial(cast_kernel, wanted, n_units), in_specs=...  4.39 us
    pallas_call x2, Pallas kernels, merge(): pl.pallas_call(functools.partial(merge_kernel, [fold[2] for fold in folds...  3.12 us
  transfers between devices with their start and end apart: 17, of which 9 were waited for; matrix products, arithmetic and copies ran while one was open for 1% of the time, Pallas kernels for 41%

profile of v6, /device:TPU:0, one launch (start us, length us, event | category | flops | bytes accessed | tf_op | source)
XLA Modules:
  0.0 61.3 jit_solution(5098003767334578450)
XLA Ops:
  0.6 1.4 %cast_units.3 = bf16[640,640]{1,0:T(8,128)(2,1)S(1)} custom-call(f32[640,2048]{1,0:T(8,128)} %bitcast.5), custom_call_target="tpu_custom_call" | custom-call | flops 1 | bytes 1 | tf_op jit(solution)/shard_map/cast_units/pallas_call | solution.py:120
  2.6 1.4 %cast_units.4.refs_0_ = bf16[640,640]{1,0:T(8,128)(2,1)S(1)} custom-call(f32[640,2048]{1,0:T(8,128)} %bitcast.6), custom_call_target="tpu_custom_call" | custom-call | flops 1 | bytes 1 | tf_op jit(solution)/shard_map/cast_units/pallas_call | solution.py:120
  4.8 2.9 %collective-permute-start.4 = (bf16[640,640]{1,0:T(8,128)(2,1)S(1)}, bf16[640,640]{1,0:T(8,128)(2,1)S(1)}, u32[]{:S(2)}, u32[]{:S(2)}) collective-permute-start(bf16[640,640]{1,0:T(8,128)(2,1)S(1)} %sum_pieces.4.refs_0_), channel_id=1, source_target_pairs={{0,16},{8,24},{16,0},{24,8},{1,17},{9,25},{17,1},{25,9},{2,18},{10... | collective-permute-start | bytes 2457608 | tf_op jit(solution)/shard_map/ppermute | solution.py:439
  7.8 0.6 token_pieces.1
  8.4 1.5 %cast_units.5 = (bf16[320,384]{1,0:T(8,128)(2,1)S(1)}, bf16[320,384]{1,0:T(8,128)(2,1)S(1)}, bf16[640,384]{1,0:T(8,128)(2,1)S(1)}) custom-call(f32[640,2048]{1,0:T(8,128)} %bitcast.7), custom_call_target="tpu_custom_call" | custom-call | flops 1 | bytes 1 | tf_op jit(solution)/shard_map/cast_units/pallas_call | solution.py:120
  10.5 2.6 %collective-permute-start.5 = (bf16[64,640]{1,0:T(8,128)(2,1)S(1)}, bf16[64,640]{1,0:T(8,128)(2,1)S(1)}, u32[]{:S(2)}, u32[]{:S(2)}) collective-permute-start(bf16[64,640]{1,0:T(8,128)(2,1)S(1)} %stack_blocks.2), channel_id=1, source_target_pairs={{0,4},{2,6},{4,0},{6,2},{1,5},{3,7},{5,1},{7,3},{8,12},{10,14},{12... | collective-permute-start | bytes 245768 | tf_op jit(solution)/shard_map/ppermute | solution.py:439
  13.3 6.7 %cache_attention.1 = (bf16[4,8,32,128]{3,2,1,0:T(8,128)(2,1)S(1)}, f32[4,8,32,128]{3,2,1,0:T(8,128)S(1)}, f32[4,8,32,128]{3,2,1,0:T(8,128)S(1)}) custom-call(s32[8]{0:T(128)S(1)} %copy-done.1, bf16[8,4,2560]{2,1,0:T(4,128)(2,1)} %q, bf16[8,512,512]{2,1,0:T(8,128)(2,1)} %k.1, bf16[8,512,512]{2,1,0:T(8,128)(2,1)} %v.1), custom_call_target="tpu_custom_call" | custom-call | flops 1 | bytes 17500000 | tf_op jit(solution)/shard_map/cache_attention/pallas_call | solution.py:344
  20.0 1.6 %collective-permute-start.6 = (bf16[64,640]{1,0:T(8,128)(2,1)S(1)}, bf16[64,640]{1,0:T(8,128)(2,1)S(1)}, u32[]{:S(2)}, u32[]{:S(2)}) collective-permute-start(bf16[64,640]{1,0:T(8,128)(2,1)S(1)} %stack_blocks.3), channel_id=1, source_target_pairs={{0,2},{2,0},{4,6},{6,4},{1,3},{3,1},{5,7},{7,5},{8,10},{10,8},{12,... | collective-permute-start | bytes 245768 | tf_op jit(solution)/shard_map/ppermute | solution.py:439
  22.2 2.3 %collective-permute-done.6.refs_9_.refs_10_ = bf16[64,640]{1,0:T(8,128)(2,1)S(1)} collective-permute-done((bf16[64,640]{1,0:T(8,128)(2,1)S(1)}, bf16[64,640]{1,0:T(8,128)(2,1)S(1)}, u32[]{:S(2)}, u32[]{:S(2)}) %collective-permute-start.6) | collective-permute-done | bytes 81952 | tf_op jit(solution)/shard_map/ppermute | solution.py:439
  24.6 2.2 %collective-permute-done.4.refs_1_ = bf16[640,640]{1,0:T(8,128)(2,1)S(1)} collective-permute-done((bf16[640,640]{1,0:T(8,128)(2,1)S(1)}, bf16[640,640]{1,0:T(8,128)(2,1)S(1)}, u32[]{:S(2)}, u32[]{:S(2)}) %collective-permute-start.4) | collective-permute-done | bytes 819232 | tf_op jit(solution)/shard_map/ppermute | solution.py:439
  27.6 1.2 %collective-permute-done.7.refs_2_ = bf16[320,640]{1,0:T(8,128)(2,1)S(1)} collective-permute-done((bf16[320,640]{1,0:T(8,128)(2,1)S(1)}, bf16[320,640]{1,0:T(8,128)(2,1)S(1)}, u32[]{:S(2)}, u32[]{:S(2)}) %collective-permute-start.7) | collective-permute-done | bytes 409632 | tf_op jit(solution)/shard_map/ppermute | solution.py:439
  28.7 0.6 collective-permute-done.8.refs_3_
  29.3 7.9 %adam_project.2 = (f32[640,2048]{1,0:T(8,128)}, f32[640,2048]{1,0:T(8,128)}, f32[640,2048]{1,0:T(8,128)}, bf16[128,640]{1,0:T(8,128)(2,1)S(1)}, f32[128,640]{1,0:T(8,128)S(1)}) custom-call(s32[6]{0:T(128)S(1)} %stack.19.place, bf16[320,640]{1,0:T(8,128)(2,1)S(1)} %get-tuple-element.56.refs_0_, bf16[320,640]{1,0:T(8,128)(2,1)S(1)} %get-tuple-element.57.refs_1_, ...), custom_call_target="tpu_custom_call" | custom-call | flops 1 | bytes 1 | tf_op jit(solution)/shard_map/adam_project/pallas_call | solution.py:268
  38.0 2.1 %collective-permute-start.11 = (bf16[128,640]{1,0:T(8,128)(2,1)S(1)}, bf16[128,640]{1,0:T(8,128)(2,1)S(1)}, u32[]{:S(2)}, u32[]{:S(2)}) collective-permute-start(bf16[128,640]{1,0:T(8,128)(2,1)S(1)} %get-tuple-element.58), channel_id=1, source_target_pairs={{0,1},{1,0},{2,3},{3,2},{4,5},{5,4},{6,7},{7,6},{8,9},{9,8},{10,11... | collective-permute-start | bytes 491528 | tf_op jit(solution)/shard_map/ppermute | solution.py:439
  40.3 5.4 %adam_project.3 = (f32[640,2048]{1,0:T(8,128)}, f32[640,2048]{1,0:T(8,128)}, f32[640,2048]{1,0:T(8,128)}, bf16[128,384]{1,0:T(8,128)(2,1)S(1)}, f32[128,384]{1,0:T(8,128)S(1)}) custom-call(s32[6]{0:T(128)S(1)} %stack.19.place, bf16[320,384]{1,0:T(8,128)(2,1)S(1)} %get-tuple-element.60.refs_0_, ...), custom_call_target="tpu_custom_call", output_to_operand_aliasing={{0}: (12, {}), {1}: (13, {}), {2}: (14, {})} | custom-call | flops 1 | bytes 1 | tf_op jit(solution)/shard_map/adam_project/pallas_call | solution.py:268
  45.6 1.1 %collective-permute-start.14 = (bf16[128,384]{1,0:T(8,128)(2,1)S(1)}, bf16[128,384]{1,0:T(8,128)(2,1)S(1)}, u32[]{:S(2)}, u32[]{:S(2)}) collective-permute-start(bf16[128,384]{1,0:T(8,128)(2,1)S(1)} %get-tuple-element.69), channel_id=1, source_target_pairs={{0,1},{1,0},{2,3},{3,2},{4,5},{5,4},{6,7},{7,6},{8,9},{9,8},{10,11... | collective-permute-start | bytes 294920 | tf_op jit(solution)/shard_map/ppermute | solution.py:439
  46.8 1.6 %collective-permute-start.12 = (bf16[64,640]{1,0:T(8,128)(2,1)S(1)}, bf16[64,640]{1,0:T(8,128)(2,1)S(1)}, u32[]{:S(2)}, u32[]{:S(2)}) collective-permute-start(bf16[64,640]{1,0:T(8,128)(2,1)S(1)} %slice.50), channel_id=1, source_target_pairs={{0,2},{2,0},{4,6},{6,4},{1,3},{3,1},{5,7},{7,5},{8,10},{10,8},{12,... | collective-permute-start | bytes 245768 | tf_op jit(solution)/shard_map/ppermute | solution.py:439
  48.5 1.8 %collective-permute-done.14 = bf16[128,384]{1,0:T(8,128)(2,1)S(1)} collective-permute-done((bf16[128,384]{1,0:T(8,128)(2,1)S(1)}, bf16[128,384]{1,0:T(8,128)(2,1)S(1)}, u32[]{:S(2)}, u32[]{:S(2)}) %collective-permute-start.14) | collective-permute-done | bytes 98336 | tf_op jit(solution)/shard_map/ppermute | solution.py:439
  50.4 1.6 %collective-permute-start.15 = (bf16[64,384]{1,0:T(8,128)(2,1)S(1)}, bf16[64,384]{1,0:T(8,128)(2,1)S(1)}, u32[]{:S(2)}, u32[]{:S(2)}) collective-permute-start(bf16[64,384]{1,0:T(8,128)(2,1)S(1)} %slice.51), channel_id=1, source_target_pairs={{0,2},{2,0},{4,6},{6,4},{1,3},{3,1},{5,7},{7,5},{8,10},{10,8},{12,... | collective-permute-start | bytes 147464 | tf_op jit(solution)/shard_map/ppermute | solution.py:439
  52.0 2.7 %collective-permute-start.13 = (bf16[32,640]{1,0:T(8,128)(2,1)S(1)}, bf16[32,640]{1,0:T(8,128)(2,1)S(1)}, u32[]{:S(2)}, u32[]{:S(2)}) collective-permute-start(bf16[32,640]{1,0:T(8,128)(2,1)S(1)} %slice.52), channel_id=1, source_target_pairs={{0,4},{2,6},{4,0},{6,2},{1,5},{3,7},{5,1},{7,3},{8,12},{10,14},{12... | collective-permute-start | bytes 122888 | tf_op jit(solution)/shard_map/ppermute | solution.py:439
  55.0 2.2 %collective-permute-start.16 = (bf16[32,384]{1,0:T(8,128)(2,1)S(1)}, bf16[32,384]{1,0:T(8,128)(2,1)S(1)}, u32[]{:S(2)}, u32[]{:S(2)}) collective-permute-start(bf16[32,384]{1,0:T(8,128)(2,1)S(1)} %slice.53), channel_id=1, source_target_pairs={{0,4},{2,6},{4,0},{6,2},{1,5},{3,7},{5,1},{7,3},{8,12},{10,14},{12... | collective-permute-start | bytes 73736 | tf_op jit(solution)/shard_map/ppermute | solution.py:439
  57.3 0.5 collective-permute-done.13.refs_0_
  57.8 1.6 %merge_new.2 = (bf16[8,4,1024]{2,1,0:T(4,128)(2,1)}, bf16[8,4,2560]{2,1,0:T(4,128)(2,1)}) custom-call(bf16[32,640]{1,0:T(8,128)(2,1)S(1)} %collective-permute-done.13.refs_0_, f32[32,640]{1,0:T(8,128)S(1)} %slice.39.refs_1_, f32[32,128]{1,0:T(8,128)S(1)} %get-tuple-element.80.refs_2_.refs_4_, f32[32,128]{1,0:T(8,128)S(1)} %get-tuple-element.81.refs_3_.refs_5_, ...), custom_call_target="tpu_custom_call" | custom-call | flops 1 | bytes 1 | tf_op jit(solution)/shard_map/merge_new/pallas_call | solution.py:424
  59.8 1.6 %merge_new.3 = (bf16[8,4,1024]{2,1,0:T(4,128)(2,1)}, bf16[8,4,2560]{2,1,0:T(4,128)(2,1)}) custom-call(bf16[32,640]{1,0:T(8,128)(2,1)S(1)} %collective-permute-done.13.refs_0_, f32[32,640]{1,0:T(8,128)S(1)} %slice.39.refs_1_, bf16[32,384]{1,0:T(8,128)(2,1)S(1)} %collective-permute-done.16.refs_2_, ...), custom_call_target="tpu_custom_call", output_to_operand_aliasing={{0}: (9, {}), {1}: (10, {})} | custom-call | flops 1 | bytes 1 | tf_op jit(solution)/shard_map/merge_new/pallas_call | solution.py:424
  (45 shorter events, 5.2 us)
Async XLA Ops:
  2.1 5.7 %copy-start = (bf16[8,4,5120]{2,1,0:T(4,128)(2,1)S(1)}, bf16[8,4,5120]{2,1,0:T(4,128)(2,1)}, u32[]{:S(2)}) copy-start(bf16[8,4,5120]{2,1,0:T(4,128)(2,1)} %source) | copy-start | bytes 983044
  2.1 2.5 %collective-permute-start = (bf16[640,640]{1,0:T(8,128)(2,1)S(1)}, bf16[640,640]{1,0:T(8,128)(2,1)S(1)}, u32[]{:S(2)}, u32[]{:S(2)}) collective-permute-start(bf16[640,640]{1,0:T(8,128)(2,1)S(1)} %cast_units.3), channel_id=1, source_target_pairs={{0,8},{8,0},{16,24},{24,16},{1,9},{9,1},{17,25},{25,17},{2,10},{10... | collective-permute-start | bytes 2457608 | tf_op jit(solution)/shard_map/ppermute | solution.py:439
  4.0 9.3 %copy-start.1 = (s32[8]{0:T(128)S(1)}, s32[8]{0:T(128)}, u32[]{:S(2)}) copy-start(s32[8]{0:T(128)} %lens.1) | copy-start | bytes 100
  4.8 22.0 %collective-permute-start.4 = (bf16[640,640]{1,0:T(8,128)(2,1)S(1)}, bf16[640,640]{1,0:T(8,128)(2,1)S(1)}, u32[]{:S(2)}, u32[]{:S(2)}) collective-permute-start(bf16[640,640]{1,0:T(8,128)(2,1)S(1)} %sum_pieces.4.refs_0_), channel_id=1, source_target_pairs={{0,16},{8,24},{16,0},{24,8},{1,17},{9,25},{17,1},{25,9},{2,18},{10... | collective-permute-start | bytes 2457608 | tf_op jit(solution)/shard_map/ppermute | solution.py:439
  9.9 3.2 %collective-permute-start.1 = (bf16[320,384]{1,0:T(8,128)(2,1)S(1)}, bf16[320,384]{1,0:T(8,128)(2,1)S(1)}, u32[]{:S(2)}, u32[]{:S(2)}) collective-permute-start(bf16[320,384]{1,0:T(8,128)(2,1)S(1)} %get-tuple-element.49), channel_id=1, source_target_pairs={{0,8},{8,0},{16,24},{24,16},{1,9},{9,1},{17,25},{25,17},{2,10},{10... | collective-permute-start | bytes 737288 | tf_op jit(solution)/shard_map/ppermute | solution.py:439
  10.0 3.2 %collective-permute-start.2 = (bf16[320,384]{1,0:T(8,128)(2,1)S(1)}, bf16[320,384]{1,0:T(8,128)(2,1)S(1)}, u32[]{:S(2)}, u32[]{:S(2)}) collective-permute-start(bf16[320,384]{1,0:T(8,128)(2,1)S(1)} %get-tuple-element.50), channel_id=1, source_target_pairs={{0,8},{8,0},{16,24},{24,16},{1,9},{9,1},{17,25},{25,17},{2,10},{10... | collective-permute-start | bytes 737288 | tf_op jit(solution)/shard_map/ppermute | solution.py:439
  10.5 9.5 %collective-permute-start.5 = (bf16[64,640]{1,0:T(8,128)(2,1)S(1)}, bf16[64,640]{1,0:T(8,128)(2,1)S(1)}, u32[]{:S(2)}, u32[]{:S(2)}) collective-permute-start(bf16[64,640]{1,0:T(8,128)(2,1)S(1)} %stack_blocks.2), channel_id=1, source_target_pairs={{0,4},{2,6},{4,0},{6,2},{1,5},{3,7},{5,1},{7,3},{8,12},{10,14},{12... | collective-permute-start | bytes 245768 | tf_op jit(solution)/shard_map/ppermute | solution.py:439
  20.0 4.5 %collective-permute-start.6 = (bf16[64,640]{1,0:T(8,128)(2,1)S(1)}, bf16[64,640]{1,0:T(8,128)(2,1)S(1)}, u32[]{:S(2)}, u32[]{:S(2)}) collective-permute-start(bf16[64,640]{1,0:T(8,128)(2,1)S(1)} %stack_blocks.3), channel_id=1, source_target_pairs={{0,2},{2,0},{4,6},{6,4},{1,3},{3,1},{5,7},{7,5},{8,10},{10,8},{12,... | collective-permute-start | bytes 245768 | tf_op jit(solution)/shard_map/ppermute | solution.py:439
  21.7 15.5 %collective-permute-start.3 = (bf16[640,384]{1,0:T(8,128)(2,1)S(1)}, bf16[640,384]{1,0:T(8,128)(2,1)S(1)}, u32[]{:S(2)}, u32[]{:S(2)}) collective-permute-start(bf16[640,384]{1,0:T(8,128)(2,1)S(1)} %sum_pieces.5.refs_0_), channel_id=1, source_target_pairs={{0,16},{8,24},{16,0},{24,8},{1,17},{9,25},{17,1},{25,9},{2,18},{10... | collective-permute-start | bytes 1474568 | tf_op jit(solution)/shard_map/ppermute | solution.py:439
  26.9 1.8 %collective-permute-start.7 = (bf16[320,640]{1,0:T(8,128)(2,1)S(1)}, bf16[320,640]{1,0:T(8,128)(2,1)S(1)}, u32[]{:S(2)}, u32[]{:S(2)}) collective-permute-start(bf16[320,640]{1,0:T(8,128)(2,1)S(1)} %get-tuple-element.56.refs_0_), channel_id=1, source_target_pairs={{0,8},{8,0},{16,24},{24,16},{1,9},{9,1},{17,25},{25,17},{2,10},{10... | collective-permute-start | bytes 1228808 | tf_op jit(solution)/shard_map/ppermute | solution.py:439
  27.0 2.3 %collective-permute-start.8 = (bf16[320,640]{1,0:T(8,128)(2,1)S(1)}, bf16[320,640]{1,0:T(8,128)(2,1)S(1)}, u32[]{:S(2)}, u32[]{:S(2)}) collective-permute-start(bf16[320,640]{1,0:T(8,128)(2,1)S(1)} %get-tuple-element.57.refs_1_), channel_id=1, source_target_pairs={{0,8},{8,0},{16,24},{24,16},{1,9},{9,1},{17,25},{25,17},{2,10},{10... | collective-permute-start | bytes 1228808 | tf_op jit(solution)/shard_map/ppermute | solution.py:439
  37.3 2.9 %collective-permute-start.9 = (bf16[320,384]{1,0:T(8,128)(2,1)S(1)}, bf16[320,384]{1,0:T(8,128)(2,1)S(1)}, u32[]{:S(2)}, u32[]{:S(2)}) collective-permute-start(bf16[320,384]{1,0:T(8,128)(2,1)S(1)} %get-tuple-element.60.refs_0_), channel_id=1, source_target_pairs={{0,8},{8,0},{16,24},{24,16},{1,9},{9,1},{17,25},{25,17},{2,10},{10... | collective-permute-start | bytes 737288 | tf_op jit(solution)/shard_map/ppermute | solution.py:439
  37.5 2.7 %collective-permute-start.10 = (bf16[320,384]{1,0:T(8,128)(2,1)S(1)}, bf16[320,384]{1,0:T(8,128)(2,1)S(1)}, u32[]{:S(2)}, u32[]{:S(2)}) collective-permute-start(bf16[320,384]{1,0:T(8,128)(2,1)S(1)} %get-tuple-element.61.refs_1_), channel_id=1, source_target_pairs={{0,8},{8,0},{16,24},{24,16},{1,9},{9,1},{17,25},{25,17},{2,10},{10... | collective-permute-start | bytes 737288 | tf_op jit(solution)/shard_map/ppermute | solution.py:439
  38.0 8.8 %collective-permute-start.11 = (bf16[128,640]{1,0:T(8,128)(2,1)S(1)}, bf16[128,640]{1,0:T(8,128)(2,1)S(1)}, u32[]{:S(2)}, u32[]{:S(2)}) collective-permute-start(bf16[128,640]{1,0:T(8,128)(2,1)S(1)} %get-tuple-element.58), channel_id=1, source_target_pairs={{0,1},{1,0},{2,3},{3,2},{4,5},{5,4},{6,7},{7,6},{8,9},{9,8},{10,11... | collective-permute-start | bytes 491528 | tf_op jit(solution)/shard_map/ppermute | solution.py:439
  45.6 4.7 %collective-permute-start.14 = (bf16[128,384]{1,0:T(8,128)(2,1)S(1)}, bf16[128,384]{1,0:T(8,128)(2,1)S(1)}, u32[]{:S(2)}, u32[]{:S(2)}) collective-permute-start(bf16[128,384]{1,0:T(8,128)(2,1)S(1)} %get-tuple-element.69), channel_id=1, source_target_pairs={{0,1},{1,0},{2,3},{3,2},{4,5},{5,4},{6,7},{7,6},{8,9},{9,8},{10,11... | collective-permute-start | bytes 294920 | tf_op jit(solution)/shard_map/ppermute | solution.py:439
  46.8 5.2 %collective-permute-start.12 = (bf16[64,640]{1,0:T(8,128)(2,1)S(1)}, bf16[64,640]{1,0:T(8,128)(2,1)S(1)}, u32[]{:S(2)}, u32[]{:S(2)}) collective-permute-start(bf16[64,640]{1,0:T(8,128)(2,1)S(1)} %slice.50), channel_id=1, source_target_pairs={{0,2},{2,0},{4,6},{6,4},{1,3},{3,1},{5,7},{7,5},{8,10},{10,8},{12,... | collective-permute-start | bytes 245768 | tf_op jit(solution)/shard_map/ppermute | solution.py:439
  50.4 4.6 %collective-permute-start.15 = (bf16[64,384]{1,0:T(8,128)(2,1)S(1)}, bf16[64,384]{1,0:T(8,128)(2,1)S(1)}, u32[]{:S(2)}, u32[]{:S(2)}) collective-permute-start(bf16[64,384]{1,0:T(8,128)(2,1)S(1)} %slice.51), channel_id=1, source_target_pairs={{0,2},{2,0},{4,6},{6,4},{1,3},{3,1},{5,7},{7,5},{8,10},{10,8},{12,... | collective-permute-start | bytes 147464 | tf_op jit(solution)/shard_map/ppermute | solution.py:439
  52.0 5.8 %collective-permute-start.13 = (bf16[32,640]{1,0:T(8,128)(2,1)S(1)}, bf16[32,640]{1,0:T(8,128)(2,1)S(1)}, u32[]{:S(2)}, u32[]{:S(2)}) collective-permute-start(bf16[32,640]{1,0:T(8,128)(2,1)S(1)} %slice.52), channel_id=1, source_target_pairs={{0,4},{2,6},{4,0},{6,2},{1,5},{3,7},{5,1},{7,3},{8,12},{10,14},{12... | collective-permute-start | bytes 122888 | tf_op jit(solution)/shard_map/ppermute | solution.py:439
  55.0 4.8 %collective-permute-start.16 = (bf16[32,384]{1,0:T(8,128)(2,1)S(1)}, bf16[32,384]{1,0:T(8,128)(2,1)S(1)}, u32[]{:S(2)}, u32[]{:S(2)}) collective-permute-start(bf16[32,384]{1,0:T(8,128)(2,1)S(1)} %slice.53), channel_id=1, source_target_pairs={{0,4},{2,6},{4,0},{6,2},{1,5},{3,7},{5,1},{7,3},{8,12},{10,14},{12... | collective-permute-start | bytes 73736 | tf_op jit(solution)/shard_map/ppermute | solution.py:439

commit v7 on v6

--- a/solution.py
+++ b/solution.py
@@ -468,8 +468,9 @@
         [core, tp, jnp.full_like(core, n_units), fsdp, jnp.full_like(core, tp_count * rows), tp * rows]
     ).astype(jnp.int32)
 
-    n_first = n_units // 2 + n_units // 8
-    n_early = n_first
+    n_first = n_units // 2
+    n_extra = n_units // 8
+    n_early = n_first + n_extra
     n_late = n_units - n_early
 
     def chip_sum(away, home, cuts):
@@ -485,7 +486,7 @@
     source = after(local, begun, *[t for t, _ in blocks])
     n_rest = n_units - n_first
     away, (home,) = cast_units(source, n_units, [(1, n_first, n_rest, N_PIECES), (0, n_first, n_rest, 1)])
-    *more, last = chip_sum(away, home, [n_late * HD])
+    *more, last = chip_sum(away, home, [n * HD for n in (n_extra, n_late) if n])
     early += more
     crossed += [swap(m, "group", 2) for m in more]
     crossed_last = swap(last, "group", 2)
@@ -518,7 +519,7 @@
     both = total(early, crossed, N_PIECES, *step)
     updated, (sent, kept) = adam_units(place, both, state, toks, 0, n_early, None)
     moving = [(swap(sent, "tp", 1), kept)]
-    both = total([last], [crossed_last], N_PIECES, sent)
+    both = total([last], [crossed_last], 1, sent)
     updated, (sent, kept) = adam_units(place, both, state, toks, n_early, n_late, updated)
     moving.append((swap(sent, "tp", 1), kept))
     distance = 1

time: 61.6 us -> 60.9 us (0.989)
  waiting for transfers between devices: 9.8 us -> 7.36 us
  starting transfers between devices: 21.4 us -> 23.1 us
    ppermute x17, waiting for transfers between devices: 9.8 us -> 7.36 us  [swap(): return lax.ppermute(array, axis, [(i, i ^ bit) for i in range(size)])]
    ppermute x17, starting transfers between devices: 21.4 us -> 23.1 us  [swap(): return lax.ppermute(array, axis, [(i, i ^ bit) for i in range(size)])]
  transfers between devices with their start and end apart: 17 -> 17, of which waited for: 9 -> 8; matrix products, arithmetic and copies ran while one was open for 1% -> 1% of each run, Pallas kernels for 41% -> 42%
where the time goes in v7:
time: 60.9 us; the launch traced here: 60.6 us
  Pallas kernels  28.7 us (47%)
  starting transfers between devices  23.1 us (38%)
  waiting for transfers between devices  7.36 us (12%)
  between operations  0.84 us (1%)
    ppermute x17, starting transfers between devices, swap(): return lax.ppermute(array, axis, [(i, i ^ bit) for i in range(size)])  23.1 us
    pallas_call x2, Pallas kernels, adam_units(): pl.pallas_call(functools.partial(adam_kernel, first, n, len(mine), len(pa...  13.3 us
    ppermute x17, waiting for transfers between devices, swap(): return lax.ppermute(array, axis, [(i, i ^ bit) for i in range(size)])  7.36 us
    pallas_call x1, Pallas kernels, cache_attention(): pl.pallas_call(functools.partial(cache_kernel, heads, first), grid_spec=p...  6.71 us
    pallas_call x3, Pallas kernels, cast_units(): pl.pallas_call(functools.partial(cast_kernel, wanted, n_units), in_specs=...  4.38 us
    pallas_call x2, Pallas kernels, merge(): pl.pallas_call(functools.partial(merge_kernel, [fold[2] for fold in folds...  3.12 us
  transfers between devices with their start and end apart: 17, of which 8 were waited for; matrix products, arithmetic and copies ran while one was open for 1% of the time, Pallas kernels for 42%

profile of v7, /device:TPU:0, one launch (start us, length us, event | category | flops | bytes accessed | tf_op | source)
XLA Modules:
  0.0 60.6 jit_solution(15580301252613089430)
XLA Ops:
  0.6 1.3 %cast_units.3 = bf16[640,512]{1,0:T(8,128)(2,1)S(1)} custom-call(f32[640,2048]{1,0:T(8,128)} %bitcast.5), custom_call_target="tpu_custom_call" | custom-call | flops 1 | bytes 1 | tf_op jit(solution)/shard_map/cast_units/pallas_call | solution.py:120
  2.5 1.3 %cast_units.4.refs_0_ = bf16[640,512]{1,0:T(8,128)(2,1)S(1)} custom-call(f32[640,2048]{1,0:T(8,128)} %bitcast.6), custom_call_target="tpu_custom_call" | custom-call | flops 1 | bytes 1 | tf_op jit(solution)/shard_map/cast_units/pallas_call | solution.py:120
  4.4 2.9 %collective-permute-start.4 = (bf16[640,512]{1,0:T(8,128)(2,1)S(1)}, bf16[640,512]{1,0:T(8,128)(2,1)S(1)}, u32[]{:S(2)}, u32[]{:S(2)}) collective-permute-start(bf16[640,512]{1,0:T(8,128)(2,1)S(1)} %sum_pieces.4.refs_0_), channel_id=1, source_target_pairs={{0,16},{8,24},{16,0},{24,8},{1,17},{9,25},{17,1},{25,9},{2,18},{10... | collective-permute-start | bytes 1966088 | tf_op jit(solution)/shard_map/ppermute | solution.py:439
  7.4 0.6 token_pieces.1
  8.0 1.8 %cast_units.5 = (bf16[320,512]{1,0:T(8,128)(2,1)S(1)}, bf16[320,512]{1,0:T(8,128)(2,1)S(1)}, bf16[640,512]{1,0:T(8,128)(2,1)S(1)}) custom-call(f32[640,2048]{1,0:T(8,128)} %bitcast.7), custom_call_target="tpu_custom_call" | custom-call | flops 1 | bytes 1 | tf_op jit(solution)/shard_map/cast_units/pallas_call | solution.py:120
  10.3 2.6 %collective-permute-start.6 = (bf16[64,640]{1,0:T(8,128)(2,1)S(1)}, bf16[64,640]{1,0:T(8,128)(2,1)S(1)}, u32[]{:S(2)}, u32[]{:S(2)}) collective-permute-start(bf16[64,640]{1,0:T(8,128)(2,1)S(1)} %stack_blocks.2), channel_id=1, source_target_pairs={{0,4},{2,6},{4,0},{6,2},{1,5},{3,7},{5,1},{7,3},{8,12},{10,14},{12... | collective-permute-start | bytes 245768 | tf_op jit(solution)/shard_map/ppermute | solution.py:439
  13.1 0.6 collective-permute-start.5
  13.7 6.7 %cache_attention.1 = (bf16[4,8,32,128]{3,2,1,0:T(8,128)(2,1)S(1)}, f32[4,8,32,128]{3,2,1,0:T(8,128)S(1)}, f32[4,8,32,128]{3,2,1,0:T(8,128)S(1)}) custom-call(s32[8]{0:T(128)S(1)} %copy-done.1, bf16[8,4,2560]{2,1,0:T(4,128)(2,1)} %q, bf16[8,512,512]{2,1,0:T(8,128)(2,1)} %k.1, bf16[8,512,512]{2,1,0:T(8,128)(2,1)} %v.1), custom_call_target="tpu_custom_call" | custom-call | flops 1 | bytes 17500000 | tf_op jit(solution)/shard_map/cache_attention/pallas_call | solution.py:344
  20.5 1.6 %collective-permute-start.7 = (bf16[64,640]{1,0:T(8,128)(2,1)S(1)}, bf16[64,640]{1,0:T(8,128)(2,1)S(1)}, u32[]{:S(2)}, u32[]{:S(2)}) collective-permute-start(bf16[64,640]{1,0:T(8,128)(2,1)S(1)} %stack_blocks.3), channel_id=1, source_target_pairs={{0,2},{2,0},{4,6},{6,4},{1,3},{3,1},{5,7},{7,5},{8,10},{10,8},{12,... | collective-permute-start | bytes 245768 | tf_op jit(solution)/shard_map/ppermute | solution.py:439
  22.1 1.5 %collective-permute-start.3 = (bf16[640,384]{1,0:T(8,128)(2,1)S(1)}, bf16[640,384]{1,0:T(8,128)(2,1)S(1)}, u32[]{:S(2)}, u32[]{:S(2)}) collective-permute-start(bf16[640,384]{1,0:T(8,128)(2,1)S(1)} %get-tuple-element.52.refs_0_), channel_id=1, source_target_pairs={{0,16},{8,24},{16,0},{24,8},{1,17},{9,25},{17,1},{25,9},{2,18},{10... | collective-permute-start | bytes 1474568 | tf_op jit(solution)/shard_map/ppermute | solution.py:439
  23.6 1.4 %collective-permute-done.7.refs_9_.refs_10_.refs_7_.refs_8_ = bf16[64,640]{1,0:T(8,128)(2,1)S(1)} collective-permute-done((bf16[64,640]{1,0:T(8,128)(2,1)S(1)}, bf16[64,640]{1,0:T(8,128)(2,1)S(1)}, u32[]{:S(2)}, u32[]{:S(2)}) %collective-permute-start.7) | collective-permute-done | bytes 81952 | tf_op jit(solution)/shard_map/ppermute | solution.py:439
  25.0 1.3 %collective-permute-done.5.refs_3_ = bf16[640,128]{1,0:T(8,128)(2,1)S(1)} collective-permute-done((bf16[640,128]{1,0:T(8,128)(2,1)S(1)}, bf16[640,128]{1,0:T(8,128)(2,1)S(1)}, u32[]{:S(2)}, u32[]{:S(2)}) %collective-permute-start.5) | collective-permute-done | bytes 163872 | tf_op jit(solution)/shard_map/ppermute | solution.py:439
  27.1 1.2 %collective-permute-done.8.refs_2_ = bf16[320,640]{1,0:T(8,128)(2,1)S(1)} collective-permute-done((bf16[320,640]{1,0:T(8,128)(2,1)S(1)}, bf16[320,640]{1,0:T(8,128)(2,1)S(1)}, u32[]{:S(2)}, u32[]{:S(2)}) %collective-permute-start.8) | collective-permute-done | bytes 409632 | tf_op jit(solution)/shard_map/ppermute | solution.py:439
  28.9 7.9 %adam_project.2 = (f32[640,2048]{1,0:T(8,128)}, f32[640,2048]{1,0:T(8,128)}, f32[640,2048]{1,0:T(8,128)}, bf16[128,640]{1,0:T(8,128)(2,1)S(1)}, f32[128,640]{1,0:T(8,128)S(1)}) custom-call(s32[6]{0:T(128)S(1)} %stack.19.place, bf16[320,640]{1,0:T(8,128)(2,1)S(1)} %get-tuple-element.60.refs_0_, bf16[320,640]{1,0:T(8,128)(2,1)S(1)} %get-tuple-element.61.refs_1_, ...), custom_call_target="tpu_custom_call" | custom-call | flops 1 | bytes 1 | tf_op jit(solution)/shard_map/adam_project/pallas_call | solution.py:268
  37.3 2.2 %collective-permute-start.11 = (bf16[128,640]{1,0:T(8,128)(2,1)S(1)}, bf16[128,640]{1,0:T(8,128)(2,1)S(1)}, u32[]{:S(2)}, u32[]{:S(2)}) collective-permute-start(bf16[128,640]{1,0:T(8,128)(2,1)S(1)} %get-tuple-element.62), channel_id=1, source_target_pairs={{0,1},{1,0},{2,3},{3,2},{4,5},{5,4},{6,7},{7,6},{8,9},{9,8},{10,11... | collective-permute-start | bytes 491528 | tf_op jit(solution)/shard_map/ppermute | solution.py:439
  39.7 5.4 %adam_project.3 = (f32[640,2048]{1,0:T(8,128)}, f32[640,2048]{1,0:T(8,128)}, f32[640,2048]{1,0:T(8,128)}, bf16[128,384]{1,0:T(8,128)(2,1)S(1)}, f32[128,384]{1,0:T(8,128)S(1)}) custom-call(s32[6]{0:T(128)S(1)} %stack.19.place, bf16[640,384]{1,0:T(8,128)(2,1)S(1)} %sum_pieces.7.refs_0_, ...), custom_call_target="tpu_custom_call", output_to_operand_aliasing={{0}: (10, {}), {1}: (11, {}), {2}: (12, {})} | custom-call | flops 1 | bytes 1 | tf_op jit(solution)/shard_map/adam_project/pallas_call | solution.py:268
  45.0 1.4 %collective-permute-start.14 = (bf16[128,384]{1,0:T(8,128)(2,1)S(1)}, bf16[128,384]{1,0:T(8,128)(2,1)S(1)}, u32[]{:S(2)}, u32[]{:S(2)}) collective-permute-start(bf16[128,384]{1,0:T(8,128)(2,1)S(1)} %get-tuple-element.71), channel_id=1, source_target_pairs={{0,1},{1,0},{2,3},{3,2},{4,5},{5,4},{6,7},{7,6},{8,9},{9,8},{10,11... | collective-permute-start | bytes 294920 | tf_op jit(solution)/shard_map/ppermute | solution.py:439
  46.5 1.6 %collective-permute-start.12 = (bf16[64,640]{1,0:T(8,128)(2,1)S(1)}, bf16[64,640]{1,0:T(8,128)(2,1)S(1)}, u32[]{:S(2)}, u32[]{:S(2)}) collective-permute-start(bf16[64,640]{1,0:T(8,128)(2,1)S(1)} %slice.50), channel_id=1, source_target_pairs={{0,2},{2,0},{4,6},{6,4},{1,3},{3,1},{5,7},{7,5},{8,10},{10,8},{12,... | collective-permute-start | bytes 245768 | tf_op jit(solution)/shard_map/ppermute | solution.py:439
  48.1 1.8 %collective-permute-done.14 = bf16[128,384]{1,0:T(8,128)(2,1)S(1)} collective-permute-done((bf16[128,384]{1,0:T(8,128)(2,1)S(1)}, bf16[128,384]{1,0:T(8,128)(2,1)S(1)}, u32[]{:S(2)}, u32[]{:S(2)}) %collective-permute-start.14) | collective-permute-done | bytes 98336 | tf_op jit(solution)/shard_map/ppermute | solution.py:439
  49.9 1.6 %collective-permute-start.15 = (bf16[64,384]{1,0:T(8,128)(2,1)S(1)}, bf16[64,384]{1,0:T(8,128)(2,1)S(1)}, u32[]{:S(2)}, u32[]{:S(2)}) collective-permute-start(bf16[64,384]{1,0:T(8,128)(2,1)S(1)} %slice.51), channel_id=1, source_target_pairs={{0,2},{2,0},{4,6},{6,4},{1,3},{3,1},{5,7},{7,5},{8,10},{10,8},{12,... | collective-permute-start | bytes 147464 | tf_op jit(solution)/shard_map/ppermute | solution.py:439
  51.6 2.7 %collective-permute-start.13 = (bf16[32,640]{1,0:T(8,128)(2,1)S(1)}, bf16[32,640]{1,0:T(8,128)(2,1)S(1)}, u32[]{:S(2)}, u32[]{:S(2)}) collective-permute-start(bf16[32,640]{1,0:T(8,128)(2,1)S(1)} %slice.52), channel_id=1, source_target_pairs={{0,4},{2,6},{4,0},{6,2},{1,5},{3,7},{5,1},{7,3},{8,12},{10,14},{12... | collective-permute-start | bytes 122888 | tf_op jit(solution)/shard_map/ppermute | solution.py:439
  54.3 2.5 %collective-permute-start.16 = (bf16[32,384]{1,0:T(8,128)(2,1)S(1)}, bf16[32,384]{1,0:T(8,128)(2,1)S(1)}, u32[]{:S(2)}, u32[]{:S(2)}) collective-permute-start(bf16[32,384]{1,0:T(8,128)(2,1)S(1)} %slice.53), channel_id=1, source_target_pairs={{0,4},{2,6},{4,0},{6,2},{1,5},{3,7},{5,1},{7,3},{8,12},{10,14},{12... | collective-permute-start | bytes 73736 | tf_op jit(solution)/shard_map/ppermute | solution.py:439
  57.4 1.6 %merge_new.2 = (bf16[8,4,1024]{2,1,0:T(4,128)(2,1)}, bf16[8,4,2560]{2,1,0:T(4,128)(2,1)}) custom-call(bf16[32,640]{1,0:T(8,128)(2,1)S(1)} %collective-permute-done.13.refs_0_, f32[32,640]{1,0:T(8,128)S(1)} %slice.39.refs_1_, f32[32,128]{1,0:T(8,128)S(1)} %get-tuple-element.82.refs_2_.refs_4_, f32[32,128]{1,0:T(8,128)S(1)} %get-tuple-element.83.refs_3_.refs_5_, ...), custom_call_target="tpu_custom_call" | custom-call | flops 1 | bytes 1 | tf_op jit(solution)/shard_map/merge_new/pallas_call | solution.py:424
  59.1 1.6 %merge_new.3 = (bf16[8,4,1024]{2,1,0:T(4,128)(2,1)}, bf16[8,4,2560]{2,1,0:T(4,128)(2,1)}) custom-call(bf16[32,640]{1,0:T(8,128)(2,1)S(1)} %collective-permute-done.13.refs_0_, f32[32,640]{1,0:T(8,128)S(1)} %slice.39.refs_1_, bf16[32,384]{1,0:T(8,128)(2,1)S(1)} %collective-permute-done.16.refs_2_, ...), custom_call_target="tpu_custom_call", output_to_operand_aliasing={{0}: (9, {}), {1}: (10, {})} | custom-call | flops 1 | bytes 1 | tf_op jit(solution)/shard_map/merge_new/pallas_call | solution.py:424
  (45 shorter events, 4.8 us)
Async XLA Ops:
  2.0 5.4 %copy-start = (bf16[8,4,5120]{2,1,0:T(4,128)(2,1)S(1)}, bf16[8,4,5120]{2,1,0:T(4,128)(2,1)}, u32[]{:S(2)}) copy-start(bf16[8,4,5120]{2,1,0:T(4,128)(2,1)} %source) | copy-start | bytes 983044
  2.0 2.2 %collective-permute-start = (bf16[640,512]{1,0:T(8,128)(2,1)S(1)}, bf16[640,512]{1,0:T(8,128)(2,1)S(1)}, u32[]{:S(2)}, u32[]{:S(2)}) collective-permute-start(bf16[640,512]{1,0:T(8,128)(2,1)S(1)} %cast_units.3), channel_id=1, source_target_pairs={{0,8},{8,0},{16,24},{24,16},{1,9},{9,1},{17,25},{25,17},{2,10},{10... | collective-permute-start | bytes 1966088 | tf_op jit(solution)/shard_map/ppermute | solution.py:439
  3.8 9.9 %copy-start.1 = (s32[8]{0:T(128)S(1)}, s32[8]{0:T(128)}, u32[]{:S(2)}) copy-start(s32[8]{0:T(128)} %lens.1) | copy-start | bytes 100
  4.4 22.0 %collective-permute-start.4 = (bf16[640,512]{1,0:T(8,128)(2,1)S(1)}, bf16[640,512]{1,0:T(8,128)(2,1)S(1)}, u32[]{:S(2)}, u32[]{:S(2)}) collective-permute-start(bf16[640,512]{1,0:T(8,128)(2,1)S(1)} %sum_pieces.4.refs_0_), channel_id=1, source_target_pairs={{0,16},{8,24},{16,0},{24,8},{1,17},{9,25},{17,1},{25,9},{2,18},{10... | collective-permute-start | bytes 1966088 | tf_op jit(solution)/shard_map/ppermute | solution.py:439
  9.7 3.2 %collective-permute-start.1 = (bf16[320,512]{1,0:T(8,128)(2,1)S(1)}, bf16[320,512]{1,0:T(8,128)(2,1)S(1)}, u32[]{:S(2)}, u32[]{:S(2)}) collective-permute-start(bf16[320,512]{1,0:T(8,128)(2,1)S(1)} %get-tuple-element.50), channel_id=1, source_target_pairs={{0,8},{8,0},{16,24},{24,16},{1,9},{9,1},{17,25},{25,17},{2,10},{10... | collective-permute-start | bytes 983048 | tf_op jit(solution)/shard_map/ppermute | solution.py:439
  9.8 3.2 %collective-permute-start.2 = (bf16[320,512]{1,0:T(8,128)(2,1)S(1)}, bf16[320,512]{1,0:T(8,128)(2,1)S(1)}, u32[]{:S(2)}, u32[]{:S(2)}) collective-permute-start(bf16[320,512]{1,0:T(8,128)(2,1)S(1)} %get-tuple-element.51), channel_id=1, source_target_pairs={{0,8},{8,0},{16,24},{24,16},{1,9},{9,1},{17,25},{25,17},{2,10},{10... | collective-permute-start | bytes 983048 | tf_op jit(solution)/shard_map/ppermute | solution.py:439
  10.3 10.2 %collective-permute-start.6 = (bf16[64,640]{1,0:T(8,128)(2,1)S(1)}, bf16[64,640]{1,0:T(8,128)(2,1)S(1)}, u32[]{:S(2)}, u32[]{:S(2)}) collective-permute-start(bf16[64,640]{1,0:T(8,128)(2,1)S(1)} %stack_blocks.2), channel_id=1, source_target_pairs={{0,4},{2,6},{4,0},{6,2},{1,5},{3,7},{5,1},{7,3},{8,12},{10,14},{12... | collective-permute-start | bytes 245768 | tf_op jit(solution)/shard_map/ppermute | solution.py:439
  13.1 13.2 %collective-permute-start.5 = (bf16[640,128]{1,0:T(8,128)(2,1)S(1)}, bf16[640,128]{1,0:T(8,128)(2,1)S(1)}, u32[]{:S(2)}, u32[]{:S(2)}) collective-permute-start(bf16[640,128]{1,0:T(8,128)(2,1)S(1)} %get-tuple-element.53.refs_1_), channel_id=1, source_target_pairs={{0,16},{8,24},{16,0},{24,8},{1,17},{9,25},{17,1},{25,9},{2,18},{10... | collective-permute-start | bytes 491528 | tf_op jit(solution)/shard_map/ppermute | solution.py:439
  20.5 4.5 %collective-permute-start.7 = (bf16[64,640]{1,0:T(8,128)(2,1)S(1)}, bf16[64,640]{1,0:T(8,128)(2,1)S(1)}, u32[]{:S(2)}, u32[]{:S(2)}) collective-permute-start(bf16[64,640]{1,0:T(8,128)(2,1)S(1)} %stack_blocks.3), channel_id=1, source_target_pairs={{0,2},{2,0},{4,6},{6,4},{1,3},{3,1},{5,7},{7,5},{8,10},{10,8},{12,... | collective-permute-start | bytes 245768 | tf_op jit(solution)/shard_map/ppermute | solution.py:439
  22.1 14.7 %collective-permute-start.3 = (bf16[640,384]{1,0:T(8,128)(2,1)S(1)}, bf16[640,384]{1,0:T(8,128)(2,1)S(1)}, u32[]{:S(2)}, u32[]{:S(2)}) collective-permute-start(bf16[640,384]{1,0:T(8,128)(2,1)S(1)} %get-tuple-element.52.refs_0_), channel_id=1, source_target_pairs={{0,16},{8,24},{16,0},{24,8},{1,17},{9,25},{17,1},{25,9},{2,18},{10... | collective-permute-start | bytes 1474568 | tf_op jit(solution)/shard_map/ppermute | solution.py:439
  26.5 1.8 %collective-permute-start.8 = (bf16[320,640]{1,0:T(8,128)(2,1)S(1)}, bf16[320,640]{1,0:T(8,128)(2,1)S(1)}, u32[]{:S(2)}, u32[]{:S(2)}) collective-permute-start(bf16[320,640]{1,0:T(8,128)(2,1)S(1)} %get-tuple-element.60.refs_0_), channel_id=1, source_target_pairs={{0,8},{8,0},{16,24},{24,16},{1,9},{9,1},{17,25},{25,17},{2,10},{10... | collective-permute-start | bytes 1228808 | tf_op jit(solution)/shard_map/ppermute | solution.py:439
  26.6 2.3 %collective-permute-start.9 = (bf16[320,640]{1,0:T(8,128)(2,1)S(1)}, bf16[320,640]{1,0:T(8,128)(2,1)S(1)}, u32[]{:S(2)}, u32[]{:S(2)}) collective-permute-start(bf16[320,640]{1,0:T(8,128)(2,1)S(1)} %get-tuple-element.61.refs_1_), channel_id=1, source_target_pairs={{0,8},{8,0},{16,24},{24,16},{1,9},{9,1},{17,25},{25,17},{2,10},{10... | collective-permute-start | bytes 1228808 | tf_op jit(solution)/shard_map/ppermute | solution.py:439
  37.0 2.7 %collective-permute-start.10 = (bf16[640,384]{1,0:T(8,128)(2,1)S(1)}, bf16[640,384]{1,0:T(8,128)(2,1)S(1)}, u32[]{:S(2)}, u32[]{:S(2)}) collective-permute-start(bf16[640,384]{1,0:T(8,128)(2,1)S(1)} %sum_pieces.7.refs_0_), channel_id=1, source_target_pairs={{0,8},{8,0},{16,24},{24,16},{1,9},{9,1},{17,25},{25,17},{2,10},{10... | collective-permute-start | bytes 1474568 | tf_op jit(solution)/shard_map/ppermute | solution.py:439
  37.3 9.1 %collective-permute-start.11 = (bf16[128,640]{1,0:T(8,128)(2,1)S(1)}, bf16[128,640]{1,0:T(8,128)(2,1)S(1)}, u32[]{:S(2)}, u32[]{:S(2)}) collective-permute-start(bf16[128,640]{1,0:T(8,128)(2,1)S(1)} %get-tuple-element.62), channel_id=1, source_target_pairs={{0,1},{1,0},{2,3},{3,2},{4,5},{5,4},{6,7},{7,6},{8,9},{9,8},{10,11... | collective-permute-start | bytes 491528 | tf_op jit(solution)/shard_map/ppermute | solution.py:439
  45.0 4.8 %collective-permute-start.14 = (bf16[128,384]{1,0:T(8,128)(2,1)S(1)}, bf16[128,384]{1,0:T(8,128)(2,1)S(1)}, u32[]{:S(2)}, u32[]{:S(2)}) collective-permute-start(bf16[128,384]{1,0:T(8,128)(2,1)S(1)} %get-tuple-element.71), channel_id=1, source_target_pairs={{0,1},{1,0},{2,3},{3,2},{4,5},{5,4},{6,7},{7,6},{8,9},{9,8},{10,11... | collective-permute-start | bytes 294920 | tf_op jit(solution)/shard_map/ppermute | solution.py:439
  46.5 5.1 %collective-permute-start.12 = (bf16[64,640]{1,0:T(8,128)(2,1)S(1)}, bf16[64,640]{1,0:T(8,128)(2,1)S(1)}, u32[]{:S(2)}, u32[]{:S(2)}) collective-permute-start(bf16[64,640]{1,0:T(8,128)(2,1)S(1)} %slice.50), channel_id=1, source_target_pairs={{0,2},{2,0},{4,6},{6,4},{1,3},{3,1},{5,7},{7,5},{8,10},{10,8},{12,... | collective-permute-start | bytes 245768 | tf_op jit(solution)/shard_map/ppermute | solution.py:439
  49.9 4.3 %collective-permute-start.15 = (bf16[64,384]{1,0:T(8,128)(2,1)S(1)}, bf16[64,384]{1,0:T(8,128)(2,1)S(1)}, u32[]{:S(2)}, u32[]{:S(2)}) collective-permute-start(bf16[64,384]{1,0:T(8,128)(2,1)S(1)} %slice.51), channel_id=1, source_target_pairs={{0,2},{2,0},{4,6},{6,4},{1,3},{3,1},{5,7},{7,5},{8,10},{10,8},{12,... | collective-permute-start | bytes 147464 | tf_op jit(solution)/shard_map/ppermute | solution.py:439
  51.6 5.8 %collective-permute-start.13 = (bf16[32,640]{1,0:T(8,128)(2,1)S(1)}, bf16[32,640]{1,0:T(8,128)(2,1)S(1)}, u32[]{:S(2)}, u32[]{:S(2)}) collective-permute-start(bf16[32,640]{1,0:T(8,128)(2,1)S(1)} %slice.52), channel_id=1, source_target_pairs={{0,4},{2,6},{4,0},{6,2},{1,5},{3,7},{5,1},{7,3},{8,12},{10,14},{12... | collective-permute-start | bytes 122888 | tf_op jit(solution)/shard_map/ppermute | solution.py:439
  54.3 4.8 %collective-permute-start.16 = (bf16[32,384]{1,0:T(8,128)(2,1)S(1)}, bf16[32,384]{1,0:T(8,128)(2,1)S(1)}, u32[]{:S(2)}, u32[]{:S(2)}) collective-permute-start(bf16[32,384]{1,0:T(8,128)(2,1)S(1)} %slice.53), channel_id=1, source_target_pairs={{0,4},{2,6},{4,0},{6,2},{1,5},{3,7},{5,1},{7,3},{8,12},{10,14},{12... | collective-permute-start | bytes 73736 | tf_op jit(solution)/shard_map/ppermute | solution.py:439

commit v8 on v7

--- a/solution.py
+++ b/solution.py
@@ -82,6 +82,10 @@
     if rows % HD:
         return [(0, rows)]
     return [(r, min(r + 2 * HD, rows)) for r in range(0, rows, 2 * HD)]
+
+
+def held_from(rows):
+    return slab_ends(rows)[-2:][0][0]
 
 
 def cast_kernel(wanted, n_units, source, *refs):
@@ -202,7 +206,7 @@
     return jnp.concatenate([p[...] for p in pieces], axis=axis)
 
 
-def adam_kernel(first, n, n_mine, n_partner, tok_places, previous, place, *refs):
+def adam_kernel(first, n, n_mine, n_partner, tok_places, previous, hold, place, *refs):
     refs = list(refs)
     take = lambda n: [refs.pop(0) for _ in range(n)]
     pieces = take(n_mine + n_partner)
@@ -210,9 +214,12 @@
     toks = take(len(tok_places))
     take(3 * previous)
     updated = take(3)
-    sent, kept, in_sems, out_sems, buffer = refs
-
-    slabs = [(part, slice(*ends)) for part in range(2) for ends in slab_ends(buffer.shape[2])]
+    sent, kept = take(2)
+    held = take(3 * hold)
+    in_sems, out_sems, buffer = refs
+
+    rows = buffer.shape[2]
+    slabs = [(part, slice(*ends)) for part in range(2) for ends in slab_ends(rows)]
     columns = [columns_at(place, part, first, n) for part in range(2)]
     incoming = []
     for i, (part, at) in enumerate(slabs):
@@ -236,6 +243,9 @@
         gradient = totals[part][at].astype(jnp.float32)
         results = adam_update(buffer[0, part, at], buffer[1, part, at], buffer[2, part, at], gradient)
         for q in range(3):
+            if hold and part == 1 and at.start >= held_from(rows):
+                held[q][at.start - held_from(rows) : at.stop - held_from(rows)] = results[q]
+                continue
             buffer[q, part, at] = results[q]
             outgoing.append(
                 pltpu.make_async_copy(
@@ -252,7 +262,7 @@
         copy.wait()
 
 
-def adam_units(place, total, state, toks, first, n, previous):
+def adam_units(place, total, state, toks, first, n, previous, hold):
     mine, partner = total
     rows, width = state[0].shape
     n_slabs = 2 * len(slab_ends(rows))
@@ -267,13 +277,13 @@
     shape = (n_tokens, n * HD)
     out = pl.pallas_call(
         functools.partial(
-            adam_kernel, first, n, len(mine), len(partner), [at for _, at in toks], previous is not None
+            adam_kernel, first, n, len(mine), len(partner), [at for _, at in toks], previous is not None, hold
         ),
         grid_spec=pltpu.PrefetchScalarGridSpec(
             num_scalar_prefetch=1,
             grid=(),
             in_specs=in_specs,
-            out_specs=[ANYWHERE] * 3 + [VMEM] * 2,
+            out_specs=[ANYWHERE] * 3 + [VMEM] * (2 + 3 * hold),
             scratch_shapes=[
                 pltpu.SemaphoreType.DMA((3, n_slabs)),
                 pltpu.SemaphoreType.DMA((3, n_slabs)),
@@ -281,13 +291,48 @@
             ],
         ),
         out_shape=[jax.ShapeDtypeStruct((rows, width), jnp.float32)] * 3
-        + [jax.ShapeDtypeStruct(shape, jnp.bfloat16), jax.ShapeDtypeStruct(shape, jnp.float32)],
+        + [jax.ShapeDtypeStruct(shape, jnp.bfloat16), jax.ShapeDtypeStruct(shape, jnp.float32)]
+        + [jax.ShapeDtypeStruct((rows - held_from(rows), n * HD), jnp.float32)] * (3 * hold),
         input_output_aliases=aliases,
         compiler_params=pltpu.CompilerParams(vmem_limit_bytes=15 * MIB),
         cost_estimate=cost(0),
         name="adam_project",
     )(place, *operands)
-    return out[:3], out[3:]
+    return out[:3], out[3:5], out[5:]
+
+
+def write_kernel(first, n, place, *refs):
+    held, outs, sems = refs[:3], refs[6:9], refs[9]
+    copies = [
+        pltpu.make_async_copy(
+            held[q],
+            outs[q].at[outs[q].shape[0] - held[q].shape[0] :, columns_at(place, 1, first, n)],
+            sems.at[q],
+        )
+        for q in range(3)
+    ]
+    for copy in copies:
+        copy.start()
+    for copy in copies:
+        copy.wait()
+
+
+def write_held(place, held, previous, first, n):
+    return pl.pallas_call(
+        functools.partial(write_kernel, first, n),
+        grid_spec=pltpu.PrefetchScalarGridSpec(
+            num_scalar_prefetch=1,
+            grid=(),
+            in_specs=[VMEM] * 3 + [ANYWHERE] * 3,
+            out_specs=[ANYWHERE] * 3,
+            scratch_shapes=[pltpu.SemaphoreType.DMA((3,))],
+        ),
+        out_shape=[jax.ShapeDtypeStruct(p.shape, p.dtype) for p in previous],
+        input_output_aliases={4: 0, 5: 1, 6: 2},
+        compiler_params=pltpu.CompilerParams(vmem_limit_bytes=6 * MIB),
+        cost_estimate=cost(2),
+        name="write_held",
+    )(place, *held, *previous)
 
 
 SLOT = 32
@@ -517,11 +562,12 @@
         return one, [swap(p, "group", 1) for p in one]
 
     both = total(early, crossed, N_PIECES, *step)
-    updated, (sent, kept) = adam_units(place, both, state, toks, 0, n_early, None)
+    updated, (sent, kept), _ = adam_units(place, both, state, toks, 0, n_early, None, False)
     moving = [(swap(sent, "tp", 1), kept)]
     both = total([last], [crossed_last], 1, sent)
-    updated, (sent, kept) = adam_units(place, both, state, toks, n_early, n_late, updated)
-    moving.append((swap(sent, "tp", 1), kept))
+    updated, (sent, kept), held = adam_units(place, both, state, toks, n_early, n_late, updated, True)
+    updated = write_held(after(place, sent), held, updated, n_early, n_late)
+    moving.append((after(swap(sent, "tp", 1), updated[0]), kept))
     distance = 1
     while distance < fsdp_count:
         for f, (got, kept) in enumerate(moving):

time: 60.9 us -> 60.3 us (level)
  waiting for transfers between devices: 7.36 us -> 5.57 us
  Pallas kernels: 28.7 us -> 29.9 us
    ppermute x17, waiting for transfers between devices: 7.36 us -> 5.57 us  [swap(): return lax.ppermute(array, axis, [(i, i ^ bit) for i in range(size)])]
    pallas_call x0 -> x1, Pallas kernels: none -> 1.77 us  [write_held(): pl.pallas_call(functools.partial(write_kernel, first, n), grid_spec=pltpu...]
  transfers between devices with their start and end apart: 17 -> 17, of which waited for: 8 -> 7; matrix products, arithmetic and copies ran while one was open for 1% -> 1% of each run, Pallas kernels for 42% -> 45%
where the time goes in v8:
time: 60.3 us; the launch traced here: 60 us
  Pallas kernels  29.9 us (50%)
  starting transfers between devices  23.1 us (38%)
  waiting for transfers between devices  5.57 us (9%)
  between operations  0.86 us (1%)
    ppermute x17, starting transfers between devices, swap(): return lax.ppermute(array, axis, [(i, i ^ bit) for i in range(size)])  23.1 us
    pallas_call x2, Pallas kernels, adam_units(): pl.pallas_call(functools.partial(adam_kernel, first, n, len(mine), len(pa...  12.7 us
    pallas_call x1, Pallas kernels, cache_attention(): pl.pallas_call(functools.partial(cache_kernel, heads, first), grid_spec=p...  6.71 us
    ppermute x17, waiting for transfers between devices, swap(): return lax.ppermute(array, axis, [(i, i ^ bit) for i in range(size)])  5.57 us
    pallas_call x3, Pallas kernels, cast_units(): pl.pallas_call(functools.partial(cast_kernel, wanted, n_units), in_specs=...  4.38 us
    pallas_call x2, Pallas kernels, merge(): pl.pallas_call(functools.partial(merge_kernel, [fold[2] for fold in folds...  3.12 us
    pallas_call x1, Pallas kernels, write_held(): pl.pallas_call(functools.partial(write_kernel, first, n), grid_spec=pltpu...  1.77 us
  transfers between devices with their start and end apart: 17, of which 7 were waited for; matrix products, arithmetic and copies ran while one was open for 1% of the time, Pallas kernels for 45%

profile of v8, /device:TPU:0, one launch (start us, length us, event | category | flops | bytes accessed | tf_op | source)
XLA Modules:
  0.0 60.0 jit_solution(2978596188197787681)
XLA Ops:
  0.6 1.3 %cast_units.3 = bf16[640,512]{1,0:T(8,128)(2,1)S(1)} custom-call(f32[640,2048]{1,0:T(8,128)} %bitcast.5), custom_call_target="tpu_custom_call" | custom-call | flops 1 | bytes 1 | tf_op jit(solution)/shard_map/cast_units/pallas_call | solution.py:124
  2.5 1.3 %cast_units.4.refs_0_ = bf16[640,512]{1,0:T(8,128)(2,1)S(1)} custom-call(f32[640,2048]{1,0:T(8,128)} %bitcast.6), custom_call_target="tpu_custom_call" | custom-call | flops 1 | bytes 1 | tf_op jit(solution)/shard_map/cast_units/pallas_call | solution.py:124
  4.4 2.9 %collective-permute-start.4 = (bf16[640,512]{1,0:T(8,128)(2,1)S(1)}, bf16[640,512]{1,0:T(8,128)(2,1)S(1)}, u32[]{:S(2)}, u32[]{:S(2)}) collective-permute-start(bf16[640,512]{1,0:T(8,128)(2,1)S(1)} %sum_pieces.4.refs_0_), channel_id=1, source_target_pairs={{0,16},{8,24},{16,0},{24,8},{1,17},{9,25},{17,1},{25,9},{2,18},{10... | collective-permute-start | bytes 1966088 | tf_op jit(solution)/shard_map/ppermute | solution.py:484
  7.4 0.6 token_pieces.1
  8.0 1.8 %cast_units.5 = (bf16[320,512]{1,0:T(8,128)(2,1)S(1)}, bf16[320,512]{1,0:T(8,128)(2,1)S(1)}, bf16[640,512]{1,0:T(8,128)(2,1)S(1)}) custom-call(f32[640,2048]{1,0:T(8,128)} %bitcast.7), custom_call_target="tpu_custom_call" | custom-call | flops 1 | bytes 1 | tf_op jit(solution)/shard_map/cast_units/pallas_call | solution.py:124
  10.3 2.6 %collective-permute-start.6 = (bf16[64,640]{1,0:T(8,128)(2,1)S(1)}, bf16[64,640]{1,0:T(8,128)(2,1)S(1)}, u32[]{:S(2)}, u32[]{:S(2)}) collective-permute-start(bf16[64,640]{1,0:T(8,128)(2,1)S(1)} %stack_blocks.2), channel_id=1, source_target_pairs={{0,4},{2,6},{4,0},{6,2},{1,5},{3,7},{5,1},{7,3},{8,12},{10,14},{12... | collective-permute-start | bytes 245768 | tf_op jit(solution)/shard_map/ppermute | solution.py:484
  13.1 0.6 collective-permute-start.5
  13.7 6.7 %cache_attention.1 = (bf16[4,8,32,128]{3,2,1,0:T(8,128)(2,1)S(1)}, f32[4,8,32,128]{3,2,1,0:T(8,128)S(1)}, f32[4,8,32,128]{3,2,1,0:T(8,128)S(1)}) custom-call(s32[8]{0:T(128)S(1)} %copy-done.1, bf16[8,4,2560]{2,1,0:T(4,128)(2,1)} %q, bf16[8,512,512]{2,1,0:T(8,128)(2,1)} %k.1, bf16[8,512,512]{2,1,0:T(8,128)(2,1)} %v.1), custom_call_target="tpu_custom_call" | custom-call | flops 1 | bytes 17500000 | tf_op jit(solution)/shard_map/cache_attention/pallas_call | solution.py:389
  20.5 1.6 %collective-permute-start.7 = (bf16[64,640]{1,0:T(8,128)(2,1)S(1)}, bf16[64,640]{1,0:T(8,128)(2,1)S(1)}, u32[]{:S(2)}, u32[]{:S(2)}) collective-permute-start(bf16[64,640]{1,0:T(8,128)(2,1)S(1)} %stack_blocks.3), channel_id=1, source_target_pairs={{0,2},{2,0},{4,6},{6,4},{1,3},{3,1},{5,7},{7,5},{8,10},{10,8},{12,... | collective-permute-start | bytes 245768 | tf_op jit(solution)/shard_map/ppermute | solution.py:484
  22.1 1.5 %collective-permute-start.3 = (bf16[640,384]{1,0:T(8,128)(2,1)S(1)}, bf16[640,384]{1,0:T(8,128)(2,1)S(1)}, u32[]{:S(2)}, u32[]{:S(2)}) collective-permute-start(bf16[640,384]{1,0:T(8,128)(2,1)S(1)} %get-tuple-element.60.refs_0_), channel_id=1, source_target_pairs={{0,16},{8,24},{16,0},{24,8},{1,17},{9,25},{17,1},{25,9},{2,18},{10... | collective-permute-start | bytes 1474568 | tf_op jit(solution)/shard_map/ppermute | solution.py:484
  23.6 1.4 %collective-permute-done.7.refs_9_.refs_10_.refs_7_.refs_8_ = bf16[64,640]{1,0:T(8,128)(2,1)S(1)} collective-permute-done((bf16[64,640]{1,0:T(8,128)(2,1)S(1)}, bf16[64,640]{1,0:T(8,128)(2,1)S(1)}, u32[]{:S(2)}, u32[]{:S(2)}) %collective-permute-start.7) | collective-permute-done | bytes 81952 | tf_op jit(solution)/shard_map/ppermute | solution.py:484
  25.0 1.3 %collective-permute-done.5.refs_3_ = bf16[640,128]{1,0:T(8,128)(2,1)S(1)} collective-permute-done((bf16[640,128]{1,0:T(8,128)(2,1)S(1)}, bf16[640,128]{1,0:T(8,128)(2,1)S(1)}, u32[]{:S(2)}, u32[]{:S(2)}) %collective-permute-start.5) | collective-permute-done | bytes 163872 | tf_op jit(solution)/shard_map/ppermute | solution.py:484
  27.1 1.2 %collective-permute-done.8.refs_2_ = bf16[320,640]{1,0:T(8,128)(2,1)S(1)} collective-permute-done((bf16[320,640]{1,0:T(8,128)(2,1)S(1)}, bf16[320,640]{1,0:T(8,128)(2,1)S(1)}, u32[]{:S(2)}, u32[]{:S(2)}) %collective-permute-start.8) | collective-permute-done | bytes 409632 | tf_op jit(solution)/shard_map/ppermute | solution.py:484
  28.9 7.9 %adam_project.2 = (f32[640,2048]{1,0:T(8,128)}, f32[640,2048]{1,0:T(8,128)}, f32[640,2048]{1,0:T(8,128)}, bf16[128,640]{1,0:T(8,128)(2,1)S(1)}, f32[128,640]{1,0:T(8,128)S(1)}) custom-call(s32[6]{0:T(128)S(1)} %stack.19.place, bf16[320,640]{1,0:T(8,128)(2,1)S(1)} %get-tuple-element.68.refs_0_, bf16[320,640]{1,0:T(8,128)(2,1)S(1)} %get-tuple-element.69.refs_1_, ...), custom_call_target="tpu_custom_call" | custom-call | flops 1 | bytes 1 | tf_op jit(solution)/shard_map/adam_project/pallas_call | solution.py:278
  37.3 2.2 %collective-permute-start.11 = (bf16[128,640]{1,0:T(8,128)(2,1)S(1)}, bf16[128,640]{1,0:T(8,128)(2,1)S(1)}, u32[]{:S(2)}, u32[]{:S(2)}) collective-permute-start(bf16[128,640]{1,0:T(8,128)(2,1)S(1)} %get-tuple-element.70), channel_id=1, source_target_pairs={{0,1},{1,0},{2,3},{3,2},{4,5},{5,4},{6,7},{7,6},{8,9},{9,8},{10,11... | collective-permute-start | bytes 491528 | tf_op jit(solution)/shard_map/ppermute | solution.py:484
  39.7 4.8 %adam_project.3 = (f32[640,2048]{1,0:T(8,128)}, f32[640,2048]{1,0:T(8,128)}, f32[640,2048]{1,0:T(8,128)}, bf16[128,384]{1,0:T(8,128)(2,1)S(1)}, f32[128,384]{1,0...) custom-call(s32[6]{0:T(128)S(1)} %stack.19.place, ...), custom_call_target="tpu_custom_call", output_to_operand_aliasing={{0}: (10, {}), {1}: (11, {}), {2}: (12, {})} | custom-call | flops 1 | bytes 1 | tf_op jit(solution)/shard_map/adam_project/pallas_call | solution.py:278
  44.4 1.4 %collective-permute-start.14 = (bf16[128,384]{1,0:T(8,128)(2,1)S(1)}, bf16[128,384]{1,0:T(8,128)(2,1)S(1)}, u32[]{:S(2)}, u32[]{:S(2)}) collective-permute-start(bf16[128,384]{1,0:T(8,128)(2,1)S(1)} %get-tuple-element.75), channel_id=1, source_target_pairs={{0,1},{1,0},{2,3},{3,2},{4,5},{5,4},{6,7},{7,6},{8,9},{9,8},{10,11... | collective-permute-start | bytes 294920 | tf_op jit(solution)/shard_map/ppermute | solution.py:484
  45.9 1.6 %collective-permute-start.12 = (bf16[64,640]{1,0:T(8,128)(2,1)S(1)}, bf16[64,640]{1,0:T(8,128)(2,1)S(1)}, u32[]{:S(2)}, u32[]{:S(2)}) collective-permute-start(bf16[64,640]{1,0:T(8,128)(2,1)S(1)} %slice.50), channel_id=1, source_target_pairs={{0,2},{2,0},{4,6},{6,4},{1,3},{3,1},{5,7},{7,5},{8,10},{10,8},{12,... | collective-permute-start | bytes 245768 | tf_op jit(solution)/shard_map/ppermute | solution.py:484
  47.5 1.8 %write_held.1 = (f32[640,2048]{1,0:T(8,128)}, f32[640,2048]{1,0:T(8,128)}, f32[640,2048]{1,0:T(8,128)}) custom-call(s32[6]{0:T(128)S(1)} %stack.19.place, f32[384,384]{1,0:T(8,128)S(1)} %get-tuple-element.77.refs_0_, f32[384,384]{1,0:T(8,128)S(1)} %get-tuple-element.78.refs_1_, ...), custom_call_target="tpu_custom_call", output_to_operand_aliasing={{0}: (4, {}), {1}: (5, {}), {2}: (6, {})} | custom-call | flops 1 | bytes 5000000 | tf_op jit(solution)/shard_map/write_held/pallas_call | solution.py:321
  49.3 1.6 %collective-permute-start.15 = (bf16[64,384]{1,0:T(8,128)(2,1)S(1)}, bf16[64,384]{1,0:T(8,128)(2,1)S(1)}, u32[]{:S(2)}, u32[]{:S(2)}) collective-permute-start(bf16[64,384]{1,0:T(8,128)(2,1)S(1)} %slice.51), channel_id=1, source_target_pairs={{0,2},{2,0},{4,6},{6,4},{1,3},{3,1},{5,7},{7,5},{8,10},{10,8},{12,... | collective-permute-start | bytes 147464 | tf_op jit(solution)/shard_map/ppermute | solution.py:484
  51.0 2.7 %collective-permute-start.13 = (bf16[32,640]{1,0:T(8,128)(2,1)S(1)}, bf16[32,640]{1,0:T(8,128)(2,1)S(1)}, u32[]{:S(2)}, u32[]{:S(2)}) collective-permute-start(bf16[32,640]{1,0:T(8,128)(2,1)S(1)} %slice.52), channel_id=1, source_target_pairs={{0,4},{2,6},{4,0},{6,2},{1,5},{3,7},{5,1},{7,3},{8,12},{10,14},{12... | collective-permute-start | bytes 122888 | tf_op jit(solution)/shard_map/ppermute | solution.py:484
  53.7 2.5 %collective-permute-start.16 = (bf16[32,384]{1,0:T(8,128)(2,1)S(1)}, bf16[32,384]{1,0:T(8,128)(2,1)S(1)}, u32[]{:S(2)}, u32[]{:S(2)}) collective-permute-start(bf16[32,384]{1,0:T(8,128)(2,1)S(1)} %slice.53), channel_id=1, source_target_pairs={{0,4},{2,6},{4,0},{6,2},{1,5},{3,7},{5,1},{7,3},{8,12},{10,14},{12... | collective-permute-start | bytes 73736 | tf_op jit(solution)/shard_map/ppermute | solution.py:484
  56.8 1.6 %merge_new.2 = (bf16[8,4,1024]{2,1,0:T(4,128)(2,1)}, bf16[8,4,2560]{2,1,0:T(4,128)(2,1)}) custom-call(bf16[32,640]{1,0:T(8,128)(2,1)S(1)} %collective-permute-done.13.refs_0_, f32[32,640]{1,0:T(8,128)S(1)} %slice.39.refs_1_, f32[32,128]{1,0:T(8,128)S(1)} %get-tuple-element.98.refs_2_.refs_4_, f32[32,128]{1,0:T(8,128)S(1)} %get-tuple-element.99.refs_3_.refs_5_, ...), custom_call_target="tpu_custom_call" | custom-call | flops 1 | bytes 1 | tf_op jit(solution)/shard_map/merge_new/pallas_call | solution.py:469
  58.5 1.6 %merge_new.3 = (bf16[8,4,1024]{2,1,0:T(4,128)(2,1)}, bf16[8,4,2560]{2,1,0:T(4,128)(2,1)}) custom-call(bf16[32,640]{1,0:T(8,128)(2,1)S(1)} %collective-permute-done.13.refs_0_, f32[32,640]{1,0:T(8,128)S(1)} %slice.39.refs_1_, bf16[32,384]{1,0:T(8,128)(2,1)S(1)} %collective-permute-done.16.refs_2_, ...), custom_call_target="tpu_custom_call", output_to_operand_aliasing={{0}: (9, {}), {1}: (10, {})} | custom-call | flops 1 | bytes 1 | tf_op jit(solution)/shard_map/merge_new/pallas_call | solution.py:469
  (46 shorter events, 4.7 us)
Async XLA Ops:
  2.0 5.4 %copy-start = (bf16[8,4,5120]{2,1,0:T(4,128)(2,1)S(1)}, bf16[8,4,5120]{2,1,0:T(4,128)(2,1)}, u32[]{:S(2)}) copy-start(bf16[8,4,5120]{2,1,0:T(4,128)(2,1)} %source) | copy-start | bytes 983044
  2.0 2.2 %collective-permute-start = (bf16[640,512]{1,0:T(8,128)(2,1)S(1)}, bf16[640,512]{1,0:T(8,128)(2,1)S(1)}, u32[]{:S(2)}, u32[]{:S(2)}) collective-permute-start(bf16[640,512]{1,0:T(8,128)(2,1)S(1)} %cast_units.3), channel_id=1, source_target_pairs={{0,8},{8,0},{16,24},{24,16},{1,9},{9,1},{17,25},{25,17},{2,10},{10... | collective-permute-start | bytes 1966088 | tf_op jit(solution)/shard_map/ppermute | solution.py:484
  3.8 9.9 %copy-start.1 = (s32[8]{0:T(128)S(1)}, s32[8]{0:T(128)}, u32[]{:S(2)}) copy-start(s32[8]{0:T(128)} %lens.1) | copy-start | bytes 100
  4.4 22.0 %collective-permute-start.4 = (bf16[640,512]{1,0:T(8,128)(2,1)S(1)}, bf16[640,512]{1,0:T(8,128)(2,1)S(1)}, u32[]{:S(2)}, u32[]{:S(2)}) collective-permute-start(bf16[640,512]{1,0:T(8,128)(2,1)S(1)} %sum_pieces.4.refs_0_), channel_id=1, source_target_pairs={{0,16},{8,24},{16,0},{24,8},{1,17},{9,25},{17,1},{25,9},{2,18},{10... | collective-permute-start | bytes 1966088 | tf_op jit(solution)/shard_map/ppermute | solution.py:484
  9.7 3.2 %collective-permute-start.1 = (bf16[320,512]{1,0:T(8,128)(2,1)S(1)}, bf16[320,512]{1,0:T(8,128)(2,1)S(1)}, u32[]{:S(2)}, u32[]{:S(2)}) collective-permute-start(bf16[320,512]{1,0:T(8,128)(2,1)S(1)} %get-tuple-element.58), channel_id=1, source_target_pairs={{0,8},{8,0},{16,24},{24,16},{1,9},{9,1},{17,25},{25,17},{2,10},{10... | collective-permute-start | bytes 983048 | tf_op jit(solution)/shard_map/ppermute | solution.py:484
  9.8 3.2 %collective-permute-start.2 = (bf16[320,512]{1,0:T(8,128)(2,1)S(1)}, bf16[320,512]{1,0:T(8,128)(2,1)S(1)}, u32[]{:S(2)}, u32[]{:S(2)}) collective-permute-start(bf16[320,512]{1,0:T(8,128)(2,1)S(1)} %get-tuple-element.59), channel_id=1, source_target_pairs={{0,8},{8,0},{16,24},{24,16},{1,9},{9,1},{17,25},{25,17},{2,10},{10... | collective-permute-start | bytes 983048 | tf_op jit(solution)/shard_map/ppermute | solution.py:484
  10.3 10.2 %collective-permute-start.6 = (bf16[64,640]{1,0:T(8,128)(2,1)S(1)}, bf16[64,640]{1,0:T(8,128)(2,1)S(1)}, u32[]{:S(2)}, u32[]{:S(2)}) collective-permute-start(bf16[64,640]{1,0:T(8,128)(2,1)S(1)} %stack_blocks.2), channel_id=1, source_target_pairs={{0,4},{2,6},{4,0},{6,2},{1,5},{3,7},{5,1},{7,3},{8,12},{10,14},{12... | collective-permute-start | bytes 245768 | tf_op jit(solution)/shard_map/ppermute | solution.py:484
  13.1 13.2 %collective-permute-start.5 = (bf16[640,128]{1,0:T(8,128)(2,1)S(1)}, bf16[640,128]{1,0:T(8,128)(2,1)S(1)}, u32[]{:S(2)}, u32[]{:S(2)}) collective-permute-start(bf16[640,128]{1,0:T(8,128)(2,1)S(1)} %get-tuple-element.61.refs_1_), channel_id=1, source_target_pairs={{0,16},{8,24},{16,0},{24,8},{1,17},{9,25},{17,1},{25,9},{2,18},{10... | collective-permute-start | bytes 491528 | tf_op jit(solution)/shard_map/ppermute | solution.py:484
  20.5 4.5 %collective-permute-start.7 = (bf16[64,640]{1,0:T(8,128)(2,1)S(1)}, bf16[64,640]{1,0:T(8,128)(2,1)S(1)}, u32[]{:S(2)}, u32[]{:S(2)}) collective-permute-start(bf16[64,640]{1,0:T(8,128)(2,1)S(1)} %stack_blocks.3), channel_id=1, source_target_pairs={{0,2},{2,0},{4,6},{6,4},{1,3},{3,1},{5,7},{7,5},{8,10},{10,8},{12,... | collective-permute-start | bytes 245768 | tf_op jit(solution)/shard_map/ppermute | solution.py:484
  22.1 14.7 %collective-permute-start.3 = (bf16[640,384]{1,0:T(8,128)(2,1)S(1)}, bf16[640,384]{1,0:T(8,128)(2,1)S(1)}, u32[]{:S(2)}, u32[]{:S(2)}) collective-permute-start(bf16[640,384]{1,0:T(8,128)(2,1)S(1)} %get-tuple-element.60.refs_0_), channel_id=1, source_target_pairs={{0,16},{8,24},{16,0},{24,8},{1,17},{9,25},{17,1},{25,9},{2,18},{10... | collective-permute-start | bytes 1474568 | tf_op jit(solution)/shard_map/ppermute | solution.py:484
  26.5 1.8 %collective-permute-start.8 = (bf16[320,640]{1,0:T(8,128)(2,1)S(1)}, bf16[320,640]{1,0:T(8,128)(2,1)S(1)}, u32[]{:S(2)}, u32[]{:S(2)}) collective-permute-start(bf16[320,640]{1,0:T(8,128)(2,1)S(1)} %get-tuple-element.68.refs_0_), channel_id=1, source_target_pairs={{0,8},{8,0},{16,24},{24,16},{1,9},{9,1},{17,25},{25,17},{2,10},{10... | collective-permute-start | bytes 1228808 | tf_op jit(solution)/shard_map/ppermute | solution.py:484
  26.6 2.3 %collective-permute-start.9 = (bf16[320,640]{1,0:T(8,128)(2,1)S(1)}, bf16[320,640]{1,0:T(8,128)(2,1)S(1)}, u32[]{:S(2)}, u32[]{:S(2)}) collective-permute-start(bf16[320,640]{1,0:T(8,128)(2,1)S(1)} %get-tuple-element.69.refs_1_), channel_id=1, source_target_pairs={{0,8},{8,0},{16,24},{24,16},{1,9},{9,1},{17,25},{25,17},{2,10},{10... | collective-permute-start | bytes 1228808 | tf_op jit(solution)/shard_map/ppermute | solution.py:484
  37.0 2.7 %collective-permute-start.10 = (bf16[640,384]{1,0:T(8,128)(2,1)S(1)}, bf16[640,384]{1,0:T(8,128)(2,1)S(1)}, u32[]{:S(2)}, u32[]{:S(2)}) collective-permute-start(bf16[640,384]{1,0:T(8,128)(2,1)S(1)} %sum_pieces.7.refs_0_), channel_id=1, source_target_pairs={{0,8},{8,0},{16,24},{24,16},{1,9},{9,1},{17,25},{25,17},{2,10},{10... | collective-permute-start | bytes 1474568 | tf_op jit(solution)/shard_map/ppermute | solution.py:484
  37.3 8.5 %collective-permute-start.11 = (bf16[128,640]{1,0:T(8,128)(2,1)S(1)}, bf16[128,640]{1,0:T(8,128)(2,1)S(1)}, u32[]{:S(2)}, u32[]{:S(2)}) collective-permute-start(bf16[128,640]{1,0:T(8,128)(2,1)S(1)} %get-tuple-element.70), channel_id=1, source_target_pairs={{0,1},{1,0},{2,3},{3,2},{4,5},{5,4},{6,7},{7,6},{8,9},{9,8},{10,11... | collective-permute-start | bytes 491528 | tf_op jit(solution)/shard_map/ppermute | solution.py:484
  44.4 4.9 %collective-permute-start.14 = (bf16[128,384]{1,0:T(8,128)(2,1)S(1)}, bf16[128,384]{1,0:T(8,128)(2,1)S(1)}, u32[]{:S(2)}, u32[]{:S(2)}) collective-permute-start(bf16[128,384]{1,0:T(8,128)(2,1)S(1)} %get-tuple-element.75), channel_id=1, source_target_pairs={{0,1},{1,0},{2,3},{3,2},{4,5},{5,4},{6,7},{7,6},{8,9},{9,8},{10,11... | collective-permute-start | bytes 294920 | tf_op jit(solution)/shard_map/ppermute | solution.py:484
  45.9 5.1 %collective-permute-start.12 = (bf16[64,640]{1,0:T(8,128)(2,1)S(1)}, bf16[64,640]{1,0:T(8,128)(2,1)S(1)}, u32[]{:S(2)}, u32[]{:S(2)}) collective-permute-start(bf16[64,640]{1,0:T(8,128)(2,1)S(1)} %slice.50), channel_id=1, source_target_pairs={{0,2},{2,0},{4,6},{6,4},{1,3},{3,1},{5,7},{7,5},{8,10},{10,8},{12,... | collective-permute-start | bytes 245768 | tf_op jit(solution)/shard_map/ppermute | solution.py:484
  49.3 4.3 %collective-permute-start.15 = (bf16[64,384]{1,0:T(8,128)(2,1)S(1)}, bf16[64,384]{1,0:T(8,128)(2,1)S(1)}, u32[]{:S(2)}, u32[]{:S(2)}) collective-permute-start(bf16[64,384]{1,0:T(8,128)(2,1)S(1)} %slice.51), channel_id=1, source_target_pairs={{0,2},{2,0},{4,6},{6,4},{1,3},{3,1},{5,7},{7,5},{8,10},{10,8},{12,... | collective-permute-start | bytes 147464 | tf_op jit(solution)/shard_map/ppermute | solution.py:484
  51.0 5.8 %collective-permute-start.13 = (bf16[32,640]{1,0:T(8,128)(2,1)S(1)}, bf16[32,640]{1,0:T(8,128)(2,1)S(1)}, u32[]{:S(2)}, u32[]{:S(2)}) collective-permute-start(bf16[32,640]{1,0:T(8,128)(2,1)S(1)} %slice.52), channel_id=1, source_target_pairs={{0,4},{2,6},{4,0},{6,2},{1,5},{3,7},{5,1},{7,3},{8,12},{10,14},{12... | collective-permute-start | bytes 122888 | tf_op jit(solution)/shard_map/ppermute | solution.py:484
  53.7 4.8 %collective-permute-start.16 = (bf16[32,384]{1,0:T(8,128)(2,1)S(1)}, bf16[32,384]{1,0:T(8,128)(2,1)S(1)}, u32[]{:S(2)}, u32[]{:S(2)}) collective-permute-start(bf16[32,384]{1,0:T(8,128)(2,1)S(1)} %slice.53), channel_id=1, source_target_pairs={{0,4},{2,6},{4,0},{6,2},{1,5},{3,7},{5,1},{7,3},{8,12},{10,14},{12... | collective-permute-start | bytes 73736 | tf_op jit(solution)/shard_map/ppermute | solution.py:484

commit v9 on v8

--- a/solution.py
+++ b/solution.py
@@ -252,7 +252,7 @@
                     buffer.at[q, part, at], updated[q].at[at, columns[part]], out_sems.at[q, i]
                 )
             )
-            outgoing[-1].start()
+            outgoing[-1].start(priority=1)
         terms = jnp.dot(tok[:, at], results[0].astype(jnp.bfloat16), preferred_element_type=jnp.float32)
         products[part] = terms if products[part] is None else products[part] + terms
     stays = place[0] == place[1]
@@ -538,7 +538,7 @@
 
     cosine, sine = rotation_tables(lengths)
     ready = [*early, last]
-    attended = cache_attention(after(queries, *ready), cache_keys, cache_values, lengths, 0, row_count)
+    attended = cache_attention(after(queries, *ready, cosine, sine), cache_keys, cache_values, lengths, 0, row_count)
     distance = fsdp_count // 2
     step = (attended[1],)
     while distance:

time: 60.3 us -> 60.2 us (level)
  transfers between devices with their start and end apart: 17 -> 17, of which waited for: 7 -> 6; matrix products, arithmetic and copies ran while one was open for 1% -> 1% of each run, Pallas kernels for 45% -> 45%
where the time goes in v9:
time: 60.2 us; the launch traced here: 59.9 us
  Pallas kernels  29.9 us (50%)
  starting transfers between devices  23.4 us (39%)
  waiting for transfers between devices  5.11 us (8%)
  between operations  0.87 us (1%)
    ppermute x17, starting transfers between devices, swap(): return lax.ppermute(array, axis, [(i, i ^ bit) for i in range(size)])  23.4 us
    pallas_call x2, Pallas kernels, adam_units(): pl.pallas_call(functools.partial(adam_kernel, first, n, len(mine), len(pa...  12.7 us
    pallas_call x1, Pallas kernels, cache_attention(): pl.pallas_call(functools.partial(cache_kernel, heads, first), grid_spec=p...  6.71 us
    ppermute x17, waiting for transfers between devices, swap(): return lax.ppermute(array, axis, [(i, i ^ bit) for i in range(size)])  5.11 us
    pallas_call x3, Pallas kernels, cast_units(): pl.pallas_call(functools.partial(cast_kernel, wanted, n_units), in_specs=...  4.38 us
    pallas_call x2, Pallas kernels, merge(): pl.pallas_call(functools.partial(merge_kernel, [fold[2] for fold in folds...  3.12 us
    pallas_call x1, Pallas kernels, write_held(): pl.pallas_call(functools.partial(write_kernel, first, n), grid_spec=pltpu...  1.77 us
  transfers between devices with their start and end apart: 17, of which 6 were waited for; matrix products, arithmetic and copies ran while one was open for 1% of the time, Pallas kernels for 45%

profile of v9, /device:TPU:0, one launch (start us, length us, event | category | flops | bytes accessed | tf_op | source)
XLA Modules:
  0.0 59.9 jit_solution(7553456182760346227)
XLA Ops:
  0.6 1.3 %cast_units.3 = bf16[640,512]{1,0:T(8,128)(2,1)S(1)} custom-call(f32[640,2048]{1,0:T(8,128)} %bitcast.5), custom_call_target="tpu_custom_call" | custom-call | flops 1 | bytes 1 | tf_op jit(solution)/shard_map/cast_units/pallas_call | solution.py:124
  2.5 1.3 %cast_units.4.refs_0_ = bf16[640,512]{1,0:T(8,128)(2,1)S(1)} custom-call(f32[640,2048]{1,0:T(8,128)} %bitcast.6), custom_call_target="tpu_custom_call" | custom-call | flops 1 | bytes 1 | tf_op jit(solution)/shard_map/cast_units/pallas_call | solution.py:124
  4.4 2.9 %collective-permute-start.4 = (bf16[640,512]{1,0:T(8,128)(2,1)S(1)}, bf16[640,512]{1,0:T(8,128)(2,1)S(1)}, u32[]{:S(2)}, u32[]{:S(2)}) collective-permute-start(bf16[640,512]{1,0:T(8,128)(2,1)S(1)} %sum_pieces.4.refs_0_), channel_id=1, source_target_pairs={{0,16},{8,24},{16,0},{24,8},{1,17},{9,25},{17,1},{25,9},{2,18},{10... | collective-permute-start | bytes 1966088 | tf_op jit(solution)/shard_map/ppermute | solution.py:484
  7.6 0.6 token_pieces.1
  8.2 1.8 %cast_units.5 = (bf16[320,512]{1,0:T(8,128)(2,1)S(1)}, bf16[320,512]{1,0:T(8,128)(2,1)S(1)}, bf16[640,512]{1,0:T(8,128)(2,1)S(1)}) custom-call(f32[640,2048]{1,0:T(8,128)} %bitcast.7), custom_call_target="tpu_custom_call" | custom-call | flops 1 | bytes 1 | tf_op jit(solution)/shard_map/cast_units/pallas_call | solution.py:124
  10.7 2.7 %collective-permute-start.6 = (bf16[64,640]{1,0:T(8,128)(2,1)S(1)}, bf16[64,640]{1,0:T(8,128)(2,1)S(1)}, u32[]{:S(2)}, u32[]{:S(2)}) collective-permute-start(bf16[64,640]{1,0:T(8,128)(2,1)S(1)} %stack_blocks.2), channel_id=1, source_target_pairs={{0,4},{2,6},{4,0},{6,2},{1,5},{3,7},{5,1},{7,3},{8,12},{10,14},{12... | collective-permute-start | bytes 245768 | tf_op jit(solution)/shard_map/ppermute | solution.py:484
  13.5 0.6 %collective-permute-start.5 = (bf16[640,128]{1,0:T(8,128)(2,1)S(1)}, bf16[640,128]{1,0:T(8,128)(2,1)S(1)}, u32[]{:S(2)}, u32[]{:S(2)}) collective-permute-start(bf16[640,128]{1,0:T(8,128)(2,1)S(1)} %get-tuple-element.61.refs_1_), channel_id=1, source_target_pairs={{0,16},{8,24},{16,0},{24,8},{1,17},{9,25},{17,1},{25,9},{2,18},{10... | collective-permute-start | bytes 491528 | tf_op jit(solution)/shard_map/ppermute | solution.py:484
  14.2 6.7 %cache_attention.1 = (bf16[4,8,32,128]{3,2,1,0:T(8,128)(2,1)S(1)}, f32[4,8,32,128]{3,2,1,0:T(8,128)S(1)}, f32[4,8,32,128]{3,2,1,0:T(8,128)S(1)}) custom-call(s32[8]{0:T(128)S(1)} %copy-done.1, bf16[8,4,2560]{2,1,0:T(4,128)(2,1)} %q, bf16[8,512,512]{2,1,0:T(8,128)(2,1)} %k.1, bf16[8,512,512]{2,1,0:T(8,128)(2,1)} %v.1), custom_call_target="tpu_custom_call" | custom-call | flops 1 | bytes 17500000 | tf_op jit(solution)/shard_map/cache_attention/pallas_call | solution.py:389
  20.9 1.6 %collective-permute-start.7 = (bf16[64,640]{1,0:T(8,128)(2,1)S(1)}, bf16[64,640]{1,0:T(8,128)(2,1)S(1)}, u32[]{:S(2)}, u32[]{:S(2)}) collective-permute-start(bf16[64,640]{1,0:T(8,128)(2,1)S(1)} %stack_blocks.3), channel_id=1, source_target_pairs={{0,2},{2,0},{4,6},{6,4},{1,3},{3,1},{5,7},{7,5},{8,10},{10,8},{12,... | collective-permute-start | bytes 245768 | tf_op jit(solution)/shard_map/ppermute | solution.py:484
  22.6 1.5 %collective-permute-start.3 = (bf16[640,384]{1,0:T(8,128)(2,1)S(1)}, bf16[640,384]{1,0:T(8,128)(2,1)S(1)}, u32[]{:S(2)}, u32[]{:S(2)}) collective-permute-start(bf16[640,384]{1,0:T(8,128)(2,1)S(1)} %get-tuple-element.60.refs_0_), channel_id=1, source_target_pairs={{0,16},{8,24},{16,0},{24,8},{1,17},{9,25},{17,1},{25,9},{2,18},{10... | collective-permute-start | bytes 1474568 | tf_op jit(solution)/shard_map/ppermute | solution.py:484
  24.1 1.4 %collective-permute-done.7.refs_9_.refs_10_.refs_7_.refs_8_ = bf16[64,640]{1,0:T(8,128)(2,1)S(1)} collective-permute-done((bf16[64,640]{1,0:T(8,128)(2,1)S(1)}, bf16[64,640]{1,0:T(8,128)(2,1)S(1)}, u32[]{:S(2)}, u32[]{:S(2)}) %collective-permute-start.7) | collective-permute-done | bytes 81952 | tf_op jit(solution)/shard_map/ppermute | solution.py:484
  25.4 0.9 %collective-permute-done.5.refs_3_ = bf16[640,128]{1,0:T(8,128)(2,1)S(1)} collective-permute-done((bf16[640,128]{1,0:T(8,128)(2,1)S(1)}, bf16[640,128]{1,0:T(8,128)(2,1)S(1)}, u32[]{:S(2)}, u32[]{:S(2)}) %collective-permute-start.5) | collective-permute-done | bytes 163872 | tf_op jit(solution)/shard_map/ppermute | solution.py:484
  27.1 1.2 %collective-permute-done.8.refs_2_ = bf16[320,640]{1,0:T(8,128)(2,1)S(1)} collective-permute-done((bf16[320,640]{1,0:T(8,128)(2,1)S(1)}, bf16[320,640]{1,0:T(8,128)(2,1)S(1)}, u32[]{:S(2)}, u32[]{:S(2)}) %collective-permute-start.8) | collective-permute-done | bytes 409632 | tf_op jit(solution)/shard_map/ppermute | solution.py:484
  28.9 7.9 %adam_project.2 = (f32[640,2048]{1,0:T(8,128)}, f32[640,2048]{1,0:T(8,128)}, f32[640,2048]{1,0:T(8,128)}, bf16[128,640]{1,0:T(8,128)(2,1)S(1)}, f32[128,640]{1,0:T(8,128)S(1)}) custom-call(s32[6]{0:T(128)S(1)} %stack.19.place, bf16[320,640]{1,0:T(8,128)(2,1)S(1)} %get-tuple-element.68.refs_0_, bf16[320,640]{1,0:T(8,128)(2,1)S(1)} %get-tuple-element.69.refs_1_, ...), custom_call_target="tpu_custom_call" | custom-call | flops 1 | bytes 1 | tf_op jit(solution)/shard_map/adam_project/pallas_call | solution.py:278
  37.2 2.1 %collective-permute-start.11 = (bf16[128,640]{1,0:T(8,128)(2,1)S(1)}, bf16[128,640]{1,0:T(8,128)(2,1)S(1)}, u32[]{:S(2)}, u32[]{:S(2)}) collective-permute-start(bf16[128,640]{1,0:T(8,128)(2,1)S(1)} %get-tuple-element.70), channel_id=1, source_target_pairs={{0,1},{1,0},{2,3},{3,2},{4,5},{5,4},{6,7},{7,6},{8,9},{9,8},{10,11... | collective-permute-start | bytes 491528 | tf_op jit(solution)/shard_map/ppermute | solution.py:484
  39.3 4.8 %adam_project.3 = (f32[640,2048]{1,0:T(8,128)}, f32[640,2048]{1,0:T(8,128)}, f32[640,2048]{1,0:T(8,128)}, bf16[128,384]{1,0:T(8,128)(2,1)S(1)}, f32[128,384]{1,0...) custom-call(s32[6]{0:T(128)S(1)} %stack.19.place, ...), custom_call_target="tpu_custom_call", output_to_operand_aliasing={{0}: (10, {}), {1}: (11, {}), {2}: (12, {})} | custom-call | flops 1 | bytes 1 | tf_op jit(solution)/shard_map/adam_project/pallas_call | solution.py:278
  44.1 1.8 %collective-permute-start.14 = (bf16[128,384]{1,0:T(8,128)(2,1)S(1)}, bf16[128,384]{1,0:T(8,128)(2,1)S(1)}, u32[]{:S(2)}, u32[]{:S(2)}) collective-permute-start(bf16[128,384]{1,0:T(8,128)(2,1)S(1)} %get-tuple-element.75), channel_id=1, source_target_pairs={{0,1},{1,0},{2,3},{3,2},{4,5},{5,4},{6,7},{7,6},{8,9},{9,8},{10,11... | collective-permute-start | bytes 294920 | tf_op jit(solution)/shard_map/ppermute | solution.py:484
  45.9 1.6 %collective-permute-start.12 = (bf16[64,640]{1,0:T(8,128)(2,1)S(1)}, bf16[64,640]{1,0:T(8,128)(2,1)S(1)}, u32[]{:S(2)}, u32[]{:S(2)}) collective-permute-start(bf16[64,640]{1,0:T(8,128)(2,1)S(1)} %slice.50), channel_id=1, source_target_pairs={{0,2},{2,0},{4,6},{6,4},{1,3},{3,1},{5,7},{7,5},{8,10},{10,8},{12,... | collective-permute-start | bytes 245768 | tf_op jit(solution)/shard_map/ppermute | solution.py:484
  47.5 1.8 %write_held.1 = (f32[640,2048]{1,0:T(8,128)}, f32[640,2048]{1,0:T(8,128)}, f32[640,2048]{1,0:T(8,128)}) custom-call(s32[6]{0:T(128)S(1)} %stack.19.place, f32[384,384]{1,0:T(8,128)S(1)} %get-tuple-element.77.refs_0_, f32[384,384]{1,0:T(8,128)S(1)} %get-tuple-element.78.refs_1_, ...), custom_call_target="tpu_custom_call", output_to_operand_aliasing={{0}: (4, {}), {1}: (5, {}), {2}: (6, {})} | custom-call | flops 1 | bytes 5000000 | tf_op jit(solution)/shard_map/write_held/pallas_call | solution.py:321
  49.4 1.5 %collective-permute-start.15 = (bf16[64,384]{1,0:T(8,128)(2,1)S(1)}, bf16[64,384]{1,0:T(8,128)(2,1)S(1)}, u32[]{:S(2)}, u32[]{:S(2)}) collective-permute-start(bf16[64,384]{1,0:T(8,128)(2,1)S(1)} %slice.51), channel_id=1, source_target_pairs={{0,2},{2,0},{4,6},{6,4},{1,3},{3,1},{5,7},{7,5},{8,10},{10,8},{12,... | collective-permute-start | bytes 147464 | tf_op jit(solution)/shard_map/ppermute | solution.py:484
  50.9 2.7 %collective-permute-start.13 = (bf16[32,640]{1,0:T(8,128)(2,1)S(1)}, bf16[32,640]{1,0:T(8,128)(2,1)S(1)}, u32[]{:S(2)}, u32[]{:S(2)}) collective-permute-start(bf16[32,640]{1,0:T(8,128)(2,1)S(1)} %slice.52), channel_id=1, source_target_pairs={{0,4},{2,6},{4,0},{6,2},{1,5},{3,7},{5,1},{7,3},{8,12},{10,14},{12... | collective-permute-start | bytes 122888 | tf_op jit(solution)/shard_map/ppermute | solution.py:484
  53.6 2.6 %collective-permute-start.16 = (bf16[32,384]{1,0:T(8,128)(2,1)S(1)}, bf16[32,384]{1,0:T(8,128)(2,1)S(1)}, u32[]{:S(2)}, u32[]{:S(2)}) collective-permute-start(bf16[32,384]{1,0:T(8,128)(2,1)S(1)} %slice.53), channel_id=1, source_target_pairs={{0,4},{2,6},{4,0},{6,2},{1,5},{3,7},{5,1},{7,3},{8,12},{10,14},{12... | collective-permute-start | bytes 73736 | tf_op jit(solution)/shard_map/ppermute | solution.py:484
  56.2 1.6 %merge_new.2 = (bf16[8,4,1024]{2,1,0:T(4,128)(2,1)}, bf16[8,4,2560]{2,1,0:T(4,128)(2,1)}) custom-call(bf16[32,640]{1,0:T(8,128)(2,1)S(1)} %collective-permute-done.13.refs_0_, f32[32,640]{1,0:T(8,128)S(1)} %slice.39.refs_1_, f32[32,128]{1,0:T(8,128)S(1)} %get-tuple-element.98.refs_2_.refs_4_, f32[32,128]{1,0:T(8,128)S(1)} %get-tuple-element.99.refs_3_.refs_5_, ...), custom_call_target="tpu_custom_call" | custom-call | flops 1 | bytes 1 | tf_op jit(solution)/shard_map/merge_new/pallas_call | solution.py:469
  58.4 1.6 %merge_new.3 = (bf16[8,4,1024]{2,1,0:T(4,128)(2,1)}, bf16[8,4,2560]{2,1,0:T(4,128)(2,1)}) custom-call(bf16[32,640]{1,0:T(8,128)(2,1)S(1)} %collective-permute-done.13.refs_0_, f32[32,640]{1,0:T(8,128)S(1)} %slice.39.refs_1_, bf16[32,384]{1,0:T(8,128)(2,1)S(1)} %collective-permute-done.16.refs_2_, ...), custom_call_target="tpu_custom_call", output_to_operand_aliasing={{0}: (9, {}), {1}: (10, {})} | custom-call | flops 1 | bytes 1 | tf_op jit(solution)/shard_map/merge_new/pallas_call | solution.py:469
  (46 shorter events, 4.7 us)
Async XLA Ops:
  2.0 5.3 %copy-start.1 = (s32[8]{0:T(128)S(1)}, s32[8]{0:T(128)}, u32[]{:S(2)}) copy-start(s32[8]{0:T(128)} %lens.1) | copy-start | bytes 100
  2.0 5.6 %copy-start = (bf16[8,4,5120]{2,1,0:T(4,128)(2,1)S(1)}, bf16[8,4,5120]{2,1,0:T(4,128)(2,1)}, u32[]{:S(2)}) copy-start(bf16[8,4,5120]{2,1,0:T(4,128)(2,1)} %source) | copy-start | bytes 983044
  2.0 2.2 %collective-permute-start = (bf16[640,512]{1,0:T(8,128)(2,1)S(1)}, bf16[640,512]{1,0:T(8,128)(2,1)S(1)}, u32[]{:S(2)}, u32[]{:S(2)}) collective-permute-start(bf16[640,512]{1,0:T(8,128)(2,1)S(1)} %cast_units.3), channel_id=1, source_target_pairs={{0,8},{8,0},{16,24},{24,16},{1,9},{9,1},{17,25},{25,17},{2,10},{10... | collective-permute-start | bytes 1966088 | tf_op jit(solution)/shard_map/ppermute | solution.py:484
  4.4 22.0 %collective-permute-start.4 = (bf16[640,512]{1,0:T(8,128)(2,1)S(1)}, bf16[640,512]{1,0:T(8,128)(2,1)S(1)}, u32[]{:S(2)}, u32[]{:S(2)}) collective-permute-start(bf16[640,512]{1,0:T(8,128)(2,1)S(1)} %sum_pieces.4.refs_0_), channel_id=1, source_target_pairs={{0,16},{8,24},{16,0},{24,8},{1,17},{9,25},{17,1},{25,9},{2,18},{10... | collective-permute-start | bytes 1966088 | tf_op jit(solution)/shard_map/ppermute | solution.py:484
  9.9 3.4 %collective-permute-start.1 = (bf16[320,512]{1,0:T(8,128)(2,1)S(1)}, bf16[320,512]{1,0:T(8,128)(2,1)S(1)}, u32[]{:S(2)}, u32[]{:S(2)}) collective-permute-start(bf16[320,512]{1,0:T(8,128)(2,1)S(1)} %get-tuple-element.58), channel_id=1, source_target_pairs={{0,8},{8,0},{16,24},{24,16},{1,9},{9,1},{17,25},{25,17},{2,10},{10... | collective-permute-start | bytes 983048 | tf_op jit(solution)/shard_map/ppermute | solution.py:484
  10.0 3.3 %collective-permute-start.2 = (bf16[320,512]{1,0:T(8,128)(2,1)S(1)}, bf16[320,512]{1,0:T(8,128)(2,1)S(1)}, u32[]{:S(2)}, u32[]{:S(2)}) collective-permute-start(bf16[320,512]{1,0:T(8,128)(2,1)S(1)} %get-tuple-element.59), channel_id=1, source_target_pairs={{0,8},{8,0},{16,24},{24,16},{1,9},{9,1},{17,25},{25,17},{2,10},{10... | collective-permute-start | bytes 983048 | tf_op jit(solution)/shard_map/ppermute | solution.py:484
  10.7 10.2 %collective-permute-start.6 = (bf16[64,640]{1,0:T(8,128)(2,1)S(1)}, bf16[64,640]{1,0:T(8,128)(2,1)S(1)}, u32[]{:S(2)}, u32[]{:S(2)}) collective-permute-start(bf16[64,640]{1,0:T(8,128)(2,1)S(1)} %stack_blocks.2), channel_id=1, source_target_pairs={{0,4},{2,6},{4,0},{6,2},{1,5},{3,7},{5,1},{7,3},{8,12},{10,14},{12... | collective-permute-start | bytes 245768 | tf_op jit(solution)/shard_map/ppermute | solution.py:484
  13.5 12.8 %collective-permute-start.5 = (bf16[640,128]{1,0:T(8,128)(2,1)S(1)}, bf16[640,128]{1,0:T(8,128)(2,1)S(1)}, u32[]{:S(2)}, u32[]{:S(2)}) collective-permute-start(bf16[640,128]{1,0:T(8,128)(2,1)S(1)} %get-tuple-element.61.refs_1_), channel_id=1, source_target_pairs={{0,16},{8,24},{16,0},{24,8},{1,17},{9,25},{17,1},{25,9},{2,18},{10... | collective-permute-start | bytes 491528 | tf_op jit(solution)/shard_map/ppermute | solution.py:484
  20.9 4.5 %collective-permute-start.7 = (bf16[64,640]{1,0:T(8,128)(2,1)S(1)}, bf16[64,640]{1,0:T(8,128)(2,1)S(1)}, u32[]{:S(2)}, u32[]{:S(2)}) collective-permute-start(bf16[64,640]{1,0:T(8,128)(2,1)S(1)} %stack_blocks.3), channel_id=1, source_target_pairs={{0,2},{2,0},{4,6},{6,4},{1,3},{3,1},{5,7},{7,5},{8,10},{10,8},{12,... | collective-permute-start | bytes 245768 | tf_op jit(solution)/shard_map/ppermute | solution.py:484
  22.6 14.3 %collective-permute-start.3 = (bf16[640,384]{1,0:T(8,128)(2,1)S(1)}, bf16[640,384]{1,0:T(8,128)(2,1)S(1)}, u32[]{:S(2)}, u32[]{:S(2)}) collective-permute-start(bf16[640,384]{1,0:T(8,128)(2,1)S(1)} %get-tuple-element.60.refs_0_), channel_id=1, source_target_pairs={{0,16},{8,24},{16,0},{24,8},{1,17},{9,25},{17,1},{25,9},{2,18},{10... | collective-permute-start | bytes 1474568 | tf_op jit(solution)/shard_map/ppermute | solution.py:484
  26.6 1.8 %collective-permute-start.8 = (bf16[320,640]{1,0:T(8,128)(2,1)S(1)}, bf16[320,640]{1,0:T(8,128)(2,1)S(1)}, u32[]{:S(2)}, u32[]{:S(2)}) collective-permute-start(bf16[320,640]{1,0:T(8,128)(2,1)S(1)} %get-tuple-element.68.refs_0_), channel_id=1, source_target_pairs={{0,8},{8,0},{16,24},{24,16},{1,9},{9,1},{17,25},{25,17},{2,10},{10... | collective-permute-start | bytes 1228808 | tf_op jit(solution)/shard_map/ppermute | solution.py:484
  26.6 2.3 %collective-permute-start.9 = (bf16[320,640]{1,0:T(8,128)(2,1)S(1)}, bf16[320,640]{1,0:T(8,128)(2,1)S(1)}, u32[]{:S(2)}, u32[]{:S(2)}) collective-permute-start(bf16[320,640]{1,0:T(8,128)(2,1)S(1)} %get-tuple-element.69.refs_1_), channel_id=1, source_target_pairs={{0,8},{8,0},{16,24},{24,16},{1,9},{9,1},{17,25},{25,17},{2,10},{10... | collective-permute-start | bytes 1228808 | tf_op jit(solution)/shard_map/ppermute | solution.py:484
  37.0 2.3 %collective-permute-start.10 = (bf16[640,384]{1,0:T(8,128)(2,1)S(1)}, bf16[640,384]{1,0:T(8,128)(2,1)S(1)}, u32[]{:S(2)}, u32[]{:S(2)}) collective-permute-start(bf16[640,384]{1,0:T(8,128)(2,1)S(1)} %sum_pieces.7.refs_0_), channel_id=1, source_target_pairs={{0,8},{8,0},{16,24},{24,16},{1,9},{9,1},{17,25},{25,17},{2,10},{10... | collective-permute-start | bytes 1474568 | tf_op jit(solution)/shard_map/ppermute | solution.py:484
  37.2 8.6 %collective-permute-start.11 = (bf16[128,640]{1,0:T(8,128)(2,1)S(1)}, bf16[128,640]{1,0:T(8,128)(2,1)S(1)}, u32[]{:S(2)}, u32[]{:S(2)}) collective-permute-start(bf16[128,640]{1,0:T(8,128)(2,1)S(1)} %get-tuple-element.70), channel_id=1, source_target_pairs={{0,1},{1,0},{2,3},{3,2},{4,5},{5,4},{6,7},{7,6},{8,9},{9,8},{10,11... | collective-permute-start | bytes 491528 | tf_op jit(solution)/shard_map/ppermute | solution.py:484
  44.1 5.3 %collective-permute-start.14 = (bf16[128,384]{1,0:T(8,128)(2,1)S(1)}, bf16[128,384]{1,0:T(8,128)(2,1)S(1)}, u32[]{:S(2)}, u32[]{:S(2)}) collective-permute-start(bf16[128,384]{1,0:T(8,128)(2,1)S(1)} %get-tuple-element.75), channel_id=1, source_target_pairs={{0,1},{1,0},{2,3},{3,2},{4,5},{5,4},{6,7},{7,6},{8,9},{9,8},{10,11... | collective-permute-start | bytes 294920 | tf_op jit(solution)/shard_map/ppermute | solution.py:484
  45.9 4.9 %collective-permute-start.12 = (bf16[64,640]{1,0:T(8,128)(2,1)S(1)}, bf16[64,640]{1,0:T(8,128)(2,1)S(1)}, u32[]{:S(2)}, u32[]{:S(2)}) collective-permute-start(bf16[64,640]{1,0:T(8,128)(2,1)S(1)} %slice.50), channel_id=1, source_target_pairs={{0,2},{2,0},{4,6},{6,4},{1,3},{3,1},{5,7},{7,5},{8,10},{10,8},{12,... | collective-permute-start | bytes 245768 | tf_op jit(solution)/shard_map/ppermute | solution.py:484
  49.4 4.2 %collective-permute-start.15 = (bf16[64,384]{1,0:T(8,128)(2,1)S(1)}, bf16[64,384]{1,0:T(8,128)(2,1)S(1)}, u32[]{:S(2)}, u32[]{:S(2)}) collective-permute-start(bf16[64,384]{1,0:T(8,128)(2,1)S(1)} %slice.51), channel_id=1, source_target_pairs={{0,2},{2,0},{4,6},{6,4},{1,3},{3,1},{5,7},{7,5},{8,10},{10,8},{12,... | collective-permute-start | bytes 147464 | tf_op jit(solution)/shard_map/ppermute | solution.py:484
  50.9 5.4 %collective-permute-start.13 = (bf16[32,640]{1,0:T(8,128)(2,1)S(1)}, bf16[32,640]{1,0:T(8,128)(2,1)S(1)}, u32[]{:S(2)}, u32[]{:S(2)}) collective-permute-start(bf16[32,640]{1,0:T(8,128)(2,1)S(1)} %slice.52), channel_id=1, source_target_pairs={{0,4},{2,6},{4,0},{6,2},{1,5},{3,7},{5,1},{7,3},{8,12},{10,14},{12... | collective-permute-start | bytes 122888 | tf_op jit(solution)/shard_map/ppermute | solution.py:484
  53.6 4.8 %collective-permute-start.16 = (bf16[32,384]{1,0:T(8,128)(2,1)S(1)}, bf16[32,384]{1,0:T(8,128)(2,1)S(1)}, u32[]{:S(2)}, u32[]{:S(2)}) collective-permute-start(bf16[32,384]{1,0:T(8,128)(2,1)S(1)} %slice.53), channel_id=1, source_target_pairs={{0,4},{2,6},{4,0},{6,2},{1,5},{3,7},{5,1},{7,3},{8,12},{10,14},{12... | collective-permute-start | bytes 73736 | tf_op jit(solution)/shard_map/ppermute | solution.py:484

commit v10 on v9

--- a/solution.py
+++ b/solution.py
@@ -447,12 +447,15 @@
         scale = jnp.exp(old_highest - highest)
         denominator = jnp.sum(weight, axis=-1, keepdims=True) + scale * old_total
         out = jnp.dot(weight.astype(jnp.bfloat16), values, preferred_element_type=jnp.float32)
-        out = (out + scale * rows_of(acc, u)) / denominator
+        out = (out + scale * rows_of(acc, u)) * (1.0 / denominator)
         for r in range(row_count):
-            for g in range(PER_GROUP):
-                at_row = r * SLOT + g * STEPS
-                at_col = (u * PER_GROUP + g) * HD
-                context[r, :, at_col : at_col + HD] = out[at_row : at_row + STEPS].astype(jnp.bfloat16)
+            pieces = [
+                out[r * SLOT + g * STEPS : r * SLOT + (g + 1) * STEPS] for g in range(PER_GROUP)
+            ]
+            at_col = u * PER_GROUP * HD
+            context[r, :, at_col : at_col + PER_GROUP * HD] = jnp.concatenate(pieces, axis=1).astype(
+                jnp.bfloat16
+            )
 
 
 def merge(folds, cosine, sine, attended, row_count, first, n_heads, previous):

time: 60.2 us -> 60.2 us (level)
  no operation moved by 1% of the time
where the time goes in v10:
time: 60.2 us; the launch traced here: 59.9 us
  Pallas kernels  29.9 us (50%)
  starting transfers between devices  23.4 us (39%)
  waiting for transfers between devices  5.13 us (9%)
  between operations  0.87 us (1%)
    ppermute x17, starting transfers between devices, swap(): return lax.ppermute(array, axis, [(i, i ^ bit) for i in range(size)])  23.4 us
    pallas_call x2, Pallas kernels, adam_units(): pl.pallas_call(functools.partial(adam_kernel, first, n, len(mine), len(pa...  12.6 us
    pallas_call x1, Pallas kernels, cache_attention(): pl.pallas_call(functools.partial(cache_kernel, heads, first), grid_spec=p...  6.71 us
    ppermute x17, waiting for transfers between devices, swap(): return lax.ppermute(array, axis, [(i, i ^ bit) for i in range(size)])  5.13 us
    pallas_call x3, Pallas kernels, cast_units(): pl.pallas_call(functools.partial(cast_kernel, wanted, n_units), in_specs=...  4.38 us
    pallas_call x2, Pallas kernels, merge(): pl.pallas_call(functools.partial(merge_kernel, [fold[2] for fold in folds...  3.11 us
    pallas_call x1, Pallas kernels, write_held(): pl.pallas_call(functools.partial(write_kernel, first, n), grid_spec=pltpu...  1.77 us
  transfers between devices with their start and end apart: 17, of which 6 were waited for; matrix products, arithmetic and copies ran while one was open for 1% of the time, Pallas kernels for 45%

profile of v10, /device:TPU:0, one launch (start us, length us, event | category | flops | bytes accessed | tf_op | source)
XLA Modules:
  0.0 59.9 jit_solution(4080077197178554470)
XLA Ops:
  0.6 1.3 %cast_units.3 = bf16[640,512]{1,0:T(8,128)(2,1)S(1)} custom-call(f32[640,2048]{1,0:T(8,128)} %bitcast.5), custom_call_target="tpu_custom_call" | custom-call | flops 1 | bytes 1 | tf_op jit(solution)/shard_map/cast_units/pallas_call | solution.py:124
  2.5 1.3 %cast_units.4.refs_0_ = bf16[640,512]{1,0:T(8,128)(2,1)S(1)} custom-call(f32[640,2048]{1,0:T(8,128)} %bitcast.6), custom_call_target="tpu_custom_call" | custom-call | flops 1 | bytes 1 | tf_op jit(solution)/shard_map/cast_units/pallas_call | solution.py:124
  4.4 2.9 %collective-permute-start.4 = (bf16[640,512]{1,0:T(8,128)(2,1)S(1)}, bf16[640,512]{1,0:T(8,128)(2,1)S(1)}, u32[]{:S(2)}, u32[]{:S(2)}) collective-permute-start(bf16[640,512]{1,0:T(8,128)(2,1)S(1)} %sum_pieces.4.refs_0_), channel_id=1, source_target_pairs={{0,16},{8,24},{16,0},{24,8},{1,17},{9,25},{17,1},{25,9},{2,18},{10... | collective-permute-start | bytes 1966088 | tf_op jit(solution)/shard_map/ppermute | solution.py:487
  7.6 0.6 token_pieces.1
  8.2 1.8 %cast_units.5 = (bf16[320,512]{1,0:T(8,128)(2,1)S(1)}, bf16[320,512]{1,0:T(8,128)(2,1)S(1)}, bf16[640,512]{1,0:T(8,128)(2,1)S(1)}) custom-call(f32[640,2048]{1,0:T(8,128)} %bitcast.7), custom_call_target="tpu_custom_call" | custom-call | flops 1 | bytes 1 | tf_op jit(solution)/shard_map/cast_units/pallas_call | solution.py:124
  10.7 2.7 %collective-permute-start.6 = (bf16[64,640]{1,0:T(8,128)(2,1)S(1)}, bf16[64,640]{1,0:T(8,128)(2,1)S(1)}, u32[]{:S(2)}, u32[]{:S(2)}) collective-permute-start(bf16[64,640]{1,0:T(8,128)(2,1)S(1)} %stack_blocks.2), channel_id=1, source_target_pairs={{0,4},{2,6},{4,0},{6,2},{1,5},{3,7},{5,1},{7,3},{8,12},{10,14},{12... | collective-permute-start | bytes 245768 | tf_op jit(solution)/shard_map/ppermute | solution.py:487
  13.5 0.6 %collective-permute-start.5 = (bf16[640,128]{1,0:T(8,128)(2,1)S(1)}, bf16[640,128]{1,0:T(8,128)(2,1)S(1)}, u32[]{:S(2)}, u32[]{:S(2)}) collective-permute-start(bf16[640,128]{1,0:T(8,128)(2,1)S(1)} %get-tuple-element.61.refs_1_), channel_id=1, source_target_pairs={{0,16},{8,24},{16,0},{24,8},{1,17},{9,25},{17,1},{25,9},{2,18},{10... | collective-permute-start | bytes 491528 | tf_op jit(solution)/shard_map/ppermute | solution.py:487
  14.2 6.7 %cache_attention.1 = (bf16[4,8,32,128]{3,2,1,0:T(8,128)(2,1)S(1)}, f32[4,8,32,128]{3,2,1,0:T(8,128)S(1)}, f32[4,8,32,128]{3,2,1,0:T(8,128)S(1)}) custom-call(s32[8]{0:T(128)S(1)} %copy-done.1, bf16[8,4,2560]{2,1,0:T(4,128)(2,1)} %q, bf16[8,512,512]{2,1,0:T(8,128)(2,1)} %k.1, bf16[8,512,512]{2,1,0:T(8,128)(2,1)} %v.1), custom_call_target="tpu_custom_call" | custom-call | flops 1 | bytes 17500000 | tf_op jit(solution)/shard_map/cache_attention/pallas_call | solution.py:389
  20.9 1.6 %collective-permute-start.7 = (bf16[64,640]{1,0:T(8,128)(2,1)S(1)}, bf16[64,640]{1,0:T(8,128)(2,1)S(1)}, u32[]{:S(2)}, u32[]{:S(2)}) collective-permute-start(bf16[64,640]{1,0:T(8,128)(2,1)S(1)} %stack_blocks.3), channel_id=1, source_target_pairs={{0,2},{2,0},{4,6},{6,4},{1,3},{3,1},{5,7},{7,5},{8,10},{10,8},{12,... | collective-permute-start | bytes 245768 | tf_op jit(solution)/shard_map/ppermute | solution.py:487
  22.6 1.5 %collective-permute-start.3 = (bf16[640,384]{1,0:T(8,128)(2,1)S(1)}, bf16[640,384]{1,0:T(8,128)(2,1)S(1)}, u32[]{:S(2)}, u32[]{:S(2)}) collective-permute-start(bf16[640,384]{1,0:T(8,128)(2,1)S(1)} %get-tuple-element.60.refs_0_), channel_id=1, source_target_pairs={{0,16},{8,24},{16,0},{24,8},{1,17},{9,25},{17,1},{25,9},{2,18},{10... | collective-permute-start | bytes 1474568 | tf_op jit(solution)/shard_map/ppermute | solution.py:487
  24.1 1.4 %collective-permute-done.7.refs_9_.refs_10_.refs_7_.refs_8_ = bf16[64,640]{1,0:T(8,128)(2,1)S(1)} collective-permute-done((bf16[64,640]{1,0:T(8,128)(2,1)S(1)}, bf16[64,640]{1,0:T(8,128)(2,1)S(1)}, u32[]{:S(2)}, u32[]{:S(2)}) %collective-permute-start.7) | collective-permute-done | bytes 81952 | tf_op jit(solution)/shard_map/ppermute | solution.py:487
  25.4 0.9 %collective-permute-done.5.refs_3_ = bf16[640,128]{1,0:T(8,128)(2,1)S(1)} collective-permute-done((bf16[640,128]{1,0:T(8,128)(2,1)S(1)}, bf16[640,128]{1,0:T(8,128)(2,1)S(1)}, u32[]{:S(2)}, u32[]{:S(2)}) %collective-permute-start.5) | collective-permute-done | bytes 163872 | tf_op jit(solution)/shard_map/ppermute | solution.py:487
  27.1 1.2 %collective-permute-done.8.refs_2_ = bf16[320,640]{1,0:T(8,128)(2,1)S(1)} collective-permute-done((bf16[320,640]{1,0:T(8,128)(2,1)S(1)}, bf16[320,640]{1,0:T(8,128)(2,1)S(1)}, u32[]{:S(2)}, u32[]{:S(2)}) %collective-permute-start.8) | collective-permute-done | bytes 409632 | tf_op jit(solution)/shard_map/ppermute | solution.py:487
  28.9 7.9 %adam_project.2 = (f32[640,2048]{1,0:T(8,128)}, f32[640,2048]{1,0:T(8,128)}, f32[640,2048]{1,0:T(8,128)}, bf16[128,640]{1,0:T(8,128)(2,1)S(1)}, f32[128,640]{1,0:T(8,128)S(1)}) custom-call(s32[6]{0:T(128)S(1)} %stack.19.place, bf16[320,640]{1,0:T(8,128)(2,1)S(1)} %get-tuple-element.68.refs_0_, bf16[320,640]{1,0:T(8,128)(2,1)S(1)} %get-tuple-element.69.refs_1_, ...), custom_call_target="tpu_custom_call" | custom-call | flops 1 | bytes 1 | tf_op jit(solution)/shard_map/adam_project/pallas_call | solution.py:278
  37.2 2.1 %collective-permute-start.11 = (bf16[128,640]{1,0:T(8,128)(2,1)S(1)}, bf16[128,640]{1,0:T(8,128)(2,1)S(1)}, u32[]{:S(2)}, u32[]{:S(2)}) collective-permute-start(bf16[128,640]{1,0:T(8,128)(2,1)S(1)} %get-tuple-element.70), channel_id=1, source_target_pairs={{0,1},{1,0},{2,3},{3,2},{4,5},{5,4},{6,7},{7,6},{8,9},{9,8},{10,11... | collective-permute-start | bytes 491528 | tf_op jit(solution)/shard_map/ppermute | solution.py:487
  39.3 4.8 %adam_project.3 = (f32[640,2048]{1,0:T(8,128)}, f32[640,2048]{1,0:T(8,128)}, f32[640,2048]{1,0:T(8,128)}, bf16[128,384]{1,0:T(8,128)(2,1)S(1)}, f32[128,384]{1,0...) custom-call(s32[6]{0:T(128)S(1)} %stack.19.place, ...), custom_call_target="tpu_custom_call", output_to_operand_aliasing={{0}: (10, {}), {1}: (11, {}), {2}: (12, {})} | custom-call | flops 1 | bytes 1 | tf_op jit(solution)/shard_map/adam_project/pallas_call | solution.py:278
  44.1 1.8 %collective-permute-start.14 = (bf16[128,384]{1,0:T(8,128)(2,1)S(1)}, bf16[128,384]{1,0:T(8,128)(2,1)S(1)}, u32[]{:S(2)}, u32[]{:S(2)}) collective-permute-start(bf16[128,384]{1,0:T(8,128)(2,1)S(1)} %get-tuple-element.75), channel_id=1, source_target_pairs={{0,1},{1,0},{2,3},{3,2},{4,5},{5,4},{6,7},{7,6},{8,9},{9,8},{10,11... | collective-permute-start | bytes 294920 | tf_op jit(solution)/shard_map/ppermute | solution.py:487
  45.9 1.6 %collective-permute-start.12 = (bf16[64,640]{1,0:T(8,128)(2,1)S(1)}, bf16[64,640]{1,0:T(8,128)(2,1)S(1)}, u32[]{:S(2)}, u32[]{:S(2)}) collective-permute-start(bf16[64,640]{1,0:T(8,128)(2,1)S(1)} %slice.50), channel_id=1, source_target_pairs={{0,2},{2,0},{4,6},{6,4},{1,3},{3,1},{5,7},{7,5},{8,10},{10,8},{12,... | collective-permute-start | bytes 245768 | tf_op jit(solution)/shard_map/ppermute | solution.py:487
  47.5 1.8 %write_held.1 = (f32[640,2048]{1,0:T(8,128)}, f32[640,2048]{1,0:T(8,128)}, f32[640,2048]{1,0:T(8,128)}) custom-call(s32[6]{0:T(128)S(1)} %stack.19.place, f32[384,384]{1,0:T(8,128)S(1)} %get-tuple-element.77.refs_0_, f32[384,384]{1,0:T(8,128)S(1)} %get-tuple-element.78.refs_1_, ...), custom_call_target="tpu_custom_call", output_to_operand_aliasing={{0}: (4, {}), {1}: (5, {}), {2}: (6, {})} | custom-call | flops 1 | bytes 5000000 | tf_op jit(solution)/shard_map/write_held/pallas_call | solution.py:321
  49.4 1.5 %collective-permute-start.15 = (bf16[64,384]{1,0:T(8,128)(2,1)S(1)}, bf16[64,384]{1,0:T(8,128)(2,1)S(1)}, u32[]{:S(2)}, u32[]{:S(2)}) collective-permute-start(bf16[64,384]{1,0:T(8,128)(2,1)S(1)} %slice.51), channel_id=1, source_target_pairs={{0,2},{2,0},{4,6},{6,4},{1,3},{3,1},{5,7},{7,5},{8,10},{10,8},{12,... | collective-permute-start | bytes 147464 | tf_op jit(solution)/shard_map/ppermute | solution.py:487
  50.9 2.7 %collective-permute-start.13 = (bf16[32,640]{1,0:T(8,128)(2,1)S(1)}, bf16[32,640]{1,0:T(8,128)(2,1)S(1)}, u32[]{:S(2)}, u32[]{:S(2)}) collective-permute-start(bf16[32,640]{1,0:T(8,128)(2,1)S(1)} %slice.52), channel_id=1, source_target_pairs={{0,4},{2,6},{4,0},{6,2},{1,5},{3,7},{5,1},{7,3},{8,12},{10,14},{12... | collective-permute-start | bytes 122888 | tf_op jit(solution)/shard_map/ppermute | solution.py:487
  53.6 2.6 %collective-permute-start.16 = (bf16[32,384]{1,0:T(8,128)(2,1)S(1)}, bf16[32,384]{1,0:T(8,128)(2,1)S(1)}, u32[]{:S(2)}, u32[]{:S(2)}) collective-permute-start(bf16[32,384]{1,0:T(8,128)(2,1)S(1)} %slice.53), channel_id=1, source_target_pairs={{0,4},{2,6},{4,0},{6,2},{1,5},{3,7},{5,1},{7,3},{8,12},{10,14},{12... | collective-permute-start | bytes 73736 | tf_op jit(solution)/shard_map/ppermute | solution.py:487
  56.2 1.5 %merge_new.2 = (bf16[8,4,1024]{2,1,0:T(4,128)(2,1)}, bf16[8,4,2560]{2,1,0:T(4,128)(2,1)}) custom-call(bf16[32,640]{1,0:T(8,128)(2,1)S(1)} %collective-permute-done.13.refs_0_, f32[32,640]{1,0:T(8,128)S(1)} %slice.39.refs_1_, f32[32,128]{1,0:T(8,128)S(1)} %get-tuple-element.98.refs_2_.refs_4_, f32[32,128]{1,0:T(8,128)S(1)} %get-tuple-element.99.refs_3_.refs_5_, ...), custom_call_target="tpu_custom_call" | custom-call | flops 1 | bytes 1 | tf_op jit(solution)/shard_map/merge_new/pallas_call | solution.py:472
  58.4 1.6 %merge_new.3 = (bf16[8,4,1024]{2,1,0:T(4,128)(2,1)}, bf16[8,4,2560]{2,1,0:T(4,128)(2,1)}) custom-call(bf16[32,640]{1,0:T(8,128)(2,1)S(1)} %collective-permute-done.13.refs_0_, f32[32,640]{1,0:T(8,128)S(1)} %slice.39.refs_1_, bf16[32,384]{1,0:T(8,128)(2,1)S(1)} %collective-permute-done.16.refs_2_, ...), custom_call_target="tpu_custom_call", output_to_operand_aliasing={{0}: (9, {}), {1}: (10, {})} | custom-call | flops 1 | bytes 1 | tf_op jit(solution)/shard_map/merge_new/pallas_call | solution.py:472
  (46 shorter events, 4.7 us)
Async XLA Ops:
  2.0 5.3 %copy-start.1 = (s32[8]{0:T(128)S(1)}, s32[8]{0:T(128)}, u32[]{:S(2)}) copy-start(s32[8]{0:T(128)} %lens.1) | copy-start | bytes 100
  2.0 5.6 %copy-start = (bf16[8,4,5120]{2,1,0:T(4,128)(2,1)S(1)}, bf16[8,4,5120]{2,1,0:T(4,128)(2,1)}, u32[]{:S(2)}) copy-start(bf16[8,4,5120]{2,1,0:T(4,128)(2,1)} %source) | copy-start | bytes 983044
  2.0 2.2 %collective-permute-start = (bf16[640,512]{1,0:T(8,128)(2,1)S(1)}, bf16[640,512]{1,0:T(8,128)(2,1)S(1)}, u32[]{:S(2)}, u32[]{:S(2)}) collective-permute-start(bf16[640,512]{1,0:T(8,128)(2,1)S(1)} %cast_units.3), channel_id=1, source_target_pairs={{0,8},{8,0},{16,24},{24,16},{1,9},{9,1},{17,25},{25,17},{2,10},{10... | collective-permute-start | bytes 1966088 | tf_op jit(solution)/shard_map/ppermute | solution.py:487
  4.4 22.0 %collective-permute-start.4 = (bf16[640,512]{1,0:T(8,128)(2,1)S(1)}, bf16[640,512]{1,0:T(8,128)(2,1)S(1)}, u32[]{:S(2)}, u32[]{:S(2)}) collective-permute-start(bf16[640,512]{1,0:T(8,128)(2,1)S(1)} %sum_pieces.4.refs_0_), channel_id=1, source_target_pairs={{0,16},{8,24},{16,0},{24,8},{1,17},{9,25},{17,1},{25,9},{2,18},{10... | collective-permute-start | bytes 1966088 | tf_op jit(solution)/shard_map/ppermute | solution.py:487
  9.9 3.4 %collective-permute-start.1 = (bf16[320,512]{1,0:T(8,128)(2,1)S(1)}, bf16[320,512]{1,0:T(8,128)(2,1)S(1)}, u32[]{:S(2)}, u32[]{:S(2)}) collective-permute-start(bf16[320,512]{1,0:T(8,128)(2,1)S(1)} %get-tuple-element.58), channel_id=1, source_target_pairs={{0,8},{8,0},{16,24},{24,16},{1,9},{9,1},{17,25},{25,17},{2,10},{10... | collective-permute-start | bytes 983048 | tf_op jit(solution)/shard_map/ppermute | solution.py:487
  10.0 3.3 %collective-permute-start.2 = (bf16[320,512]{1,0:T(8,128)(2,1)S(1)}, bf16[320,512]{1,0:T(8,128)(2,1)S(1)}, u32[]{:S(2)}, u32[]{:S(2)}) collective-permute-start(bf16[320,512]{1,0:T(8,128)(2,1)S(1)} %get-tuple-element.59), channel_id=1, source_target_pairs={{0,8},{8,0},{16,24},{24,16},{1,9},{9,1},{17,25},{25,17},{2,10},{10... | collective-permute-start | bytes 983048 | tf_op jit(solution)/shard_map/ppermute | solution.py:487
  10.7 10.2 %collective-permute-start.6 = (bf16[64,640]{1,0:T(8,128)(2,1)S(1)}, bf16[64,640]{1,0:T(8,128)(2,1)S(1)}, u32[]{:S(2)}, u32[]{:S(2)}) collective-permute-start(bf16[64,640]{1,0:T(8,128)(2,1)S(1)} %stack_blocks.2), channel_id=1, source_target_pairs={{0,4},{2,6},{4,0},{6,2},{1,5},{3,7},{5,1},{7,3},{8,12},{10,14},{12... | collective-permute-start | bytes 245768 | tf_op jit(solution)/shard_map/ppermute | solution.py:487
  13.5 12.8 %collective-permute-start.5 = (bf16[640,128]{1,0:T(8,128)(2,1)S(1)}, bf16[640,128]{1,0:T(8,128)(2,1)S(1)}, u32[]{:S(2)}, u32[]{:S(2)}) collective-permute-start(bf16[640,128]{1,0:T(8,128)(2,1)S(1)} %get-tuple-element.61.refs_1_), channel_id=1, source_target_pairs={{0,16},{8,24},{16,0},{24,8},{1,17},{9,25},{17,1},{25,9},{2,18},{10... | collective-permute-start | bytes 491528 | tf_op jit(solution)/shard_map/ppermute | solution.py:487
  20.9 4.5 %collective-permute-start.7 = (bf16[64,640]{1,0:T(8,128)(2,1)S(1)}, bf16[64,640]{1,0:T(8,128)(2,1)S(1)}, u32[]{:S(2)}, u32[]{:S(2)}) collective-permute-start(bf16[64,640]{1,0:T(8,128)(2,1)S(1)} %stack_blocks.3), channel_id=1, source_target_pairs={{0,2},{2,0},{4,6},{6,4},{1,3},{3,1},{5,7},{7,5},{8,10},{10,8},{12,... | collective-permute-start | bytes 245768 | tf_op jit(solution)/shard_map/ppermute | solution.py:487
  22.6 14.3 %collective-permute-start.3 = (bf16[640,384]{1,0:T(8,128)(2,1)S(1)}, bf16[640,384]{1,0:T(8,128)(2,1)S(1)}, u32[]{:S(2)}, u32[]{:S(2)}) collective-permute-start(bf16[640,384]{1,0:T(8,128)(2,1)S(1)} %get-tuple-element.60.refs_0_), channel_id=1, source_target_pairs={{0,16},{8,24},{16,0},{24,8},{1,17},{9,25},{17,1},{25,9},{2,18},{10... | collective-permute-start | bytes 1474568 | tf_op jit(solution)/shard_map/ppermute | solution.py:487
  26.6 1.8 %collective-permute-start.8 = (bf16[320,640]{1,0:T(8,128)(2,1)S(1)}, bf16[320,640]{1,0:T(8,128)(2,1)S(1)}, u32[]{:S(2)}, u32[]{:S(2)}) collective-permute-start(bf16[320,640]{1,0:T(8,128)(2,1)S(1)} %get-tuple-element.68.refs_0_), channel_id=1, source_target_pairs={{0,8},{8,0},{16,24},{24,16},{1,9},{9,1},{17,25},{25,17},{2,10},{10... | collective-permute-start | bytes 1228808 | tf_op jit(solution)/shard_map/ppermute | solution.py:487
  26.6 2.3 %collective-permute-start.9 = (bf16[320,640]{1,0:T(8,128)(2,1)S(1)}, bf16[320,640]{1,0:T(8,128)(2,1)S(1)}, u32[]{:S(2)}, u32[]{:S(2)}) collective-permute-start(bf16[320,640]{1,0:T(8,128)(2,1)S(1)} %get-tuple-element.69.refs_1_), channel_id=1, source_target_pairs={{0,8},{8,0},{16,24},{24,16},{1,9},{9,1},{17,25},{25,17},{2,10},{10... | collective-permute-start | bytes 1228808 | tf_op jit(solution)/shard_map/ppermute | solution.py:487
  37.0 2.3 %collective-permute-start.10 = (bf16[640,384]{1,0:T(8,128)(2,1)S(1)}, bf16[640,384]{1,0:T(8,128)(2,1)S(1)}, u32[]{:S(2)}, u32[]{:S(2)}) collective-permute-start(bf16[640,384]{1,0:T(8,128)(2,1)S(1)} %sum_pieces.7.refs_0_), channel_id=1, source_target_pairs={{0,8},{8,0},{16,24},{24,16},{1,9},{9,1},{17,25},{25,17},{2,10},{10... | collective-permute-start | bytes 1474568 | tf_op jit(solution)/shard_map/ppermute | solution.py:487
  37.2 8.6 %collective-permute-start.11 = (bf16[128,640]{1,0:T(8,128)(2,1)S(1)}, bf16[128,640]{1,0:T(8,128)(2,1)S(1)}, u32[]{:S(2)}, u32[]{:S(2)}) collective-permute-start(bf16[128,640]{1,0:T(8,128)(2,1)S(1)} %get-tuple-element.70), channel_id=1, source_target_pairs={{0,1},{1,0},{2,3},{3,2},{4,5},{5,4},{6,7},{7,6},{8,9},{9,8},{10,11... | collective-permute-start | bytes 491528 | tf_op jit(solution)/shard_map/ppermute | solution.py:487
  44.1 5.3 %collective-permute-start.14 = (bf16[128,384]{1,0:T(8,128)(2,1)S(1)}, bf16[128,384]{1,0:T(8,128)(2,1)S(1)}, u32[]{:S(2)}, u32[]{:S(2)}) collective-permute-start(bf16[128,384]{1,0:T(8,128)(2,1)S(1)} %get-tuple-element.75), channel_id=1, source_target_pairs={{0,1},{1,0},{2,3},{3,2},{4,5},{5,4},{6,7},{7,6},{8,9},{9,8},{10,11... | collective-permute-start | bytes 294920 | tf_op jit(solution)/shard_map/ppermute | solution.py:487
  45.9 4.9 %collective-permute-start.12 = (bf16[64,640]{1,0:T(8,128)(2,1)S(1)}, bf16[64,640]{1,0:T(8,128)(2,1)S(1)}, u32[]{:S(2)}, u32[]{:S(2)}) collective-permute-start(bf16[64,640]{1,0:T(8,128)(2,1)S(1)} %slice.50), channel_id=1, source_target_pairs={{0,2},{2,0},{4,6},{6,4},{1,3},{3,1},{5,7},{7,5},{8,10},{10,8},{12,... | collective-permute-start | bytes 245768 | tf_op jit(solution)/shard_map/ppermute | solution.py:487
  49.4 4.2 %collective-permute-start.15 = (bf16[64,384]{1,0:T(8,128)(2,1)S(1)}, bf16[64,384]{1,0:T(8,128)(2,1)S(1)}, u32[]{:S(2)}, u32[]{:S(2)}) collective-permute-start(bf16[64,384]{1,0:T(8,128)(2,1)S(1)} %slice.51), channel_id=1, source_target_pairs={{0,2},{2,0},{4,6},{6,4},{1,3},{3,1},{5,7},{7,5},{8,10},{10,8},{12,... | collective-permute-start | bytes 147464 | tf_op jit(solution)/shard_map/ppermute | solution.py:487
  50.9 5.4 %collective-permute-start.13 = (bf16[32,640]{1,0:T(8,128)(2,1)S(1)}, bf16[32,640]{1,0:T(8,128)(2,1)S(1)}, u32[]{:S(2)}, u32[]{:S(2)}) collective-permute-start(bf16[32,640]{1,0:T(8,128)(2,1)S(1)} %slice.52), channel_id=1, source_target_pairs={{0,4},{2,6},{4,0},{6,2},{1,5},{3,7},{5,1},{7,3},{8,12},{10,14},{12... | collective-permute-start | bytes 122888 | tf_op jit(solution)/shard_map/ppermute | solution.py:487
  53.6 4.8 %collective-permute-start.16 = (bf16[32,384]{1,0:T(8,128)(2,1)S(1)}, bf16[32,384]{1,0:T(8,128)(2,1)S(1)}, u32[]{:S(2)}, u32[]{:S(2)}) collective-permute-start(bf16[32,384]{1,0:T(8,128)(2,1)S(1)} %slice.53), channel_id=1, source_target_pairs={{0,4},{2,6},{4,0},{6,2},{1,5},{3,7},{5,1},{7,3},{8,12},{10,14},{12... | collective-permute-start | bytes 73736 | tf_op jit(solution)/shard_map/ppermute | solution.py:487
